TPU v7x, 32 devices: a whole 2x2x4 slice. The times are simulated.
32 devices in a mesh: groups: 2 (over x), row: 16 (over z, y, core).
Axes of the slice: x: 2, y: 2, z: 4, core: 2. Of those that a mesh axis runs over, the one named last changes fastest.
Arguments:
- pair_rep: bfloat16 [128, 64, 128], P(('groups', 'row')), parts along dimension 0, may hold values from -6 to 6
- pair_mask: int32 [128, 64], P(('groups', 'row')), parts along dimension 0, may hold values 0 or 1
- proj_weight: bfloat16 [2, 128, 256], replicated, may hold values from -0.5 to 0.5
- gate_weight: bfloat16 [2, 128, 128], replicated, may hold values from -0.5 to 0.5
- out_weight: bfloat16 [2, 64, 128], replicated, may hold values from -0.75 to 0.75
- norm_gain: float32 [2, 128], replicated, may hold values from 0.1 to 1.9
- mid_gain: float32 [2, 64], replicated, may hold values from 0.1 to 1.9
Outputs:
- pair_out: bfloat16 [128, 64, 128], P(('groups', 'row')), parts along dimension 0
There are 2 independent parts, one for each index of `groups`. A program takes and returns all parts, laid end to end along the dimension named above; an argument that names none is the same for every part. Nothing has to cross between parts.
All inputs are finite; a program needn't handle non-finite values. No bound on the sum of `pair_mask` on one device may be relied on, other than what follows from the above.
Results may differ from a plain program's by a relative error of at most 0.013.
Values may be sent and summed in bfloat16 or wider, within the bound.
No kernel may reach another device: no remote copies, remote signals or barrier semaphores. Data moves between devices by JAX's collectives and lax.ppermute only.
A program may use at most 192 MiB of HBM per device.

v0:
```python
import jax
import jax.numpy as jnp
from jax import lax
from jax.sharding import PartitionSpec as P

HW = 64


small_eps = 1e-05


def layer_norm(values, gain, axis, epsilon):
    average = jnp.mean(values, axis=axis, keepdims=True)
    centred = values - average
    variance = jnp.mean(centred * centred, axis=axis, keepdims=True)
    return centred * lax.rsqrt(variance + epsilon) * gain


def outgoing_sum(factor_left, factor_right):
    return jnp.einsum(
        "cik,cjk->cij",
        factor_left,
        lax.all_gather(factor_right, "row", axis=1, tiled=True),
        preferred_element_type=jnp.float32,
    )


def incoming_sum(factor_left, factor_right):
    row_count = factor_left.shape[1]
    own_offset = lax.axis_index("row") * row_count
    columns = lax.dynamic_slice_in_dim(
        lax.all_gather(factor_left, "row", axis=1, tiled=True), own_offset, row_count, 2
    )
    return jnp.einsum(
        "cki,ckj->cij",
        columns,
        lax.all_gather(factor_right, "row", axis=1, tiled=True),
        preferred_element_type=jnp.float32,
    )


def update_half(pair_now, pair_mask, proj_one, gate_one, out_one, gain_one, mid_one, orient):
    floats = pair_now.astype(jnp.float32)
    normed = layer_norm(floats, gain_one, -1, small_eps).astype(jnp.bfloat16)
    projected = jnp.einsum("ijd,de->eij", normed, proj_one, preferred_element_type=jnp.float32)
    weight_mask = pair_mask.astype(jnp.float32)[None]
    factor_left = (weight_mask * jax.nn.sigmoid(projected[HW : 2 * HW]) * projected[:HW]).astype(
        jnp.bfloat16
    )
    factor_right = (
        weight_mask * jax.nn.sigmoid(projected[3 * HW :]) * projected[2 * HW : 3 * HW]
    ).astype(jnp.bfloat16)
    if orient == 0:
        summed = outgoing_sum(factor_left, factor_right)
    else:
        summed = incoming_sum(factor_left, factor_right)
    hidden = layer_norm(summed, mid_one[:, None, None], 0, small_eps).astype(jnp.bfloat16)
    gating = jax.nn.sigmoid(
        jnp.einsum("ijd,de->ije", normed, gate_one, preferred_element_type=jnp.float32)
    )
    update = jnp.einsum("cij,cd->ijd", hidden, out_one, preferred_element_type=jnp.float32)
    return (floats + gating * update).astype(jnp.bfloat16)


def shards(pair_rep, pair_mask, proj_weight, gate_weight, out_weight, norm_gain, mid_gain):
    current = pair_rep
    for orient in range(2):
        current = update_half(
            current,
            pair_mask,
            proj_weight[orient],
            gate_weight[orient],
            out_weight[orient],
            norm_gain[orient],
            mid_gain[orient],
            orient,
        )
    return current


def solution(mesh):
    return jax.shard_map(
        shards,
        mesh=mesh,
        in_specs=(
            P(("groups", "row"), None, None),
            P(("groups", "row"), None),
            P(),
            P(),
            P(),
            P(),
            P(),
        ),
        out_specs=P(("groups", "row"), None, None),
        check_vma=False,
    )
```

profile of v0, /device:TPU:0, one launch (start us, length us, event | category | flops | bytes accessed | tf_op | source)
XLA Modules:
  0.0 83.4 jit_solution(13543905198973211041)
XLA Ops:
  0.0 0.8 slice_bitcast_fusion.1
  0.8 0.8 slice_bitcast_fusion
  1.5 0.7 convert_element_type.42
  2.2 0.9 %convert_reduce_fusion = f32[4,64]{1,0:T(4,128)S(1)} fusion(bf16[4,64,128]{2,1,0:T(8,128)(2,1)} %param.7), kind=kLoop, calls=%fused_computation.23 | loop fusion | flops 65280 | bytes 66560 | tf_op jit(solution)/shard_map/reduce_sum | solution.py:13
  3.2 0.2 fusion.20
  3.4 1.1 %convolution_bitcast_fusion.1 = f32[256,4,64]{0,2,1:T(8,128)S(1)} fusion(bf16[4,64,128]{2,1,0:T(8,128)(2,1)S(1)} %copy-done, bf16[2,128,256]{2,1,0:T(8,128)(2,1)} %param.9, f32[128]{0:T(128)S(1)} %get-tuple-element.12, f32[4,64]{1,0:T(4,128)S(1)} %add_rsqrt_fusion.3, f32[4,64]{1,0:T(4,128)S(1)} %broadcast_multiply_fusion.3), kind=kOutput, calls=%fused_computation.1 | convolution fusion | flops 16941056 | bytes 395776 | tf_op jit(solution)/shard_map/ijd,de->eij/dot_general | solution.py:45
  4.5 0.2 fusion.33
  4.7 0.1 copy.14
  4.8 0.1 copy.15
  4.9 26.2 %all_gather.9 = bf16[64,64,64]{2,0,1:T(8,128)(2,1)S(1)} all-gather(bf16[64,4,64]{2,0,1:T(8,128)(2,1)S(1)} %copy.14), channel_id=1, replica_groups=mesh['groups'=2,'row'=16] {'row'}, dimensions={1}, use_global_device_ids=true | all-gather | bytes 557056 | tf_op jit(solution)/shard_map/all_gather | solution.py:23
  31.1 0.8 fusion.73
  31.9 0.1 multiply_reduce_fusion.2
  32.0 0.1 multiply_convert_fusion.2
  32.2 0.6 copy-done.2
  32.8 0.2 fusion.49
  33.0 0.6 copy-done.3
  33.6 0.4 fusion.74
  34.0 0.0 copy-start.1
  34.0 0.2 multiply_reduce_fusion.1
  34.2 0.7 copy-done.1
  34.9 0.2 convolution_bitcast_fusion
  35.1 0.2 fusion.23
  35.3 0.1 copy.20
  35.4 0.1 copy.18
  35.5 20.5 %all_gather.10 = bf16[64,64,64]{2,0,1:T(8,128)(2,1)S(1)} all-gather(bf16[64,4,64]{2,0,1:T(8,128)(2,1)S(1)} %copy.18), channel_id=1, replica_groups=mesh['groups'=2,'row'=16] {'row'}, dimensions={1}, use_global_device_ids=true | all-gather | bytes 557056 | tf_op jit(solution)/shard_map/all_gather | solution.py:32
  56.0 0.4 constant_dynamic-slice_fusion
  56.4 24.4 %all_gather.11 = bf16[64,64,64]{2,0,1:T(8,128)(2,1)S(1)} all-gather(bf16[64,4,64]{2,0,1:T(8,128)(2,1)S(1)} %copy.20), channel_id=1, replica_groups=mesh['groups'=2,'row'=16] {'row'}, dimensions={1}, use_global_device_ids=true | all-gather | bytes 557056 | tf_op jit(solution)/shard_map/all_gather | solution.py:37
  80.8 1.3 %fusion.75 = (f32[4,64]{1,0:T(4,128)S(1)}, f32[64,4,64]{2,1,0:T(4,128)S(1)}) fusion(bf16[64,64,64]{2,0,1:T(8,128)(2,1)S(1)} %all_gather.11, bf16[64,64,4]{2,0,1:T(8,128)(2,1)S(1)} %constant_dynamic-slice_fusion), kind=kOutput, calls=%fused_computation.106 | convolution fusion | flops 2113280 | bytes 623616 | tf_op jit(solution)/shard_map/cki,ckj->cij/dot_general | solution.py:34
  82.1 0.1 multiply_reduce_fusion
  82.2 0.1 multiply_convert_fusion
  82.3 0.2 fusion.47
  82.5 0.9 %fusion.10 = bf16[4,64,128]{2,1,0:T(8,128)(2,1)} fusion(f32[4,64,128]{2,1,0:T(8,128)S(1)} %get-tuple-element.16, f32[4,64,128]{2,1,0:T(8,128)S(1)} %fusion.47, f32[128]{0:T(128)S(1)} %get-tuple-element.11, f32[4,64]{1,0:T(4,128)S(1)} %add_rsqrt_fusion.1, f32[4,64]{1,0:T(4,128)S(1)} %broadcast_multiply_fusion.2, bf16[2,128,128]{2,1,0:T(8,128)(2,1)S(1)} %copy-done.3), kind=kOutput, calls=%fused_computation.14 | convolution fusion | flops 8716288 | bytes 496128 | tf_op jit(solution)/shard_map/ijd,de->ije/dot_general | solution.py:59
  (12 shorter events, 0.1 us)
Async XLA Ops:
  0.0 3.2 %copy-start = (bf16[4,64,128]{2,1,0:T(8,128)(2,1)S(1)}, bf16[4,64,128]{2,1,0:T(8,128)(2,1)}, u32[]{:S(2)}) copy-start(bf16[4,64,128]{2,1,0:T(8,128)(2,1)} %param.7) | copy-start | bytes 196612
  32.0 0.8 copy-start.2
  32.8 0.8 %copy-start.3 = (bf16[2,128,128]{2,1,0:T(8,128)(2,1)S(1)}, bf16[2,128,128]{2,1,0:T(8,128)(2,1)}, u32[]{:S(2)}) copy-start(bf16[2,128,128]{2,1,0:T(8,128)(2,1)} %param.10) | copy-start | bytes 196612
  34.0 0.9 %copy-start.1 = (bf16[2,128,256]{2,1,0:T(8,128)(2,1)S(1)}, bf16[2,128,256]{2,1,0:T(8,128)(2,1)}, u32[]{:S(2)}) copy-start(bf16[2,128,256]{2,1,0:T(8,128)(2,1)} %param.9) | copy-start | bytes 393220
where the time goes:
time: 83.9 us; the launch traced here: 83.4 us
  blocking collectives  71.1 us (85%)
  matrix products  5.09 us (6%)
  local copies, waits for them, and re-layouts  4.29 us (5%)
  other arithmetic  2.81 us (3%)
    all_gather x1, blocking collectives, outgoing_sum(): lax.all_gather(factor_right, 'row', axis=1, tiled=True)  26.2 us
    all_gather x1, blocking collectives, incoming_sum(): lax.all_gather(factor_right, 'row', axis=1, tiled=True)  24.4 us
    all_gather x1, blocking collectives, incoming_sum(): lax.all_gather(factor_left, 'row', axis=1, tiled=True)  20.5 us
    unnamed x8, local copies, waits for them, and re-layouts  1.97 us

commit v1 on v0

v1 whole, which is shorter than its diff:
```python
import jax
import jax.numpy as jnp
from jax import lax
from jax.sharding import PartitionSpec as P

EPS = 1e-05


def layer_norm(values, gain, axis):
    average = jnp.mean(values, axis=axis, keepdims=True)
    centred = values - average
    variance = jnp.mean(centred * centred, axis=axis, keepdims=True)
    return centred * lax.rsqrt(variance + EPS) * gain


def factors(normed, mask, proj):
    hw = proj.shape[1] // 4
    projected = jnp.einsum("ijd,de->eij", normed, proj, preferred_element_type=jnp.float32)
    left = mask * jax.nn.sigmoid(projected[hw : 2 * hw]) * projected[:hw]
    right = mask * jax.nn.sigmoid(projected[3 * hw :]) * projected[2 * hw : 3 * hw]
    return left.astype(jnp.bfloat16), right.astype(jnp.bfloat16)


def gather_rows(factor):
    c, rows, k = factor.shape
    half = rows // 2
    packed = jnp.concatenate([factor[:, :half], factor[:, half:]], axis=-1).transpose(1, 0, 2)
    everywhere = lax.all_gather(packed, "row", axis=0, tiled=False)
    n = everywhere.shape[0]
    both = jnp.stack([everywhere[..., :k], everywhere[..., k:]], axis=1)
    return both.reshape(n * rows, c, k).transpose(1, 0, 2)


def finish(floats, normed, summed, gate, out, mid):
    hidden = layer_norm(summed, mid[:, None, None], 0).astype(jnp.bfloat16)
    gating = jax.nn.sigmoid(
        jnp.einsum("ijd,de->ije", normed, gate, preferred_element_type=jnp.float32)
    )
    update = jnp.einsum("cij,cd->ijd", hidden, out, preferred_element_type=jnp.float32)
    return (floats + gating * update).astype(jnp.bfloat16)


def shards(pair_rep, pair_mask, proj_weight, gate_weight, out_weight, norm_gain, mid_gain):
    mask = pair_mask.astype(jnp.float32)[None]
    rows, tokens = pair_mask.shape
    devices = tokens // rows

    floats = pair_rep.astype(jnp.float32)
    normed = layer_norm(floats, norm_gain[0], -1).astype(jnp.bfloat16)
    left, right = factors(normed, mask, proj_weight[0])
    summed = jnp.einsum("cik,cjk->cij", left, gather_rows(right), preferred_element_type=jnp.float32)
    current = finish(floats, normed, summed, gate_weight[0], out_weight[0], mid_gain[0])

    floats = current.astype(jnp.float32)
    normed = layer_norm(floats, norm_gain[1], -1).astype(jnp.bfloat16)
    left, right = factors(normed, mask, proj_weight[1])
    c = left.shape[0]
    blocks = left.reshape(c, rows, devices, rows).transpose(2, 1, 3, 0)
    blocks = blocks.reshape(devices, rows * rows * c // 128, 128)
    columns = lax.all_to_all(blocks, "row", 0, 0, tiled=True)
    columns = columns.reshape(devices * rows, rows, c).transpose(2, 0, 1)
    summed = jnp.einsum(
        "cki,ckj->cij", columns, gather_rows(right), preferred_element_type=jnp.float32
    )
    return finish(floats, normed, summed, gate_weight[1], out_weight[1], mid_gain[1])


def solution(mesh):
    return jax.shard_map(
        shards,
        mesh=mesh,
        in_specs=(P(("groups", "row")), P(("groups", "row")), P(), P(), P(), P(), P()),
        out_specs=P(("groups", "row")),
        check_vma=False,
    )
```

time: 83.9 us -> 68.4 us (0.82)
  blocking collectives: 71.1 us -> 47.8 us
  starting transfers between devices: 0 us -> 3.5 us
  other arithmetic: 2.81 us -> 5.7 us
  local copies, waits for them, and re-layouts: 4.29 us -> 6.66 us
  matrix products: 5.09 us -> 4.02 us
    all_gather x3 -> x2, blocking collectives: 71.1 us -> 47.8 us  [gather_rows(): everywhere = lax.all_gather(packed, 'row', axis=0, tiled=False)]
    another operation x0 -> x2, other arithmetic: none -> 3.52 us  [gather_rows(): both = jnp.stack([everywhere[..., :k], everywhere[..., k:]], axis=1)]
    all_to_all x0 -> x1, starting transfers between devices: none -> 3.5 us  [shards(): columns = lax.all_to_all(blocks, 'row', 0, 0, tiled=True)]
    unnamed x8 -> x14, local copies, waits for them, and re-layouts: 1.97 us -> 3.06 us
    another operation x0 -> x1, local copies, waits for them, and re-layouts: none -> 1.08 us  [gather_rows(): both = jnp.stack([everywhere[..., :k], everywhere[..., k:]], axis=1)]
    dot_general x8, matrix products: 5.09 us -> 4.02 us  [the longest x2 1.35 us: factors(): jnp.einsum('ijd,de->eij', normed, proj, preferred_element_type=jnp.float32)]
    reshape x0 -> x4, local copies, waits for them, and re-layouts: none -> 0.95 us  [the longest x1 0.71 us: shards(): blocks = blocks.reshape(devices, rows * rows * c // 128, 128)]
  transfers between devices with their start and end apart: 0 -> 1, of which waited for: 0 -> 0; matrix products, arithmetic and copies ran while one was open for 0% -> 5% of each run, Pallas kernels for 0% -> 0%
where the time goes in v1:
time: 68.4 us; the launch traced here: 68 us
  blocking collectives  47.8 us (70%)
  local copies, waits for them, and re-layouts  6.66 us (10%)
  other arithmetic  5.7 us (8%)
  matrix products  4.02 us (6%)
  starting transfers between devices  3.5 us (5%)
    all_gather x2, blocking collectives, gather_rows(): everywhere = lax.all_gather(packed, 'row', axis=0, tiled=False)  47.8 us
    another operation x2, other arithmetic, gather_rows(): both = jnp.stack([everywhere[..., :k], everywhere[..., k:]], axis=1)  3.52 us
    all_to_all x1, starting transfers between devices, shards(): columns = lax.all_to_all(blocks, 'row', 0, 0, tiled=True)  3.5 us
    unnamed x14, local copies, waits for them, and re-layouts  3.06 us
  transfers between devices with their start and end apart: 1, of which 0 were waited for; matrix products, arithmetic and copies ran while one was open for 5% of the time, Pallas kernels for 0%

profile of v1, /device:TPU:0, one launch (start us, length us, event | category | flops | bytes accessed | tf_op | source)
XLA Modules:
  0.0 68.0 jit_solution(14118655273347542321)
XLA Ops:
  0.0 0.8 %slice_bitcast_fusion.1 = (f32[128]{0:T(128)S(1)}, f32[128]{0:T(128)S(1)}) fusion(f32[2,128]{1,0:T(2,128)} %param.12), kind=kLoop, calls=%fused_computation.106 | loop fusion | bytes 2048 | tf_op jit(solution)/shard_map/mul | solution.py:13
  0.8 1.0 %convert_reduce_fusion = f32[4,64]{1,0:T(4,128)S(1)} fusion(bf16[4,64,128]{2,1,0:T(8,128)(2,1)} %param.7), kind=kLoop, calls=%fused_computation.24 | loop fusion | flops 65280 | bytes 66560 | tf_op jit(solution)/shard_map/reduce_sum | solution.py:10
  1.8 0.2 fusion.15
  2.0 1.1 %convolution_bitcast_fusion.1 = f32[256,4,64]{0,2,1:T(8,128)S(1)} fusion(bf16[4,64,128]{2,1,0:T(8,128)(2,1)S(1)} %copy-done, bf16[2,128,256]{2,1,0:T(8,128)(2,1)} %param.9, f32[128]{0:T(128)S(1)} %get-tuple-element.20, f32[4,64]{1,0:T(4,128)S(1)} %add_rsqrt_fusion.3, f32[4,64]{1,0:T(4,128)S(1)} %broadcast_multiply_fusion.3), kind=kOutput, calls=%fused_computation.1 | convolution fusion | flops 16941056 | bytes 395776 | tf_op jit(solution)/shard_map/ijd,de->eij/dot_general | solution.py:18
  3.1 0.2 fusion.28
  3.4 0.1 copy.23
  3.5 24.6 %all-gather = bf16[32,64,128]{2,1,0:T(8,128)(2,1)S(1)} all-gather(bf16[2,64,128]{2,1,0:T(8,128)(2,1)S(1)} %copy.20), channel_id=2, replica_groups=mesh['groups'=2,'row'=16] {'row'}, dimensions={0}, use_global_device_ids=true | all-gather | bytes 557056 | tf_op jit(solution)/shard_map/all_gather | solution.py:28
  28.1 0.2 fusion.71
  28.4 1.1 %copy_bitcast_fusion.2 = (bf16[16,1,2,64,64]{4,2,1,0,3:T(2,128)(2,1)S(1)}, bf16[16,1,2,64,64]{4,2,1,0,3:T(2,128)(2,1)S(1)}) fusion(bf16[16,2,64,64]{3,2,1,0:T(8,128)(2,1)S(1)} %get-tuple-element.8, bf16[16,2,64,64]{3,2,1,0:T(8,128)(2,1)S(1)} %get-tuple-element.7), kind=kLoop, calls=%fused_computation.21 | loop fusion | bytes 1048576 | tf_op jit(solution)/shard_map/stack | solution.py:30
  29.4 1.8 %pad_maximum_fusion = bf16[16,2,2,64,64]{4,2,1,0,3:T(2,128)(2,1)S(1)} fusion(bf16[16,1,2,64,64]{4,2,1,0,3:T(2,128)(2,1)S(1)} %get-tuple-element.27, bf16[16,1,2,64,64]{4,2,1,0,3:T(2,128)(2,1)S(1)} %get-tuple-element.28), kind=kLoop, calls=%fused_computation.17 | loop fusion | flops 262144 | bytes 1048576 | tf_op jit(solution)/shard_map/stack | solution.py:30
  31.2 0.7 fusion.74
  32.0 0.1 multiply_convert_fusion.2
  32.1 0.6 copy-done.2
  32.7 0.2 fusion.46
  32.9 0.6 copy-done.5
  33.6 0.4 fusion.75
  34.0 0.2 multiply_reduce_fusion.1
  34.1 0.7 %copy-done.1 = bf16[2,128,256]{2,1,0:T(8,128)(2,1)S(1)} copy-done((bf16[2,128,256]{2,1,0:T(8,128)(2,1)S(1)}, bf16[2,128,256]{2,1,0:T(8,128)(2,1)}, u32[]{:S(2)}) %copy-start.1) | copy-done | bytes 131096
  34.8 0.3 convolution_bitcast_fusion
  35.1 0.2 fusion.23
  35.3 0.7 %reshape.70 = bf16[16,8,128]{2,1,0:T(8,128)(2,1)} reshape(bf16[16,4,4,64]{3,2,1,0:T(4,128)(2,1)S(1)} %bitcast.79) | data formatting | bytes 65536 | tf_op jit(solution)/shard_map/reshape | solution.py:59
  36.0 3.5 %all-to-all-start = ((bf16[16,8,128]{2,1,0:T(8,128)(2,1)}), bf16[16,8,128]{2,1,0:T(8,128)(2,1)S(1)}, u32[]{:S(2)}, u32[]{:S(2)}) async-start(bf16[16,8,128]{2,1,0:T(8,128)(2,1)} %reshape.70), calls=%async_computation | async-start | bytes 65536 | tf_op jit(solution)/shard_map/all_to_all | solution.py:60
  39.7 23.2 %all-gather.1 = bf16[32,64,128]{2,1,0:T(8,128)(2,1)S(1)} all-gather(bf16[2,64,128]{2,1,0:T(8,128)(2,1)S(1)} %copy.27), channel_id=3, replica_groups=mesh['groups'=2,'row'=16] {'row'}, dimensions={0}, use_global_device_ids=true | all-gather | bytes 557056 | tf_op jit(solution)/shard_map/all_gather | solution.py:28
  62.9 0.2 fusion.70
  63.1 0.5 copy.45
  63.7 0.5 copy.44
  64.2 1.8 %pad_maximum_fusion.1 = bf16[16,2,2,64,64]{4,2,1,0,3:T(2,128)(2,1)S(1)} fusion(bf16[16,1,2,64,64]{4,2,1,0,3:T(2,128)(2,1)S(1)} %bitcast.77, bf16[16,1,2,64,64]{4,2,1,0,3:T(2,128)(2,1)S(1)} %bitcast.76), kind=kLoop, calls=%fused_computation.18 | loop fusion | flops 262144 | bytes 1048576 | tf_op jit(solution)/shard_map/stack | solution.py:30
  66.1 0.1 copy.26
  66.2 0.4 fusion.76
  66.7 0.1 multiply_convert_fusion
  66.9 0.2 fusion.44
  67.0 0.9 %fusion.10 = bf16[4,64,128]{2,1,0:T(8,128)(2,1)} fusion(f32[4,64,128]{2,1,0:T(8,128)S(1)} %get-tuple-element.24, f32[4,64,128]{2,1,0:T(8,128)S(1)} %fusion.44, f32[128]{0:T(128)S(1)} %get-tuple-element.19, f32[4,64]{1,0:T(4,128)S(1)} %add_rsqrt_fusion.1, f32[4,64]{1,0:T(4,128)S(1)} %broadcast_multiply_fusion.2, bf16[2,128,128]{2,1,0:T(8,128)(2,1)S(1)} %copy-done.5), kind=kOutput, calls=%fused_computation.14 | convolution fusion | flops 8716288 | bytes 496128 | tf_op jit(solution)/shard_map/ijd,de->ije/dot_general | solution.py:37
  (30 shorter events, 0.6 us)
Async XLA Ops:
  0.0 0.8 %copy-start.4 = (f32[2,64]{1,0:T(2,128)S(1)}, f32[2,64]{1,0:T(2,128)}, u32[]{:S(2)}) copy-start(f32[2,64]{1,0:T(2,128)} %param.13) | copy-start | bytes 1540
  0.0 0.8 %copy-start.3 = (s32[4,64]{1,0:T(4,128)S(1)}, s32[4,64]{1,0:T(4,128)}, u32[]{:S(2)}) copy-start(s32[4,64]{1,0:T(4,128)} %param.8) | copy-start | bytes 3076
  0.0 1.8 %copy-start = (bf16[4,64,128]{2,1,0:T(8,128)(2,1)S(1)}, bf16[4,64,128]{2,1,0:T(8,128)(2,1)}, u32[]{:S(2)}) copy-start(bf16[4,64,128]{2,1,0:T(8,128)(2,1)} %param.7) | copy-start | bytes 196612
  32.0 0.8 %copy-start.2 = (bf16[2,64,128]{2,1,0:T(8,128)(2,1)S(1)}, bf16[2,64,128]{2,1,0:T(8,128)(2,1)}, u32[]{:S(2)}) copy-start(bf16[2,64,128]{2,1,0:T(8,128)(2,1)} %param.11) | copy-start | bytes 98308
  32.7 0.8 %copy-start.5 = (bf16[2,128,128]{2,1,0:T(8,128)(2,1)S(1)}, bf16[2,128,128]{2,1,0:T(8,128)(2,1)}, u32[]{:S(2)}) copy-start(bf16[2,128,128]{2,1,0:T(8,128)(2,1)} %param.10) | copy-start | bytes 196612
  33.9 0.9 %copy-start.1 = (bf16[2,128,256]{2,1,0:T(8,128)(2,1)S(1)}, bf16[2,128,256]{2,1,0:T(8,128)(2,1)}, u32[]{:S(2)}) copy-start(bf16[2,128,256]{2,1,0:T(8,128)(2,1)} %param.9) | copy-start | bytes 393220
  36.0 30.0 %all-to-all-start = ((bf16[16,8,128]{2,1,0:T(8,128)(2,1)}), bf16[16,8,128]{2,1,0:T(8,128)(2,1)S(1)}, u32[]{:S(2)}, u32[]{:S(2)}) async-start(bf16[16,8,128]{2,1,0:T(8,128)(2,1)} %reshape.70), calls=%async_computation | async-start | bytes 65536 | tf_op jit(solution)/shard_map/all_to_all | solution.py:60

commit v2 on v1

v2 whole, which is shorter than its diff:
```python
import jax
import jax.numpy as jnp
from jax import lax
from jax.sharding import PartitionSpec as P

EPS = 1e-05


def layer_norm(values, gain, axis):
    average = jnp.mean(values, axis=axis, keepdims=True)
    centred = values - average
    variance = jnp.mean(centred * centred, axis=axis, keepdims=True)
    return centred * lax.rsqrt(variance + EPS) * gain


def by_device(proj, devices):
    d = proj.shape[0]
    grouped = proj.reshape(d, 2, 2, devices, -1).transpose(2, 0, 3, 1, 4)
    return grouped.reshape(2, d, -1)


def triangle(pair, mask, proj, gate, out, gain, mid, orient):
    rows, tokens, _ = pair.shape
    devices = tokens // rows
    hw = out.shape[0]
    floats = pair.astype(jnp.float32)
    normed = layer_norm(floats, gain, -1).astype(jnp.bfloat16)
    flat = normed.reshape(rows * tokens, -1)
    weights = by_device(proj, devices)
    value = jnp.einsum("pd,de->ep", flat, weights[0], preferred_element_type=jnp.float32)
    gates = jnp.einsum("pd,de->ep", flat, weights[1], preferred_element_type=jnp.float32)
    factor = (mask * jax.nn.sigmoid(gates) * value).astype(jnp.bfloat16)
    factor = lax.all_to_all(factor.reshape(devices, -1, rows * tokens), "row", 0, 0, tiled=True)
    c = hw // devices
    factor = factor.reshape(devices, 2, c, rows, tokens).transpose(1, 2, 0, 3, 4)
    left, right = factor.reshape(2, c, tokens, tokens)
    spec = "cik,cjk->cij" if orient == 0 else "cki,ckj->cij"
    summed = jnp.einsum(spec, left, right, preferred_element_type=jnp.float32)
    summed = summed.astype(jnp.bfloat16).reshape(c, devices, rows * tokens).transpose(1, 0, 2)
    summed = lax.all_to_all(summed, "row", 0, 0, tiled=True)
    summed = summed.reshape(hw, rows * tokens).astype(jnp.float32)
    hidden = layer_norm(summed, mid[:, None], 0).astype(jnp.bfloat16)
    gating = jax.nn.sigmoid(jnp.dot(flat, gate, preferred_element_type=jnp.float32))
    update = jnp.einsum("cp,cd->pd", hidden, out, preferred_element_type=jnp.float32)
    return (floats + (gating * update).reshape(pair.shape)).astype(jnp.bfloat16)


def factors(normed, mask, proj):
    hw = proj.shape[1] // 4
    projected = jnp.einsum("ijd,de->eij", normed, proj, preferred_element_type=jnp.float32)
    left = mask * jax.nn.sigmoid(projected[hw : 2 * hw]) * projected[:hw]
    right = mask * jax.nn.sigmoid(projected[3 * hw :]) * projected[2 * hw : 3 * hw]
    return left.astype(jnp.bfloat16), right.astype(jnp.bfloat16)


def triangle_gathered(pair, mask, proj, gate, out, gain, mid, orient):
    rows, tokens, _ = pair.shape
    devices = tokens // rows
    floats = pair.astype(jnp.float32)
    normed = layer_norm(floats, gain, -1).astype(jnp.bfloat16)
    left, right = factors(normed, mask.reshape(1, rows, tokens), proj)
    everywhere = lax.all_gather(right, "row", axis=1, tiled=True)
    if orient == 1:
        c = left.shape[0]
        blocks = left.reshape(c, rows, devices, rows).transpose(2, 1, 3, 0)
        left = lax.all_to_all(blocks, "row", 0, 0, tiled=True)
        left = left.reshape(tokens, rows, c).transpose(2, 0, 1)
    spec = "cik,cjk->cij" if orient == 0 else "cki,ckj->cij"
    summed = jnp.einsum(spec, left, everywhere, preferred_element_type=jnp.float32)
    hidden = layer_norm(summed, mid[:, None, None], 0).astype(jnp.bfloat16)
    gating = jax.nn.sigmoid(
        jnp.einsum("ijd,de->ije", normed, gate, preferred_element_type=jnp.float32)
    )
    update = jnp.einsum("cij,cd->ijd", hidden, out, preferred_element_type=jnp.float32)
    return (floats + gating * update).astype(jnp.bfloat16)


def shards(pair_rep, pair_mask, proj_weight, gate_weight, out_weight, norm_gain, mid_gain):
    mask = pair_mask.astype(jnp.float32).reshape(1, -1)
    current = pair_rep
    devices = pair_rep.shape[1] // pair_rep.shape[0]
    update = triangle if out_weight.shape[1] % devices == 0 else triangle_gathered
    for orient in range(2):
        current = update(
            current, mask, proj_weight[orient], gate_weight[orient], out_weight[orient],
            norm_gain[orient], mid_gain[orient], orient,
        )
    return current


def solution(mesh):
    return jax.shard_map(
        shards,
        mesh=mesh,
        in_specs=(P(("groups", "row")), P(("groups", "row")), P(), P(), P(), P(), P()),
        out_specs=P(("groups", "row")),
        check_vma=False,
    )
```

time: 68.4 us -> 56.3 us (0.82)
  blocking collectives: 47.8 us -> 9.48 us
  waiting for transfers between devices: 0.01 us -> 19.7 us
  starting transfers between devices: 3.5 us -> 14.5 us
  other arithmetic: 5.7 us -> 2.81 us
  matrix products: 4.02 us -> 1.8 us
    all_gather x2 -> x0, blocking collectives: 47.8 us -> none  [gather_rows(): everywhere = lax.all_gather(packed, 'row', axis=0, tiled=False)]
    all_to_all x1 -> x3, waiting for transfers between devices: 0.01 us -> 19.7 us  [the longest x2 12.9 us: triangle(): summed = lax.all_to_all(summed, 'row', 0, 0, tiled=True)]
    all_to_all x1 -> x3, starting transfers between devices: 3.5 us -> 14.5 us  [the longest x1 7.39 us: triangle(): lax.all_to_all(factor.reshape(devices, -1, rows * tokens), 'row', 0, 0, t...]
    all_to_all x0 -> x1, blocking collectives: none -> 9.48 us  [triangle(): lax.all_to_all(factor.reshape(devices, -1, rows * tokens), 'row', 0, 0, t...]
    another operation x2 -> x0, other arithmetic: 3.52 us -> none  [gather_rows(): both = jnp.stack([everywhere[..., :k], everywhere[..., k:]], axis=1)]
    dot_general x8 -> x10, matrix products: 4.02 us -> 1.8 us  [the longest x2 0.4 us: triangle(): jnp.einsum('pd,de->ep', flat, weights[1], preferred_element_type=jnp.floa...]
    another operation x1 -> x6, local copies, waits for them, and re-layouts: 1.08 us -> 0.2 us  [triangle(): left, right = factor.reshape(2, c, tokens, tokens)]
    reshape x4 -> x6, local copies, waits for them, and re-layouts: 0.95 us -> 1.74 us  [the longest x4 1.51 us: triangle(): summed.astype(jnp.bfloat16).reshape(c, devices, rows * tokens)]
  transfers between devices with their start and end apart: 1 -> 3, of which waited for: 0 -> 3; matrix products, arithmetic and copies ran while one was open for 5% -> 1% of each run, Pallas kernels for 0% -> 0%
where the time goes in v2:
time: 56.3 us; the launch traced here: 55.7 us
  waiting for transfers between devices  19.7 us (35%)
  starting transfers between devices  14.5 us (26%)
  blocking collectives  9.48 us (17%)
  local copies, waits for them, and re-layouts  7.03 us (12%)
  other arithmetic  2.81 us (5%)
  matrix products  1.8 us (3%)
    all_to_all x2, waiting for transfers between devices, triangle(): summed = lax.all_to_all(summed, 'row', 0, 0, tiled=True)  12.9 us
    all_to_all x1, blocking collectives, triangle(): lax.all_to_all(factor.reshape(devices, -1, rows * tokens), 'row', 0, 0, t...  9.48 us
    all_to_all x1, starting transfers between devices, triangle(): lax.all_to_all(factor.reshape(devices, -1, rows * tokens), 'row', 0, 0, t...  7.39 us
    all_to_all x2, starting transfers between devices, triangle(): summed = lax.all_to_all(summed, 'row', 0, 0, tiled=True)  7.13 us
    all_to_all x1, waiting for transfers between devices, triangle(): lax.all_to_all(factor.reshape(devices, -1, rows * tokens), 'row', 0, 0, t...  6.74 us
    unnamed x14, local copies, waits for them, and re-layouts  2.94 us
    reshape x4, local copies, waits for them, and re-layouts, triangle(): summed.astype(jnp.bfloat16).reshape(c, devices, rows * tokens)  1.51 us
    reduce_sum x4, other arithmetic, layer_norm(): average = jnp.mean(values, axis=axis, keepdims=True)  1.21 us
  transfers between devices with their start and end apart: 3, of which 3 were waited for; matrix products, arithmetic and copies ran while one was open for 1% of the time, Pallas kernels for 0%

profile of v2, /device:TPU:0, one launch (start us, length us, event | category | flops | bytes accessed | tf_op | source)
XLA Modules:
  0.0 55.7 jit_solution(6065815280042965074)
XLA Ops:
  0.0 1.0 %convert_reduce_fusion.1 = f32[4,64]{1,0:T(4,128)S(1)} fusion(bf16[4,64,128]{2,1,0:T(8,128)(2,1)} %param.7), kind=kLoop, calls=%fused_computation.33 | loop fusion | flops 65280 | bytes 66560 | tf_op jit(solution)/shard_map/reduce_sum | solution.py:10
  1.0 0.2 fusion.29
  1.3 0.7 %copy-done.3 = f32[2,128]{1,0:T(2,128)S(1)} copy-done((f32[2,128]{1,0:T(2,128)S(1)}, f32[2,128]{1,0:T(2,128)}, u32[]{:S(2)}) %copy-start.3) | copy-done | bytes 1048
  1.9 0.9 %fusion.56 = (bf16[1,128,256]{2,1,0:T(8,128)(2,1)S(1)}, bf16[1,128,256]{2,1,0:T(8,128)(2,1)S(1)}) fusion(bf16[2,128,256]{2,1,0:T(8,128)(2,1)} %param.9), kind=kLoop, calls=%fused_computation.85 | loop fusion | bytes 262144 | tf_op jit(solution)/shard_map/slice | solution.py:85
  3.0 0.7 %copy-done.2 = s32[4,64]{1,0:T(4,128)S(1)} copy-done((s32[4,64]{1,0:T(4,128)S(1)}, s32[4,64]{1,0:T(4,128)}, u32[]{:S(2)}) %copy-start.2) | copy-done | bytes 1048
  3.8 0.1 fusion.31
  3.9 0.2 fusion.60
  4.1 0.2 fusion.20
  4.3 0.7 %copy.22 = bf16[128,256]{1,0:T(8,128)(2,1)} copy(bf16[128,256]{0,1:T(8,128)(2,1)S(1)} %fusion.20) | data formatting | bytes 131072 | tf_op jit(solution)/shard_map/convert_element_type | solution.py:32
  5.0 7.4 %all-to-all-start = ((bf16[16,8,256]{2,1,0:T(8,128)(2,1)}), bf16[16,8,256]{2,1,0:T(8,128)(2,1)S(1)}, u32[]{:S(2)}, u32[]{:S(2)}) async-start(bf16[16,8,256]{2,1,0:T(8,128)(2,1)} %bitcast.9), calls=%async_computation | async-start | bytes 131072 | tf_op jit(solution)/shard_map/all_to_all | solution.py:33
  12.6 6.7 %all-to-all-done = bf16[16,8,256]{2,1,0:T(8,128)(2,1)S(1)} async-done(((bf16[16,8,256]{2,1,0:T(8,128)(2,1)}), bf16[16,8,256]{2,1,0:T(8,128)(2,1)S(1)}, u32[]{:S(2)}, u32[]{:S(2)}) %all-to-all-start) | async-done | bytes 65568 | tf_op jit(solution)/shard_map/all_to_all | solution.py:33
  19.5 0.1 convolution_convert_fusion.1
  19.7 0.1 reshape.151
  19.8 0.6 %copy.46 = bf16[4,16,256]{2,0,1:T(4,128)(2,1)} copy(bf16[4,16,256]{2,1,0:T(8,128)(2,1)S(1)} %reshape.151) | data formatting | bytes 65536 | tf_op jit(solution)/shard_map/reshape | solution.py:39
  20.5 3.6 %all-to-all-start.1 = ((bf16[16,4,256]{2,1,0:T(4,128)(2,1)}), bf16[16,4,256]{2,1,0:T(4,128)(2,1)S(1)}, u32[]{:S(2)}, u32[]{:S(2)}) async-start(bf16[16,4,256]{2,1,0:T(4,128)(2,1)} %bitcast.63), calls=%async_computation.1 | async-start | bytes 65536 | tf_op jit(solution)/shard_map/all_to_all | solution.py:40
  24.3 6.4 %all-to-all-done.1 = bf16[16,4,256]{2,1,0:T(4,128)(2,1)S(1)} async-done(((bf16[16,4,256]{2,1,0:T(4,128)(2,1)}), bf16[16,4,256]{2,1,0:T(4,128)(2,1)S(1)}, u32[]{:S(2)}, u32[]{:S(2)}) %all-to-all-start.1) | async-done | bytes 32800 | tf_op jit(solution)/shard_map/all_to_all | solution.py:40
  30.9 0.7 %copy-done.1 = bf16[2,64,128]{2,1,0:T(8,128)(2,1)S(1)} copy-done((bf16[2,64,128]{2,1,0:T(8,128)(2,1)S(1)}, bf16[2,64,128]{2,1,0:T(8,128)(2,1)}, u32[]{:S(2)}) %copy-start.1) | copy-done | bytes 32792
  31.7 0.2 fusion.50
  31.8 0.7 %copy-done.5 = bf16[2,128,128]{2,1,0:T(8,128)(2,1)S(1)} copy-done((bf16[2,128,128]{2,1,0:T(8,128)(2,1)S(1)}, bf16[2,128,128]{2,1,0:T(8,128)(2,1)}, u32[]{:S(2)}) %copy-start.5) | copy-done | bytes 65560
  32.5 0.2 fusion.6
  32.8 0.2 fusion.26
  33.0 0.1 fusion.28
  33.1 0.2 fusion.61
  33.3 0.2 fusion.21
  33.6 9.5 %all_to_all.20 = bf16[16,8,256]{2,1,0:T(8,128)(2,1)S(1)} all-to-all(bf16[16,8,256]{2,1,0:T(8,128)(2,1)S(1)} %bitcast.78), channel_id=1, replica_groups=mesh['groups'=2,'row'=16] {'row'}, dimensions={0} | all-to-all | bytes 131072 | tf_op jit(solution)/shard_map/all_to_all | solution.py:33
  43.4 0.2 convolution_convert_fusion
  43.7 0.6 %copy.45 = bf16[4,16,256]{2,0,1:T(4,128)(2,1)} copy(bf16[4,16,256]{2,1,0:T(8,128)(2,1)S(1)} %reshape.156) | data formatting | bytes 65536 | tf_op jit(solution)/shard_map/reshape | solution.py:39
  44.3 3.5 %all-to-all-start.3 = ((bf16[16,4,256]{2,1,0:T(4,128)(2,1)}), bf16[16,4,256]{2,1,0:T(4,128)(2,1)S(1)}, u32[]{:S(2)}, u32[]{:S(2)}) async-start(bf16[16,4,256]{2,1,0:T(4,128)(2,1)} %bitcast.62), calls=%async_computation.3 | async-start | bytes 65536 | tf_op jit(solution)/shard_map/all_to_all | solution.py:40
  47.9 6.5 %all-to-all-done.3 = bf16[16,4,256]{2,1,0:T(4,128)(2,1)S(1)} async-done(((bf16[16,4,256]{2,1,0:T(4,128)(2,1)}), bf16[16,4,256]{2,1,0:T(4,128)(2,1)S(1)}, u32[]{:S(2)}, u32[]{:S(2)}) %all-to-all-start.3) | async-done | bytes 32800 | tf_op jit(solution)/shard_map/all_to_all | solution.py:40
  54.6 0.2 fusion.48
  54.8 0.2 fusion.13
  55.0 0.6 %fusion.33 = bf16[4,64,128]{2,1,0:T(8,128)(2,1)} fusion(f32[4,64,128]{2,1,0:T(8,128)S(1)} %bitcast.82, bf16[4,64,128]{2,1,0:T(8,128)(2,1)S(1)} %get-tuple-element.8), kind=kLoop, calls=%fused_computation.45 | loop fusion | flops 98304 | bytes 262144 | tf_op jit(solution)/shard_map/convert_element_type | solution.py:45
  (49 shorter events, 1.8 us)
Async XLA Ops:
  0.0 1.0 %copy-start = (bf16[4,64,128]{2,1,0:T(8,128)(2,1)S(1)}, bf16[4,64,128]{2,1,0:T(8,128)(2,1)}, u32[]{:S(2)}) copy-start(bf16[4,64,128]{2,1,0:T(8,128)(2,1)} %param.7) | copy-start | bytes 196612
  1.2 0.7 %copy-start.3 = (f32[2,128]{1,0:T(2,128)S(1)}, f32[2,128]{1,0:T(2,128)}, u32[]{:S(2)}) copy-start(f32[2,128]{1,0:T(2,128)} %param.12) | copy-start | bytes 3076
  3.0 0.7 %copy-start.2 = (s32[4,64]{1,0:T(4,128)S(1)}, s32[4,64]{1,0:T(4,128)}, u32[]{:S(2)}) copy-start(s32[4,64]{1,0:T(4,128)} %param.8) | copy-start | bytes 3076
  5.0 14.3 %all-to-all-start = ((bf16[16,8,256]{2,1,0:T(8,128)(2,1)}), bf16[16,8,256]{2,1,0:T(8,128)(2,1)S(1)}, u32[]{:S(2)}, u32[]{:S(2)}) async-start(bf16[16,8,256]{2,1,0:T(8,128)(2,1)} %bitcast.9), calls=%async_computation | async-start | bytes 131072 | tf_op jit(solution)/shard_map/all_to_all | solution.py:33
  20.5 3.6 %copy-start.4 = (f32[2,64]{1,0:T(2,128)S(1)}, f32[2,64]{1,0:T(2,128)}, u32[]{:S(2)}) copy-start(f32[2,64]{1,0:T(2,128)} %param.13) | copy-start | bytes 1540
  20.5 10.2 %all-to-all-start.1 = ((bf16[16,4,256]{2,1,0:T(4,128)(2,1)}), bf16[16,4,256]{2,1,0:T(4,128)(2,1)S(1)}, u32[]{:S(2)}, u32[]{:S(2)}) async-start(bf16[16,4,256]{2,1,0:T(4,128)(2,1)} %bitcast.63), calls=%async_computation.1 | async-start | bytes 65536 | tf_op jit(solution)/shard_map/all_to_all | solution.py:40
  30.9 0.8 %copy-start.1 = (bf16[2,64,128]{2,1,0:T(8,128)(2,1)S(1)}, bf16[2,64,128]{2,1,0:T(8,128)(2,1)}, u32[]{:S(2)}) copy-start(bf16[2,64,128]{2,1,0:T(8,128)(2,1)} %param.11) | copy-start | bytes 98308
  31.6 0.8 %copy-start.5 = (bf16[2,128,128]{2,1,0:T(8,128)(2,1)S(1)}, bf16[2,128,128]{2,1,0:T(8,128)(2,1)}, u32[]{:S(2)}) copy-start(bf16[2,128,128]{2,1,0:T(8,128)(2,1)} %param.10) | copy-start | bytes 196612
  44.3 10.1 %all-to-all-start.3 = ((bf16[16,4,256]{2,1,0:T(4,128)(2,1)}), bf16[16,4,256]{2,1,0:T(4,128)(2,1)S(1)}, u32[]{:S(2)}, u32[]{:S(2)}) async-start(bf16[16,4,256]{2,1,0:T(4,128)(2,1)} %bitcast.62), calls=%async_computation.3 | async-start | bytes 65536 | tf_op jit(solution)/shard_map/all_to_all | solution.py:40

commit v3 on v1

v3 whole, which is shorter than its diff:
```python
import functools

import jax
import jax.numpy as jnp
from jax import lax
from jax.experimental import pallas as pl
from jax.experimental.pallas import tpu as pltpu
from jax.sharding import PartitionSpec as P

EPS = 1e-05
F32, BF16 = jnp.float32, jnp.bfloat16
LANES = 128
MASK_ROWS = 16
NT = (((1,), (1,)), ((), ()))


def dot(a, b):
    return jnp.dot(a, b, preferred_element_type=F32)


def dot_nt(a, b):
    return lax.dot_general(a, b, NT, preferred_element_type=F32)


def sigmoid(x):
    return 0.5 * jnp.tanh(0.5 * x) + 0.5


def iota(shape, axis):
    return lax.broadcasted_iota(jnp.int32, shape, axis)


def token_of(t, rows, tokens):
    devices = tokens // rows
    return (t % devices) * rows + t // devices


def column_norm(values, gain):
    average = jnp.mean(values, axis=0, keepdims=True)
    centred = values - average
    variance = jnp.mean(centred * centred, axis=0, keepdims=True)
    return (centred * lax.rsqrt(variance + EPS) * gain).astype(BF16)


def position_permutation(rows, tokens, by_lane):
    size = rows * tokens
    shape = (size, size)
    lane = iota(shape, 0 if by_lane else 1)
    position = iota(shape, 1 if by_lane else 0)
    source = lane // tokens * tokens + token_of(lane % tokens, rows, tokens)
    return (source == position).astype(F32).astype(BF16)


def pack_kernel(rows, tokens, pair_ref, mask_ref, packed_ref):
    channels = pair_ref.shape[-1]
    size = rows * tokens
    permuted = dot(position_permutation(rows, tokens, True), pair_ref[...]).astype(BF16)
    identity = (iota((channels, channels), 0) == iota((channels, channels), 1)).astype(F32)
    packed_ref[:channels, :] = dot_nt(identity.astype(BF16), permuted).astype(BF16)
    lane = iota((tokens, size), 1)
    place = token_of(lane % tokens, rows, tokens) == iota((tokens, size), 0)
    spread = dot(mask_ref[...].astype(F32).astype(BF16), place.astype(F32).astype(BF16))
    own = iota((rows, size), 0) == iota((rows, size), 1) // tokens
    line = jnp.sum(jnp.where(own, spread, 0.0), axis=0, keepdims=True)
    packed_ref[channels:, :] = jnp.broadcast_to(line, (MASK_ROWS, size)).astype(BF16)


def both_kernel(
    rows, tokens, me_ref, packed_ref, proj_ref, gate_ref, out_ref, gain_ref, mid_ref,
    result_ref, left_s, right_s, normed_s, sum_s, now_s, second_left_s, second_right_s,
):
    devices = tokens // rows
    size = rows * tokens
    channels = proj_ref.shape[1]
    hw = out_ref.shape[1]
    tiles = size // LANES
    me = me_ref[0]

    def flipped(weight):
        return weight.astype(F32).T.astype(BF16)

    def column(line, width):
        tall = jnp.broadcast_to(line, (LANES, line.shape[1])).T
        return jnp.concatenate([tall] * (width // LANES), axis=1)

    def factors(projected, mask):
        left = mask * sigmoid(projected[hw : 2 * hw]) * projected[:hw]
        right = mask * sigmoid(projected[3 * hw :]) * projected[2 * hw : 3 * hw]
        return left, right

    gains = [column(gain_ref[o : o + 1, :], size) for o in range(2)]
    mids = [column(mid_ref[o : o + 1, :], size) for o in range(2)]
    proj_t = [flipped(proj_ref[o]) for o in range(2)]
    gate_t = [flipped(gate_ref[o]) for o in range(2)]
    out_t = [flipped(out_ref[o]) for o in range(2)]

    def block_of(b):
        return packed_ref[b, :channels, :].astype(F32)

    def mask_of(b):
        return packed_ref[b, channels : channels + MASK_ROWS, :].astype(F32)[:1]

    def project_first(b, _):
        normed = column_norm(block_of(b), gains[0])
        normed_s[b] = normed
        left, right = factors(dot(proj_t[0], normed), mask_of(b))
        here = pl.ds(pl.multiple_of(b * hw, hw), hw)
        for h in range(tiles):
            left_s[h, here, :] = left[:, h * LANES : (h + 1) * LANES]
            right_s[h, here, :] = right[:, h * LANES : (h + 1) * LANES]
        return 0

    lax.fori_loop(0, devices, project_first, 0, unroll=2)

    low = iota((devices, LANES), 1) < tokens

    def channel_sum(c, _):
        here = pl.ds(c, devices, stride=hw)
        left = jnp.concatenate([left_s[h, here, :] for h in range(tiles)], axis=0)
        halves = [[], []]
        for h in range(tiles):
            right = right_s[h, here, :]
            turned = pltpu.roll(right, tokens, 1)
            for q in range(2):
                straight, other = (right, turned) if q == 0 else (turned, right)
                halves[0].append(jnp.where(low, straight, 0.0))
                halves[1].append(jnp.where(low, 0.0, other))
        against = jnp.concatenate(halves[0] + halves[1], axis=0).astype(BF16)
        here = pl.ds(pl.multiple_of(c * tiles * devices, tiles * devices), tiles * devices)
        sum_s[here, :] = dot_nt(left.astype(BF16), against)
        return 0

    lax.fori_loop(0, hw, channel_sum, 0, unroll=8)

    def second_factors(b, _):
        summed = jnp.concatenate(
            [sum_s[pl.ds(h * devices + b, hw, stride=tiles * devices), :] for h in range(tiles)],
            axis=1,
        )
        update = dot(out_t[0], column_norm(summed, mids[0]))
        gating = sigmoid(dot(gate_t[0], normed_s[b]))
        now = (block_of(b) + gating * update).astype(BF16)
        now_s[b] = now
        normed = column_norm(now.astype(F32), gains[1])
        normed_s[b] = normed
        left, right = factors(dot(proj_t[1], normed), mask_of(b))
        second_left_s[b] = left.astype(BF16)
        second_right_s[b] = right.astype(BF16)
        return 0

    lax.fori_loop(0, devices, second_factors, 0, unroll=2)

    row_group, row_lane = iota((size, size), 0) // tokens, iota((size, size), 0) % tokens
    same = row_group == iota((size, size), 1) // tokens
    sums = []
    for i in range(rows):
        spread = (same & (row_lane == i * devices + me)).astype(F32).astype(BF16)

        def add(b, total):
            return total + dot(second_left_s[b], spread) * second_right_s[b].astype(F32)

        total = lax.fori_loop(0, devices, add, jnp.zeros((hw, size), F32), unroll=4)
        total = sum(total[:, h * LANES : (h + 1) * LANES] for h in range(tiles))
        sums.append(total + pltpu.roll(total, tokens, 1))
    low = iota((hw, LANES), 1) < tokens
    summed = jnp.concatenate(
        [jnp.where(low, sums[2 * h], sums[2 * h + 1]) for h in range(tiles)], axis=1
    )
    update = dot(out_t[1], column_norm(summed, mids[1]))
    gating = sigmoid(dot(gate_t[1], normed_s[me]))
    final = (now_s[me].astype(F32) + gating * update).astype(BF16)
    result_ref[...] = dot_nt(position_permutation(rows, tokens, False), final).astype(BF16)


def small_plan(pair, mask, proj, gate, out, gain, mid):
    rows, tokens, channels = pair.shape
    devices, size, hw = tokens // rows, rows * tokens, out.shape[1]
    packed = pl.pallas_call(
        functools.partial(pack_kernel, rows, tokens),
        out_shape=jax.ShapeDtypeStruct((channels + MASK_ROWS, size), BF16),
        name="pack",
    )(pair.reshape(size, channels), mask)
    everywhere = lax.all_gather(packed, "row", axis=0)
    me = lax.axis_index("row").reshape(1).astype(jnp.int32)
    vmem = pl.BlockSpec(memory_space=pltpu.VMEM)
    result = pl.pallas_call(
        functools.partial(both_kernel, rows, tokens),
        out_shape=jax.ShapeDtypeStruct((size, channels), BF16),
        in_specs=[pl.BlockSpec(memory_space=pltpu.SMEM)] + [vmem] * 6,
        out_specs=vmem,
        scratch_shapes=[
            pltpu.VMEM((size // LANES, devices * hw, LANES), F32),
            pltpu.VMEM((size // LANES, devices * hw, LANES), F32),
            pltpu.VMEM((devices, channels, size), BF16),
            pltpu.VMEM((hw * devices * size // LANES, LANES), F32),
            pltpu.VMEM((devices, channels, size), BF16),
            pltpu.VMEM((devices, hw, size), BF16),
            pltpu.VMEM((devices, hw, size), BF16),
        ],
        compiler_params=pltpu.CompilerParams(vmem_limit_bytes=40 * 1024 * 1024),
        name="both",
    )(me, everywhere, proj, gate, out, gain, mid)
    return result.reshape(pair.shape)


def layer_norm(values, gain, axis):
    average = jnp.mean(values, axis=axis, keepdims=True)
    centred = values - average
    variance = jnp.mean(centred * centred, axis=axis, keepdims=True)
    return centred * lax.rsqrt(variance + EPS) * gain


def factors(normed, mask, proj):
    hw = proj.shape[1] // 4
    projected = jnp.einsum("ijd,de->eij", normed, proj, preferred_element_type=F32)
    left = mask * jax.nn.sigmoid(projected[hw : 2 * hw]) * projected[:hw]
    right = mask * jax.nn.sigmoid(projected[3 * hw :]) * projected[2 * hw : 3 * hw]
    return left.astype(BF16), right.astype(BF16)


def gathered_update(pair, mask, proj, gate, out, gain, mid, orient):
    rows, tokens, _ = pair.shape
    devices = tokens // rows
    floats = pair.astype(F32)
    normed = layer_norm(floats, gain, -1).astype(BF16)
    left, right = factors(normed, mask, proj)
    everywhere = lax.all_gather(right, "row", axis=1, tiled=True)
    if orient == 1:
        c = left.shape[0]
        blocks = left.reshape(c, rows, devices, rows).transpose(2, 1, 3, 0)
        left = lax.all_to_all(blocks, "row", 0, 0, tiled=True)
        left = left.reshape(tokens, rows, c).transpose(2, 0, 1)
    spec = "cik,cjk->cij" if orient == 0 else "cki,ckj->cij"
    summed = jnp.einsum(spec, left, everywhere, preferred_element_type=F32)
    hidden = layer_norm(summed, mid[:, None, None], 0).astype(BF16)
    gating = jax.nn.sigmoid(jnp.einsum("ijd,de->ije", normed, gate, preferred_element_type=F32))
    update = jnp.einsum("cij,cd->ijd", hidden, out, preferred_element_type=F32)
    return (floats + gating * update).astype(BF16)


def shards(pair, pair_mask, proj, gate, out, gain, mid):
    rows, tokens, _ = pair.shape
    if rows == 4 and 2 * tokens == LANES:
        return small_plan(pair, pair_mask, proj, gate, out, gain, mid)
    mask = pair_mask.astype(F32)[None]
    for o in range(2):
        pair = gathered_update(pair, mask, proj[o], gate[o], out[o], gain[o], mid[o], o)
    return pair


def solution(mesh):
    return jax.shard_map(
        shards,
        mesh=mesh,
        in_specs=(P(("groups", "row")), P(("groups", "row")), P(), P(), P(), P(), P()),
        out_specs=P(("groups", "row")),
        check_vma=False,
    )
```

time: 68.4 us -> 79.8 us (1.17)
  blocking collectives: 47.8 us -> 0 us
  waiting for transfers between devices: 0.01 us -> 42.3 us
  Pallas kernels: 0 us -> 18.6 us
  between operations: 0.28 us -> 13.4 us
  other arithmetic: 5.7 us -> 0 us
  matrix products: 4.02 us -> 0 us
  starting transfers between devices: 3.5 us -> 0.01 us
  local copies, waits for them, and re-layouts: 6.66 us -> 5.13 us
    all_gather x2 -> x0, blocking collectives: 47.8 us -> none  [gather_rows(): everywhere = lax.all_gather(packed, 'row', axis=0, tiled=False)]
    all_gather x0 -> x1, waiting for transfers between devices: none -> 42.3 us  [small_plan(): everywhere = lax.all_gather(packed, 'row', axis=0)]
    pallas_call x0 -> x2, Pallas kernels: none -> 18.6 us  [the longest x1 16.8 us: small_plan(): pl.pallas_call(functools.partial(both_kernel, rows, tokens), out_shape=ja...]
    dot_general x8 -> x0, matrix products: 4.02 us -> none  [the longest x2 1.35 us: factors(): jnp.einsum('ijd,de->eij', normed, proj, preferred_element_type=jnp.float32)]
    another operation x2 -> x0, other arithmetic: 3.52 us -> none  [gather_rows(): both = jnp.stack([everywhere[..., :k], everywhere[..., k:]], axis=1)]
    all_to_all x1 -> x0, starting transfers between devices: 3.5 us -> none  [shards(): columns = lax.all_to_all(blocks, 'row', 0, 0, tiled=True)]
    unnamed x14 -> x12, local copies, waits for them, and re-layouts: 3.06 us -> 5.13 us
    reduce_sum x5 -> x0, other arithmetic: 1.48 us -> none  [the longest x1 0.95 us: layer_norm(): average = jnp.mean(values, axis=axis, keepdims=True)]
  transfers between devices with their start and end apart: 1 -> 1, of which waited for: 0 -> 1; matrix products, arithmetic and copies ran while one was open for 5% -> 0% of each run, Pallas kernels for 0% -> 0%
where the time goes in v3:
time: 79.8 us; the launch traced here: 79.5 us
  waiting for transfers between devices  42.3 us (53%)
  Pallas kernels  18.6 us (23%)
  between operations  13.4 us (17%)
  local copies, waits for them, and re-layouts  5.13 us (6%)
    all_gather x1, waiting for transfers between devices, small_plan(): everywhere = lax.all_gather(packed, 'row', axis=0)  42.3 us
    pallas_call x1, Pallas kernels, small_plan(): pl.pallas_call(functools.partial(both_kernel, rows, tokens), out_shape=ja...  16.8 us
    unnamed x12, local copies, waits for them, and re-layouts  5.13 us
    pallas_call x1, Pallas kernels, small_plan(): pl.pallas_call(functools.partial(pack_kernel, rows, tokens), out_shape=ja...  1.83 us
  transfers between devices with their start and end apart: 1, of which 1 were waited for; matrix products, arithmetic and copies ran while one was open for 0% of the time, Pallas kernels for 0%

profile of v3, /device:TPU:0, one launch (start us, length us, event | category | flops | bytes accessed | tf_op | source)
XLA Modules:
  0.0 79.5 jit_solution(3769370256307719190)
XLA Ops:
  6.5 0.0 all-gather.3.cloned.1.call-start
  6.5 1.8 %pack.1 = bf16[144,256]{1,0:T(8,128)(2,1)} custom-call(bf16[256,128]{1,0:T(8,128)(2,1)} %bitcast.5, s32[4,64]{1,0:T(4,128)} %mask_ref.1), custom_call_target="tpu_custom_call" | custom-call | tf_op jit(solution)/shard_map/pack/pallas_call | solution.py:178
  8.4 0.0 all-gather.3.cloned.1.call-update
  8.4 42.3 %all-gather.3.cloned.1.call-done = bf16[2304,256]{1,0:T(8,128)(2,1)} async-done(((bf16[144,256]{1,0:T(8,128)(2,1)}), bf16[2304,256]{1,0:T(8,128)(2,1)}) %all-gather.3.cloned.1.call-update) | async-done | bytes 1179664 | tf_op jit(solution)/shard_map/all_gather | solution.py:183
  50.7 0.0 copy-start
  50.7 1.3 %copy-done = bf16[2304,256]{1,0:T(8,128)(2,1)S(1)} copy-done((bf16[2304,256]{1,0:T(8,128)(2,1)S(1)}, bf16[2304,256]{1,0:T(8,128)(2,1)}, u32[]{:S(2)}) %copy-start) | copy-done | bytes 1179672
  52.0 0.0 copy-start.1
  52.0 0.9 %copy-done.1 = bf16[2,128,256]{2,1,0:T(8,128)(2,1)S(1)} copy-done((bf16[2,128,256]{2,1,0:T(8,128)(2,1)S(1)}, bf16[2,128,256]{2,1,0:T(8,128)(2,1)}, u32[]{:S(2)}) %copy-start.1) | copy-done | bytes 131096
  52.9 0.0 copy-start.2
  52.9 0.8 %copy-done.2 = bf16[2,128,128]{2,1,0:T(8,128)(2,1)S(1)} copy-done((bf16[2,128,128]{2,1,0:T(8,128)(2,1)S(1)}, bf16[2,128,128]{2,1,0:T(8,128)(2,1)}, u32[]{:S(2)}) %copy-start.2) | copy-done | bytes 65560
  53.7 0.0 copy-start.3
  53.7 0.8 copy-done.3
  54.5 0.0 copy-start.4
  54.5 0.7 copy-done.4
  55.2 0.0 copy-start.5
  55.2 0.7 copy-done.5
  55.8 16.8 %both.1 = bf16[256,128]{1,0:T(8,128)(2,1)} custom-call(s32[1]{0:T(128)} %bitcast.me_ref, bf16[16,144,256]{2,1,0:T(8,128)(2,1)S(1)} %bitcast.4, bf16[2,128,256]{2,1,0:T(8,128)(2,1)S(1)} %copy-done.1, bf16[2,128,128]{2,1,0:T(8,128)(2,1)S(1)} %copy-done.2, bf16[2,64,128]{2,1,0:T(8,128)(2,1)S(1)} %copy-done.3, f32[2,128]{1,0:T(2,128)S(1)} %copy-done.4, ...), custom_call_target="tpu_custom_call" | custom-call | tf_op jit(solution)/shard_map/both/pallas_call | solution.py:186
Async XLA Ops:
  6.5 44.2 %all-gather.3.cloned.1.call-start = ((), (), s32[]{:S(2)}) async-start(), calls=%async_computation | async-start | bytes 1253376 | tf_op jit(solution)/shard_map/all_gather | solution.py:183
  50.7 1.3 %copy-start = (bf16[2304,256]{1,0:T(8,128)(2,1)S(1)}, bf16[2304,256]{1,0:T(8,128)(2,1)}, u32[]{:S(2)}) copy-start(bf16[2304,256]{1,0:T(8,128)(2,1)} %all-gather.3.cloned.1.call-done) | copy-start | bytes 3538948
  52.0 0.9 %copy-start.1 = (bf16[2,128,256]{2,1,0:T(8,128)(2,1)S(1)}, bf16[2,128,256]{2,1,0:T(8,128)(2,1)}, u32[]{:S(2)}) copy-start(bf16[2,128,256]{2,1,0:T(8,128)(2,1)} %proj_ref.1) | copy-start | bytes 393220
  52.9 0.8 %copy-start.2 = (bf16[2,128,128]{2,1,0:T(8,128)(2,1)S(1)}, bf16[2,128,128]{2,1,0:T(8,128)(2,1)}, u32[]{:S(2)}) copy-start(bf16[2,128,128]{2,1,0:T(8,128)(2,1)} %gate_ref.1) | copy-start | bytes 196612
  53.7 0.8 copy-start.3
  54.5 0.7 copy-start.4
  55.2 0.7 copy-start.5
Sparse Core Ops, SparseCore 0:
  9.6 41.0 all-gather.2

commit v4 on v3

--- a/solution.py
+++ b/solution.py
@@ -65,52 +65,69 @@
     packed_ref[channels:, :] = jnp.broadcast_to(line, (MASK_ROWS, size)).astype(BF16)
 
 
+def prepare_kernel(
+    rows, tokens, me_ref, proj_ref, gate_ref, out_ref, gain_ref, mid_ref,
+    proj_t_ref, gate_t_ref, out_t_ref, gain_t_ref, mid_t_ref, restore_ref, spread_ref,
+):
+    size, devices = rows * tokens, tokens // rows
+
+    def flipped(weight):
+        return weight.astype(F32).T.astype(BF16)
+
+    def column(line):
+        return jnp.broadcast_to(line, (LANES, line.shape[1])).T
+
+    for o in range(2):
+        proj_t_ref[o] = flipped(proj_ref[o])
+        gate_t_ref[o] = flipped(gate_ref[o])
+        out_t_ref[o] = flipped(out_ref[o])
+        gain_t_ref[o] = column(gain_ref[o : o + 1, :])
+        mid_t_ref[o] = column(mid_ref[o : o + 1, :])
+    restore_ref[...] = position_permutation(rows, tokens, False)
+    group, lane = iota((size, size), 0) // tokens, iota((size, size), 0) % tokens
+    same = group == iota((size, size), 1) // tokens
+    for i in range(rows):
+        spread_ref[i] = (same & (lane == i * devices + me_ref[0])).astype(F32).astype(BF16)
+
+
 def both_kernel(
-    rows, tokens, me_ref, packed_ref, proj_ref, gate_ref, out_ref, gain_ref, mid_ref,
-    result_ref, left_s, right_s, normed_s, sum_s, now_s, second_left_s, second_right_s,
+    rows, tokens, me_ref, *refs,
 ):
     devices = tokens // rows
+    packed_refs, refs = refs[:devices], refs[devices:]
+    (
+        proj_ref, gate_ref, out_ref, gain_ref, mid_ref, restore_ref, spread_ref, result_ref,
+        left_s, right_s, normed_s, sum_s, now_s, second_left_s, second_right_s,
+    ) = refs
     size = rows * tokens
-    channels = proj_ref.shape[1]
-    hw = out_ref.shape[1]
+    channels = gate_ref.shape[1]
+    hw = mid_ref.shape[1]
     tiles = size // LANES
     me = me_ref[0]
 
-    def flipped(weight):
-        return weight.astype(F32).T.astype(BF16)
-
-    def column(line, width):
-        tall = jnp.broadcast_to(line, (LANES, line.shape[1])).T
-        return jnp.concatenate([tall] * (width // LANES), axis=1)
+    def wide(column):
+        return jnp.concatenate([column] * tiles, axis=1)
 
     def factors(projected, mask):
         left = mask * sigmoid(projected[hw : 2 * hw]) * projected[:hw]
         right = mask * sigmoid(projected[3 * hw :]) * projected[2 * hw : 3 * hw]
         return left, right
 
-    gains = [column(gain_ref[o : o + 1, :], size) for o in range(2)]
-    mids = [column(mid_ref[o : o + 1, :], size) for o in range(2)]
-    proj_t = [flipped(proj_ref[o]) for o in range(2)]
-    gate_t = [flipped(gate_ref[o]) for o in range(2)]
-    out_t = [flipped(out_ref[o]) for o in range(2)]
-
-    def block_of(b):
-        return packed_ref[b, :channels, :].astype(F32)
-
-    def mask_of(b):
-        return packed_ref[b, channels : channels + MASK_ROWS, :].astype(F32)[:1]
-
-    def project_first(b, _):
-        normed = column_norm(block_of(b), gains[0])
-        normed_s[b] = normed
-        left, right = factors(dot(proj_t[0], normed), mask_of(b))
+    def block_of(packed_ref):
+        return packed_ref[:channels, :].astype(F32)
+
+    def mask_of(packed_ref):
+        return packed_ref[channels:, :].astype(F32)[:1]
+
+    for m, packed_ref in enumerate(packed_refs):
+        b = me ^ m
+        normed = column_norm(block_of(packed_ref), wide(gain_ref[0]))
+        normed_s[m] = normed
+        left, right = factors(dot(proj_ref[0], normed), mask_of(packed_ref))
         here = pl.ds(pl.multiple_of(b * hw, hw), hw)
         for h in range(tiles):
             left_s[h, here, :] = left[:, h * LANES : (h + 1) * LANES]
             right_s[h, here, :] = right[:, h * LANES : (h + 1) * LANES]
-        return 0
-
-    lax.fori_loop(0, devices, project_first, 0, unroll=2)
 
     low = iota((devices, LANES), 1) < tokens
 
@@ -130,34 +147,30 @@
         sum_s[here, :] = dot_nt(left.astype(BF16), against)
         return 0
 
-    lax.fori_loop(0, hw, channel_sum, 0, unroll=8)
-
-    def second_factors(b, _):
+    lax.fori_loop(0, hw, channel_sum, 0, unroll=16)
+
+    for m, packed_ref in enumerate(packed_refs):
+        b = me ^ m
         summed = jnp.concatenate(
             [sum_s[pl.ds(h * devices + b, hw, stride=tiles * devices), :] for h in range(tiles)],
             axis=1,
         )
-        update = dot(out_t[0], column_norm(summed, mids[0]))
-        gating = sigmoid(dot(gate_t[0], normed_s[b]))
-        now = (block_of(b) + gating * update).astype(BF16)
-        now_s[b] = now
-        normed = column_norm(now.astype(F32), gains[1])
-        normed_s[b] = normed
-        left, right = factors(dot(proj_t[1], normed), mask_of(b))
-        second_left_s[b] = left.astype(BF16)
-        second_right_s[b] = right.astype(BF16)
-        return 0
-
-    lax.fori_loop(0, devices, second_factors, 0, unroll=2)
-
-    row_group, row_lane = iota((size, size), 0) // tokens, iota((size, size), 0) % tokens
-    same = row_group == iota((size, size), 1) // tokens
+        update = dot(out_ref[0], column_norm(summed, wide(mid_ref[0])))
+        gating = sigmoid(dot(gate_ref[0], normed_s[m]))
+        now = (block_of(packed_ref) + gating * update).astype(BF16)
+        normed = column_norm(now.astype(F32), wide(gain_ref[1]))
+        if m == 0:
+            now_s[...] = now
+            normed_s[0] = normed
+        left, right = factors(dot(proj_ref[1], normed), mask_of(packed_ref))
+        second_left_s[m] = left.astype(BF16)
+        second_right_s[m] = right.astype(BF16)
+
     sums = []
     for i in range(rows):
-        spread = (same & (row_lane == i * devices + me)).astype(F32).astype(BF16)
-
-        def add(b, total):
-            return total + dot(second_left_s[b], spread) * second_right_s[b].astype(F32)
+
+        def add(m, total):
+            return total + dot(second_left_s[m], spread_ref[i]) * second_right_s[m].astype(F32)
 
         total = lax.fori_loop(0, devices, add, jnp.zeros((hw, size), F32), unroll=4)
         total = sum(total[:, h * LANES : (h + 1) * LANES] for h in range(tiles))
@@ -166,10 +179,25 @@
     summed = jnp.concatenate(
         [jnp.where(low, sums[2 * h], sums[2 * h + 1]) for h in range(tiles)], axis=1
     )
-    update = dot(out_t[1], column_norm(summed, mids[1]))
-    gating = sigmoid(dot(gate_t[1], normed_s[me]))
-    final = (now_s[me].astype(F32) + gating * update).astype(BF16)
-    result_ref[...] = dot_nt(position_permutation(rows, tokens, False), final).astype(BF16)
+    update = dot(out_ref[1], column_norm(summed, wide(mid_ref[1])))
+    gating = sigmoid(dot(gate_ref[1], normed_s[0]))
+    final = (now_s[...].astype(F32) + gating * update).astype(BF16)
+    result_ref[...] = dot_nt(restore_ref[...], final).astype(BF16)
+
+
+def exchange(block, partner_bits, devices):
+    pairs = [(d, d ^ partner_bits) for d in range(devices)]
+    return lax.ppermute(block, "row", pairs)
+
+
+def everyone(packed, devices):
+    blocks = {0: packed}
+    for m in range(4, devices, 4):
+        blocks[m] = exchange(packed, m, devices)
+    for step in (2, 1):
+        for m in sorted(blocks):
+            blocks[m ^ step] = exchange(blocks[m], step, devices)
+    return [blocks[m] for m in range(devices)]
 
 
 def small_plan(pair, mask, proj, gate, out, gain, mid):
@@ -180,26 +208,40 @@
         out_shape=jax.ShapeDtypeStruct((channels + MASK_ROWS, size), BF16),
         name="pack",
     )(pair.reshape(size, channels), mask)
-    everywhere = lax.all_gather(packed, "row", axis=0)
     me = lax.axis_index("row").reshape(1).astype(jnp.int32)
-    vmem = pl.BlockSpec(memory_space=pltpu.VMEM)
+    whole = pl.BlockSpec()
+    index = pl.BlockSpec(memory_space=pltpu.SMEM)
+    weights = pl.pallas_call(
+        functools.partial(prepare_kernel, rows, tokens),
+        in_specs=[index] + [whole] * 5,
+        out_shape=(
+            jax.ShapeDtypeStruct((2, 4 * hw, channels), BF16),
+            jax.ShapeDtypeStruct((2, channels, channels), BF16),
+            jax.ShapeDtypeStruct((2, channels, hw), BF16),
+            jax.ShapeDtypeStruct((2, channels, LANES), F32),
+            jax.ShapeDtypeStruct((2, hw, LANES), F32),
+            jax.ShapeDtypeStruct((size, size), BF16),
+            jax.ShapeDtypeStruct((rows, size, size), BF16),
+        ),
+        name="prepare",
+    )(me, proj, gate, out, gain, mid)
+    blocks = everyone(packed, devices)
     result = pl.pallas_call(
         functools.partial(both_kernel, rows, tokens),
         out_shape=jax.ShapeDtypeStruct((size, channels), BF16),
-        in_specs=[pl.BlockSpec(memory_space=pltpu.SMEM)] + [vmem] * 6,
-        out_specs=vmem,
+        in_specs=[index] + [whole] * (devices + len(weights)),
         scratch_shapes=[
             pltpu.VMEM((size // LANES, devices * hw, LANES), F32),
             pltpu.VMEM((size // LANES, devices * hw, LANES), F32),
             pltpu.VMEM((devices, channels, size), BF16),
             pltpu.VMEM((hw * devices * size // LANES, LANES), F32),
-            pltpu.VMEM((devices, channels, size), BF16),
+            pltpu.VMEM((channels, size), BF16),
             pltpu.VMEM((devices, hw, size), BF16),
             pltpu.VMEM((devices, hw, size), BF16),
         ],
         compiler_params=pltpu.CompilerParams(vmem_limit_bytes=40 * 1024 * 1024),
         name="both",
-    )(me, everywhere, proj, gate, out, gain, mid)
+    )(me, *blocks, *weights)
     return result.reshape(pair.shape)
 
 

time: 79.8 us -> 39.5 us (0.49)
  waiting for transfers between devices: 42.3 us -> 5.25 us
  between operations: 13.4 us -> 0.07 us
  starting transfers between devices: 0.01 us -> 12.5 us
  Pallas kernels: 18.6 us -> 15 us
  local copies, waits for them, and re-layouts: 5.13 us -> 6.27 us
    all_gather x1 -> x0, waiting for transfers between devices: 42.3 us -> none  [small_plan(): everywhere = lax.all_gather(packed, 'row', axis=0)]
    ppermute x0 -> x15, starting transfers between devices: none -> 12.5 us  [exchange(): return lax.ppermute(block, 'row', pairs)]
    pallas_call x1, Pallas kernels: 16.8 us -> 11 us  [small_plan(): pl.pallas_call(functools.partial(both_kernel, rows, tokens), out_shape=ja...]
    ppermute x0 -> x15, waiting for transfers between devices: none -> 5.25 us  [exchange(): return lax.ppermute(block, 'row', pairs)]
    pallas_call x0 -> x1, Pallas kernels: none -> 2.17 us  [small_plan(): pl.pallas_call(functools.partial(prepare_kernel, rows, tokens), in_specs=...]
    unnamed x12 -> x16, local copies, waits for them, and re-layouts: 5.13 us -> 6.27 us
  transfers between devices with their start and end apart: 1 -> 15, of which waited for: 1 -> 4; matrix products, arithmetic and copies ran while one was open for 0% -> 0% of each run, Pallas kernels for 0% -> 6%
where the time goes in v4:
time: 39.5 us; the launch traced here: 39 us
  Pallas kernels  15 us (38%)
  starting transfers between devices  12.5 us (32%)
  local copies, waits for them, and re-layouts  6.27 us (16%)
  waiting for transfers between devices  5.25 us (13%)
    ppermute x15, starting transfers between devices, exchange(): return lax.ppermute(block, 'row', pairs)  12.5 us
    pallas_call x1, Pallas kernels, small_plan(): pl.pallas_call(functools.partial(both_kernel, rows, tokens), out_shape=ja...  11 us
    unnamed x16, local copies, waits for them, and re-layouts  6.27 us
    ppermute x15, waiting for transfers between devices, exchange(): return lax.ppermute(block, 'row', pairs)  5.25 us
    pallas_call x1, Pallas kernels, small_plan(): pl.pallas_call(functools.partial(prepare_kernel, rows, tokens), in_specs=...  2.17 us
    pallas_call x1, Pallas kernels, small_plan(): pl.pallas_call(functools.partial(pack_kernel, rows, tokens), out_shape=ja...  1.83 us
  transfers between devices with their start and end apart: 15, of which 4 were waited for; matrix products, arithmetic and copies ran while one was open for 0% of the time, Pallas kernels for 6%

profile of v4, /device:TPU:0, one launch (start us, length us, event | category | flops | bytes accessed | tf_op | source)
XLA Modules:
  0.0 39.0 jit_solution(111136972576075637)
XLA Ops:
  0.0 1.8 %pack.1.refs_0_ = bf16[144,256]{1,0:T(8,128)(2,1)} custom-call(bf16[256,128]{1,0:T(8,128)(2,1)} %bitcast.3, s32[4,64]{1,0:T(4,128)} %mask_ref.1), custom_call_target="tpu_custom_call" | custom-call | tf_op jit(solution)/shard_map/pack/pallas_call | solution.py:206
  1.8 5.0 %collective-permute-start.11 = (bf16[144,256]{1,0:T(8,128)(2,1)}, bf16[144,256]{1,0:T(8,128)(2,1)S(1)}, u32[]{:S(2)}, u32[]{:S(2)}) collective-permute-start(bf16[144,256]{1,0:T(8,128)(2,1)} %pack.1.refs_0_), channel_id=1, source_target_pairs={{0,12},{1,13},{2,14},{3,15},{4,8},{5,9},{6,10},{7,11},{8,4},{9,5},... | collective-permute-start | bytes 221192 | tf_op jit(solution)/shard_map/ppermute | solution.py:190
  6.9 0.0 collective-permute-start.7
  6.9 0.6 %collective-permute-start.3 = (bf16[144,256]{1,0:T(8,128)(2,1)}, bf16[144,256]{1,0:T(8,128)(2,1)S(1)}, u32[]{:S(2)}, u32[]{:S(2)}) collective-permute-start(bf16[144,256]{1,0:T(8,128)(2,1)} %pack.1.refs_0_), channel_id=1, source_target_pairs={{0,4},{1,5},{2,6},{3,7},{4,0},{5,1},{6,2},{7,3},{8,12},{9,13},{10,... | collective-permute-start | bytes 221192 | tf_op jit(solution)/shard_map/ppermute | solution.py:190
  7.4 1.7 %collective-permute-start.1 = (bf16[144,256]{1,0:T(8,128)(2,1)}, bf16[144,256]{1,0:T(8,128)(2,1)S(1)}, u32[]{:S(2)}, u32[]{:S(2)}) collective-permute-start(bf16[144,256]{1,0:T(8,128)(2,1)} %pack.1.refs_0_), channel_id=1, source_target_pairs={{0,2},{1,3},{2,0},{3,1},{4,6},{5,7},{6,4},{7,5},{8,10},{9,11},{10,... | collective-permute-start | bytes 221192 | tf_op jit(solution)/shard_map/ppermute | solution.py:190
  9.2 0.7 %collective-permute-done.11.refs_12_ = bf16[144,256]{1,0:T(8,128)(2,1)S(1)} collective-permute-done((bf16[144,256]{1,0:T(8,128)(2,1)}, bf16[144,256]{1,0:T(8,128)(2,1)S(1)}, u32[]{:S(2)}, u32[]{:S(2)}) %collective-permute-start.11) | collective-permute-done | bytes 73760 | tf_op jit(solution)/shard_map/ppermute | solution.py:190
  9.9 1.9 %collective-permute-start.13 = (bf16[144,256]{1,0:T(8,128)(2,1)S(1)}, bf16[144,256]{1,0:T(8,128)(2,1)S(1)}, u32[]{:S(2)}, u32[]{:S(2)}) collective-permute-start(bf16[144,256]{1,0:T(8,128)(2,1)S(1)} %collective-permute-done.11.refs_12_), channel_id=1, source_target_pairs={{0,2},{1,3},{2,0},{3,1},{4,6},{5,7},{6,4},{7,5},{8,10},{9,11},{10,... | collective-permute-start | bytes 221192 | tf_op jit(solution)/shard_map/ppermute | solution.py:190
  11.7 1.6 %collective-permute-done.7.refs_8_ = bf16[144,256]{1,0:T(8,128)(2,1)S(1)} collective-permute-done((bf16[144,256]{1,0:T(8,128)(2,1)}, bf16[144,256]{1,0:T(8,128)(2,1)S(1)}, u32[]{:S(2)}, u32[]{:S(2)}) %collective-permute-start.7) | collective-permute-done | bytes 73760 | tf_op jit(solution)/shard_map/ppermute | solution.py:190
  13.3 0.0 collective-permute-start.12
  13.3 0.0 collective-permute-done.3.refs_4_
  13.3 1.5 %collective-permute-start.9 = (bf16[144,256]{1,0:T(8,128)(2,1)S(1)}, bf16[144,256]{1,0:T(8,128)(2,1)S(1)}, u32[]{:S(2)}, u32[]{:S(2)}) collective-permute-start(bf16[144,256]{1,0:T(8,128)(2,1)S(1)} %collective-permute-done.7.refs_8_), channel_id=1, source_target_pairs={{0,2},{1,3},{2,0},{3,1},{4,6},{5,7},{6,4},{7,5},{8,10},{9,11},{10,... | collective-permute-start | bytes 221192 | tf_op jit(solution)/shard_map/ppermute | solution.py:190
  14.8 0.0 collective-permute-done.1.refs_2_
  14.8 0.2 collective-permute-start.8
  15.1 0.5 %collective-permute-start.5 = (bf16[144,256]{1,0:T(8,128)(2,1)S(1)}, bf16[144,256]{1,0:T(8,128)(2,1)S(1)}, u32[]{:S(2)}, u32[]{:S(2)}) collective-permute-start(bf16[144,256]{1,0:T(8,128)(2,1)S(1)} %collective-permute-done.3.refs_4_), channel_id=1, source_target_pairs={{0,2},{1,3},{2,0},{3,1},{4,6},{5,7},{6,4},{7,5},{8,10},{9,11},{10,... | collective-permute-start | bytes 221192 | tf_op jit(solution)/shard_map/ppermute | solution.py:190
  15.6 0.0 collective-permute-start.4
  15.6 0.0 collective-permute-done.12.refs_13_
  15.6 0.5 %collective-permute-start.2 = (bf16[144,256]{1,0:T(8,128)(2,1)S(1)}, bf16[144,256]{1,0:T(8,128)(2,1)S(1)}, u32[]{:S(2)}, u32[]{:S(2)}) collective-permute-start(bf16[144,256]{1,0:T(8,128)(2,1)S(1)} %collective-permute-done.1.refs_2_), channel_id=1, source_target_pairs={{0,1},{1,0},{2,3},{3,2},{4,5},{5,4},{6,7},{7,6},{8,9},{9,8},{10,11... | collective-permute-start | bytes 221192 | tf_op jit(solution)/shard_map/ppermute | solution.py:190
  16.1 1.9 %collective-permute-done.9.refs_10_ = bf16[144,256]{1,0:T(8,128)(2,1)S(1)} collective-permute-done((bf16[144,256]{1,0:T(8,128)(2,1)S(1)}, bf16[144,256]{1,0:T(8,128)(2,1)S(1)}, u32[]{:S(2)}, u32[]{:S(2)}) %collective-permute-start.9) | collective-permute-done | bytes 73760 | tf_op jit(solution)/shard_map/ppermute | solution.py:190
  18.0 0.0 collective-permute-start.14
  18.0 0.0 collective-permute-done.8.refs_9_
  18.0 0.5 %collective-permute-start.10 = (bf16[144,256]{1,0:T(8,128)(2,1)S(1)}, bf16[144,256]{1,0:T(8,128)(2,1)S(1)}, u32[]{:S(2)}, u32[]{:S(2)}) collective-permute-start(bf16[144,256]{1,0:T(8,128)(2,1)S(1)} %collective-permute-done.9.refs_10_), channel_id=1, source_target_pairs={{0,1},{1,0},{2,3},{3,2},{4,5},{5,4},{6,7},{7,6},{8,9},{9,8},{10,11... | collective-permute-start | bytes 221192 | tf_op jit(solution)/shard_map/ppermute | solution.py:190
  18.5 1.0 %collective-permute-done.5.refs_6_ = bf16[144,256]{1,0:T(8,128)(2,1)S(1)} collective-permute-done((bf16[144,256]{1,0:T(8,128)(2,1)S(1)}, bf16[144,256]{1,0:T(8,128)(2,1)S(1)}, u32[]{:S(2)}, u32[]{:S(2)}) %collective-permute-start.5) | collective-permute-done | bytes 73760 | tf_op jit(solution)/shard_map/ppermute | solution.py:190
  19.6 2.2 %prepare.1 = (bf16[2,256,128]{2,1,0:T(8,128)(2,1)}, bf16[2,128,128]{2,1,0:T(8,128)(2,1)}, bf16[2,128,64]{2,1,0:T(8,128)(2,1)}, f32[2,128,128]{2,1,0:T(8,128)}, f...) custom-call(s32[1]{0:T(128)} %bitcast.me_ref, bf16[2,128,256]{2,1,0:T(8,128)(2,1)} %proj_ref.1, ...), custom_call_target="tpu_custom_call" | custom-call | tf_op jit(solution)/shard_map/prepare/pallas_call | solution.py:214
  21.7 0.0 collective-permute-done.4.refs_5_
  21.8 1.0 %copy-done = bf16[4,256,256]{2,1,0:T(8,128)(2,1)S(1)} copy-done((bf16[4,256,256]{2,1,0:T(8,128)(2,1)S(1)}, bf16[4,256,256]{2,1,0:T(8,128)(2,1)}, u32[]{:S(2)}) %copy-start) | copy-done | bytes 524312
  22.8 0.9 %copy-done.2 = bf16[2,256,128]{2,1,0:T(8,128)(2,1)S(1)} copy-done((bf16[2,256,128]{2,1,0:T(8,128)(2,1)S(1)}, bf16[2,256,128]{2,1,0:T(8,128)(2,1)}, u32[]{:S(2)}) %copy-start.2) | copy-done | bytes 131096
  23.7 0.9 %copy-done.3 = f32[2,128,128]{2,1,0:T(8,128)S(1)} copy-done((f32[2,128,128]{2,1,0:T(8,128)S(1)}, f32[2,128,128]{2,1,0:T(8,128)}, u32[]{:S(2)}) %copy-start.3) | copy-done | bytes 131096
  24.6 0.9 %copy-done.4 = bf16[256,256]{1,0:T(8,128)(2,1)S(1)} copy-done((bf16[256,256]{1,0:T(8,128)(2,1)S(1)}, bf16[256,256]{1,0:T(8,128)(2,1)}, u32[]{:S(2)}) %copy-start.4) | copy-done | bytes 131096
  25.6 0.8 %copy-done.5 = bf16[2,128,128]{2,1,0:T(8,128)(2,1)S(1)} copy-done((bf16[2,128,128]{2,1,0:T(8,128)(2,1)S(1)}, bf16[2,128,128]{2,1,0:T(8,128)(2,1)}, u32[]{:S(2)}) %copy-start.5) | copy-done | bytes 65560
  26.4 0.8 %copy-done.6 = bf16[2,128,64]{2,1,0:T(8,128)(2,1)S(1)} copy-done((bf16[2,128,64]{2,1,0:T(8,128)(2,1)S(1)}, bf16[2,128,64]{2,1,0:T(8,128)(2,1)}, u32[]{:S(2)}) %copy-start.6) | copy-done | bytes 32792
  27.2 0.8 %copy-done.7 = f32[2,64,128]{2,1,0:T(8,128)S(1)} copy-done((f32[2,64,128]{2,1,0:T(8,128)S(1)}, f32[2,64,128]{2,1,0:T(8,128)}, u32[]{:S(2)}) %copy-start.7) | copy-done | bytes 65560
  28.1 11.0 %both.1 = bf16[256,128]{1,0:T(8,128)(2,1)} custom-call(s32[1]{0:T(128)} %bitcast.me_ref, bf16[144,256]{1,0:T(8,128)(2,1)S(1)} %copy-done.1, bf16[144,256]{1,0:T(8,128)(2,1)S(1)} %collective-permute-done.refs_1_, bf16[144,256]{1,0:T(8,128)(2,1)S(1)} %collective-permute-done.1.refs_2_, bf16[144,256]{1,0:T(8,128)(2,1)S(1)} %collective-permute-done.2.refs_3_, ...), custom_call_target="tpu_custom_call" | custom-call | tf_op jit(solution)/shard_map/both/pallas_call | solution.py:229
  (17 shorter events, 0.0 us)
Async XLA Ops:
  1.8 8.0 %collective-permute-start.11 = (bf16[144,256]{1,0:T(8,128)(2,1)}, bf16[144,256]{1,0:T(8,128)(2,1)S(1)}, u32[]{:S(2)}, u32[]{:S(2)}) collective-permute-start(bf16[144,256]{1,0:T(8,128)(2,1)} %pack.1.refs_0_), channel_id=1, source_target_pairs={{0,12},{1,13},{2,14},{3,15},{4,8},{5,9},{6,10},{7,11},{8,4},{9,5},... | collective-permute-start | bytes 221192 | tf_op jit(solution)/shard_map/ppermute | solution.py:190
  6.9 6.4 %collective-permute-start.7 = (bf16[144,256]{1,0:T(8,128)(2,1)}, bf16[144,256]{1,0:T(8,128)(2,1)S(1)}, u32[]{:S(2)}, u32[]{:S(2)}) collective-permute-start(bf16[144,256]{1,0:T(8,128)(2,1)} %pack.1.refs_0_), channel_id=1, source_target_pairs={{0,8},{1,9},{2,10},{3,11},{4,12},{5,13},{6,14},{7,15},{8,0},{9,1},... | collective-permute-start | bytes 221192 | tf_op jit(solution)/shard_map/ppermute | solution.py:190
  6.9 6.4 %collective-permute-start.3 = (bf16[144,256]{1,0:T(8,128)(2,1)}, bf16[144,256]{1,0:T(8,128)(2,1)S(1)}, u32[]{:S(2)}, u32[]{:S(2)}) collective-permute-start(bf16[144,256]{1,0:T(8,128)(2,1)} %pack.1.refs_0_), channel_id=1, source_target_pairs={{0,4},{1,5},{2,6},{3,7},{4,0},{5,1},{6,2},{7,3},{8,12},{9,13},{10,... | collective-permute-start | bytes 221192 | tf_op jit(solution)/shard_map/ppermute | solution.py:190
  7.4 7.4 %collective-permute-start.1 = (bf16[144,256]{1,0:T(8,128)(2,1)}, bf16[144,256]{1,0:T(8,128)(2,1)S(1)}, u32[]{:S(2)}, u32[]{:S(2)}) collective-permute-start(bf16[144,256]{1,0:T(8,128)(2,1)} %pack.1.refs_0_), channel_id=1, source_target_pairs={{0,2},{1,3},{2,0},{3,1},{4,6},{5,7},{6,4},{7,5},{8,10},{9,11},{10,... | collective-permute-start | bytes 221192 | tf_op jit(solution)/shard_map/ppermute | solution.py:190
  9.2 5.9 %collective-permute-start = (bf16[144,256]{1,0:T(8,128)(2,1)}, bf16[144,256]{1,0:T(8,128)(2,1)S(1)}, u32[]{:S(2)}, u32[]{:S(2)}) collective-permute-start(bf16[144,256]{1,0:T(8,128)(2,1)} %pack.1.refs_0_), channel_id=1, source_target_pairs={{0,1},{1,0},{2,3},{3,2},{4,5},{5,4},{6,7},{7,6},{8,9},{9,8},{10,11... | collective-permute-start | bytes 221192 | tf_op jit(solution)/shard_map/ppermute | solution.py:190
  9.9 5.7 %collective-permute-start.13 = (bf16[144,256]{1,0:T(8,128)(2,1)S(1)}, bf16[144,256]{1,0:T(8,128)(2,1)S(1)}, u32[]{:S(2)}, u32[]{:S(2)}) collective-permute-start(bf16[144,256]{1,0:T(8,128)(2,1)S(1)} %collective-permute-done.11.refs_12_), channel_id=1, source_target_pairs={{0,2},{1,3},{2,0},{3,1},{4,6},{5,7},{6,4},{7,5},{8,10},{9,11},{10,... | collective-permute-start | bytes 221192 | tf_op jit(solution)/shard_map/ppermute | solution.py:190
  13.3 2.3 %collective-permute-start.12 = (bf16[144,256]{1,0:T(8,128)(2,1)S(1)}, bf16[144,256]{1,0:T(8,128)(2,1)S(1)}, u32[]{:S(2)}, u32[]{:S(2)}) collective-permute-start(bf16[144,256]{1,0:T(8,128)(2,1)S(1)} %collective-permute-done.11.refs_12_), channel_id=1, source_target_pairs={{0,1},{1,0},{2,3},{3,2},{4,5},{5,4},{6,7},{7,6},{8,9},{9,8},{10,11... | collective-permute-start | bytes 221192 | tf_op jit(solution)/shard_map/ppermute | solution.py:190
  13.3 4.7 %collective-permute-start.9 = (bf16[144,256]{1,0:T(8,128)(2,1)S(1)}, bf16[144,256]{1,0:T(8,128)(2,1)S(1)}, u32[]{:S(2)}, u32[]{:S(2)}) collective-permute-start(bf16[144,256]{1,0:T(8,128)(2,1)S(1)} %collective-permute-done.7.refs_8_), channel_id=1, source_target_pairs={{0,2},{1,3},{2,0},{3,1},{4,6},{5,7},{6,4},{7,5},{8,10},{9,11},{10,... | collective-permute-start | bytes 221192 | tf_op jit(solution)/shard_map/ppermute | solution.py:190
  14.8 3.2 %collective-permute-start.8 = (bf16[144,256]{1,0:T(8,128)(2,1)S(1)}, bf16[144,256]{1,0:T(8,128)(2,1)S(1)}, u32[]{:S(2)}, u32[]{:S(2)}) collective-permute-start(bf16[144,256]{1,0:T(8,128)(2,1)S(1)} %collective-permute-done.7.refs_8_), channel_id=1, source_target_pairs={{0,1},{1,0},{2,3},{3,2},{4,5},{5,4},{6,7},{7,6},{8,9},{9,8},{10,11... | collective-permute-start | bytes 221192 | tf_op jit(solution)/shard_map/ppermute | solution.py:190
  15.1 4.5 %collective-permute-start.5 = (bf16[144,256]{1,0:T(8,128)(2,1)S(1)}, bf16[144,256]{1,0:T(8,128)(2,1)S(1)}, u32[]{:S(2)}, u32[]{:S(2)}) collective-permute-start(bf16[144,256]{1,0:T(8,128)(2,1)S(1)} %collective-permute-done.3.refs_4_), channel_id=1, source_target_pairs={{0,2},{1,3},{2,0},{3,1},{4,6},{5,7},{6,4},{7,5},{8,10},{9,11},{10,... | collective-permute-start | bytes 221192 | tf_op jit(solution)/shard_map/ppermute | solution.py:190
  15.6 6.2 %collective-permute-start.4 = (bf16[144,256]{1,0:T(8,128)(2,1)S(1)}, bf16[144,256]{1,0:T(8,128)(2,1)S(1)}, u32[]{:S(2)}, u32[]{:S(2)}) collective-permute-start(bf16[144,256]{1,0:T(8,128)(2,1)S(1)} %collective-permute-done.3.refs_4_), channel_id=1, source_target_pairs={{0,1},{1,0},{2,3},{3,2},{4,5},{5,4},{6,7},{7,6},{8,9},{9,8},{10,11... | collective-permute-start | bytes 221192 | tf_op jit(solution)/shard_map/ppermute | solution.py:190
  15.6 6.2 %collective-permute-start.2 = (bf16[144,256]{1,0:T(8,128)(2,1)S(1)}, bf16[144,256]{1,0:T(8,128)(2,1)S(1)}, u32[]{:S(2)}, u32[]{:S(2)}) collective-permute-start(bf16[144,256]{1,0:T(8,128)(2,1)S(1)} %collective-permute-done.1.refs_2_), channel_id=1, source_target_pairs={{0,1},{1,0},{2,3},{3,2},{4,5},{5,4},{6,7},{7,6},{8,9},{9,8},{10,11... | collective-permute-start | bytes 221192 | tf_op jit(solution)/shard_map/ppermute | solution.py:190
  18.0 3.7 %collective-permute-start.14 = (bf16[144,256]{1,0:T(8,128)(2,1)S(1)}, bf16[144,256]{1,0:T(8,128)(2,1)S(1)}, u32[]{:S(2)}, u32[]{:S(2)}) collective-permute-start(bf16[144,256]{1,0:T(8,128)(2,1)S(1)} %collective-permute-done.13.refs_14_), channel_id=1, source_target_pairs={{0,1},{1,0},{2,3},{3,2},{4,5},{5,4},{6,7},{7,6},{8,9},{9,8},{10,11... | collective-permute-start | bytes 221192 | tf_op jit(solution)/shard_map/ppermute | solution.py:190
  18.0 3.7 %collective-permute-start.10 = (bf16[144,256]{1,0:T(8,128)(2,1)S(1)}, bf16[144,256]{1,0:T(8,128)(2,1)S(1)}, u32[]{:S(2)}, u32[]{:S(2)}) collective-permute-start(bf16[144,256]{1,0:T(8,128)(2,1)S(1)} %collective-permute-done.9.refs_10_), channel_id=1, source_target_pairs={{0,1},{1,0},{2,3},{3,2},{4,5},{5,4},{6,7},{7,6},{8,9},{9,8},{10,11... | collective-permute-start | bytes 221192 | tf_op jit(solution)/shard_map/ppermute | solution.py:190
  19.6 2.2 %collective-permute-start.6 = (bf16[144,256]{1,0:T(8,128)(2,1)S(1)}, bf16[144,256]{1,0:T(8,128)(2,1)S(1)}, u32[]{:S(2)}, u32[]{:S(2)}) collective-permute-start(bf16[144,256]{1,0:T(8,128)(2,1)S(1)} %collective-permute-done.5.refs_6_), channel_id=1, source_target_pairs={{0,1},{1,0},{2,3},{3,2},{4,5},{5,4},{6,7},{7,6},{8,9},{9,8},{10,11... | collective-permute-start | bytes 221192 | tf_op jit(solution)/shard_map/ppermute | solution.py:190
  19.6 2.2 %copy-start.1 = (bf16[144,256]{1,0:T(8,128)(2,1)S(1)}, bf16[144,256]{1,0:T(8,128)(2,1)}, u32[]{:S(2)}) copy-start(bf16[144,256]{1,0:T(8,128)(2,1)} %pack.1.refs_0_) | copy-start | bytes 221188
  21.8 1.0 %copy-start = (bf16[4,256,256]{2,1,0:T(8,128)(2,1)S(1)}, bf16[4,256,256]{2,1,0:T(8,128)(2,1)}, u32[]{:S(2)}) copy-start(bf16[4,256,256]{2,1,0:T(8,128)(2,1)} %get-tuple-element.18.refs_22_) | copy-start | bytes 1572868
  22.8 0.9 %copy-start.2 = (bf16[2,256,128]{2,1,0:T(8,128)(2,1)S(1)}, bf16[2,256,128]{2,1,0:T(8,128)(2,1)}, u32[]{:S(2)}) copy-start(bf16[2,256,128]{2,1,0:T(8,128)(2,1)} %get-tuple-element.12.refs_16_) | copy-start | bytes 393220
  23.7 0.9 %copy-start.3 = (f32[2,128,128]{2,1,0:T(8,128)S(1)}, f32[2,128,128]{2,1,0:T(8,128)}, u32[]{:S(2)}) copy-start(f32[2,128,128]{2,1,0:T(8,128)} %get-tuple-element.15.refs_19_) | copy-start | bytes 393220
  24.6 0.9 %copy-start.4 = (bf16[256,256]{1,0:T(8,128)(2,1)S(1)}, bf16[256,256]{1,0:T(8,128)(2,1)}, u32[]{:S(2)}) copy-start(bf16[256,256]{1,0:T(8,128)(2,1)} %get-tuple-element.17.refs_21_) | copy-start | bytes 393220
  25.6 0.8 %copy-start.5 = (bf16[2,128,128]{2,1,0:T(8,128)(2,1)S(1)}, bf16[2,128,128]{2,1,0:T(8,128)(2,1)}, u32[]{:S(2)}) copy-start(bf16[2,128,128]{2,1,0:T(8,128)(2,1)} %get-tuple-element.13.refs_17_) | copy-start | bytes 196612
  26.4 0.8 %copy-start.6 = (bf16[2,128,64]{2,1,0:T(8,128)(2,1)S(1)}, bf16[2,128,64]{2,1,0:T(8,128)(2,1)}, u32[]{:S(2)}) copy-start(bf16[2,128,64]{2,1,0:T(8,128)(2,1)} %get-tuple-element.14.refs_18_) | copy-start | bytes 98308
  27.2 0.8 %copy-start.7 = (f32[2,64,128]{2,1,0:T(8,128)S(1)}, f32[2,64,128]{2,1,0:T(8,128)}, u32[]{:S(2)}) copy-start(f32[2,64,128]{2,1,0:T(8,128)} %get-tuple-element.16.refs_20_) | copy-start | bytes 196612

commit v5 on v4

--- a/solution.py
+++ b/solution.py
@@ -192,10 +192,10 @@
 
 def everyone(packed, devices):
     blocks = {0: packed}
-    for m in range(4, devices, 4):
+    for m in range(devices - 4, 0, -4):
         blocks[m] = exchange(packed, m, devices)
     for step in (2, 1):
-        for m in sorted(blocks):
+        for m in sorted(blocks, reverse=True):
             blocks[m ^ step] = exchange(blocks[m], step, devices)
     return [blocks[m] for m in range(devices)]
 
@@ -203,17 +203,19 @@
 def small_plan(pair, mask, proj, gate, out, gain, mid):
     rows, tokens, channels = pair.shape
     devices, size, hw = tokens // rows, rows * tokens, out.shape[1]
+    index = pl.BlockSpec(memory_space=pltpu.SMEM)
+    vmem = pl.BlockSpec(memory_space=pltpu.VMEM)
     packed = pl.pallas_call(
         functools.partial(pack_kernel, rows, tokens),
         out_shape=jax.ShapeDtypeStruct((channels + MASK_ROWS, size), BF16),
+        out_specs=vmem,
         name="pack",
     )(pair.reshape(size, channels), mask)
     me = lax.axis_index("row").reshape(1).astype(jnp.int32)
-    whole = pl.BlockSpec()
-    index = pl.BlockSpec(memory_space=pltpu.SMEM)
     weights = pl.pallas_call(
         functools.partial(prepare_kernel, rows, tokens),
-        in_specs=[index] + [whole] * 5,
+        in_specs=[index] + [pl.BlockSpec()] * 5,
+        out_specs=(vmem,) * 7,
         out_shape=(
             jax.ShapeDtypeStruct((2, 4 * hw, channels), BF16),
             jax.ShapeDtypeStruct((2, channels, channels), BF16),
@@ -229,7 +231,7 @@
     result = pl.pallas_call(
         functools.partial(both_kernel, rows, tokens),
         out_shape=jax.ShapeDtypeStruct((size, channels), BF16),
-        in_specs=[index] + [whole] * (devices + len(weights)),
+        in_specs=[index] + [vmem] * (devices + len(weights)),
         scratch_shapes=[
             pltpu.VMEM((size // LANES, devices * hw, LANES), F32),
             pltpu.VMEM((size // LANES, devices * hw, LANES), F32),

time: 39.5 us -> 39.5 us (level)
  no operation moved by 1% of the time
where the time goes in v5:
time: 39.5 us; the launch traced here: 39 us
  Pallas kernels  15 us (38%)
  starting transfers between devices  12.5 us (32%)
  local copies, waits for them, and re-layouts  6.27 us (16%)
  waiting for transfers between devices  5.25 us (13%)
    ppermute x15, starting transfers between devices, exchange(): return lax.ppermute(block, 'row', pairs)  12.5 us
    pallas_call x1, Pallas kernels, small_plan(): pl.pallas_call(functools.partial(both_kernel, rows, tokens), out_shape=ja...  11 us
    unnamed x16, local copies, waits for them, and re-layouts  6.27 us
    ppermute x15, waiting for transfers between devices, exchange(): return lax.ppermute(block, 'row', pairs)  5.25 us
    pallas_call x1, Pallas kernels, small_plan(): pl.pallas_call(functools.partial(prepare_kernel, rows, tokens), in_specs=...  2.17 us
    pallas_call x1, Pallas kernels, small_plan(): pl.pallas_call(functools.partial(pack_kernel, rows, tokens), out_shape=ja...  1.83 us
  transfers between devices with their start and end apart: 15, of which 4 were waited for; matrix products, arithmetic and copies ran while one was open for 0% of the time, Pallas kernels for 6%

profile of v5, /device:TPU:0, one launch (start us, length us, event | category | flops | bytes accessed | tf_op | source)
XLA Modules:
  0.0 39.0 jit_solution(111136972576075637)
XLA Ops:
  0.0 1.8 %pack.1.refs_0_ = bf16[144,256]{1,0:T(8,128)(2,1)} custom-call(bf16[256,128]{1,0:T(8,128)(2,1)} %bitcast.3, s32[4,64]{1,0:T(4,128)} %mask_ref.1), custom_call_target="tpu_custom_call" | custom-call | tf_op jit(solution)/shard_map/pack/pallas_call | solution.py:208
  1.8 5.0 %collective-permute-start.11 = (bf16[144,256]{1,0:T(8,128)(2,1)}, bf16[144,256]{1,0:T(8,128)(2,1)S(1)}, u32[]{:S(2)}, u32[]{:S(2)}) collective-permute-start(bf16[144,256]{1,0:T(8,128)(2,1)} %pack.1.refs_0_), channel_id=1, source_target_pairs={{0,12},{1,13},{2,14},{3,15},{4,8},{5,9},{6,10},{7,11},{8,4},{9,5},... | collective-permute-start | bytes 221192 | tf_op jit(solution)/shard_map/ppermute | solution.py:190
  6.9 0.0 collective-permute-start.7
  6.9 0.6 %collective-permute-start.3 = (bf16[144,256]{1,0:T(8,128)(2,1)}, bf16[144,256]{1,0:T(8,128)(2,1)S(1)}, u32[]{:S(2)}, u32[]{:S(2)}) collective-permute-start(bf16[144,256]{1,0:T(8,128)(2,1)} %pack.1.refs_0_), channel_id=1, source_target_pairs={{0,4},{1,5},{2,6},{3,7},{4,0},{5,1},{6,2},{7,3},{8,12},{9,13},{10,... | collective-permute-start | bytes 221192 | tf_op jit(solution)/shard_map/ppermute | solution.py:190
  7.4 1.7 %collective-permute-start.1 = (bf16[144,256]{1,0:T(8,128)(2,1)}, bf16[144,256]{1,0:T(8,128)(2,1)S(1)}, u32[]{:S(2)}, u32[]{:S(2)}) collective-permute-start(bf16[144,256]{1,0:T(8,128)(2,1)} %pack.1.refs_0_), channel_id=1, source_target_pairs={{0,2},{1,3},{2,0},{3,1},{4,6},{5,7},{6,4},{7,5},{8,10},{9,11},{10,... | collective-permute-start | bytes 221192 | tf_op jit(solution)/shard_map/ppermute | solution.py:190
  9.2 0.7 %collective-permute-done.11.refs_12_ = bf16[144,256]{1,0:T(8,128)(2,1)S(1)} collective-permute-done((bf16[144,256]{1,0:T(8,128)(2,1)}, bf16[144,256]{1,0:T(8,128)(2,1)S(1)}, u32[]{:S(2)}, u32[]{:S(2)}) %collective-permute-start.11) | collective-permute-done | bytes 73760 | tf_op jit(solution)/shard_map/ppermute | solution.py:190
  9.9 1.9 %collective-permute-start.13 = (bf16[144,256]{1,0:T(8,128)(2,1)S(1)}, bf16[144,256]{1,0:T(8,128)(2,1)S(1)}, u32[]{:S(2)}, u32[]{:S(2)}) collective-permute-start(bf16[144,256]{1,0:T(8,128)(2,1)S(1)} %collective-permute-done.11.refs_12_), channel_id=1, source_target_pairs={{0,2},{1,3},{2,0},{3,1},{4,6},{5,7},{6,4},{7,5},{8,10},{9,11},{10,... | collective-permute-start | bytes 221192 | tf_op jit(solution)/shard_map/ppermute | solution.py:190
  11.7 1.6 %collective-permute-done.7.refs_8_ = bf16[144,256]{1,0:T(8,128)(2,1)S(1)} collective-permute-done((bf16[144,256]{1,0:T(8,128)(2,1)}, bf16[144,256]{1,0:T(8,128)(2,1)S(1)}, u32[]{:S(2)}, u32[]{:S(2)}) %collective-permute-start.7) | collective-permute-done | bytes 73760 | tf_op jit(solution)/shard_map/ppermute | solution.py:190
  13.3 0.0 collective-permute-start.12
  13.3 0.0 collective-permute-done.3.refs_4_
  13.3 1.5 %collective-permute-start.9 = (bf16[144,256]{1,0:T(8,128)(2,1)S(1)}, bf16[144,256]{1,0:T(8,128)(2,1)S(1)}, u32[]{:S(2)}, u32[]{:S(2)}) collective-permute-start(bf16[144,256]{1,0:T(8,128)(2,1)S(1)} %collective-permute-done.7.refs_8_), channel_id=1, source_target_pairs={{0,2},{1,3},{2,0},{3,1},{4,6},{5,7},{6,4},{7,5},{8,10},{9,11},{10,... | collective-permute-start | bytes 221192 | tf_op jit(solution)/shard_map/ppermute | solution.py:190
  14.8 0.0 collective-permute-done.1.refs_2_
  14.8 0.2 collective-permute-start.8
  15.1 0.5 %collective-permute-start.5 = (bf16[144,256]{1,0:T(8,128)(2,1)S(1)}, bf16[144,256]{1,0:T(8,128)(2,1)S(1)}, u32[]{:S(2)}, u32[]{:S(2)}) collective-permute-start(bf16[144,256]{1,0:T(8,128)(2,1)S(1)} %collective-permute-done.3.refs_4_), channel_id=1, source_target_pairs={{0,2},{1,3},{2,0},{3,1},{4,6},{5,7},{6,4},{7,5},{8,10},{9,11},{10,... | collective-permute-start | bytes 221192 | tf_op jit(solution)/shard_map/ppermute | solution.py:190
  15.6 0.0 collective-permute-start.4
  15.6 0.0 collective-permute-done.12.refs_13_
  15.6 0.5 %collective-permute-start.2 = (bf16[144,256]{1,0:T(8,128)(2,1)S(1)}, bf16[144,256]{1,0:T(8,128)(2,1)S(1)}, u32[]{:S(2)}, u32[]{:S(2)}) collective-permute-start(bf16[144,256]{1,0:T(8,128)(2,1)S(1)} %collective-permute-done.1.refs_2_), channel_id=1, source_target_pairs={{0,1},{1,0},{2,3},{3,2},{4,5},{5,4},{6,7},{7,6},{8,9},{9,8},{10,11... | collective-permute-start | bytes 221192 | tf_op jit(solution)/shard_map/ppermute | solution.py:190
  16.1 1.9 %collective-permute-done.9.refs_10_ = bf16[144,256]{1,0:T(8,128)(2,1)S(1)} collective-permute-done((bf16[144,256]{1,0:T(8,128)(2,1)S(1)}, bf16[144,256]{1,0:T(8,128)(2,1)S(1)}, u32[]{:S(2)}, u32[]{:S(2)}) %collective-permute-start.9) | collective-permute-done | bytes 73760 | tf_op jit(solution)/shard_map/ppermute | solution.py:190
  18.0 0.0 collective-permute-start.14
  18.0 0.0 collective-permute-done.8.refs_9_
  18.0 0.5 %collective-permute-start.10 = (bf16[144,256]{1,0:T(8,128)(2,1)S(1)}, bf16[144,256]{1,0:T(8,128)(2,1)S(1)}, u32[]{:S(2)}, u32[]{:S(2)}) collective-permute-start(bf16[144,256]{1,0:T(8,128)(2,1)S(1)} %collective-permute-done.9.refs_10_), channel_id=1, source_target_pairs={{0,1},{1,0},{2,3},{3,2},{4,5},{5,4},{6,7},{7,6},{8,9},{9,8},{10,11... | collective-permute-start | bytes 221192 | tf_op jit(solution)/shard_map/ppermute | solution.py:190
  18.5 1.0 %collective-permute-done.5.refs_6_ = bf16[144,256]{1,0:T(8,128)(2,1)S(1)} collective-permute-done((bf16[144,256]{1,0:T(8,128)(2,1)S(1)}, bf16[144,256]{1,0:T(8,128)(2,1)S(1)}, u32[]{:S(2)}, u32[]{:S(2)}) %collective-permute-start.5) | collective-permute-done | bytes 73760 | tf_op jit(solution)/shard_map/ppermute | solution.py:190
  19.6 2.2 %prepare.1 = (bf16[2,256,128]{2,1,0:T(8,128)(2,1)}, bf16[2,128,128]{2,1,0:T(8,128)(2,1)}, bf16[2,128,64]{2,1,0:T(8,128)(2,1)}, f32[2,128,128]{2,1,0:T(8,128)}, f...) custom-call(s32[1]{0:T(128)} %bitcast.me_ref, bf16[2,128,256]{2,1,0:T(8,128)(2,1)} %proj_ref.1, ...), custom_call_target="tpu_custom_call" | custom-call | tf_op jit(solution)/shard_map/prepare/pallas_call | solution.py:215
  21.7 0.0 collective-permute-done.4.refs_5_
  21.8 1.0 %copy-done = bf16[4,256,256]{2,1,0:T(8,128)(2,1)S(1)} copy-done((bf16[4,256,256]{2,1,0:T(8,128)(2,1)S(1)}, bf16[4,256,256]{2,1,0:T(8,128)(2,1)}, u32[]{:S(2)}) %copy-start) | copy-done | bytes 524312
  22.8 0.9 %copy-done.2 = bf16[2,256,128]{2,1,0:T(8,128)(2,1)S(1)} copy-done((bf16[2,256,128]{2,1,0:T(8,128)(2,1)S(1)}, bf16[2,256,128]{2,1,0:T(8,128)(2,1)}, u32[]{:S(2)}) %copy-start.2) | copy-done | bytes 131096
  23.7 0.9 %copy-done.3 = f32[2,128,128]{2,1,0:T(8,128)S(1)} copy-done((f32[2,128,128]{2,1,0:T(8,128)S(1)}, f32[2,128,128]{2,1,0:T(8,128)}, u32[]{:S(2)}) %copy-start.3) | copy-done | bytes 131096
  24.6 0.9 %copy-done.4 = bf16[256,256]{1,0:T(8,128)(2,1)S(1)} copy-done((bf16[256,256]{1,0:T(8,128)(2,1)S(1)}, bf16[256,256]{1,0:T(8,128)(2,1)}, u32[]{:S(2)}) %copy-start.4) | copy-done | bytes 131096
  25.6 0.8 %copy-done.5 = bf16[2,128,128]{2,1,0:T(8,128)(2,1)S(1)} copy-done((bf16[2,128,128]{2,1,0:T(8,128)(2,1)S(1)}, bf16[2,128,128]{2,1,0:T(8,128)(2,1)}, u32[]{:S(2)}) %copy-start.5) | copy-done | bytes 65560
  26.4 0.8 %copy-done.6 = bf16[2,128,64]{2,1,0:T(8,128)(2,1)S(1)} copy-done((bf16[2,128,64]{2,1,0:T(8,128)(2,1)S(1)}, bf16[2,128,64]{2,1,0:T(8,128)(2,1)}, u32[]{:S(2)}) %copy-start.6) | copy-done | bytes 32792
  27.2 0.8 %copy-done.7 = f32[2,64,128]{2,1,0:T(8,128)S(1)} copy-done((f32[2,64,128]{2,1,0:T(8,128)S(1)}, f32[2,64,128]{2,1,0:T(8,128)}, u32[]{:S(2)}) %copy-start.7) | copy-done | bytes 65560
  28.1 11.0 %both.1 = bf16[256,128]{1,0:T(8,128)(2,1)} custom-call(s32[1]{0:T(128)} %bitcast.me_ref, bf16[144,256]{1,0:T(8,128)(2,1)S(1)} %copy-done.1, bf16[144,256]{1,0:T(8,128)(2,1)S(1)} %collective-permute-done.refs_1_, bf16[144,256]{1,0:T(8,128)(2,1)S(1)} %collective-permute-done.1.refs_2_, bf16[144,256]{1,0:T(8,128)(2,1)S(1)} %collective-permute-done.2.refs_3_, ...), custom_call_target="tpu_custom_call" | custom-call | tf_op jit(solution)/shard_map/both/pallas_call | solution.py:231
  (17 shorter events, 0.0 us)
Async XLA Ops:
  1.8 8.0 %collective-permute-start.11 = (bf16[144,256]{1,0:T(8,128)(2,1)}, bf16[144,256]{1,0:T(8,128)(2,1)S(1)}, u32[]{:S(2)}, u32[]{:S(2)}) collective-permute-start(bf16[144,256]{1,0:T(8,128)(2,1)} %pack.1.refs_0_), channel_id=1, source_target_pairs={{0,12},{1,13},{2,14},{3,15},{4,8},{5,9},{6,10},{7,11},{8,4},{9,5},... | collective-permute-start | bytes 221192 | tf_op jit(solution)/shard_map/ppermute | solution.py:190
  6.9 6.4 %collective-permute-start.7 = (bf16[144,256]{1,0:T(8,128)(2,1)}, bf16[144,256]{1,0:T(8,128)(2,1)S(1)}, u32[]{:S(2)}, u32[]{:S(2)}) collective-permute-start(bf16[144,256]{1,0:T(8,128)(2,1)} %pack.1.refs_0_), channel_id=1, source_target_pairs={{0,8},{1,9},{2,10},{3,11},{4,12},{5,13},{6,14},{7,15},{8,0},{9,1},... | collective-permute-start | bytes 221192 | tf_op jit(solution)/shard_map/ppermute | solution.py:190
  6.9 6.4 %collective-permute-start.3 = (bf16[144,256]{1,0:T(8,128)(2,1)}, bf16[144,256]{1,0:T(8,128)(2,1)S(1)}, u32[]{:S(2)}, u32[]{:S(2)}) collective-permute-start(bf16[144,256]{1,0:T(8,128)(2,1)} %pack.1.refs_0_), channel_id=1, source_target_pairs={{0,4},{1,5},{2,6},{3,7},{4,0},{5,1},{6,2},{7,3},{8,12},{9,13},{10,... | collective-permute-start | bytes 221192 | tf_op jit(solution)/shard_map/ppermute | solution.py:190
  7.4 7.4 %collective-permute-start.1 = (bf16[144,256]{1,0:T(8,128)(2,1)}, bf16[144,256]{1,0:T(8,128)(2,1)S(1)}, u32[]{:S(2)}, u32[]{:S(2)}) collective-permute-start(bf16[144,256]{1,0:T(8,128)(2,1)} %pack.1.refs_0_), channel_id=1, source_target_pairs={{0,2},{1,3},{2,0},{3,1},{4,6},{5,7},{6,4},{7,5},{8,10},{9,11},{10,... | collective-permute-start | bytes 221192 | tf_op jit(solution)/shard_map/ppermute | solution.py:190
  9.2 5.9 %collective-permute-start = (bf16[144,256]{1,0:T(8,128)(2,1)}, bf16[144,256]{1,0:T(8,128)(2,1)S(1)}, u32[]{:S(2)}, u32[]{:S(2)}) collective-permute-start(bf16[144,256]{1,0:T(8,128)(2,1)} %pack.1.refs_0_), channel_id=1, source_target_pairs={{0,1},{1,0},{2,3},{3,2},{4,5},{5,4},{6,7},{7,6},{8,9},{9,8},{10,11... | collective-permute-start | bytes 221192 | tf_op jit(solution)/shard_map/ppermute | solution.py:190
  9.9 5.7 %collective-permute-start.13 = (bf16[144,256]{1,0:T(8,128)(2,1)S(1)}, bf16[144,256]{1,0:T(8,128)(2,1)S(1)}, u32[]{:S(2)}, u32[]{:S(2)}) collective-permute-start(bf16[144,256]{1,0:T(8,128)(2,1)S(1)} %collective-permute-done.11.refs_12_), channel_id=1, source_target_pairs={{0,2},{1,3},{2,0},{3,1},{4,6},{5,7},{6,4},{7,5},{8,10},{9,11},{10,... | collective-permute-start | bytes 221192 | tf_op jit(solution)/shard_map/ppermute | solution.py:190
  13.3 2.3 %collective-permute-start.12 = (bf16[144,256]{1,0:T(8,128)(2,1)S(1)}, bf16[144,256]{1,0:T(8,128)(2,1)S(1)}, u32[]{:S(2)}, u32[]{:S(2)}) collective-permute-start(bf16[144,256]{1,0:T(8,128)(2,1)S(1)} %collective-permute-done.11.refs_12_), channel_id=1, source_target_pairs={{0,1},{1,0},{2,3},{3,2},{4,5},{5,4},{6,7},{7,6},{8,9},{9,8},{10,11... | collective-permute-start | bytes 221192 | tf_op jit(solution)/shard_map/ppermute | solution.py:190
  13.3 4.7 %collective-permute-start.9 = (bf16[144,256]{1,0:T(8,128)(2,1)S(1)}, bf16[144,256]{1,0:T(8,128)(2,1)S(1)}, u32[]{:S(2)}, u32[]{:S(2)}) collective-permute-start(bf16[144,256]{1,0:T(8,128)(2,1)S(1)} %collective-permute-done.7.refs_8_), channel_id=1, source_target_pairs={{0,2},{1,3},{2,0},{3,1},{4,6},{5,7},{6,4},{7,5},{8,10},{9,11},{10,... | collective-permute-start | bytes 221192 | tf_op jit(solution)/shard_map/ppermute | solution.py:190
  14.8 3.2 %collective-permute-start.8 = (bf16[144,256]{1,0:T(8,128)(2,1)S(1)}, bf16[144,256]{1,0:T(8,128)(2,1)S(1)}, u32[]{:S(2)}, u32[]{:S(2)}) collective-permute-start(bf16[144,256]{1,0:T(8,128)(2,1)S(1)} %collective-permute-done.7.refs_8_), channel_id=1, source_target_pairs={{0,1},{1,0},{2,3},{3,2},{4,5},{5,4},{6,7},{7,6},{8,9},{9,8},{10,11... | collective-permute-start | bytes 221192 | tf_op jit(solution)/shard_map/ppermute | solution.py:190
  15.1 4.5 %collective-permute-start.5 = (bf16[144,256]{1,0:T(8,128)(2,1)S(1)}, bf16[144,256]{1,0:T(8,128)(2,1)S(1)}, u32[]{:S(2)}, u32[]{:S(2)}) collective-permute-start(bf16[144,256]{1,0:T(8,128)(2,1)S(1)} %collective-permute-done.3.refs_4_), channel_id=1, source_target_pairs={{0,2},{1,3},{2,0},{3,1},{4,6},{5,7},{6,4},{7,5},{8,10},{9,11},{10,... | collective-permute-start | bytes 221192 | tf_op jit(solution)/shard_map/ppermute | solution.py:190
  15.6 6.2 %collective-permute-start.4 = (bf16[144,256]{1,0:T(8,128)(2,1)S(1)}, bf16[144,256]{1,0:T(8,128)(2,1)S(1)}, u32[]{:S(2)}, u32[]{:S(2)}) collective-permute-start(bf16[144,256]{1,0:T(8,128)(2,1)S(1)} %collective-permute-done.3.refs_4_), channel_id=1, source_target_pairs={{0,1},{1,0},{2,3},{3,2},{4,5},{5,4},{6,7},{7,6},{8,9},{9,8},{10,11... | collective-permute-start | bytes 221192 | tf_op jit(solution)/shard_map/ppermute | solution.py:190
  15.6 6.2 %collective-permute-start.2 = (bf16[144,256]{1,0:T(8,128)(2,1)S(1)}, bf16[144,256]{1,0:T(8,128)(2,1)S(1)}, u32[]{:S(2)}, u32[]{:S(2)}) collective-permute-start(bf16[144,256]{1,0:T(8,128)(2,1)S(1)} %collective-permute-done.1.refs_2_), channel_id=1, source_target_pairs={{0,1},{1,0},{2,3},{3,2},{4,5},{5,4},{6,7},{7,6},{8,9},{9,8},{10,11... | collective-permute-start | bytes 221192 | tf_op jit(solution)/shard_map/ppermute | solution.py:190
  18.0 3.7 %collective-permute-start.14 = (bf16[144,256]{1,0:T(8,128)(2,1)S(1)}, bf16[144,256]{1,0:T(8,128)(2,1)S(1)}, u32[]{:S(2)}, u32[]{:S(2)}) collective-permute-start(bf16[144,256]{1,0:T(8,128)(2,1)S(1)} %collective-permute-done.13.refs_14_), channel_id=1, source_target_pairs={{0,1},{1,0},{2,3},{3,2},{4,5},{5,4},{6,7},{7,6},{8,9},{9,8},{10,11... | collective-permute-start | bytes 221192 | tf_op jit(solution)/shard_map/ppermute | solution.py:190
  18.0 3.7 %collective-permute-start.10 = (bf16[144,256]{1,0:T(8,128)(2,1)S(1)}, bf16[144,256]{1,0:T(8,128)(2,1)S(1)}, u32[]{:S(2)}, u32[]{:S(2)}) collective-permute-start(bf16[144,256]{1,0:T(8,128)(2,1)S(1)} %collective-permute-done.9.refs_10_), channel_id=1, source_target_pairs={{0,1},{1,0},{2,3},{3,2},{4,5},{5,4},{6,7},{7,6},{8,9},{9,8},{10,11... | collective-permute-start | bytes 221192 | tf_op jit(solution)/shard_map/ppermute | solution.py:190
  19.6 2.2 %collective-permute-start.6 = (bf16[144,256]{1,0:T(8,128)(2,1)S(1)}, bf16[144,256]{1,0:T(8,128)(2,1)S(1)}, u32[]{:S(2)}, u32[]{:S(2)}) collective-permute-start(bf16[144,256]{1,0:T(8,128)(2,1)S(1)} %collective-permute-done.5.refs_6_), channel_id=1, source_target_pairs={{0,1},{1,0},{2,3},{3,2},{4,5},{5,4},{6,7},{7,6},{8,9},{9,8},{10,11... | collective-permute-start | bytes 221192 | tf_op jit(solution)/shard_map/ppermute | solution.py:190
  19.6 2.2 %copy-start.1 = (bf16[144,256]{1,0:T(8,128)(2,1)S(1)}, bf16[144,256]{1,0:T(8,128)(2,1)}, u32[]{:S(2)}) copy-start(bf16[144,256]{1,0:T(8,128)(2,1)} %pack.1.refs_0_) | copy-start | bytes 221188
  21.8 1.0 %copy-start = (bf16[4,256,256]{2,1,0:T(8,128)(2,1)S(1)}, bf16[4,256,256]{2,1,0:T(8,128)(2,1)}, u32[]{:S(2)}) copy-start(bf16[4,256,256]{2,1,0:T(8,128)(2,1)} %get-tuple-element.18.refs_22_) | copy-start | bytes 1572868
  22.8 0.9 %copy-start.2 = (bf16[2,256,128]{2,1,0:T(8,128)(2,1)S(1)}, bf16[2,256,128]{2,1,0:T(8,128)(2,1)}, u32[]{:S(2)}) copy-start(bf16[2,256,128]{2,1,0:T(8,128)(2,1)} %get-tuple-element.12.refs_16_) | copy-start | bytes 393220
  23.7 0.9 %copy-start.3 = (f32[2,128,128]{2,1,0:T(8,128)S(1)}, f32[2,128,128]{2,1,0:T(8,128)}, u32[]{:S(2)}) copy-start(f32[2,128,128]{2,1,0:T(8,128)} %get-tuple-element.15.refs_19_) | copy-start | bytes 393220
  24.6 0.9 %copy-start.4 = (bf16[256,256]{1,0:T(8,128)(2,1)S(1)}, bf16[256,256]{1,0:T(8,128)(2,1)}, u32[]{:S(2)}) copy-start(bf16[256,256]{1,0:T(8,128)(2,1)} %get-tuple-element.17.refs_21_) | copy-start | bytes 393220
  25.6 0.8 %copy-start.5 = (bf16[2,128,128]{2,1,0:T(8,128)(2,1)S(1)}, bf16[2,128,128]{2,1,0:T(8,128)(2,1)}, u32[]{:S(2)}) copy-start(bf16[2,128,128]{2,1,0:T(8,128)(2,1)} %get-tuple-element.13.refs_17_) | copy-start | bytes 196612
  26.4 0.8 %copy-start.6 = (bf16[2,128,64]{2,1,0:T(8,128)(2,1)S(1)}, bf16[2,128,64]{2,1,0:T(8,128)(2,1)}, u32[]{:S(2)}) copy-start(bf16[2,128,64]{2,1,0:T(8,128)(2,1)} %get-tuple-element.14.refs_18_) | copy-start | bytes 98308
  27.2 0.8 %copy-start.7 = (f32[2,64,128]{2,1,0:T(8,128)S(1)}, f32[2,64,128]{2,1,0:T(8,128)}, u32[]{:S(2)}) copy-start(f32[2,64,128]{2,1,0:T(8,128)} %get-tuple-element.16.refs_20_) | copy-start | bytes 196612

commit v6 on v5

--- a/solution.py
+++ b/solution.py
@@ -56,20 +56,20 @@
     size = rows * tokens
     permuted = dot(position_permutation(rows, tokens, True), pair_ref[...]).astype(BF16)
     identity = (iota((channels, channels), 0) == iota((channels, channels), 1)).astype(F32)
-    packed_ref[:channels, :] = dot_nt(identity.astype(BF16), permuted).astype(BF16)
+    packed_ref[0, :channels, :] = dot_nt(identity.astype(BF16), permuted).astype(BF16)
     lane = iota((tokens, size), 1)
     place = token_of(lane % tokens, rows, tokens) == iota((tokens, size), 0)
     spread = dot(mask_ref[...].astype(F32).astype(BF16), place.astype(F32).astype(BF16))
     own = iota((rows, size), 0) == iota((rows, size), 1) // tokens
     line = jnp.sum(jnp.where(own, spread, 0.0), axis=0, keepdims=True)
-    packed_ref[channels:, :] = jnp.broadcast_to(line, (MASK_ROWS, size)).astype(BF16)
+    packed_ref[0, channels:, :] = jnp.broadcast_to(line, (MASK_ROWS, size)).astype(BF16)
 
 
 def prepare_kernel(
     rows, tokens, me_ref, proj_ref, gate_ref, out_ref, gain_ref, mid_ref,
     proj_t_ref, gate_t_ref, out_t_ref, gain_t_ref, mid_t_ref, restore_ref, spread_ref,
 ):
-    size, devices = rows * tokens, tokens // rows
+    devices = tokens // rows
 
     def flipped(weight):
         return weight.astype(F32).T.astype(BF16)
@@ -84,50 +84,71 @@
         gain_t_ref[o] = column(gain_ref[o : o + 1, :])
         mid_t_ref[o] = column(mid_ref[o : o + 1, :])
     restore_ref[...] = position_permutation(rows, tokens, False)
-    group, lane = iota((size, size), 0) // tokens, iota((size, size), 0) % tokens
-    same = group == iota((size, size), 1) // tokens
+    shape = (LANES, LANES)
+    group, lane = iota(shape, 0) // tokens, iota(shape, 0) % tokens
+    same = group == iota(shape, 1) // tokens
     for i in range(rows):
         spread_ref[i] = (same & (lane == i * devices + me_ref[0])).astype(F32).astype(BF16)
 
 
-def both_kernel(
-    rows, tokens, me_ref, *refs,
-):
+def both_kernel(rows, tokens, sources, me_ref, *refs):
     devices = tokens // rows
-    packed_refs, refs = refs[:devices], refs[devices:]
+    block_refs, refs = refs[: len(sources)], refs[len(sources) :]
+    weight_refs, result_ref, refs = refs[:7], refs[7], refs[8:]
+    weights, refs = refs[:7], refs[7:]
     (
-        proj_ref, gate_ref, out_ref, gain_ref, mid_ref, restore_ref, spread_ref, result_ref,
-        left_s, right_s, normed_s, sum_s, now_s, second_left_s, second_right_s,
+        packed_s, left_s, right_s, normed_s, sum_s, now_s, second_left_s, second_right_s,
+        block_sem, weight_sem,
     ) = refs
-    size = rows * tokens
+    proj_ref, gate_ref, out_ref, gain_ref, mid_ref, restore_ref, spread_ref = weights
     channels = gate_ref.shape[1]
     hw = mid_ref.shape[1]
-    tiles = size // LANES
+    tiles = rows * tokens // LANES
     me = me_ref[0]
 
-    def wide(column):
-        return jnp.concatenate([column] * tiles, axis=1)
+    weight_copies = [
+        pltpu.make_async_copy(weight_refs[n], weights[n], weight_sem.at[n]) for n in range(7)
+    ]
+    block_copies = {}
+    for block_ref, held in zip(block_refs, sources):
+        for k, m in enumerate(held):
+            block_copies[m] = pltpu.make_async_copy(
+                block_ref.at[k], packed_s.at[me ^ m], block_sem.at[m]
+            )
+    for n in (0, 3):
+        weight_copies[n].start()
+    for m in range(devices):
+        block_copies[m].start()
+    for n in (1, 2, 4, 5, 6):
+        weight_copies[n].start()
+    for n in range(7):
+        weight_copies[n].wait()
+    for m in range(devices):
+        block_copies[m].wait()
 
     def factors(projected, mask):
         left = mask * sigmoid(projected[hw : 2 * hw]) * projected[:hw]
         right = mask * sigmoid(projected[3 * hw :]) * projected[2 * hw : 3 * hw]
         return left, right
 
-    def block_of(packed_ref):
-        return packed_ref[:channels, :].astype(F32)
-
-    def mask_of(packed_ref):
-        return packed_ref[channels:, :].astype(F32)[:1]
-
-    for m, packed_ref in enumerate(packed_refs):
-        b = me ^ m
-        normed = column_norm(block_of(packed_ref), wide(gain_ref[0]))
-        normed_s[m] = normed
-        left, right = factors(dot(proj_ref[0], normed), mask_of(packed_ref))
-        here = pl.ds(pl.multiple_of(b * hw, hw), hw)
+    def block_of(b, h):
+        return packed_s[b, :channels, h * LANES : (h + 1) * LANES].astype(F32)
+
+    def mask_of(b, h):
+        rows_of_mask = packed_s[b, channels:, h * LANES : (h + 1) * LANES]
+        return rows_of_mask.astype(F32)[:1]
+
+    def project_first(b, _):
         for h in range(tiles):
-            left_s[h, here, :] = left[:, h * LANES : (h + 1) * LANES]
-            right_s[h, here, :] = right[:, h * LANES : (h + 1) * LANES]
+            normed = column_norm(block_of(b, h), gain_ref[0])
+            normed_s[b * tiles + h] = normed
+            left, right = factors(dot(proj_ref[0], normed), mask_of(b, h))
+            here = pl.ds(pl.multiple_of(b * hw, hw), hw)
+            left_s[h, here, :] = left
+            right_s[h, here, :] = right
+        return 0
+
+    lax.fori_loop(0, devices, project_first, 0, unroll=2)
 
     low = iota((devices, LANES), 1) < tokens
 
@@ -147,41 +168,46 @@
         sum_s[here, :] = dot_nt(left.astype(BF16), against)
         return 0
 
-    lax.fori_loop(0, hw, channel_sum, 0, unroll=16)
-
-    for m, packed_ref in enumerate(packed_refs):
-        b = me ^ m
-        summed = jnp.concatenate(
-            [sum_s[pl.ds(h * devices + b, hw, stride=tiles * devices), :] for h in range(tiles)],
-            axis=1,
-        )
-        update = dot(out_ref[0], column_norm(summed, wide(mid_ref[0])))
-        gating = sigmoid(dot(gate_ref[0], normed_s[m]))
-        now = (block_of(packed_ref) + gating * update).astype(BF16)
-        normed = column_norm(now.astype(F32), wide(gain_ref[1]))
-        if m == 0:
-            now_s[...] = now
-            normed_s[0] = normed
-        left, right = factors(dot(proj_ref[1], normed), mask_of(packed_ref))
-        second_left_s[m] = left.astype(BF16)
-        second_right_s[m] = right.astype(BF16)
-
+    lax.fori_loop(0, hw, channel_sum, 0, unroll=8)
+
+    def second_factors(b, _):
+        for h in range(tiles):
+            summed = sum_s[pl.ds(h * devices + b, hw, stride=tiles * devices), :]
+            update = dot(out_ref[0], column_norm(summed, mid_ref[0]))
+            gating = sigmoid(dot(gate_ref[0], normed_s[b * tiles + h]))
+            now = (block_of(b, h) + gating * update).astype(BF16)
+            now_s[b * tiles + h] = now
+            normed = column_norm(now.astype(F32), gain_ref[1])
+            normed_s[b * tiles + h] = normed
+            left, right = factors(dot(proj_ref[1], normed), mask_of(b, h))
+            here = pl.ds(pl.multiple_of((b * tiles + h) * hw, hw), hw)
+            second_left_s[here, :] = left.astype(BF16)
+            second_right_s[here, :] = right.astype(BF16)
+        return 0
+
+    lax.fori_loop(0, devices, second_factors, 0, unroll=2)
+
+    depth = 4 * hw
     sums = []
     for i in range(rows):
 
-        def add(m, total):
-            return total + dot(second_left_s[m], spread_ref[i]) * second_right_s[m].astype(F32)
-
-        total = lax.fori_loop(0, devices, add, jnp.zeros((hw, size), F32), unroll=4)
-        total = sum(total[:, h * LANES : (h + 1) * LANES] for h in range(tiles))
+        def add(n, total):
+            here = pl.ds(pl.multiple_of(n * depth, depth), depth)
+            terms = dot(second_left_s[here, :], spread_ref[i]) * second_right_s[here, :].astype(F32)
+            return total + sum(terms[k * hw : (k + 1) * hw] for k in range(4))
+
+        total = lax.fori_loop(
+            0, devices * tiles // 4, add, jnp.zeros((hw, LANES), F32), unroll=2
+        )
         sums.append(total + pltpu.roll(total, tokens, 1))
     low = iota((hw, LANES), 1) < tokens
-    summed = jnp.concatenate(
-        [jnp.where(low, sums[2 * h], sums[2 * h + 1]) for h in range(tiles)], axis=1
-    )
-    update = dot(out_ref[1], column_norm(summed, wide(mid_ref[1])))
-    gating = sigmoid(dot(gate_ref[1], normed_s[0]))
-    final = (now_s[...].astype(F32) + gating * update).astype(BF16)
+    final = []
+    for h in range(tiles):
+        summed = jnp.where(low, sums[2 * h], sums[2 * h + 1])
+        update = dot(out_ref[1], column_norm(summed, mid_ref[1]))
+        gating = sigmoid(dot(gate_ref[1], normed_s[me * tiles + h]))
+        final.append((now_s[me * tiles + h].astype(F32) + gating * update).astype(BF16))
+    final = jnp.concatenate(final, axis=1)
     result_ref[...] = dot_nt(restore_ref[...], final).astype(BF16)
 
 
@@ -190,32 +216,35 @@
     return lax.ppermute(block, "row", pairs)
 
 
-def everyone(packed, devices):
-    blocks = {0: packed}
-    for m in range(devices - 4, 0, -4):
-        blocks[m] = exchange(packed, m, devices)
-    for step in (2, 1):
-        for m in sorted(blocks, reverse=True):
-            blocks[m ^ step] = exchange(blocks[m], step, devices)
-    return [blocks[m] for m in range(devices)]
+def everyone(packed, ready, devices):
+    far = {m: exchange(packed, m, devices) for m in range(4, devices, 4)}
+    beside = exchange(packed, 2, devices)
+    far[12], ready = lax.optimization_barrier((far[12], ready))
+    near = exchange(far[4], 2, devices)
+    rest = exchange(jnp.concatenate([far[8], far[12]]), 2, devices)
+    first = jnp.concatenate([packed, beside] + [far[m] for m in sorted(far)])
+    second = jnp.concatenate([near, rest])
+    arrays = [packed, beside, far[4], far[8], far[12], near, rest]
+    sources = [(0,), (2,), (4,), (8,), (12,), (6,), (10, 14)]
+    arrays += [exchange(first, 1, devices), exchange(second, 1, devices)]
+    sources += [(1, 3, 5, 9, 13), (7, 11, 15)]
+    return arrays, sources, ready
 
 
 def small_plan(pair, mask, proj, gate, out, gain, mid):
     rows, tokens, channels = pair.shape
     devices, size, hw = tokens // rows, rows * tokens, out.shape[1]
     index = pl.BlockSpec(memory_space=pltpu.SMEM)
-    vmem = pl.BlockSpec(memory_space=pltpu.VMEM)
+    anywhere = pl.BlockSpec(memory_space=pl.ANY)
     packed = pl.pallas_call(
         functools.partial(pack_kernel, rows, tokens),
-        out_shape=jax.ShapeDtypeStruct((channels + MASK_ROWS, size), BF16),
-        out_specs=vmem,
+        out_shape=jax.ShapeDtypeStruct((1, channels + MASK_ROWS, size), BF16),
         name="pack",
     )(pair.reshape(size, channels), mask)
     me = lax.axis_index("row").reshape(1).astype(jnp.int32)
     weights = pl.pallas_call(
         functools.partial(prepare_kernel, rows, tokens),
         in_specs=[index] + [pl.BlockSpec()] * 5,
-        out_specs=(vmem,) * 7,
         out_shape=(
             jax.ShapeDtypeStruct((2, 4 * hw, channels), BF16),
             jax.ShapeDtypeStruct((2, channels, channels), BF16),
@@ -223,27 +252,32 @@
             jax.ShapeDtypeStruct((2, channels, LANES), F32),
             jax.ShapeDtypeStruct((2, hw, LANES), F32),
             jax.ShapeDtypeStruct((size, size), BF16),
-            jax.ShapeDtypeStruct((rows, size, size), BF16),
+            jax.ShapeDtypeStruct((rows, LANES, LANES), BF16),
         ),
         name="prepare",
     )(me, proj, gate, out, gain, mid)
-    blocks = everyone(packed, devices)
+    arrays, sources, weights = everyone(packed, weights, devices)
+    chunks = devices * size // LANES
     result = pl.pallas_call(
-        functools.partial(both_kernel, rows, tokens),
+        functools.partial(both_kernel, rows, tokens, sources),
         out_shape=jax.ShapeDtypeStruct((size, channels), BF16),
-        in_specs=[index] + [vmem] * (devices + len(weights)),
-        scratch_shapes=[
+        in_specs=[index] + [anywhere] * (len(arrays) + len(weights)),
+        scratch_shapes=[pltpu.VMEM(w.shape, w.dtype) for w in weights]
+        + [
+            pltpu.VMEM((devices,) + packed.shape[1:], BF16),
             pltpu.VMEM((size // LANES, devices * hw, LANES), F32),
             pltpu.VMEM((size // LANES, devices * hw, LANES), F32),
-            pltpu.VMEM((devices, channels, size), BF16),
-            pltpu.VMEM((hw * devices * size // LANES, LANES), F32),
-            pltpu.VMEM((channels, size), BF16),
-            pltpu.VMEM((devices, hw, size), BF16),
-            pltpu.VMEM((devices, hw, size), BF16),
+            pltpu.VMEM((chunks, channels, LANES), BF16),
+            pltpu.VMEM((hw * chunks, LANES), F32),
+            pltpu.VMEM((chunks, channels, LANES), BF16),
+            pltpu.VMEM((chunks * hw, LANES), BF16),
+            pltpu.VMEM((chunks * hw, LANES), BF16),
+            pltpu.SemaphoreType.DMA((devices,)),
+            pltpu.SemaphoreType.DMA((len(weights),)),
         ],
         compiler_params=pltpu.CompilerParams(vmem_limit_bytes=40 * 1024 * 1024),
         name="both",
-    )(me, *blocks, *weights)
+    )(me, *arrays, *weights)
     return result.reshape(pair.shape)
 
 

time: 39.5 us -> 40.2 us (1.018)
  Pallas kernels: 15 us -> 22 us
  local copies, waits for them, and re-layouts: 6.27 us -> 0.07 us
  starting transfers between devices: 12.5 us -> 9.59 us
  waiting for transfers between devices: 5.25 us -> 8.1 us
    pallas_call x1, Pallas kernels: 11 us -> 18.2 us  [small_plan(): pl.pallas_call(functools.partial(both_kernel, rows, tokens, sources), out...]
    unnamed x16 -> x20, local copies, waits for them, and re-layouts: 6.27 us -> 0.06 us
    ppermute x15 -> x8, starting transfers between devices: 12.5 us -> 9.59 us  [exchange(): return lax.ppermute(block, 'row', pairs)]
    ppermute x15 -> x8, waiting for transfers between devices: 5.25 us -> 8.1 us  [exchange(): return lax.ppermute(block, 'row', pairs)]
  transfers between devices with their start and end apart: 15 -> 8, of which waited for: 4 -> 3; matrix products, arithmetic and copies ran while one was open for 0% -> 0% of each run, Pallas kernels for 6% -> 5%
where the time goes in v6:
time: 40.2 us; the launch traced here: 40 us
  Pallas kernels  22 us (55%)
  starting transfers between devices  9.59 us (24%)
  waiting for transfers between devices  8.1 us (20%)
    pallas_call x1, Pallas kernels, small_plan(): pl.pallas_call(functools.partial(both_kernel, rows, tokens, sources), out...  18.2 us
    ppermute x8, starting transfers between devices, exchange(): return lax.ppermute(block, 'row', pairs)  9.59 us
    ppermute x8, waiting for transfers between devices, exchange(): return lax.ppermute(block, 'row', pairs)  8.1 us
    pallas_call x1, Pallas kernels, small_plan(): pl.pallas_call(functools.partial(prepare_kernel, rows, tokens), in_specs=...  1.98 us
    pallas_call x1, Pallas kernels, small_plan(): pl.pallas_call(functools.partial(pack_kernel, rows, tokens), out_shape=ja...  1.83 us
  transfers between devices with their start and end apart: 8, of which 3 were waited for; matrix products, arithmetic and copies ran while one was open for 0% of the time, Pallas kernels for 5%

profile of v6, /device:TPU:0, one launch (start us, length us, event | category | flops | bytes accessed | tf_op | source)
XLA Modules:
  0.0 40.0 jit_solution(1790555572485734116)
XLA Ops:
  0.0 1.8 %pack.1.refs_0_ = bf16[1,144,256]{2,1,0:T(8,128)(2,1)} custom-call(bf16[256,128]{1,0:T(8,128)(2,1)} %bitcast.3, s32[4,64]{1,0:T(4,128)} %mask_ref.1), custom_call_target="tpu_custom_call" | custom-call | tf_op jit(solution)/shard_map/pack/pallas_call | solution.py:239
  1.8 5.0 %collective-permute-start.3 = (bf16[1,144,256]{2,1,0:T(8,128)(2,1)}, bf16[1,144,256]{2,1,0:T(8,128)(2,1)S(1)}, u32[]{:S(2)}, u32[]{:S(2)}) collective-permute-start(bf16[1,144,256]{2,1,0:T(8,128)(2,1)} %pack.1.refs_0_), channel_id=1, source_target_pairs={{0,12},{1,13},{2,14},{3,15},{4,8},{5,9},{6,10},{7,11},{8,4},{9,5},... | collective-permute-start | bytes 221192 | tf_op jit(solution)/shard_map/ppermute | solution.py:216
  6.9 1.5 %collective-permute-start = (bf16[1,144,256]{2,1,0:T(8,128)(2,1)}, bf16[1,144,256]{2,1,0:T(8,128)(2,1)S(1)}, u32[]{:S(2)}, u32[]{:S(2)}) collective-permute-start(bf16[1,144,256]{2,1,0:T(8,128)(2,1)} %pack.1.refs_0_), channel_id=1, source_target_pairs={{0,2},{1,3},{2,0},{3,1},{4,6},{5,7},{6,4},{7,5},{8,10},{9,11},{10,... | collective-permute-start | bytes 221192 | tf_op jit(solution)/shard_map/ppermute | solution.py:216
  8.4 0.0 collective-permute-start.1
  8.4 0.8 %collective-permute-start.2 = (bf16[1,144,256]{2,1,0:T(8,128)(2,1)}, bf16[1,144,256]{2,1,0:T(8,128)(2,1)S(1)}, u32[]{:S(2)}, u32[]{:S(2)}) collective-permute-start(bf16[1,144,256]{2,1,0:T(8,128)(2,1)} %pack.1.refs_0_), channel_id=1, source_target_pairs={{0,8},{1,9},{2,10},{3,11},{4,12},{5,13},{6,14},{7,15},{8,0},{9,1},... | collective-permute-start | bytes 221192 | tf_op jit(solution)/shard_map/ppermute | solution.py:216
  9.2 2.0 %prepare.1 = (bf16[2,256,128]{2,1,0:T(8,128)(2,1)}, bf16[2,128,128]{2,1,0:T(8,128)(2,1)}, bf16[2,128,64]{2,1,0:T(8,128)(2,1)}, f32[2,128,128]{2,1,0:T(8,128)}, f...) custom-call(s32[1]{0:T(128)} %bitcast.me_ref, bf16[2,128,256]{2,1,0:T(8,128)(2,1)} %proj_ref.1, ...), custom_call_target="tpu_custom_call" | custom-call | tf_op jit(solution)/shard_map/prepare/pallas_call | solution.py:245
  11.2 0.0 copy-done
  11.2 0.0 collective-permute-done.3.refs_4_
  11.2 2.9 %collective-permute-done.2.refs_3_ = bf16[1,144,256]{2,1,0:T(8,128)(2,1)S(1)} collective-permute-done((bf16[1,144,256]{2,1,0:T(8,128)(2,1)}, bf16[1,144,256]{2,1,0:T(8,128)(2,1)S(1)}, u32[]{:S(2)}, u32[]{:S(2)}) %collective-permute-start.2) | collective-permute-done | bytes 73760 | tf_op jit(solution)/shard_map/ppermute | solution.py:216
  14.2 0.6 %collective-permute-start.5 = (bf16[2,144,256]{2,1,0:T(8,128)(2,1)S(1)}, bf16[2,144,256]{2,1,0:T(8,128)(2,1)S(1)}, u32[]{:S(2)}, u32[]{:S(2)}) collective-permute-start(bf16[2,144,256]{2,1,0:T(8,128)(2,1)S(1)} %pad_maximum_fusion.1), channel_id=1, source_target_pairs={{0,2},{1,3},{2,0},{3,1},{4,6},{5,7},{6,4},{7,5},{8,10},{9,11},{10,... | collective-permute-start | bytes 442376 | tf_op jit(solution)/shard_map/ppermute | solution.py:216
  14.7 0.0 collective-permute-done.1.refs_2_
  14.7 1.5 %collective-permute-start.4 = (bf16[1,144,256]{2,1,0:T(8,128)(2,1)S(1)}, bf16[1,144,256]{2,1,0:T(8,128)(2,1)S(1)}, u32[]{:S(2)}, u32[]{:S(2)}) collective-permute-start(bf16[1,144,256]{2,1,0:T(8,128)(2,1)S(1)} %collective-permute-done.1.refs_2_), channel_id=1, source_target_pairs={{0,2},{1,3},{2,0},{3,1},{4,6},{5,7},{6,4},{7,5},{8,10},{9,11},{10,... | collective-permute-start | bytes 221192 | tf_op jit(solution)/shard_map/ppermute | solution.py:216
  16.3 0.0 collective-permute-done.refs_1_
  16.3 0.0 copy-start.6
  16.3 0.0 copy-start.7
  16.3 0.0 copy-start.4
  16.3 0.0 copy-start.5
  16.4 0.0 copy-start.1
  16.4 0.0 copy-start.2
  16.4 0.0 copy-start.3
  16.4 0.1 collective-permute-start.6
  16.5 3.7 %collective-permute-done.4.refs_5_ = bf16[1,144,256]{2,1,0:T(8,128)(2,1)S(1)} collective-permute-done((bf16[1,144,256]{2,1,0:T(8,128)(2,1)S(1)}, bf16[1,144,256]{2,1,0:T(8,128)(2,1)S(1)}, u32[]{:S(2)}, u32[]{:S(2)}) %collective-permute-start.4) | collective-permute-done | bytes 73760 | tf_op jit(solution)/shard_map/ppermute | solution.py:216
  20.2 0.0 collective-permute-done.5.refs_6_
  20.2 0.1 collective-permute-start.7
  20.3 0.0 collective-permute-done.6.refs_7_
  20.3 1.5 %collective-permute-done.7.refs_8_ = bf16[3,144,256]{2,1,0:T(8,128)(2,1)S(1)} collective-permute-done((bf16[3,144,256]{2,1,0:T(8,128)(2,1)S(1)}, bf16[3,144,256]{2,1,0:T(8,128)(2,1)S(1)}, u32[]{:S(2)}, u32[]{:S(2)}) %collective-permute-start.7) | collective-permute-done | bytes 221216 | tf_op jit(solution)/shard_map/ppermute | solution.py:216
  21.7 0.0 copy-done.6
  21.7 0.0 copy-done.7
  21.7 0.0 copy-done.4
  21.7 0.0 copy-done.5
  21.8 0.0 copy-done.1
  21.8 18.2 %both.1 = bf16[256,128]{1,0:T(8,128)(2,1)} custom-call(s32[1]{0:T(128)} %bitcast.me_ref, bf16[1,144,256]{2,1,0:T(8,128)(2,1)S(1)} %copy-done, bf16[1,144,256]{2,1,0:T(8,128)(2,1)S(1)} %collective-permute-done.refs_1_, bf16[1,144,256]{2,1,0:T(8,128)(2,1)S(1)} %collective-permute-done.1.refs_2_, bf16[1,144,256]{2,1,0:T(8,128)(2,1)S(1)} %collective-permute-done.2.refs_3_, ...), custom_call_target="tpu_custom_call" | custom-call | tf_op jit(solution)/shard_map/both/pallas_call | solution.py:261
  (10 shorter events, 0.1 us)
Async XLA Ops:
  1.8 9.4 %collective-permute-start.3 = (bf16[1,144,256]{2,1,0:T(8,128)(2,1)}, bf16[1,144,256]{2,1,0:T(8,128)(2,1)S(1)}, u32[]{:S(2)}, u32[]{:S(2)}) collective-permute-start(bf16[1,144,256]{2,1,0:T(8,128)(2,1)} %pack.1.refs_0_), channel_id=1, source_target_pairs={{0,12},{1,13},{2,14},{3,15},{4,8},{5,9},{6,10},{7,11},{8,4},{9,5},... | collective-permute-start | bytes 221192 | tf_op jit(solution)/shard_map/ppermute | solution.py:216
  6.9 9.4 %collective-permute-start = (bf16[1,144,256]{2,1,0:T(8,128)(2,1)}, bf16[1,144,256]{2,1,0:T(8,128)(2,1)S(1)}, u32[]{:S(2)}, u32[]{:S(2)}) collective-permute-start(bf16[1,144,256]{2,1,0:T(8,128)(2,1)} %pack.1.refs_0_), channel_id=1, source_target_pairs={{0,2},{1,3},{2,0},{3,1},{4,6},{5,7},{6,4},{7,5},{8,10},{9,11},{10,... | collective-permute-start | bytes 221192 | tf_op jit(solution)/shard_map/ppermute | solution.py:216
  8.4 6.3 %collective-permute-start.1 = (bf16[1,144,256]{2,1,0:T(8,128)(2,1)}, bf16[1,144,256]{2,1,0:T(8,128)(2,1)S(1)}, u32[]{:S(2)}, u32[]{:S(2)}) collective-permute-start(bf16[1,144,256]{2,1,0:T(8,128)(2,1)} %pack.1.refs_0_), channel_id=1, source_target_pairs={{0,4},{1,5},{2,6},{3,7},{4,0},{5,1},{6,2},{7,3},{8,12},{9,13},{10,... | collective-permute-start | bytes 221192 | tf_op jit(solution)/shard_map/ppermute | solution.py:216
  8.4 5.7 %collective-permute-start.2 = (bf16[1,144,256]{2,1,0:T(8,128)(2,1)}, bf16[1,144,256]{2,1,0:T(8,128)(2,1)S(1)}, u32[]{:S(2)}, u32[]{:S(2)}) collective-permute-start(bf16[1,144,256]{2,1,0:T(8,128)(2,1)} %pack.1.refs_0_), channel_id=1, source_target_pairs={{0,8},{1,9},{2,10},{3,11},{4,12},{5,13},{6,14},{7,15},{8,0},{9,1},... | collective-permute-start | bytes 221192 | tf_op jit(solution)/shard_map/ppermute | solution.py:216
  9.2 2.0 %copy-start = (bf16[1,144,256]{2,1,0:T(8,128)(2,1)S(1)}, bf16[1,144,256]{2,1,0:T(8,128)(2,1)}, u32[]{:S(2)}) copy-start(bf16[1,144,256]{2,1,0:T(8,128)(2,1)} %pack.1.refs_0_) | copy-start | bytes 221188
  14.2 6.0 %collective-permute-start.5 = (bf16[2,144,256]{2,1,0:T(8,128)(2,1)S(1)}, bf16[2,144,256]{2,1,0:T(8,128)(2,1)S(1)}, u32[]{:S(2)}, u32[]{:S(2)}) collective-permute-start(bf16[2,144,256]{2,1,0:T(8,128)(2,1)S(1)} %pad_maximum_fusion.1), channel_id=1, source_target_pairs={{0,2},{1,3},{2,0},{3,1},{4,6},{5,7},{6,4},{7,5},{8,10},{9,11},{10,... | collective-permute-start | bytes 442376 | tf_op jit(solution)/shard_map/ppermute | solution.py:216
  14.7 5.4 %collective-permute-start.4 = (bf16[1,144,256]{2,1,0:T(8,128)(2,1)S(1)}, bf16[1,144,256]{2,1,0:T(8,128)(2,1)S(1)}, u32[]{:S(2)}, u32[]{:S(2)}) collective-permute-start(bf16[1,144,256]{2,1,0:T(8,128)(2,1)S(1)} %collective-permute-done.1.refs_2_), channel_id=1, source_target_pairs={{0,2},{1,3},{2,0},{3,1},{4,6},{5,7},{6,4},{7,5},{8,10},{9,11},{10,... | collective-permute-start | bytes 221192 | tf_op jit(solution)/shard_map/ppermute | solution.py:216
  16.3 5.5 %copy-start.6 = (bf16[2,128,64]{2,1,0:T(8,128)(2,1)S(1)}, bf16[2,128,64]{2,1,0:T(8,128)(2,1)}, u32[]{:S(2)}) copy-start(bf16[2,128,64]{2,1,0:T(8,128)(2,1)} %get-tuple-element.30.refs_11_) | copy-start | bytes 98308
  16.3 5.4 %copy-start.7 = (f32[2,64,128]{2,1,0:T(8,128)S(1)}, f32[2,64,128]{2,1,0:T(8,128)}, u32[]{:S(2)}) copy-start(f32[2,64,128]{2,1,0:T(8,128)} %get-tuple-element.32.refs_13_) | copy-start | bytes 196612
  16.3 5.4 %copy-start.4 = (bf16[4,128,128]{2,1,0:T(8,128)(2,1)S(1)}, bf16[4,128,128]{2,1,0:T(8,128)(2,1)}, u32[]{:S(2)}) copy-start(bf16[4,128,128]{2,1,0:T(8,128)(2,1)} %get-tuple-element.34.refs_15_) | copy-start | bytes 393220
  16.3 5.4 %copy-start.5 = (bf16[2,128,128]{2,1,0:T(8,128)(2,1)S(1)}, bf16[2,128,128]{2,1,0:T(8,128)(2,1)}, u32[]{:S(2)}) copy-start(bf16[2,128,128]{2,1,0:T(8,128)(2,1)} %get-tuple-element.29.refs_10_) | copy-start | bytes 196612
  16.4 5.4 %copy-start.1 = (bf16[2,256,128]{2,1,0:T(8,128)(2,1)S(1)}, bf16[2,256,128]{2,1,0:T(8,128)(2,1)}, u32[]{:S(2)}) copy-start(bf16[2,256,128]{2,1,0:T(8,128)(2,1)} %get-tuple-element.28.refs_9_) | copy-start | bytes 393220
  16.4 5.4 %copy-start.2 = (f32[2,128,128]{2,1,0:T(8,128)S(1)}, f32[2,128,128]{2,1,0:T(8,128)}, u32[]{:S(2)}) copy-start(f32[2,128,128]{2,1,0:T(8,128)} %get-tuple-element.31.refs_12_) | copy-start | bytes 393220
  16.4 5.4 %copy-start.3 = (bf16[256,256]{1,0:T(8,128)(2,1)S(1)}, bf16[256,256]{1,0:T(8,128)(2,1)}, u32[]{:S(2)}) copy-start(bf16[256,256]{1,0:T(8,128)(2,1)} %get-tuple-element.33.refs_14_) | copy-start | bytes 393220
  16.4 3.9 %collective-permute-start.6 = (bf16[5,144,256]{2,1,0:T(8,128)(2,1)S(1)}, bf16[5,144,256]{2,1,0:T(8,128)(2,1)S(1)}, u32[]{:S(2)}, u32[]{:S(2)}) collective-permute-start(bf16[5,144,256]{2,1,0:T(8,128)(2,1)S(1)} %constant_dynamic-update-slice_fusion), channel_id=1, source_target_pairs={{0,1},{1,0},{2,3},{3,2},{4,5},{5,4},{6,7},{7,6},{8,9},{9,8},{10,11... | collective-permute-start | bytes 1105928 | tf_op jit(solution)/shard_map/ppermute | solution.py:216
  20.2 1.5 %collective-permute-start.7 = (bf16[3,144,256]{2,1,0:T(8,128)(2,1)S(1)}, bf16[3,144,256]{2,1,0:T(8,128)(2,1)S(1)}, u32[]{:S(2)}, u32[]{:S(2)}) collective-permute-start(bf16[3,144,256]{2,1,0:T(8,128)(2,1)S(1)} %pad_maximum_fusion), channel_id=1, source_target_pairs={{0,1},{1,0},{2,3},{3,2},{4,5},{5,4},{6,7},{7,6},{8,9},{9,8},{10,11... | collective-permute-start | bytes 663560 | tf_op jit(solution)/shard_map/ppermute | solution.py:216

commit v7 on v6

--- a/solution.py
+++ b/solution.py
@@ -143,12 +143,13 @@
             normed = column_norm(block_of(b, h), gain_ref[0])
             normed_s[b * tiles + h] = normed
             left, right = factors(dot(proj_ref[0], normed), mask_of(b, h))
-            here = pl.ds(pl.multiple_of(b * hw, hw), hw)
+            here = pl.ds(b * hw, hw)
             left_s[h, here, :] = left
             right_s[h, here, :] = right
         return 0
 
-    lax.fori_loop(0, devices, project_first, 0, unroll=2)
+    for b in range(devices):
+        project_first(b, 0)
 
     low = iota((devices, LANES), 1) < tokens
 
@@ -168,7 +169,7 @@
         sum_s[here, :] = dot_nt(left.astype(BF16), against)
         return 0
 
-    lax.fori_loop(0, hw, channel_sum, 0, unroll=8)
+    lax.fori_loop(0, hw, channel_sum, 0, unroll=16)
 
     def second_factors(b, _):
         for h in range(tiles):
@@ -180,24 +181,25 @@
             normed = column_norm(now.astype(F32), gain_ref[1])
             normed_s[b * tiles + h] = normed
             left, right = factors(dot(proj_ref[1], normed), mask_of(b, h))
-            here = pl.ds(pl.multiple_of((b * tiles + h) * hw, hw), hw)
+            here = pl.ds((b * tiles + h) * hw, hw)
             second_left_s[here, :] = left.astype(BF16)
             second_right_s[here, :] = right.astype(BF16)
         return 0
 
-    lax.fori_loop(0, devices, second_factors, 0, unroll=2)
+    for b in range(devices):
+        second_factors(b, 0)
 
     depth = 4 * hw
     sums = []
     for i in range(rows):
 
         def add(n, total):
-            here = pl.ds(pl.multiple_of(n * depth, depth), depth)
+            here = pl.ds(n * depth, depth)
             terms = dot(second_left_s[here, :], spread_ref[i]) * second_right_s[here, :].astype(F32)
             return total + sum(terms[k * hw : (k + 1) * hw] for k in range(4))
 
         total = lax.fori_loop(
-            0, devices * tiles // 4, add, jnp.zeros((hw, LANES), F32), unroll=2
+            0, devices * tiles // 4, add, jnp.zeros((hw, LANES), F32), unroll=True
         )
         sums.append(total + pltpu.roll(total, tokens, 1))
     low = iota((hw, LANES), 1) < tokens
@@ -217,17 +219,20 @@
 
 
 def everyone(packed, ready, devices):
-    far = {m: exchange(packed, m, devices) for m in range(4, devices, 4)}
-    beside = exchange(packed, 2, devices)
-    far[12], ready = lax.optimization_barrier((far[12], ready))
-    near = exchange(far[4], 2, devices)
-    rest = exchange(jnp.concatenate([far[8], far[12]]), 2, devices)
-    first = jnp.concatenate([packed, beside] + [far[m] for m in sorted(far)])
-    second = jnp.concatenate([near, rest])
-    arrays = [packed, beside, far[4], far[8], far[12], near, rest]
-    sources = [(0,), (2,), (4,), (8,), (12,), (6,), (10, 14)]
-    arrays += [exchange(first, 1, devices), exchange(second, 1, devices)]
-    sources += [(1, 3, 5, 9, 13), (7, 11, 15)]
+    held = {0: packed}
+    for m in (4, 2, 8, 12):
+        held[m] = exchange(packed, m, devices)
+    held[4], held[2] = lax.optimization_barrier((held[4], held[2]))
+    held[6] = exchange(held[4], 2, devices)
+    held[8], held[4], ready = lax.optimization_barrier((held[8], held[4], ready))
+    held[10] = exchange(held[8], 2, devices)
+    held[12], held[6] = lax.optimization_barrier((held[12], held[6]))
+    held[14] = exchange(held[12], 2, devices)
+    arrays = [held[m] for m in sorted(held)]
+    sources = [(m,) for m in sorted(held)]
+    for group in ((0, 2, 4), (6, 8), (10, 12, 14)):
+        arrays.append(exchange(jnp.concatenate([held[m] for m in group]), 1, devices))
+        sources.append(tuple(m ^ 1 for m in group))
     return arrays, sources, ready
 
 

time: 40.2 us -> 32.3 us (0.80)
  Pallas kernels: 22 us -> 14.3 us
    pallas_call x1, Pallas kernels: 18.2 us -> 10.4 us  [small_plan(): pl.pallas_call(functools.partial(both_kernel, rows, tokens, sources), out...]
    ppermute x8 -> x10, starting transfers between devices: 9.59 us -> 9.45 us  [exchange(): return lax.ppermute(block, 'row', pairs)]
    ppermute x8 -> x10, waiting for transfers between devices: 8.1 us -> 8.22 us  [exchange(): return lax.ppermute(block, 'row', pairs)]
  transfers between devices with their start and end apart: 8 -> 10, of which waited for: 3 -> 6; matrix products, arithmetic and copies ran while one was open for 0% -> 0% of each run, Pallas kernels for 5% -> 6%
where the time goes in v7:
time: 32.3 us; the launch traced here: 32.2 us
  Pallas kernels  14.3 us (44%)
  starting transfers between devices  9.45 us (29%)
  waiting for transfers between devices  8.22 us (25%)
    pallas_call x1, Pallas kernels, small_plan(): pl.pallas_call(functools.partial(both_kernel, rows, tokens, sources), out...  10.4 us
    ppermute x10, starting transfers between devices, exchange(): return lax.ppermute(block, 'row', pairs)  9.45 us
    ppermute x10, waiting for transfers between devices, exchange(): return lax.ppermute(block, 'row', pairs)  8.22 us
    pallas_call x1, Pallas kernels, small_plan(): pl.pallas_call(functools.partial(prepare_kernel, rows, tokens), in_specs=...  1.97 us
    pallas_call x1, Pallas kernels, small_plan(): pl.pallas_call(functools.partial(pack_kernel, rows, tokens), out_shape=ja...  1.84 us
  transfers between devices with their start and end apart: 10, of which 6 were waited for; matrix products, arithmetic and copies ran while one was open for 0% of the time, Pallas kernels for 6%

profile of v7, /device:TPU:0, one launch (start us, length us, event | category | flops | bytes accessed | tf_op | source)
XLA Modules:
  0.0 32.2 jit_solution(14693245284160030826)
XLA Ops:
  0.0 1.8 %pack.1.refs_0_ = bf16[1,144,256]{2,1,0:T(8,128)(2,1)} custom-call(bf16[256,128]{1,0:T(8,128)(2,1)} %bitcast.3, s32[4,64]{1,0:T(4,128)} %mask_ref.1), custom_call_target="tpu_custom_call" | custom-call | tf_op jit(solution)/shard_map/pack/pallas_call | solution.py:244
  1.8 3.0 %collective-permute-start.1 = (bf16[1,144,256]{2,1,0:T(8,128)(2,1)}, bf16[1,144,256]{2,1,0:T(8,128)(2,1)S(1)}, u32[]{:S(2)}, u32[]{:S(2)}) collective-permute-start(bf16[1,144,256]{2,1,0:T(8,128)(2,1)} %pack.1.refs_0_), channel_id=1, source_target_pairs={{0,2},{1,3},{2,0},{3,1},{4,6},{5,7},{6,4},{7,5},{8,10},{9,11},{10,... | collective-permute-start | bytes 221192 | tf_op jit(solution)/shard_map/ppermute | solution.py:218
  4.8 1.6 %collective-permute-start = (bf16[1,144,256]{2,1,0:T(8,128)(2,1)}, bf16[1,144,256]{2,1,0:T(8,128)(2,1)S(1)}, u32[]{:S(2)}, u32[]{:S(2)}) collective-permute-start(bf16[1,144,256]{2,1,0:T(8,128)(2,1)} %pack.1.refs_0_), channel_id=1, source_target_pairs={{0,4},{1,5},{2,6},{3,7},{4,0},{5,1},{6,2},{7,3},{8,12},{9,13},{10,... | collective-permute-start | bytes 221192 | tf_op jit(solution)/shard_map/ppermute | solution.py:218
  6.4 2.6 %collective-permute-start.2 = (bf16[1,144,256]{2,1,0:T(8,128)(2,1)}, bf16[1,144,256]{2,1,0:T(8,128)(2,1)S(1)}, u32[]{:S(2)}, u32[]{:S(2)}) collective-permute-start(bf16[1,144,256]{2,1,0:T(8,128)(2,1)} %pack.1.refs_0_), channel_id=1, source_target_pairs={{0,8},{1,9},{2,10},{3,11},{4,12},{5,13},{6,14},{7,15},{8,0},{9,1},... | collective-permute-start | bytes 221192 | tf_op jit(solution)/shard_map/ppermute | solution.py:218
  9.0 0.2 collective-permute-start.3
  9.2 0.0 collective-permute-done.1.refs_1_
  9.2 0.2 collective-permute-done.refs_2_
  9.4 0.2 collective-permute-start.4
  9.6 2.0 %prepare.1 = (bf16[2,256,128]{2,1,0:T(8,128)(2,1)}, bf16[2,128,128]{2,1,0:T(8,128)(2,1)}, bf16[2,128,64]{2,1,0:T(8,128)(2,1)}, f32[2,128,128]{2,1,0:T(8,128)}, f...) custom-call(s32[1]{0:T(128)} %bitcast.me_ref, bf16[2,128,256]{2,1,0:T(8,128)(2,1)} %proj_ref.1, ...), custom_call_target="tpu_custom_call" | custom-call | tf_op jit(solution)/shard_map/prepare/pallas_call | solution.py:250
  11.5 2.6 %collective-permute-done.2.refs_4_ = bf16[1,144,256]{2,1,0:T(8,128)(2,1)S(1)} collective-permute-done((bf16[1,144,256]{2,1,0:T(8,128)(2,1)}, bf16[1,144,256]{2,1,0:T(8,128)(2,1)S(1)}, u32[]{:S(2)}, u32[]{:S(2)}) %collective-permute-start.2) | collective-permute-done | bytes 73760 | tf_op jit(solution)/shard_map/ppermute | solution.py:218
  14.1 0.5 %collective-permute-start.5 = (bf16[1,144,256]{2,1,0:T(8,128)(2,1)S(1)}, bf16[1,144,256]{2,1,0:T(8,128)(2,1)S(1)}, u32[]{:S(2)}, u32[]{:S(2)}) collective-permute-start(bf16[1,144,256]{2,1,0:T(8,128)(2,1)S(1)} %collective-permute-done.2.refs_4_), channel_id=1, source_target_pairs={{0,2},{1,3},{2,0},{3,1},{4,6},{5,7},{6,4},{7,5},{8,10},{9,11},{10,... | collective-permute-start | bytes 221192 | tf_op jit(solution)/shard_map/ppermute | solution.py:218
  14.6 0.8 %collective-permute-done.3.refs_6_ = bf16[1,144,256]{2,1,0:T(8,128)(2,1)S(1)} collective-permute-done((bf16[1,144,256]{2,1,0:T(8,128)(2,1)}, bf16[1,144,256]{2,1,0:T(8,128)(2,1)S(1)}, u32[]{:S(2)}, u32[]{:S(2)}) %collective-permute-start.3) | collective-permute-done | bytes 73760 | tf_op jit(solution)/shard_map/ppermute | solution.py:218
  15.4 0.0 collective-permute-done.4.refs_3_
  15.4 0.7 %collective-permute-start.6 = (bf16[1,144,256]{2,1,0:T(8,128)(2,1)S(1)}, bf16[1,144,256]{2,1,0:T(8,128)(2,1)S(1)}, u32[]{:S(2)}, u32[]{:S(2)}) collective-permute-start(bf16[1,144,256]{2,1,0:T(8,128)(2,1)S(1)} %collective-permute-done.3.refs_6_), channel_id=1, source_target_pairs={{0,2},{1,3},{2,0},{3,1},{4,6},{5,7},{6,4},{7,5},{8,10},{9,11},{10,... | collective-permute-start | bytes 221192 | tf_op jit(solution)/shard_map/ppermute | solution.py:218
  16.2 0.0 copy-done
  16.2 0.1 collective-permute-start.7
  16.3 2.2 %collective-permute-done.5.refs_5_ = bf16[1,144,256]{2,1,0:T(8,128)(2,1)S(1)} collective-permute-done((bf16[1,144,256]{2,1,0:T(8,128)(2,1)S(1)}, bf16[1,144,256]{2,1,0:T(8,128)(2,1)S(1)}, u32[]{:S(2)}, u32[]{:S(2)}) %collective-permute-start.5) | collective-permute-done | bytes 73760 | tf_op jit(solution)/shard_map/ppermute | solution.py:218
  18.5 1.3 %collective-permute-done.6.refs_7_ = bf16[1,144,256]{2,1,0:T(8,128)(2,1)S(1)} collective-permute-done((bf16[1,144,256]{2,1,0:T(8,128)(2,1)S(1)}, bf16[1,144,256]{2,1,0:T(8,128)(2,1)S(1)}, u32[]{:S(2)}, u32[]{:S(2)}) %collective-permute-start.6) | collective-permute-done | bytes 73760 | tf_op jit(solution)/shard_map/ppermute | solution.py:218
  19.8 0.0 copy-start.7
  19.9 0.0 copy-start.1
  19.9 0.1 collective-permute-start.9
  20.0 0.6 %collective-permute-start.8 = (bf16[2,144,256]{2,1,0:T(8,128)(2,1)S(1)}, bf16[2,144,256]{2,1,0:T(8,128)(2,1)S(1)}, u32[]{:S(2)}, u32[]{:S(2)}) collective-permute-start(bf16[2,144,256]{2,1,0:T(8,128)(2,1)S(1)} %pad_maximum_fusion.2), channel_id=1, source_target_pairs={{0,1},{1,0},{2,3},{3,2},{4,5},{5,4},{6,7},{7,6},{8,9},{9,8},{10,11... | collective-permute-start | bytes 442376 | tf_op jit(solution)/shard_map/ppermute | solution.py:218
  20.5 1.1 %collective-permute-done.8.refs_9_ = bf16[2,144,256]{2,1,0:T(8,128)(2,1)S(1)} collective-permute-done((bf16[2,144,256]{2,1,0:T(8,128)(2,1)S(1)}, bf16[2,144,256]{2,1,0:T(8,128)(2,1)S(1)}, u32[]{:S(2)}, u32[]{:S(2)}) %collective-permute-start.8) | collective-permute-done | bytes 147488 | tf_op jit(solution)/shard_map/ppermute | solution.py:218
  21.6 0.0 collective-permute-done.7.refs_8_
  21.6 0.0 collective-permute-done.9.refs_10_
  21.6 0.0 copy-done.4
  21.7 0.0 copy-done.5
  21.7 0.0 copy-done.6
  21.7 0.0 copy-done.7
  21.7 0.0 copy-done.1
  21.7 0.0 copy-done.2
  21.7 10.4 %both.1 = bf16[256,128]{1,0:T(8,128)(2,1)} custom-call(s32[1]{0:T(128)} %bitcast.me_ref, bf16[1,144,256]{2,1,0:T(8,128)(2,1)S(1)} %copy-done, bf16[1,144,256]{2,1,0:T(8,128)(2,1)S(1)} %collective-permute-done.1.refs_1_, bf16[1,144,256]{2,1,0:T(8,128)(2,1)S(1)} %collective-permute-done.refs_2_, bf16[1,144,256]{2,1,0:T(8,128)(2,1)S(1)} %collective-permute-done.4.refs_3_, ...), custom_call_target="tpu_custom_call" | custom-call | tf_op jit(solution)/shard_map/both/pallas_call | solution.py:266
  (10 shorter events, 0.1 us)
Async XLA Ops:
  1.8 7.4 %collective-permute-start.1 = (bf16[1,144,256]{2,1,0:T(8,128)(2,1)}, bf16[1,144,256]{2,1,0:T(8,128)(2,1)S(1)}, u32[]{:S(2)}, u32[]{:S(2)}) collective-permute-start(bf16[1,144,256]{2,1,0:T(8,128)(2,1)} %pack.1.refs_0_), channel_id=1, source_target_pairs={{0,2},{1,3},{2,0},{3,1},{4,6},{5,7},{6,4},{7,5},{8,10},{9,11},{10,... | collective-permute-start | bytes 221192 | tf_op jit(solution)/shard_map/ppermute | solution.py:218
  4.8 4.6 %collective-permute-start = (bf16[1,144,256]{2,1,0:T(8,128)(2,1)}, bf16[1,144,256]{2,1,0:T(8,128)(2,1)S(1)}, u32[]{:S(2)}, u32[]{:S(2)}) collective-permute-start(bf16[1,144,256]{2,1,0:T(8,128)(2,1)} %pack.1.refs_0_), channel_id=1, source_target_pairs={{0,4},{1,5},{2,6},{3,7},{4,0},{5,1},{6,2},{7,3},{8,12},{9,13},{10,... | collective-permute-start | bytes 221192 | tf_op jit(solution)/shard_map/ppermute | solution.py:218
  6.4 7.7 %collective-permute-start.2 = (bf16[1,144,256]{2,1,0:T(8,128)(2,1)}, bf16[1,144,256]{2,1,0:T(8,128)(2,1)S(1)}, u32[]{:S(2)}, u32[]{:S(2)}) collective-permute-start(bf16[1,144,256]{2,1,0:T(8,128)(2,1)} %pack.1.refs_0_), channel_id=1, source_target_pairs={{0,8},{1,9},{2,10},{3,11},{4,12},{5,13},{6,14},{7,15},{8,0},{9,1},... | collective-permute-start | bytes 221192 | tf_op jit(solution)/shard_map/ppermute | solution.py:218
  9.0 6.5 %collective-permute-start.3 = (bf16[1,144,256]{2,1,0:T(8,128)(2,1)}, bf16[1,144,256]{2,1,0:T(8,128)(2,1)S(1)}, u32[]{:S(2)}, u32[]{:S(2)}) collective-permute-start(bf16[1,144,256]{2,1,0:T(8,128)(2,1)} %pack.1.refs_0_), channel_id=1, source_target_pairs={{0,12},{1,13},{2,14},{3,15},{4,8},{5,9},{6,10},{7,11},{8,4},{9,5},... | collective-permute-start | bytes 221192 | tf_op jit(solution)/shard_map/ppermute | solution.py:218
  9.4 6.1 %collective-permute-start.4 = (bf16[1,144,256]{2,1,0:T(8,128)(2,1)S(1)}, bf16[1,144,256]{2,1,0:T(8,128)(2,1)S(1)}, u32[]{:S(2)}, u32[]{:S(2)}) collective-permute-start(bf16[1,144,256]{2,1,0:T(8,128)(2,1)S(1)} %collective-permute-done.refs_2_), channel_id=1, source_target_pairs={{0,2},{1,3},{2,0},{3,1},{4,6},{5,7},{6,4},{7,5},{8,10},{9,11},{10,... | collective-permute-start | bytes 221192 | tf_op jit(solution)/shard_map/ppermute | solution.py:218
  9.6 6.6 %copy-start = (bf16[1,144,256]{2,1,0:T(8,128)(2,1)S(1)}, bf16[1,144,256]{2,1,0:T(8,128)(2,1)}, u32[]{:S(2)}) copy-start(bf16[1,144,256]{2,1,0:T(8,128)(2,1)} %pack.1.refs_0_) | copy-start | bytes 221188
  14.1 4.4 %collective-permute-start.5 = (bf16[1,144,256]{2,1,0:T(8,128)(2,1)S(1)}, bf16[1,144,256]{2,1,0:T(8,128)(2,1)S(1)}, u32[]{:S(2)}, u32[]{:S(2)}) collective-permute-start(bf16[1,144,256]{2,1,0:T(8,128)(2,1)S(1)} %collective-permute-done.2.refs_4_), channel_id=1, source_target_pairs={{0,2},{1,3},{2,0},{3,1},{4,6},{5,7},{6,4},{7,5},{8,10},{9,11},{10,... | collective-permute-start | bytes 221192 | tf_op jit(solution)/shard_map/ppermute | solution.py:218
  15.4 4.4 %collective-permute-start.6 = (bf16[1,144,256]{2,1,0:T(8,128)(2,1)S(1)}, bf16[1,144,256]{2,1,0:T(8,128)(2,1)S(1)}, u32[]{:S(2)}, u32[]{:S(2)}) collective-permute-start(bf16[1,144,256]{2,1,0:T(8,128)(2,1)S(1)} %collective-permute-done.3.refs_6_), channel_id=1, source_target_pairs={{0,2},{1,3},{2,0},{3,1},{4,6},{5,7},{6,4},{7,5},{8,10},{9,11},{10,... | collective-permute-start | bytes 221192 | tf_op jit(solution)/shard_map/ppermute | solution.py:218
  16.2 5.5 %collective-permute-start.7 = (bf16[3,144,256]{2,1,0:T(8,128)(2,1)S(1)}, bf16[3,144,256]{2,1,0:T(8,128)(2,1)S(1)}, u32[]{:S(2)}, u32[]{:S(2)}) collective-permute-start(bf16[3,144,256]{2,1,0:T(8,128)(2,1)S(1)} %pad_maximum_fusion), channel_id=1, source_target_pairs={{0,1},{1,0},{2,3},{3,2},{4,5},{5,4},{6,7},{7,6},{8,9},{9,8},{10,11... | collective-permute-start | bytes 663560 | tf_op jit(solution)/shard_map/ppermute | solution.py:218
  19.8 1.8 %copy-start.3 = (bf16[256,256]{1,0:T(8,128)(2,1)S(1)}, bf16[256,256]{1,0:T(8,128)(2,1)}, u32[]{:S(2)}) copy-start(bf16[256,256]{1,0:T(8,128)(2,1)} %get-tuple-element.43.refs_16_) | copy-start | bytes 393220
  19.8 1.8 %copy-start.4 = (bf16[4,128,128]{2,1,0:T(8,128)(2,1)S(1)}, bf16[4,128,128]{2,1,0:T(8,128)(2,1)}, u32[]{:S(2)}) copy-start(bf16[4,128,128]{2,1,0:T(8,128)(2,1)} %get-tuple-element.44.refs_17_) | copy-start | bytes 393220
  19.8 1.9 %copy-start.5 = (bf16[2,128,128]{2,1,0:T(8,128)(2,1)S(1)}, bf16[2,128,128]{2,1,0:T(8,128)(2,1)}, u32[]{:S(2)}) copy-start(bf16[2,128,128]{2,1,0:T(8,128)(2,1)} %get-tuple-element.39.refs_12_) | copy-start | bytes 196612
  19.8 1.9 %copy-start.6 = (bf16[2,128,64]{2,1,0:T(8,128)(2,1)S(1)}, bf16[2,128,64]{2,1,0:T(8,128)(2,1)}, u32[]{:S(2)}) copy-start(bf16[2,128,64]{2,1,0:T(8,128)(2,1)} %get-tuple-element.40.refs_13_) | copy-start | bytes 98308
  19.8 1.9 %copy-start.7 = (f32[2,64,128]{2,1,0:T(8,128)S(1)}, f32[2,64,128]{2,1,0:T(8,128)}, u32[]{:S(2)}) copy-start(f32[2,64,128]{2,1,0:T(8,128)} %get-tuple-element.42.refs_15_) | copy-start | bytes 196612
  19.9 1.8 %copy-start.1 = (bf16[2,256,128]{2,1,0:T(8,128)(2,1)S(1)}, bf16[2,256,128]{2,1,0:T(8,128)(2,1)}, u32[]{:S(2)}) copy-start(bf16[2,256,128]{2,1,0:T(8,128)(2,1)} %get-tuple-element.38.refs_11_) | copy-start | bytes 393220
  19.9 1.8 %copy-start.2 = (f32[2,128,128]{2,1,0:T(8,128)S(1)}, f32[2,128,128]{2,1,0:T(8,128)}, u32[]{:S(2)}) copy-start(f32[2,128,128]{2,1,0:T(8,128)} %get-tuple-element.41.refs_14_) | copy-start | bytes 393220
  19.9 1.8 %collective-permute-start.9 = (bf16[3,144,256]{2,1,0:T(8,128)(2,1)S(1)}, bf16[3,144,256]{2,1,0:T(8,128)(2,1)S(1)}, u32[]{:S(2)}, u32[]{:S(2)}) collective-permute-start(bf16[3,144,256]{2,1,0:T(8,128)(2,1)S(1)} %pad_maximum_fusion.1), channel_id=1, source_target_pairs={{0,1},{1,0},{2,3},{3,2},{4,5},{5,4},{6,7},{7,6},{8,9},{9,8},{10,11... | collective-permute-start | bytes 663560 | tf_op jit(solution)/shard_map/ppermute | solution.py:218
  20.0 1.6 %collective-permute-start.8 = (bf16[2,144,256]{2,1,0:T(8,128)(2,1)S(1)}, bf16[2,144,256]{2,1,0:T(8,128)(2,1)S(1)}, u32[]{:S(2)}, u32[]{:S(2)}) collective-permute-start(bf16[2,144,256]{2,1,0:T(8,128)(2,1)S(1)} %pad_maximum_fusion.2), channel_id=1, source_target_pairs={{0,1},{1,0},{2,3},{3,2},{4,5},{5,4},{6,7},{7,6},{8,9},{9,8},{10,11... | collective-permute-start | bytes 442376 | tf_op jit(solution)/shard_map/ppermute | solution.py:218

commit v8 on v4

v8 whole, which is shorter than its diff:
```python
import functools

import jax
import jax.numpy as jnp
from jax import lax
from jax.experimental import pallas as pl
from jax.experimental.pallas import tpu as pltpu
from jax.sharding import PartitionSpec as P

EPS = 1e-05
F32, BF16 = jnp.float32, jnp.bfloat16
LANES = 128
MASK_ROWS = 16
NT = (((1,), (1,)), ((), ()))
VMEM = pltpu.VMEM
IN_VMEM = pl.BlockSpec(memory_space=pltpu.VMEM)
IN_SMEM = pl.BlockSpec(memory_space=pltpu.SMEM)


def dot(a, b):
    return jnp.dot(a, b, preferred_element_type=F32)


def dot_nt(a, b):
    return lax.dot_general(a, b, NT, preferred_element_type=F32)


def sigmoid(x):
    return 0.5 * jnp.tanh(0.5 * x) + 0.5


def iota(shape, axis):
    return lax.broadcasted_iota(jnp.int32, shape, axis)


def one_hot(condition):
    return condition.astype(F32).astype(BF16)


def token_of(t, rows, tokens):
    devices = tokens // rows
    return (t % devices) * rows + t // devices


def column_norm(values, gain):
    average = jnp.mean(values, axis=0, keepdims=True)
    centred = values - average
    variance = jnp.mean(centred * centred, axis=0, keepdims=True)
    return (centred * lax.rsqrt(variance + EPS) * gain).astype(BF16)


def factors(projected, mask):
    hw = projected.shape[0] // 4
    left = mask * sigmoid(projected[hw : 2 * hw]) * projected[:hw]
    right = mask * sigmoid(projected[3 * hw :]) * projected[2 * hw : 3 * hw]
    return left, right


def pack_kernel(rows, tokens, pair_ref, mask_ref, packed_ref):
    channels = pair_ref.shape[-1]
    square = (tokens, tokens)
    by_lane = one_hot(token_of(iota(square, 0), rows, tokens) == iota(square, 1))
    by_token = one_hot(token_of(iota(square, 1), rows, tokens) == iota(square, 0))
    identity = one_hot(iota((channels, channels), 0) == iota((channels, channels), 1))
    masks = dot(one_hot(mask_ref[...] != 0), by_token)
    tiles = rows * tokens // LANES
    for h in range(tiles):
        pair = [dot(by_lane, pair_ref[i]).astype(BF16) for i in (2 * h, 2 * h + 1)]
        chunk = dot_nt(identity, jnp.concatenate(pair, axis=0))
        packed_ref[0, h * channels : (h + 1) * channels, :] = chunk.astype(BF16)
    lines = [
        jnp.concatenate([masks[2 * h : 2 * h + 1], masks[2 * h + 1 : 2 * h + 2]], axis=1)
        for h in range(tiles)
    ]
    shape = (MASK_ROWS, LANES)
    block = jnp.where(iota(shape, 0) < MASK_ROWS // 2, lines[0], lines[1])
    packed_ref[0, tiles * channels :, :] = block.astype(BF16)


def chunk_of(ref, channels, k, h):
    return ref[k, h * channels : (h + 1) * channels, :].astype(F32)


def mask_of(ref, channels, k, h):
    lines = ref[k, -MASK_ROWS:, :].astype(F32)
    return lines[h * MASK_ROWS // 2 : h * MASK_ROWS // 2 + 1]


def prepare_kernel(
    rows, tokens, me_ref, proj_ref, gate_ref, out_ref, gain_ref, mid_ref,
    proj_t_ref, gate_t_ref, out_t_ref, gain_t_ref, mid_t_ref, restore_ref, spread_ref,
):
    devices = tokens // rows

    def flipped(weight):
        return weight.astype(F32).T.astype(BF16)

    def column(line):
        return jnp.broadcast_to(line, (LANES, line.shape[1])).T

    for o in range(2):
        proj_t_ref[o] = flipped(proj_ref[o])
        gate_t_ref[o] = flipped(gate_ref[o])
        out_t_ref[o] = flipped(out_ref[o])
        gain_t_ref[o] = column(gain_ref[o : o + 1, :])
        mid_t_ref[o] = column(mid_ref[o : o + 1, :])
    shape = (LANES, LANES)
    lane = iota(shape, 1)
    source = lane // tokens * tokens + token_of(lane % tokens, rows, tokens)
    restore_ref[...] = one_hot(source == iota(shape, 0))
    group, lane = iota(shape, 0) // tokens, iota(shape, 0) % tokens
    same = group == iota(shape, 1) // tokens
    for i in range(rows):
        spread_ref[i] = one_hot(same & (lane == i * devices + me_ref[0]))


def early_kernel(counts, *refs):
    block_refs, (proj_ref, gain_ref, left_ref, right_ref, normed_ref) = refs[:-5], refs[-5:]
    channels, tiles = normed_ref.shape[2], normed_ref.shape[1]
    place = 0
    for block_ref, count in zip(block_refs, counts):
        for k in range(count):
            for h in range(tiles):
                normed = column_norm(chunk_of(block_ref, channels, k, h), gain_ref[0])
                normed_ref[place, h] = normed
                left, right = factors(dot(proj_ref[0], normed), mask_of(block_ref, channels, k, h))
                left_ref[place, h] = left
                right_ref[place, h] = right
            place += 1


def both_kernel(rows, tokens, sources, early, me_ref, *refs):
    devices = tokens // rows
    block_refs, refs = refs[: len(sources)], refs[len(sources) :]
    (
        proj_ref, gate_ref, out_ref, gain_ref, mid_ref, restore_ref, spread_ref,
        early_left_ref, early_right_ref, early_normed_ref, result_ref,
        left_s, right_s, normed_s, sum_s, now_s, second_left_s, second_right_s,
    ) = refs
    channels = gate_ref.shape[1]
    hw = mid_ref.shape[1]
    tiles = rows * tokens // LANES
    me = me_ref[0]

    where = {m: (ref, k) for ref, held in zip(block_refs, sources) for k, m in enumerate(held)}
    later = [m for m in range(devices) if m not in early]

    def place(m, h, left, right):
        here = pl.ds(pl.multiple_of((me ^ m) * hw, hw), hw)
        left_s[h, here, :] = left
        right_s[h, here, :] = right

    for m in later:
        for h in range(tiles):
            ref, k = where[m]
            normed = column_norm(chunk_of(ref, channels, k, h), gain_ref[0])
            normed_s[later.index(m), h] = normed
            place(m, h, *factors(dot(proj_ref[0], normed), mask_of(ref, channels, k, h)))
    for n, m in enumerate(early):
        for h in range(tiles):
            place(m, h, early_left_ref[n, h], early_right_ref[n, h])

    low = iota((devices, LANES), 1) < tokens

    def channel_sum(c, _):
        here = pl.ds(c, devices, stride=hw)
        left = jnp.concatenate([left_s[h, here, :] for h in range(tiles)], axis=0)
        halves = [[], []]
        for h in range(tiles):
            right = right_s[h, here, :]
            turned = pltpu.roll(right, tokens, 1)
            for q in range(2):
                straight, other = (right, turned) if q == 0 else (turned, right)
                halves[0].append(jnp.where(low, straight, 0.0))
                halves[1].append(jnp.where(low, 0.0, other))
        against = jnp.concatenate(halves[0] + halves[1], axis=0).astype(BF16)
        here = pl.ds(pl.multiple_of(c * tiles * devices, tiles * devices), tiles * devices)
        sum_s[here, :] = dot_nt(left.astype(BF16), against)
        return 0

    lax.fori_loop(0, hw, channel_sum, 0, unroll=16)

    for m in range(devices):
        for h in range(tiles):
            ref, k = where[m]
            first = early_normed_ref[early.index(m), h] if m in early else normed_s[later.index(m), h]
            summed = sum_s[pl.ds(h * devices + (me ^ m), hw, stride=tiles * devices), :]
            update = dot(out_ref[0], column_norm(summed, mid_ref[0]))
            gating = sigmoid(dot(gate_ref[0], first))
            now = (chunk_of(ref, channels, k, h) + gating * update).astype(BF16)
            normed = column_norm(now.astype(F32), gain_ref[1])
            if m == 0:
                now_s[h] = now
                now_s[tiles + h] = normed
            left, right = factors(dot(proj_ref[1], normed), mask_of(ref, channels, k, h))
            here = pl.ds((m * tiles + h) * hw, hw)
            second_left_s[here, :] = left.astype(BF16)
            second_right_s[here, :] = right.astype(BF16)

    depth = 4 * hw
    sums = []
    for i in range(rows):
        total = jnp.zeros((hw, LANES), F32)
        for n in range(devices * tiles // 4):
            here = pl.ds(n * depth, depth)
            terms = dot(second_left_s[here, :], spread_ref[i]) * second_right_s[here, :].astype(F32)
            total = total + sum(terms[k * hw : (k + 1) * hw] for k in range(4))
        sums.append(total + pltpu.roll(total, tokens, 1))
    low = iota((hw, LANES), 1) < tokens
    for h in range(tiles):
        summed = jnp.where(low, sums[2 * h], sums[2 * h + 1])
        update = dot(out_ref[1], column_norm(summed, mid_ref[1]))
        gating = sigmoid(dot(gate_ref[1], now_s[tiles + h]))
        final = (now_s[h].astype(F32) + gating * update).astype(BF16)
        result_ref[h * LANES : (h + 1) * LANES, :] = dot_nt(restore_ref[...], final).astype(BF16)


def exchange(block, partner_bits, devices):
    pairs = [(d, d ^ partner_bits) for d in range(devices)]
    return lax.ppermute(block, "row", pairs)


def small_plan(pair, mask, proj, gate, out, gain, mid):
    rows, tokens, channels = pair.shape
    devices, size, hw = tokens // rows, rows * tokens, out.shape[1]
    tiles = size // LANES
    packed = pl.pallas_call(
        functools.partial(pack_kernel, rows, tokens),
        out_shape=VMEM((1, tiles * channels + MASK_ROWS, LANES), BF16),
        out_specs=IN_VMEM,
        name="pack",
    )(pair, mask)
    me = lax.axis_index("row").reshape(1).astype(jnp.int32)
    weights = pl.pallas_call(
        functools.partial(prepare_kernel, rows, tokens),
        in_specs=[IN_SMEM] + [pl.BlockSpec()] * 5,
        out_shape=(
            VMEM((2, 4 * hw, channels), BF16),
            VMEM((2, channels, channels), BF16),
            VMEM((2, channels, hw), BF16),
            VMEM((2, channels, LANES), F32),
            VMEM((2, hw, LANES), F32),
            VMEM((LANES, LANES), BF16),
            VMEM((rows, LANES, LANES), BF16),
        ),
        out_specs=(IN_VMEM,) * 7,
        name="prepare",
    )(me, proj, gate, out, gain, mid)

    def swapped(group):
        return exchange(jnp.concatenate([held[m] for m in group]), 1, devices)

    held = {0: packed}
    for m in (12, 8, 4, 2):
        held[m] = exchange(packed, m, devices)
    first = (0, 2, 4)
    held[2], weights = lax.optimization_barrier((held[2], weights))
    held[6] = exchange(held[2], 4, devices)
    swaps = [swapped(first)]
    held[8], held[12] = lax.optimization_barrier((held[8], held[12]))
    held[10] = exchange(held[8], 2, devices)
    held[14] = exchange(held[12], 2, devices)

    early = (0, 2, 4, 8, 12) + tuple(m ^ 1 for m in first)
    count = len(early)
    ahead = pl.pallas_call(
        functools.partial(early_kernel, (1,) * 5 + (len(first),)),
        in_specs=[IN_VMEM] * 8,
        out_shape=(
            VMEM((count, tiles, hw, LANES), F32),
            VMEM((count, tiles, hw, LANES), F32),
            VMEM((count, tiles, channels, LANES), BF16),
        ),
        out_specs=(IN_VMEM,) * 3,
        name="early",
    )(*[held[m] for m in (0, 2, 4, 8, 12)], swaps[0], weights[0], weights[3])
    held[10], ahead = lax.optimization_barrier((held[10], ahead))
    second = (6, 8, 10, 12, 14)
    swaps.append(swapped(second))

    arrays = [held[m] for m in sorted(held)] + swaps
    sources = [(m,) for m in sorted(held)]
    sources += [tuple(m ^ 1 for m in group) for group in (first, second)]
    result = pl.pallas_call(
        functools.partial(both_kernel, rows, tokens, sources, early),
        out_shape=jax.ShapeDtypeStruct((size, channels), BF16),
        in_specs=[IN_SMEM] + [IN_VMEM] * (len(arrays) + 10),
        scratch_shapes=[
            pltpu.VMEM((tiles, devices * hw, LANES), F32),
            pltpu.VMEM((tiles, devices * hw, LANES), F32),
            pltpu.VMEM((devices - count, tiles, channels, LANES), BF16),
            pltpu.VMEM((hw * devices * tiles, LANES), F32),
            pltpu.VMEM((2 * tiles, channels, LANES), BF16),
            pltpu.VMEM((devices * tiles * hw, LANES), BF16),
            pltpu.VMEM((devices * tiles * hw, LANES), BF16),
        ],
        compiler_params=pltpu.CompilerParams(vmem_limit_bytes=24 * 1024 * 1024),
        name="both",
    )(me, *arrays, *weights, *ahead)
    return result.reshape(pair.shape)


def layer_norm(values, gain, axis):
    average = jnp.mean(values, axis=axis, keepdims=True)
    centred = values - average
    variance = jnp.mean(centred * centred, axis=axis, keepdims=True)
    return centred * lax.rsqrt(variance + EPS) * gain


def wide_factors(normed, mask, proj):
    hw = proj.shape[1] // 4
    projected = jnp.einsum("ijd,de->eij", normed, proj, preferred_element_type=F32)
    left = mask * jax.nn.sigmoid(projected[hw : 2 * hw]) * projected[:hw]
    right = mask * jax.nn.sigmoid(projected[3 * hw :]) * projected[2 * hw : 3 * hw]
    return left.astype(BF16), right.astype(BF16)


def gathered_update(pair, mask, proj, gate, out, gain, mid, orient):
    rows, tokens, _ = pair.shape
    devices = tokens // rows
    floats = pair.astype(F32)
    normed = layer_norm(floats, gain, -1).astype(BF16)
    left, right = wide_factors(normed, mask, proj)
    everywhere = lax.all_gather(right, "row", axis=1, tiled=True)
    if orient == 1:
        c = left.shape[0]
        blocks = left.reshape(c, rows, devices, rows).transpose(2, 1, 3, 0)
        left = lax.all_to_all(blocks, "row", 0, 0, tiled=True)
        left = left.reshape(tokens, rows, c).transpose(2, 0, 1)
    spec = "cik,cjk->cij" if orient == 0 else "cki,ckj->cij"
    summed = jnp.einsum(spec, left, everywhere, preferred_element_type=F32)
    hidden = layer_norm(summed, mid[:, None, None], 0).astype(BF16)
    gating = jax.nn.sigmoid(jnp.einsum("ijd,de->ije", normed, gate, preferred_element_type=F32))
    update = jnp.einsum("cij,cd->ijd", hidden, out, preferred_element_type=F32)
    return (floats + gating * update).astype(BF16)


def shards(pair, pair_mask, proj, gate, out, gain, mid):
    rows, tokens, _ = pair.shape
    if rows == 4 and 2 * tokens == LANES:
        return small_plan(pair, pair_mask, proj, gate, out, gain, mid)
    mask = pair_mask.astype(F32)[None]
    for o in range(2):
        pair = gathered_update(pair, mask, proj[o], gate[o], out[o], gain[o], mid[o], o)
    return pair


def solution(mesh):
    return jax.shard_map(
        shards,
        mesh=mesh,
        in_specs=(P(("groups", "row")), P(("groups", "row")), P(), P(), P(), P(), P()),
        out_specs=P(("groups", "row")),
        check_vma=False,
    )
```

time: 39.5 us -> 30.8 us (0.78)
  local copies, waits for them, and re-layouts: 6.27 us -> 1.98 us
  Pallas kernels: 15 us -> 11.7 us
  starting transfers between devices: 12.5 us -> 9.52 us
  waiting for transfers between devices: 5.25 us -> 7.14 us
    unnamed x16 -> x36, local copies, waits for them, and re-layouts: 6.27 us -> 1.97 us
    ppermute x15 -> x9, starting transfers between devices: 12.5 us -> 9.52 us  [exchange(): return lax.ppermute(block, 'row', pairs)]
    pallas_call x2 -> x3, Pallas kernels: 12.8 us -> 10.4 us  [the longest x1 7.36 us: small_plan(): pl.pallas_call(functools.partial(both_kernel, rows, tokens, sources, earl...]
    ppermute x15 -> x9, waiting for transfers between devices: 5.25 us -> 7.14 us  [exchange(): return lax.ppermute(block, 'row', pairs)]
    pallas_call x1, Pallas kernels: 2.17 us -> 1.21 us  [small_plan(): pl.pallas_call(functools.partial(prepare_kernel, rows, tokens), in_specs=...]
  transfers between devices with their start and end apart: 15 -> 9, of which waited for: 4 -> 3; matrix products, arithmetic and copies ran while one was open for 0% -> 0% of each run, Pallas kernels for 6% -> 10%
where the time goes in v8:
time: 30.8 us; the launch traced here: 30.6 us
  Pallas kernels  11.7 us (38%)
  starting transfers between devices  9.52 us (31%)
  waiting for transfers between devices  7.14 us (23%)
  local copies, waits for them, and re-layouts  1.98 us (6%)
    ppermute x9, starting transfers between devices, exchange(): return lax.ppermute(block, 'row', pairs)  9.52 us
    pallas_call x1, Pallas kernels, small_plan(): pl.pallas_call(functools.partial(both_kernel, rows, tokens, sources, earl...  7.36 us
    ppermute x9, waiting for transfers between devices, exchange(): return lax.ppermute(block, 'row', pairs)  7.14 us
    unnamed x36, local copies, waits for them, and re-layouts  1.97 us
    pallas_call x1, Pallas kernels, small_plan(): pl.pallas_call(functools.partial(early_kernel, (1,) * 5 + (len(first),)),...  1.94 us
    pallas_call x1, Pallas kernels, small_plan(): pl.pallas_call(functools.partial(prepare_kernel, rows, tokens), in_specs=...  1.21 us
    pallas_call x1, Pallas kernels, small_plan(): pl.pallas_call(functools.partial(pack_kernel, rows, tokens), out_shape=VM...  1.15 us
  transfers between devices with their start and end apart: 9, of which 3 were waited for; matrix products, arithmetic and copies ran while one was open for 0% of the time, Pallas kernels for 10%

profile of v8, /device:TPU:0, one launch (start us, length us, event | category | flops | bytes accessed | tf_op | source)
XLA Modules:
  0.0 30.6 jit_solution(17505452105872007419)
XLA Ops:
  0.0 1.2 %pack.1.refs_0_ = bf16[1,272,128]{2,1,0:T(8,128)(2,1)S(1)} custom-call(bf16[4,64,128]{2,1,0:T(8,128)(2,1)} %pair_ref.1, s32[4,64]{1,0:T(4,128)} %mask_ref.1), custom_call_target="tpu_custom_call" | custom-call | tf_op jit(solution)/shard_map/pack/pallas_call | solution.py:227
  1.2 0.0 copy-start
  1.2 5.1 %collective-permute-start.4 = (bf16[1,272,128]{2,1,0:T(8,128)(2,1)S(1)}, bf16[1,272,128]{2,1,0:T(8,128)(2,1)S(1)}, u32[]{:S(2)}, u32[]{:S(2)}) collective-permute-start(bf16[1,272,128]{2,1,0:T(8,128)(2,1)S(1)} %pack.1.refs_0_), channel_id=1, source_target_pairs={{0,12},{1,13},{2,14},{3,15},{4,8},{5,9},{6,10},{7,11},{8,4},{9,5},... | collective-permute-start | bytes 208904 | tf_op jit(solution)/shard_map/ppermute | solution.py:220
  6.3 0.0 collective-permute-start.3
  6.3 1.5 %collective-permute-start = (bf16[1,272,128]{2,1,0:T(8,128)(2,1)S(1)}, bf16[1,272,128]{2,1,0:T(8,128)(2,1)S(1)}, u32[]{:S(2)}, u32[]{:S(2)}) collective-permute-start(bf16[1,272,128]{2,1,0:T(8,128)(2,1)S(1)} %pack.1.refs_0_), channel_id=1, source_target_pairs={{0,2},{1,3},{2,0},{3,1},{4,6},{5,7},{6,4},{7,5},{8,10},{9,11},{10,... | collective-permute-start | bytes 208904 | tf_op jit(solution)/shard_map/ppermute | solution.py:220
  7.8 0.8 %collective-permute-start.1 = (bf16[1,272,128]{2,1,0:T(8,128)(2,1)S(1)}, bf16[1,272,128]{2,1,0:T(8,128)(2,1)S(1)}, u32[]{:S(2)}, u32[]{:S(2)}) collective-permute-start(bf16[1,272,128]{2,1,0:T(8,128)(2,1)S(1)} %pack.1.refs_0_), channel_id=1, source_target_pairs={{0,4},{1,5},{2,6},{3,7},{4,0},{5,1},{6,2},{7,3},{8,12},{9,13},{10,... | collective-permute-start | bytes 208904 | tf_op jit(solution)/shard_map/ppermute | solution.py:220
  8.6 1.2 %prepare.1 = (bf16[2,256,128]{2,1,0:T(8,128)(2,1)S(1)}, bf16[2,128,128]{2,1,0:T(8,128)(2,1)S(1)}, bf16[2,128,64]{2,1,0:T(8,128)(2,1)S(1)}, f32[2,128,128]{2,1,0:...) custom-call(s32[1]{0:T(128)} %bitcast.me_ref, ...), custom_call_target="tpu_custom_call" | custom-call | tf_op jit(solution)/shard_map/prepare/pallas_call | solution.py:234
  9.8 0.6 %copy-done.14 = f32[2,128,128]{2,1,0:T(8,128)} copy-done((f32[2,128,128]{2,1,0:T(8,128)}, f32[2,128,128]{2,1,0:T(8,128)S(1)}, u32[]{:S(2)}) %copy-start.14) | copy-done | bytes 131096
  10.4 0.0 collective-permute-done.4.refs_4_.refs_6_
  10.5 1.8 %collective-permute-done.3.refs_3_.refs_4_ = bf16[1,272,128]{2,1,0:T(8,128)(2,1)S(1)} collective-permute-done((bf16[1,272,128]{2,1,0:T(8,128)(2,1)S(1)}, bf16[1,272,128]{2,1,0:T(8,128)(2,1)S(1)}, u32[]{:S(2)}, u32[]{:S(2)}) %collective-permute-start.3) | collective-permute-done | bytes 69664 | tf_op jit(solution)/shard_map/ppermute | solution.py:220
  12.3 1.5 %collective-permute-start.5 = (bf16[1,272,128]{2,1,0:T(8,128)(2,1)S(1)}, bf16[1,272,128]{2,1,0:T(8,128)(2,1)S(1)}, u32[]{:S(2)}, u32[]{:S(2)}) collective-permute-start(bf16[1,272,128]{2,1,0:T(8,128)(2,1)S(1)} %collective-permute-done.3.refs_3_.refs_4_), channel_id=1, source_target_pairs={{0,2},{1,3},{2,0},{3,1},{4,6},{5,7},{6,4},{7,5},{8,10},{9,11},{10,... | collective-permute-start | bytes 208904 | tf_op jit(solution)/shard_map/ppermute | solution.py:220
  13.8 0.5 %collective-permute-start.7 = (bf16[1,272,128]{2,1,0:T(8,128)(2,1)S(1)}, bf16[1,272,128]{2,1,0:T(8,128)(2,1)S(1)}, u32[]{:S(2)}, u32[]{:S(2)}) collective-permute-start(bf16[1,272,128]{2,1,0:T(8,128)(2,1)S(1)} %collective-permute-done.4.refs_4_.refs_6_), channel_id=1, source_target_pairs={{0,2},{1,3},{2,0},{3,1},{4,6},{5,7},{6,4},{7,5},{8,10},{9,11},{10,... | collective-permute-start | bytes 208904 | tf_op jit(solution)/shard_map/ppermute | solution.py:220
  14.3 0.0 collective-permute-done.refs_1_
  14.3 0.0 collective-permute-start.2
  14.3 0.0 collective-permute-done.1.refs_2_
  14.4 0.5 %copy-done.4 = bf16[1,272,128]{2,1,0:T(8,128)(2,1)} copy-done((bf16[1,272,128]{2,1,0:T(8,128)(2,1)}, bf16[1,272,128]{2,1,0:T(8,128)(2,1)S(1)}, u32[]{:S(2)}) %copy-start.4) | copy-done | bytes 69656
  14.9 0.0 copy-done.6
  15.0 0.0 collective-permute-start.6
  15.0 3.6 %collective-permute-done.2.refs_3_ = bf16[1,272,128]{2,1,0:T(8,128)(2,1)S(1)} collective-permute-done((bf16[1,272,128]{2,1,0:T(8,128)(2,1)S(1)}, bf16[1,272,128]{2,1,0:T(8,128)(2,1)S(1)}, u32[]{:S(2)}, u32[]{:S(2)}) %collective-permute-start.2) | collective-permute-done | bytes 69664 | tf_op jit(solution)/shard_map/ppermute | solution.py:220
  18.7 0.0 collective-permute-done.6.refs_5_.refs_8_
  18.7 0.0 copy-start.2
  18.7 0.7 %copy-done.2 = bf16[3,272,128]{2,1,0:T(8,128)(2,1)} copy-done((bf16[3,272,128]{2,1,0:T(8,128)(2,1)}, bf16[3,272,128]{2,1,0:T(8,128)(2,1)S(1)}, u32[]{:S(2)}) %copy-start.2) | copy-done | bytes 208920
  19.4 1.9 %early.1 = (f32[8,2,64,128]{3,2,1,0:T(8,128)S(1)}, f32[8,2,64,128]{3,2,1,0:T(8,128)S(1)}, bf16[8,2,128,128]{3,2,1,0:T(8,128)(2,1)S(1)}) custom-call(bf16[1,272,128]{2,1,0:T(8,128)(2,1)} %copy-done, bf16[1,272,128]{2,1,0:T(8,128)(2,1)} %copy-done.4, bf16[1,272,128]{2,1,0:T(8,128)(2,1)} %copy-done.6, bf16[1,272,128]{2,1,0:T(8,128)(2,1)} %copy-done.10, ...), custom_call_target="tpu_custom_call" | custom-call | tf_op jit(solution)/shard_map/early/pallas_call | solution.py:266
  21.3 0.0 collective-permute-done.5.refs_5_
  21.4 0.0 copy-start.1
  21.4 0.0 copy-start.5
  21.4 0.0 collective-permute-done.7.refs_7_
  21.4 0.1 collective-permute-start.8
  21.5 1.6 %collective-permute-done.8.refs_9_ = bf16[5,272,128]{2,1,0:T(8,128)(2,1)S(1)} collective-permute-done((bf16[5,272,128]{2,1,0:T(8,128)(2,1)S(1)}, bf16[5,272,128]{2,1,0:T(8,128)(2,1)S(1)}, u32[]{:S(2)}, u32[]{:S(2)}) %collective-permute-start.8) | collective-permute-done | bytes 348192 | tf_op jit(solution)/shard_map/ppermute | solution.py:220
  23.2 0.0 copy-done.11
  23.2 0.0 copy-done.15
  23.2 7.4 %both.1 = bf16[256,128]{1,0:T(8,128)(2,1)} custom-call(s32[1]{0:T(128)} %bitcast.me_ref, bf16[1,272,128]{2,1,0:T(8,128)(2,1)S(1)} %copy-done.1, bf16[1,272,128]{2,1,0:T(8,128)(2,1)S(1)} %copy-done.5, bf16[1,272,128]{2,1,0:T(8,128)(2,1)S(1)} %copy-done.7, bf16[1,272,128]{2,1,0:T(8,128)(2,1)S(1)} %collective-permute-done.2.refs_3_, ...), custom_call_target="tpu_custom_call" | custom-call | tf_op jit(solution)/shard_map/both/pallas_call | solution.py:284
  (28 shorter events, 0.1 us)
Async XLA Ops:
  1.2 13.2 %copy-start = (bf16[1,272,128]{2,1,0:T(8,128)(2,1)}, bf16[1,272,128]{2,1,0:T(8,128)(2,1)S(1)}, u32[]{:S(2)}) copy-start(bf16[1,272,128]{2,1,0:T(8,128)(2,1)S(1)} %pack.1.refs_0_) | copy-start | bytes 208900
  1.2 9.3 %collective-permute-start.4 = (bf16[1,272,128]{2,1,0:T(8,128)(2,1)S(1)}, bf16[1,272,128]{2,1,0:T(8,128)(2,1)S(1)}, u32[]{:S(2)}, u32[]{:S(2)}) collective-permute-start(bf16[1,272,128]{2,1,0:T(8,128)(2,1)S(1)} %pack.1.refs_0_), channel_id=1, source_target_pairs={{0,12},{1,13},{2,14},{3,15},{4,8},{5,9},{6,10},{7,11},{8,4},{9,5},... | collective-permute-start | bytes 208904 | tf_op jit(solution)/shard_map/ppermute | solution.py:220
  6.3 6.0 %collective-permute-start.3 = (bf16[1,272,128]{2,1,0:T(8,128)(2,1)S(1)}, bf16[1,272,128]{2,1,0:T(8,128)(2,1)S(1)}, u32[]{:S(2)}, u32[]{:S(2)}) collective-permute-start(bf16[1,272,128]{2,1,0:T(8,128)(2,1)S(1)} %pack.1.refs_0_), channel_id=1, source_target_pairs={{0,8},{1,9},{2,10},{3,11},{4,12},{5,13},{6,14},{7,15},{8,0},{9,1},... | collective-permute-start | bytes 208904 | tf_op jit(solution)/shard_map/ppermute | solution.py:220
  6.3 8.0 %collective-permute-start = (bf16[1,272,128]{2,1,0:T(8,128)(2,1)S(1)}, bf16[1,272,128]{2,1,0:T(8,128)(2,1)S(1)}, u32[]{:S(2)}, u32[]{:S(2)}) collective-permute-start(bf16[1,272,128]{2,1,0:T(8,128)(2,1)S(1)} %pack.1.refs_0_), channel_id=1, source_target_pairs={{0,2},{1,3},{2,0},{3,1},{4,6},{5,7},{6,4},{7,5},{8,10},{9,11},{10,... | collective-permute-start | bytes 208904 | tf_op jit(solution)/shard_map/ppermute | solution.py:220
  7.8 6.5 %collective-permute-start.1 = (bf16[1,272,128]{2,1,0:T(8,128)(2,1)S(1)}, bf16[1,272,128]{2,1,0:T(8,128)(2,1)S(1)}, u32[]{:S(2)}, u32[]{:S(2)}) collective-permute-start(bf16[1,272,128]{2,1,0:T(8,128)(2,1)S(1)} %pack.1.refs_0_), channel_id=1, source_target_pairs={{0,4},{1,5},{2,6},{3,7},{4,0},{5,1},{6,2},{7,3},{8,12},{9,13},{10,... | collective-permute-start | bytes 208904 | tf_op jit(solution)/shard_map/ppermute | solution.py:220
  9.8 0.6 %copy-start.14 = (f32[2,128,128]{2,1,0:T(8,128)}, f32[2,128,128]{2,1,0:T(8,128)S(1)}, u32[]{:S(2)}) copy-start(f32[2,128,128]{2,1,0:T(8,128)S(1)} %get-tuple-element.40.refs_7_.refs_13_) | copy-start | bytes 393220
  10.4 3.9 %copy-start.12 = (bf16[2,256,128]{2,1,0:T(8,128)(2,1)}, bf16[2,256,128]{2,1,0:T(8,128)(2,1)S(1)}, u32[]{:S(2)}) copy-start(bf16[2,256,128]{2,1,0:T(8,128)(2,1)S(1)} %get-tuple-element.39.refs_6_.refs_10_) | copy-start | bytes 393220
  10.5 3.9 %copy-start.8 = (bf16[1,272,128]{2,1,0:T(8,128)(2,1)}, bf16[1,272,128]{2,1,0:T(8,128)(2,1)S(1)}, u32[]{:S(2)}) copy-start(bf16[1,272,128]{2,1,0:T(8,128)(2,1)S(1)} %collective-permute-done.4.refs_4_.refs_6_) | copy-start | bytes 208900
  12.3 6.4 %copy-start.10 = (bf16[1,272,128]{2,1,0:T(8,128)(2,1)}, bf16[1,272,128]{2,1,0:T(8,128)(2,1)S(1)}, u32[]{:S(2)}) copy-start(bf16[1,272,128]{2,1,0:T(8,128)(2,1)S(1)} %collective-permute-done.3.refs_3_.refs_4_) | copy-start | bytes 208900
  12.3 9.0 %collective-permute-start.5 = (bf16[1,272,128]{2,1,0:T(8,128)(2,1)S(1)}, bf16[1,272,128]{2,1,0:T(8,128)(2,1)S(1)}, u32[]{:S(2)}, u32[]{:S(2)}) collective-permute-start(bf16[1,272,128]{2,1,0:T(8,128)(2,1)S(1)} %collective-permute-done.3.refs_3_.refs_4_), channel_id=1, source_target_pairs={{0,2},{1,3},{2,0},{3,1},{4,6},{5,7},{6,4},{7,5},{8,10},{9,11},{10,... | collective-permute-start | bytes 208904 | tf_op jit(solution)/shard_map/ppermute | solution.py:220
  13.8 7.6 %collective-permute-start.7 = (bf16[1,272,128]{2,1,0:T(8,128)(2,1)S(1)}, bf16[1,272,128]{2,1,0:T(8,128)(2,1)S(1)}, u32[]{:S(2)}, u32[]{:S(2)}) collective-permute-start(bf16[1,272,128]{2,1,0:T(8,128)(2,1)S(1)} %collective-permute-done.4.refs_4_.refs_6_), channel_id=1, source_target_pairs={{0,2},{1,3},{2,0},{3,1},{4,6},{5,7},{6,4},{7,5},{8,10},{9,11},{10,... | collective-permute-start | bytes 208904 | tf_op jit(solution)/shard_map/ppermute | solution.py:220
  14.3 0.6 %copy-start.4 = (bf16[1,272,128]{2,1,0:T(8,128)(2,1)}, bf16[1,272,128]{2,1,0:T(8,128)(2,1)S(1)}, u32[]{:S(2)}) copy-start(bf16[1,272,128]{2,1,0:T(8,128)(2,1)S(1)} %collective-permute-done.refs_1_) | copy-start | bytes 208900
  14.3 4.3 %collective-permute-start.2 = (bf16[1,272,128]{2,1,0:T(8,128)(2,1)S(1)}, bf16[1,272,128]{2,1,0:T(8,128)(2,1)S(1)}, u32[]{:S(2)}, u32[]{:S(2)}) collective-permute-start(bf16[1,272,128]{2,1,0:T(8,128)(2,1)S(1)} %collective-permute-done.refs_1_), channel_id=1, source_target_pairs={{0,4},{1,5},{2,6},{3,7},{4,0},{5,1},{6,2},{7,3},{8,12},{9,13},{10,... | collective-permute-start | bytes 208904 | tf_op jit(solution)/shard_map/ppermute | solution.py:220
  14.3 0.6 %copy-start.6 = (bf16[1,272,128]{2,1,0:T(8,128)(2,1)}, bf16[1,272,128]{2,1,0:T(8,128)(2,1)S(1)}, u32[]{:S(2)}) copy-start(bf16[1,272,128]{2,1,0:T(8,128)(2,1)S(1)} %collective-permute-done.1.refs_2_) | copy-start | bytes 208900
  15.0 3.7 %collective-permute-start.6 = (bf16[3,272,128]{2,1,0:T(8,128)(2,1)S(1)}, bf16[3,272,128]{2,1,0:T(8,128)(2,1)S(1)}, u32[]{:S(2)}, u32[]{:S(2)}) collective-permute-start(bf16[3,272,128]{2,1,0:T(8,128)(2,1)S(1)} %pad_maximum_fusion), channel_id=1, source_target_pairs={{0,1},{1,0},{2,3},{3,2},{4,5},{5,4},{6,7},{7,6},{8,9},{9,8},{10,11... | collective-permute-start | bytes 626696 | tf_op jit(solution)/shard_map/ppermute | solution.py:220
  18.7 0.7 %copy-start.2 = (bf16[3,272,128]{2,1,0:T(8,128)(2,1)}, bf16[3,272,128]{2,1,0:T(8,128)(2,1)S(1)}, u32[]{:S(2)}) copy-start(bf16[3,272,128]{2,1,0:T(8,128)(2,1)S(1)} %collective-permute-done.6.refs_5_.refs_8_) | copy-start | bytes 626692
  19.3 2.0 %copy-start.9 = (bf16[1,272,128]{2,1,0:T(8,128)(2,1)S(1)}, bf16[1,272,128]{2,1,0:T(8,128)(2,1)}, u32[]{:S(2)}) copy-start(bf16[1,272,128]{2,1,0:T(8,128)(2,1)} %copy-done.8) | copy-start | bytes 208900
  19.4 3.8 %copy-start.11 = (bf16[1,272,128]{2,1,0:T(8,128)(2,1)S(1)}, bf16[1,272,128]{2,1,0:T(8,128)(2,1)}, u32[]{:S(2)}) copy-start(bf16[1,272,128]{2,1,0:T(8,128)(2,1)} %copy-done.10) | copy-start | bytes 208900
  19.4 3.8 %copy-start.13 = (bf16[2,256,128]{2,1,0:T(8,128)(2,1)S(1)}, bf16[2,256,128]{2,1,0:T(8,128)(2,1)}, u32[]{:S(2)}) copy-start(bf16[2,256,128]{2,1,0:T(8,128)(2,1)} %copy-done.12) | copy-start | bytes 393220
  19.4 3.8 %copy-start.15 = (f32[2,128,128]{2,1,0:T(8,128)S(1)}, f32[2,128,128]{2,1,0:T(8,128)}, u32[]{:S(2)}) copy-start(f32[2,128,128]{2,1,0:T(8,128)} %copy-done.14) | copy-start | bytes 393220
  21.3 1.9 %copy-start.3 = (bf16[3,272,128]{2,1,0:T(8,128)(2,1)S(1)}, bf16[3,272,128]{2,1,0:T(8,128)(2,1)}, u32[]{:S(2)}) copy-start(bf16[3,272,128]{2,1,0:T(8,128)(2,1)} %copy-done.2) | copy-start | bytes 626692
  21.4 1.8 %copy-start.7 = (bf16[1,272,128]{2,1,0:T(8,128)(2,1)S(1)}, bf16[1,272,128]{2,1,0:T(8,128)(2,1)}, u32[]{:S(2)}) copy-start(bf16[1,272,128]{2,1,0:T(8,128)(2,1)} %copy-done.6) | copy-start | bytes 208900
  21.4 1.8 %copy-start.1 = (bf16[1,272,128]{2,1,0:T(8,128)(2,1)S(1)}, bf16[1,272,128]{2,1,0:T(8,128)(2,1)}, u32[]{:S(2)}) copy-start(bf16[1,272,128]{2,1,0:T(8,128)(2,1)} %copy-done) | copy-start | bytes 208900
  21.4 1.8 %copy-start.5 = (bf16[1,272,128]{2,1,0:T(8,128)(2,1)S(1)}, bf16[1,272,128]{2,1,0:T(8,128)(2,1)}, u32[]{:S(2)}) copy-start(bf16[1,272,128]{2,1,0:T(8,128)(2,1)} %copy-done.4) | copy-start | bytes 208900
  21.4 1.7 %collective-permute-start.8 = (bf16[5,272,128]{2,1,0:T(8,128)(2,1)S(1)}, bf16[5,272,128]{2,1,0:T(8,128)(2,1)S(1)}, u32[]{:S(2)}, u32[]{:S(2)}) collective-permute-start(bf16[5,272,128]{2,1,0:T(8,128)(2,1)S(1)} %constant_dynamic-update-slice_fusion), channel_id=1, source_target_pairs={{0,1},{1,0},{2,3},{3,2},{4,5},{5,4},{6,7},{7,6},{8,9},{9,8},{10,11... | collective-permute-start | bytes 1044488 | tf_op jit(solution)/shard_map/ppermute | solution.py:220

commit v9 on v8

--- a/solution.py
+++ b/solution.py
@@ -15,6 +15,7 @@
 VMEM = pltpu.VMEM
 IN_VMEM = pl.BlockSpec(memory_space=pltpu.VMEM)
 IN_SMEM = pl.BlockSpec(memory_space=pltpu.SMEM)
+SMALL = pltpu.CompilerParams(vmem_limit_bytes=8 * 1024 * 1024)
 
 
 def dot(a, b):
@@ -54,6 +55,14 @@
     left = mask * sigmoid(projected[hw : 2 * hw]) * projected[:hw]
     right = mask * sigmoid(projected[3 * hw :]) * projected[2 * hw : 3 * hw]
     return left, right
+
+
+def side_by_side(chunks):
+    return jnp.concatenate(chunks, axis=1)
+
+
+def tile(values, h):
+    return values[:, h * LANES : (h + 1) * LANES]
 
 
 def pack_kernel(rows, tokens, pair_ref, mask_ref, packed_ref):
@@ -120,10 +129,13 @@
     place = 0
     for block_ref, count in zip(block_refs, counts):
         for k in range(count):
+            normed = [
+                column_norm(chunk_of(block_ref, channels, k, h), gain_ref[0]) for h in range(tiles)
+            ]
+            projected = dot(proj_ref[0], side_by_side(normed))
             for h in range(tiles):
-                normed = column_norm(chunk_of(block_ref, channels, k, h), gain_ref[0])
-                normed_ref[place, h] = normed
-                left, right = factors(dot(proj_ref[0], normed), mask_of(block_ref, channels, k, h))
+                normed_ref[place, h] = normed[h]
+                left, right = factors(tile(projected, h), mask_of(block_ref, channels, k, h))
                 left_ref[place, h] = left
                 right_ref[place, h] = right
             place += 1
@@ -151,11 +163,12 @@
         right_s[h, here, :] = right
 
     for m in later:
-        for h in range(tiles):
-            ref, k = where[m]
-            normed = column_norm(chunk_of(ref, channels, k, h), gain_ref[0])
-            normed_s[later.index(m), h] = normed
-            place(m, h, *factors(dot(proj_ref[0], normed), mask_of(ref, channels, k, h)))
+        ref, k = where[m]
+        normed = [column_norm(chunk_of(ref, channels, k, h), gain_ref[0]) for h in range(tiles)]
+        projected = dot(proj_ref[0], side_by_side(normed))
+        for h in range(tiles):
+            normed_s[later.index(m), h] = normed[h]
+            place(m, h, *factors(tile(projected, h), mask_of(ref, channels, k, h)))
     for n, m in enumerate(early):
         for h in range(tiles):
             place(m, h, early_left_ref[n, h], early_right_ref[n, h])
@@ -181,31 +194,42 @@
     lax.fori_loop(0, hw, channel_sum, 0, unroll=16)
 
     for m in range(devices):
-        for h in range(tiles):
-            ref, k = where[m]
-            first = early_normed_ref[early.index(m), h] if m in early else normed_s[later.index(m), h]
+        ref, k = where[m]
+        hidden, first = [], []
+        for h in range(tiles):
             summed = sum_s[pl.ds(h * devices + (me ^ m), hw, stride=tiles * devices), :]
-            update = dot(out_ref[0], column_norm(summed, mid_ref[0]))
-            gating = sigmoid(dot(gate_ref[0], first))
-            now = (chunk_of(ref, channels, k, h) + gating * update).astype(BF16)
-            normed = column_norm(now.astype(F32), gain_ref[1])
+            hidden.append(column_norm(summed, mid_ref[0]))
+            first.append(early_normed_ref[early.index(m), h] if m in early else normed_s[later.index(m), h])
+        update = dot(out_ref[0], side_by_side(hidden))
+        logits = dot(gate_ref[0], side_by_side(first))
+        normed = []
+        for h in range(tiles):
+            gated = sigmoid(tile(logits, h)) * tile(update, h)
+            now = (chunk_of(ref, channels, k, h) + gated).astype(BF16)
+            normed.append(column_norm(now.astype(F32), gain_ref[1]))
             if m == 0:
                 now_s[h] = now
-                now_s[tiles + h] = normed
-            left, right = factors(dot(proj_ref[1], normed), mask_of(ref, channels, k, h))
+                now_s[tiles + h] = normed[h]
+        projected = dot(proj_ref[1], side_by_side(normed))
+        for h in range(tiles):
+            left, right = factors(tile(projected, h), mask_of(ref, channels, k, h))
             here = pl.ds((m * tiles + h) * hw, hw)
             second_left_s[here, :] = left.astype(BF16)
             second_right_s[here, :] = right.astype(BF16)
 
-    depth = 4 * hw
+    depth = 2 * hw
     sums = []
-    for i in range(rows):
-        total = jnp.zeros((hw, LANES), F32)
-        for n in range(devices * tiles // 4):
+    for i in range(0, rows, 2):
+        pair = side_by_side([spread_ref[i], spread_ref[i + 1]])
+        totals = [jnp.zeros((hw, LANES), F32)] * 2
+        for n in range(devices * tiles // 2):
             here = pl.ds(n * depth, depth)
-            terms = dot(second_left_s[here, :], spread_ref[i]) * second_right_s[here, :].astype(F32)
-            total = total + sum(terms[k * hw : (k + 1) * hw] for k in range(4))
-        sums.append(total + pltpu.roll(total, tokens, 1))
+            spread = dot(second_left_s[here, :], pair)
+            right = second_right_s[here, :].astype(F32)
+            for o in range(2):
+                terms = tile(spread, o) * right
+                totals[o] = totals[o] + (terms[:hw] + terms[hw:])
+        sums += [total + pltpu.roll(total, tokens, 1) for total in totals]
     low = iota((hw, LANES), 1) < tokens
     for h in range(tiles):
         summed = jnp.where(low, sums[2 * h], sums[2 * h + 1])
@@ -228,6 +252,7 @@
         functools.partial(pack_kernel, rows, tokens),
         out_shape=VMEM((1, tiles * channels + MASK_ROWS, LANES), BF16),
         out_specs=IN_VMEM,
+        compiler_params=SMALL,
         name="pack",
     )(pair, mask)
     me = lax.axis_index("row").reshape(1).astype(jnp.int32)
@@ -244,6 +269,7 @@
             VMEM((rows, LANES, LANES), BF16),
         ),
         out_specs=(IN_VMEM,) * 7,
+        compiler_params=SMALL,
         name="prepare",
     )(me, proj, gate, out, gain, mid)
 
@@ -253,34 +279,32 @@
     held = {0: packed}
     for m in (12, 8, 4, 2):
         held[m] = exchange(packed, m, devices)
-    first = (0, 2, 4)
-    held[2], weights = lax.optimization_barrier((held[2], weights))
+    held[2], held[4], held[8], held[12], weights = lax.optimization_barrier(
+        (held[2], held[4], held[8], held[12], weights)
+    )
+    held[14] = exchange(held[12], 2, devices)
+    held[10] = exchange(held[8], 2, devices)
     held[6] = exchange(held[2], 4, devices)
-    swaps = [swapped(first)]
-    held[8], held[12] = lax.optimization_barrier((held[8], held[12]))
-    held[10] = exchange(held[8], 2, devices)
-    held[14] = exchange(held[12], 2, devices)
-
-    early = (0, 2, 4, 8, 12) + tuple(m ^ 1 for m in first)
+    early = (0, 2, 4, 8, 12)
     count = len(early)
     ahead = pl.pallas_call(
-        functools.partial(early_kernel, (1,) * 5 + (len(first),)),
-        in_specs=[IN_VMEM] * 8,
+        functools.partial(early_kernel, (1,) * 5),
+        in_specs=[IN_VMEM] * 7,
         out_shape=(
             VMEM((count, tiles, hw, LANES), F32),
             VMEM((count, tiles, hw, LANES), F32),
             VMEM((count, tiles, channels, LANES), BF16),
         ),
         out_specs=(IN_VMEM,) * 3,
+        compiler_params=SMALL,
         name="early",
-    )(*[held[m] for m in (0, 2, 4, 8, 12)], swaps[0], weights[0], weights[3])
-    held[10], ahead = lax.optimization_barrier((held[10], ahead))
-    second = (6, 8, 10, 12, 14)
-    swaps.append(swapped(second))
-
-    arrays = [held[m] for m in sorted(held)] + swaps
-    sources = [(m,) for m in sorted(held)]
-    sources += [tuple(m ^ 1 for m in group) for group in (first, second)]
+    )(*[held[m] for m in (0, 2, 4, 8, 12)], weights[0], weights[3])
+    held[14], held[10], held[6], ahead = lax.optimization_barrier(
+        (held[14], held[10], held[6], ahead)
+    )
+    group = (0, 12, 8, 4, 2, 14, 10, 6)
+    arrays = [held[m] for m in group] + [swapped(group)]
+    sources = [(m,) for m in group] + [tuple(m ^ 1 for m in group)]
     result = pl.pallas_call(
         functools.partial(both_kernel, rows, tokens, sources, early),
         out_shape=jax.ShapeDtypeStruct((size, channels), BF16),

time: 30.8 us -> 29.2 us (0.948)
  Pallas kernels: 11.7 us -> 8.45 us
  local copies, waits for them, and re-layouts: 1.98 us -> 3.91 us
  waiting for transfers between devices: 7.14 us -> 5.81 us
  starting transfers between devices: 9.52 us -> 10.7 us
    unnamed x36 -> x21, local copies, waits for them, and re-layouts: 1.97 us -> 3.9 us
    pallas_call x1, Pallas kernels: 1.94 us -> 0.45 us  [small_plan(): pl.pallas_call(functools.partial(early_kernel, (1,) * 5), in_specs=[IN_VM...]
    ppermute x9 -> x8, waiting for transfers between devices: 7.14 us -> 5.81 us  [exchange(): return lax.ppermute(block, 'row', pairs)]
    ppermute x9 -> x8, starting transfers between devices: 9.52 us -> 10.7 us  [exchange(): return lax.ppermute(block, 'row', pairs)]
    pallas_call x1, Pallas kernels: 1.21 us -> 0.2 us  [small_plan(): pl.pallas_call(functools.partial(prepare_kernel, rows, tokens), in_specs=...]
    pallas_call x1, Pallas kernels: 1.15 us -> 0.31 us  [small_plan(): pl.pallas_call(functools.partial(pack_kernel, rows, tokens), out_shape=VM...]
  transfers between devices with their start and end apart: 9 -> 8, of which waited for: 3 -> 5; matrix products, arithmetic and copies ran while one was open for 0% -> 0% of each run, Pallas kernels for 10% -> 2%
where the time goes in v9:
time: 29.2 us; the launch traced here: 28.9 us
  starting transfers between devices  10.7 us (37%)
  Pallas kernels  8.45 us (29%)
  waiting for transfers between devices  5.81 us (20%)
  local copies, waits for them, and re-layouts  3.91 us (13%)
    ppermute x8, starting transfers between devices, exchange(): return lax.ppermute(block, 'row', pairs)  10.7 us
    pallas_call x1, Pallas kernels, small_plan(): pl.pallas_call(functools.partial(both_kernel, rows, tokens, sources, earl...  7.48 us
    ppermute x8, waiting for transfers between devices, exchange(): return lax.ppermute(block, 'row', pairs)  5.81 us
    unnamed x21, local copies, waits for them, and re-layouts  3.9 us
  transfers between devices with their start and end apart: 8, of which 5 were waited for; matrix products, arithmetic and copies ran while one was open for 0% of the time, Pallas kernels for 2%

profile of v9, /device:TPU:0, one launch (start us, length us, event | category | flops | bytes accessed | tf_op | source)
XLA Modules:
  0.0 28.9 jit_solution(15130464546566111633)
XLA Ops:
  0.0 0.0 copy-start.2
  0.0 0.8 %copy-done.2 = bf16[4,64,128]{2,1,0:T(8,128)(2,1)S(1)} copy-done((bf16[4,64,128]{2,1,0:T(8,128)(2,1)S(1)}, bf16[4,64,128]{2,1,0:T(8,128)(2,1)}, u32[]{:S(2)}) %copy-start.2) | copy-done | bytes 65560
  0.8 0.0 copy-start.4
  0.8 0.7 %copy-done.4 = s32[4,64]{1,0:T(4,128)S(1)} copy-done((s32[4,64]{1,0:T(4,128)S(1)}, s32[4,64]{1,0:T(4,128)}, u32[]{:S(2)}) %copy-start.4) | copy-done | bytes 1048
  1.5 0.3 %pack.1.refs_0_ = bf16[1,272,128]{2,1,0:T(8,128)(2,1)S(1)} custom-call(bf16[4,64,128]{2,1,0:T(8,128)(2,1)S(1)} %copy-done.2, s32[4,64]{1,0:T(4,128)S(1)} %copy-done.4), custom_call_target="tpu_custom_call" | custom-call | tf_op jit(solution)/shard_map/pack/pallas_call | solution.py:251
  1.8 5.1 %collective-permute-start.3 = (bf16[1,272,128]{2,1,0:T(8,128)(2,1)S(1)}, bf16[1,272,128]{2,1,0:T(8,128)(2,1)S(1)}, u32[]{:S(2)}, u32[]{:S(2)}) collective-permute-start(bf16[1,272,128]{2,1,0:T(8,128)(2,1)S(1)} %pack.1.refs_0_), channel_id=1, source_target_pairs={{0,12},{1,13},{2,14},{3,15},{4,8},{5,9},{6,10},{7,11},{8,4},{9,5},... | collective-permute-start | bytes 208904 | tf_op jit(solution)/shard_map/ppermute | solution.py:244
  7.0 0.0 collective-permute-start.2
  7.0 0.6 %collective-permute-start.1 = (bf16[1,272,128]{2,1,0:T(8,128)(2,1)S(1)}, bf16[1,272,128]{2,1,0:T(8,128)(2,1)S(1)}, u32[]{:S(2)}, u32[]{:S(2)}) collective-permute-start(bf16[1,272,128]{2,1,0:T(8,128)(2,1)S(1)} %pack.1.refs_0_), channel_id=1, source_target_pairs={{0,4},{1,5},{2,6},{3,7},{4,0},{5,1},{6,2},{7,3},{8,12},{9,13},{10,... | collective-permute-start | bytes 208904 | tf_op jit(solution)/shard_map/ppermute | solution.py:244
  7.6 1.7 %collective-permute-start = (bf16[1,272,128]{2,1,0:T(8,128)(2,1)S(1)}, bf16[1,272,128]{2,1,0:T(8,128)(2,1)S(1)}, u32[]{:S(2)}, u32[]{:S(2)}) collective-permute-start(bf16[1,272,128]{2,1,0:T(8,128)(2,1)S(1)} %pack.1.refs_0_), channel_id=1, source_target_pairs={{0,2},{1,3},{2,0},{3,1},{4,6},{5,7},{6,4},{7,5},{8,10},{9,11},{10,... | collective-permute-start | bytes 208904 | tf_op jit(solution)/shard_map/ppermute | solution.py:244
  9.3 0.0 copy-start.6
  9.3 0.0 copy-done
  9.3 0.7 %copy-done.6 = f32[2,64]{1,0:T(2,128)S(1)} copy-done((f32[2,64]{1,0:T(2,128)S(1)}, f32[2,64]{1,0:T(2,128)}, u32[]{:S(2)}) %copy-start.6) | copy-done | bytes 536
  9.9 0.0 copy-done.5
  10.0 0.0 copy-start.1
  10.0 0.8 %copy-done.1 = bf16[2,128,128]{2,1,0:T(8,128)(2,1)S(1)} copy-done((bf16[2,128,128]{2,1,0:T(8,128)(2,1)S(1)}, bf16[2,128,128]{2,1,0:T(8,128)(2,1)}, u32[]{:S(2)}) %copy-start.1) | copy-done | bytes 65560
  10.8 0.0 copy-start.3
  10.8 0.8 %copy-done.3 = bf16[2,64,128]{2,1,0:T(8,128)(2,1)S(1)} copy-done((bf16[2,64,128]{2,1,0:T(8,128)(2,1)S(1)}, bf16[2,64,128]{2,1,0:T(8,128)(2,1)}, u32[]{:S(2)}) %copy-start.3) | copy-done | bytes 32792
  11.6 0.2 prepare.1
  11.8 0.0 collective-permute-done.3.refs_4_.refs_1_
  11.8 1.1 %collective-permute-done.2.refs_3_.refs_2_ = bf16[1,272,128]{2,1,0:T(8,128)(2,1)S(1)} collective-permute-done((bf16[1,272,128]{2,1,0:T(8,128)(2,1)S(1)}, bf16[1,272,128]{2,1,0:T(8,128)(2,1)S(1)}, u32[]{:S(2)}, u32[]{:S(2)}) %collective-permute-start.2) | collective-permute-done | bytes 69664 | tf_op jit(solution)/shard_map/ppermute | solution.py:244
  12.9 0.0 collective-permute-done.1.refs_2_.refs_3_
  12.9 0.0 collective-permute-done.refs_1_.refs_4_
  12.9 1.5 %collective-permute-start.4 = (bf16[1,272,128]{2,1,0:T(8,128)(2,1)S(1)}, bf16[1,272,128]{2,1,0:T(8,128)(2,1)S(1)}, u32[]{:S(2)}, u32[]{:S(2)}) collective-permute-start(bf16[1,272,128]{2,1,0:T(8,128)(2,1)S(1)} %collective-permute-done.3.refs_4_.refs_1_), channel_id=1, source_target_pairs={{0,2},{1,3},{2,0},{3,1},{4,6},{5,7},{6,4},{7,5},{8,10},{9,11},{10,... | collective-permute-start | bytes 208904 | tf_op jit(solution)/shard_map/ppermute | solution.py:244
  14.4 0.6 %collective-permute-start.5 = (bf16[1,272,128]{2,1,0:T(8,128)(2,1)S(1)}, bf16[1,272,128]{2,1,0:T(8,128)(2,1)S(1)}, u32[]{:S(2)}, u32[]{:S(2)}) collective-permute-start(bf16[1,272,128]{2,1,0:T(8,128)(2,1)S(1)} %collective-permute-done.2.refs_3_.refs_2_), channel_id=1, source_target_pairs={{0,2},{1,3},{2,0},{3,1},{4,6},{5,7},{6,4},{7,5},{8,10},{9,11},{10,... | collective-permute-start | bytes 208904 | tf_op jit(solution)/shard_map/ppermute | solution.py:244
  15.0 1.1 %collective-permute-start.6 = (bf16[1,272,128]{2,1,0:T(8,128)(2,1)S(1)}, bf16[1,272,128]{2,1,0:T(8,128)(2,1)S(1)}, u32[]{:S(2)}, u32[]{:S(2)}) collective-permute-start(bf16[1,272,128]{2,1,0:T(8,128)(2,1)S(1)} %collective-permute-done.refs_1_.refs_4_), channel_id=1, source_target_pairs={{0,4},{1,5},{2,6},{3,7},{4,0},{5,1},{6,2},{7,3},{8,12},{9,13},{10,... | collective-permute-start | bytes 208904 | tf_op jit(solution)/shard_map/ppermute | solution.py:244
  16.1 0.5 %early.1 = (f32[5,2,64,128]{3,2,1,0:T(8,128)S(1)}, f32[5,2,64,128]{3,2,1,0:T(8,128)S(1)}, bf16[5,2,128,128]{3,2,1,0:T(8,128)(2,1)S(1)}) custom-call(bf16[1,272,128]{2,1,0:T(8,128)(2,1)S(1)} %pack.1.refs_0_, bf16[1,272,128]{2,1,0:T(8,128)(2,1)S(1)} %collective-permute-done.refs_1_.refs_4_, bf16[1,272,128]{2,1,0:T(8,128)(2,1)S(1)} %collective-permute-done.1.refs_2_.refs_3_, ...), custom_call_target="tpu_custom_call" | custom-call | tf_op jit(solution)/shard_map/early/pallas_call | solution.py:290
  16.6 1.2 %collective-permute-done.4.refs_5_ = bf16[1,272,128]{2,1,0:T(8,128)(2,1)S(1)} collective-permute-done((bf16[1,272,128]{2,1,0:T(8,128)(2,1)S(1)}, bf16[1,272,128]{2,1,0:T(8,128)(2,1)S(1)}, u32[]{:S(2)}, u32[]{:S(2)}) %collective-permute-start.4) | collective-permute-done | bytes 69664 | tf_op jit(solution)/shard_map/ppermute | solution.py:244
  17.8 1.0 %collective-permute-done.5.refs_6_ = bf16[1,272,128]{2,1,0:T(8,128)(2,1)S(1)} collective-permute-done((bf16[1,272,128]{2,1,0:T(8,128)(2,1)S(1)}, bf16[1,272,128]{2,1,0:T(8,128)(2,1)S(1)}, u32[]{:S(2)}, u32[]{:S(2)}) %collective-permute-start.5) | collective-permute-done | bytes 69664 | tf_op jit(solution)/shard_map/ppermute | solution.py:244
  18.8 0.6 %collective-permute-done.6.refs_7_ = bf16[1,272,128]{2,1,0:T(8,128)(2,1)S(1)} collective-permute-done((bf16[1,272,128]{2,1,0:T(8,128)(2,1)S(1)}, bf16[1,272,128]{2,1,0:T(8,128)(2,1)S(1)}, u32[]{:S(2)}, u32[]{:S(2)}) %collective-permute-start.6) | collective-permute-done | bytes 69664 | tf_op jit(solution)/shard_map/ppermute | solution.py:244
  19.4 0.1 collective-permute-start.7
  19.5 1.9 %collective-permute-done.7.refs_8_ = bf16[8,272,128]{2,1,0:T(8,128)(2,1)S(1)} collective-permute-done((bf16[8,272,128]{2,1,0:T(8,128)(2,1)S(1)}, bf16[8,272,128]{2,1,0:T(8,128)(2,1)S(1)}, u32[]{:S(2)}, u32[]{:S(2)}) %collective-permute-start.7) | collective-permute-done | bytes 557088 | tf_op jit(solution)/shard_map/ppermute | solution.py:244
  21.4 7.5 %both.1 = bf16[256,128]{1,0:T(8,128)(2,1)} custom-call(s32[1]{0:T(128)} %bitcast.me_ref, bf16[1,272,128]{2,1,0:T(8,128)(2,1)S(1)} %pack.1.refs_0_, bf16[1,272,128]{2,1,0:T(8,128)(2,1)S(1)} %collective-permute-done.3.refs_4_.refs_1_, bf16[1,272,128]{2,1,0:T(8,128)(2,1)S(1)} %collective-permute-done.2.refs_3_.refs_2_, ...), custom_call_target="tpu_custom_call" | custom-call | tf_op jit(solution)/shard_map/both/pallas_call | solution.py:308
  (10 shorter events, 0.1 us)
Async XLA Ops:
  0.0 0.8 %copy-start.2 = (bf16[4,64,128]{2,1,0:T(8,128)(2,1)S(1)}, bf16[4,64,128]{2,1,0:T(8,128)(2,1)}, u32[]{:S(2)}) copy-start(bf16[4,64,128]{2,1,0:T(8,128)(2,1)} %pair_ref.1) | copy-start | bytes 196612
  0.8 0.7 %copy-start.4 = (s32[4,64]{1,0:T(4,128)S(1)}, s32[4,64]{1,0:T(4,128)}, u32[]{:S(2)}) copy-start(s32[4,64]{1,0:T(4,128)} %mask_ref.1) | copy-start | bytes 3076
  1.5 7.7 %copy-start = (bf16[2,128,256]{2,1,0:T(8,128)(2,1)S(1)}, bf16[2,128,256]{2,1,0:T(8,128)(2,1)}, u32[]{:S(2)}) copy-start(bf16[2,128,256]{2,1,0:T(8,128)(2,1)} %proj_ref.1) | copy-start | bytes 393220
  1.8 9.9 %collective-permute-start.3 = (bf16[1,272,128]{2,1,0:T(8,128)(2,1)S(1)}, bf16[1,272,128]{2,1,0:T(8,128)(2,1)S(1)}, u32[]{:S(2)}, u32[]{:S(2)}) collective-permute-start(bf16[1,272,128]{2,1,0:T(8,128)(2,1)S(1)} %pack.1.refs_0_), channel_id=1, source_target_pairs={{0,12},{1,13},{2,14},{3,15},{4,8},{5,9},{6,10},{7,11},{8,4},{9,5},... | collective-permute-start | bytes 208904 | tf_op jit(solution)/shard_map/ppermute | solution.py:244
  7.0 5.9 %collective-permute-start.2 = (bf16[1,272,128]{2,1,0:T(8,128)(2,1)S(1)}, bf16[1,272,128]{2,1,0:T(8,128)(2,1)S(1)}, u32[]{:S(2)}, u32[]{:S(2)}) collective-permute-start(bf16[1,272,128]{2,1,0:T(8,128)(2,1)S(1)} %pack.1.refs_0_), channel_id=1, source_target_pairs={{0,8},{1,9},{2,10},{3,11},{4,12},{5,13},{6,14},{7,15},{8,0},{9,1},... | collective-permute-start | bytes 208904 | tf_op jit(solution)/shard_map/ppermute | solution.py:244
  7.0 5.9 %collective-permute-start.1 = (bf16[1,272,128]{2,1,0:T(8,128)(2,1)S(1)}, bf16[1,272,128]{2,1,0:T(8,128)(2,1)S(1)}, u32[]{:S(2)}, u32[]{:S(2)}) collective-permute-start(bf16[1,272,128]{2,1,0:T(8,128)(2,1)S(1)} %pack.1.refs_0_), channel_id=1, source_target_pairs={{0,4},{1,5},{2,6},{3,7},{4,0},{5,1},{6,2},{7,3},{8,12},{9,13},{10,... | collective-permute-start | bytes 208904 | tf_op jit(solution)/shard_map/ppermute | solution.py:244
  7.6 5.3 %collective-permute-start = (bf16[1,272,128]{2,1,0:T(8,128)(2,1)S(1)}, bf16[1,272,128]{2,1,0:T(8,128)(2,1)S(1)}, u32[]{:S(2)}, u32[]{:S(2)}) collective-permute-start(bf16[1,272,128]{2,1,0:T(8,128)(2,1)S(1)} %pack.1.refs_0_), channel_id=1, source_target_pairs={{0,2},{1,3},{2,0},{3,1},{4,6},{5,7},{6,4},{7,5},{8,10},{9,11},{10,... | collective-permute-start | bytes 208904 | tf_op jit(solution)/shard_map/ppermute | solution.py:244
  9.3 0.7 %copy-start.6 = (f32[2,64]{1,0:T(2,128)S(1)}, f32[2,64]{1,0:T(2,128)}, u32[]{:S(2)}) copy-start(f32[2,64]{1,0:T(2,128)} %mid_ref.1) | copy-start | bytes 1540
  9.3 0.7 %copy-start.5 = (f32[2,128]{1,0:T(2,128)S(1)}, f32[2,128]{1,0:T(2,128)}, u32[]{:S(2)}) copy-start(f32[2,128]{1,0:T(2,128)} %gain_ref.1) | copy-start | bytes 3076
  10.0 0.8 %copy-start.1 = (bf16[2,128,128]{2,1,0:T(8,128)(2,1)S(1)}, bf16[2,128,128]{2,1,0:T(8,128)(2,1)}, u32[]{:S(2)}) copy-start(bf16[2,128,128]{2,1,0:T(8,128)(2,1)} %gate_ref.1) | copy-start | bytes 196612
  10.8 0.8 %copy-start.3 = (bf16[2,64,128]{2,1,0:T(8,128)(2,1)S(1)}, bf16[2,64,128]{2,1,0:T(8,128)(2,1)}, u32[]{:S(2)}) copy-start(bf16[2,64,128]{2,1,0:T(8,128)(2,1)} %out_ref.1) | copy-start | bytes 98308
  12.9 4.9 %collective-permute-start.4 = (bf16[1,272,128]{2,1,0:T(8,128)(2,1)S(1)}, bf16[1,272,128]{2,1,0:T(8,128)(2,1)S(1)}, u32[]{:S(2)}, u32[]{:S(2)}) collective-permute-start(bf16[1,272,128]{2,1,0:T(8,128)(2,1)S(1)} %collective-permute-done.3.refs_4_.refs_1_), channel_id=1, source_target_pairs={{0,2},{1,3},{2,0},{3,1},{4,6},{5,7},{6,4},{7,5},{8,10},{9,11},{10,... | collective-permute-start | bytes 208904 | tf_op jit(solution)/shard_map/ppermute | solution.py:244
  14.4 4.4 %collective-permute-start.5 = (bf16[1,272,128]{2,1,0:T(8,128)(2,1)S(1)}, bf16[1,272,128]{2,1,0:T(8,128)(2,1)S(1)}, u32[]{:S(2)}, u32[]{:S(2)}) collective-permute-start(bf16[1,272,128]{2,1,0:T(8,128)(2,1)S(1)} %collective-permute-done.2.refs_3_.refs_2_), channel_id=1, source_target_pairs={{0,2},{1,3},{2,0},{3,1},{4,6},{5,7},{6,4},{7,5},{8,10},{9,11},{10,... | collective-permute-start | bytes 208904 | tf_op jit(solution)/shard_map/ppermute | solution.py:244
  15.0 4.4 %collective-permute-start.6 = (bf16[1,272,128]{2,1,0:T(8,128)(2,1)S(1)}, bf16[1,272,128]{2,1,0:T(8,128)(2,1)S(1)}, u32[]{:S(2)}, u32[]{:S(2)}) collective-permute-start(bf16[1,272,128]{2,1,0:T(8,128)(2,1)S(1)} %collective-permute-done.refs_1_.refs_4_), channel_id=1, source_target_pairs={{0,4},{1,5},{2,6},{3,7},{4,0},{5,1},{6,2},{7,3},{8,12},{9,13},{10,... | collective-permute-start | bytes 208904 | tf_op jit(solution)/shard_map/ppermute | solution.py:244
  19.4 2.0 %collective-permute-start.7 = (bf16[8,272,128]{2,1,0:T(8,128)(2,1)S(1)}, bf16[8,272,128]{2,1,0:T(8,128)(2,1)S(1)}, u32[]{:S(2)}, u32[]{:S(2)}) collective-permute-start(bf16[8,272,128]{2,1,0:T(8,128)(2,1)S(1)} %constant_dynamic-update-slice_fusion), channel_id=1, source_target_pairs={{0,1},{1,0},{2,3},{3,2},{4,5},{5,4},{6,7},{7,6},{8,9},{9,8},{10,11... | collective-permute-start | bytes 1671176 | tf_op jit(solution)/shard_map/ppermute | solution.py:244

commit v10 on v9

--- a/solution.py
+++ b/solution.py
@@ -26,8 +26,8 @@
     return lax.dot_general(a, b, NT, preferred_element_type=F32)
 
 
-def sigmoid(x):
-    return 0.5 * jnp.tanh(0.5 * x) + 0.5
+def twice_sigmoid(half):
+    return jnp.tanh(half) + 1.0
 
 
 def iota(shape, axis):
@@ -50,10 +50,10 @@
     return (centred * lax.rsqrt(variance + EPS) * gain).astype(BF16)
 
 
-def factors(projected, mask):
+def factors(projected, half_mask):
     hw = projected.shape[0] // 4
-    left = mask * sigmoid(projected[hw : 2 * hw]) * projected[:hw]
-    right = mask * sigmoid(projected[3 * hw :]) * projected[2 * hw : 3 * hw]
+    left = half_mask * twice_sigmoid(projected[hw : 2 * hw]) * projected[:hw]
+    right = half_mask * twice_sigmoid(projected[3 * hw :]) * projected[2 * hw : 3 * hw]
     return left, right
 
 
@@ -71,7 +71,7 @@
     by_lane = one_hot(token_of(iota(square, 0), rows, tokens) == iota(square, 1))
     by_token = one_hot(token_of(iota(square, 1), rows, tokens) == iota(square, 0))
     identity = one_hot(iota((channels, channels), 0) == iota((channels, channels), 1))
-    masks = dot(one_hot(mask_ref[...] != 0), by_token)
+    masks = 0.5 * dot(one_hot(mask_ref[...] != 0), by_token)
     tiles = rows * tokens // LANES
     for h in range(tiles):
         pair = [dot(by_lane, pair_ref[i]).astype(BF16) for i in (2 * h, 2 * h + 1)]
@@ -102,15 +102,18 @@
     devices = tokens // rows
 
     def flipped(weight):
-        return weight.astype(F32).T.astype(BF16)
+        return weight.astype(F32).T
 
     def column(line):
         return jnp.broadcast_to(line, (LANES, line.shape[1])).T
 
+    hw = mid_ref.shape[1]
+    is_gate = iota((4 * hw, proj_ref.shape[1]), 0) // hw % 2 == 1
     for o in range(2):
-        proj_t_ref[o] = flipped(proj_ref[o])
-        gate_t_ref[o] = flipped(gate_ref[o])
-        out_t_ref[o] = flipped(out_ref[o])
+        proj = flipped(proj_ref[o])
+        proj_t_ref[o] = jnp.where(is_gate, 0.5 * proj, proj).astype(BF16)
+        gate_t_ref[o] = (0.5 * flipped(gate_ref[o])).astype(BF16)
+        out_t_ref[o] = (0.5 * flipped(out_ref[o])).astype(BF16)
         gain_t_ref[o] = column(gain_ref[o : o + 1, :])
         mid_t_ref[o] = column(mid_ref[o : o + 1, :])
     shape = (LANES, LANES)
@@ -141,13 +144,18 @@
             place += 1
 
 
-def both_kernel(rows, tokens, sources, early, me_ref, *refs):
+def both_kernel(rows, tokens, sources, early_groups, me_ref, *refs):
     devices = tokens // rows
     block_refs, refs = refs[: len(sources)], refs[len(sources) :]
+    weight_refs, refs = refs[:7], refs[7:]
+    proj_ref, gate_ref, out_ref, gain_ref, mid_ref, restore_ref, spread_ref = weight_refs
+    ahead = {}
+    for group in early_groups:
+        for n, m in enumerate(group):
+            ahead[m] = refs[:3] + (n,)
+        refs = refs[3:]
     (
-        proj_ref, gate_ref, out_ref, gain_ref, mid_ref, restore_ref, spread_ref,
-        early_left_ref, early_right_ref, early_normed_ref, result_ref,
-        left_s, right_s, normed_s, sum_s, now_s, second_left_s, second_right_s,
+        result_ref, left_s, right_s, normed_s, sum_s, now_s, second_left_s, second_right_s,
     ) = refs
     channels = gate_ref.shape[1]
     hw = mid_ref.shape[1]
@@ -155,7 +163,7 @@
     me = me_ref[0]
 
     where = {m: (ref, k) for ref, held in zip(block_refs, sources) for k, m in enumerate(held)}
-    later = [m for m in range(devices) if m not in early]
+    later = [m for m in range(devices) if m not in ahead]
 
     def place(m, h, left, right):
         here = pl.ds(pl.multiple_of((me ^ m) * hw, hw), hw)
@@ -169,13 +177,18 @@
         for h in range(tiles):
             normed_s[later.index(m), h] = normed[h]
             place(m, h, *factors(tile(projected, h), mask_of(ref, channels, k, h)))
-    for n, m in enumerate(early):
-        for h in range(tiles):
-            place(m, h, early_left_ref[n, h], early_right_ref[n, h])
+    for m, (left_ref, right_ref, _, n) in ahead.items():
+        for h in range(tiles):
+            place(m, h, left_ref[n, h], right_ref[n, h])
+
+    def normed_of(m, h):
+        if m in ahead:
+            return ahead[m][2][ahead[m][3], h]
+        return normed_s[later.index(m), h]
 
     low = iota((devices, LANES), 1) < tokens
 
-    def channel_sum(c, _):
+    def channel_sum(c):
         here = pl.ds(c, devices, stride=hw)
         left = jnp.concatenate([left_s[h, here, :] for h in range(tiles)], axis=0)
         halves = [[], []]
@@ -187,11 +200,11 @@
                 halves[0].append(jnp.where(low, straight, 0.0))
                 halves[1].append(jnp.where(low, 0.0, other))
         against = jnp.concatenate(halves[0] + halves[1], axis=0).astype(BF16)
-        here = pl.ds(pl.multiple_of(c * tiles * devices, tiles * devices), tiles * devices)
+        here = pl.ds(c * tiles * devices, tiles * devices)
         sum_s[here, :] = dot_nt(left.astype(BF16), against)
-        return 0
-
-    lax.fori_loop(0, hw, channel_sum, 0, unroll=16)
+
+    for c in range(hw):
+        channel_sum(c)
 
     for m in range(devices):
         ref, k = where[m]
@@ -199,12 +212,12 @@
         for h in range(tiles):
             summed = sum_s[pl.ds(h * devices + (me ^ m), hw, stride=tiles * devices), :]
             hidden.append(column_norm(summed, mid_ref[0]))
-            first.append(early_normed_ref[early.index(m), h] if m in early else normed_s[later.index(m), h])
+            first.append(normed_of(m, h))
         update = dot(out_ref[0], side_by_side(hidden))
         logits = dot(gate_ref[0], side_by_side(first))
         normed = []
         for h in range(tiles):
-            gated = sigmoid(tile(logits, h)) * tile(update, h)
+            gated = twice_sigmoid(tile(logits, h)) * tile(update, h)
             now = (chunk_of(ref, channels, k, h) + gated).astype(BF16)
             normed.append(column_norm(now.astype(F32), gain_ref[1]))
             if m == 0:
@@ -234,7 +247,7 @@
     for h in range(tiles):
         summed = jnp.where(low, sums[2 * h], sums[2 * h + 1])
         update = dot(out_ref[1], column_norm(summed, mid_ref[1]))
-        gating = sigmoid(dot(gate_ref[1], now_s[tiles + h]))
+        gating = twice_sigmoid(dot(gate_ref[1], now_s[tiles + h]))
         final = (now_s[h].astype(F32) + gating * update).astype(BF16)
         result_ref[h * LANES : (h + 1) * LANES, :] = dot_nt(restore_ref[...], final).astype(BF16)
 
@@ -252,7 +265,6 @@
         functools.partial(pack_kernel, rows, tokens),
         out_shape=VMEM((1, tiles * channels + MASK_ROWS, LANES), BF16),
         out_specs=IN_VMEM,
-        compiler_params=SMALL,
         name="pack",
     )(pair, mask)
     me = lax.axis_index("row").reshape(1).astype(jnp.int32)
@@ -269,50 +281,57 @@
             VMEM((rows, LANES, LANES), BF16),
         ),
         out_specs=(IN_VMEM,) * 7,
-        compiler_params=SMALL,
         name="prepare",
     )(me, proj, gate, out, gain, mid)
 
     def swapped(group):
         return exchange(jnp.concatenate([held[m] for m in group]), 1, devices)
 
+    def project_early(blocks):
+        count = sum(block.shape[0] for block in blocks)
+        return pl.pallas_call(
+            functools.partial(early_kernel, [block.shape[0] for block in blocks]),
+            in_specs=[IN_VMEM] * (len(blocks) + 2),
+            out_shape=(
+                VMEM((count, tiles, hw, LANES), F32),
+                VMEM((count, tiles, hw, LANES), F32),
+                VMEM((count, tiles, channels, LANES), BF16),
+            ),
+            out_specs=(IN_VMEM,) * 3,
+            compiler_params=SMALL,
+            name="early",
+        )(*blocks, weights[0], weights[3])
+
     held = {0: packed}
-    for m in (12, 8, 4, 2):
+    for m in (12, 8, 6, 4, 2):
         held[m] = exchange(packed, m, devices)
-    held[2], held[4], held[8], held[12], weights = lax.optimization_barrier(
-        (held[2], held[4], held[8], held[12], weights)
+    near = (2, 4, 6, 8, 12)
+    *blocks, weights = lax.optimization_barrier([held[m] for m in near] + [weights])
+    held.update(zip(near, blocks))
+    for m in (12, 8):
+        held[m ^ 2] = exchange(held[m], 2, devices)
+    first = (0, 12, 8, 4, 2, 6)
+    last = (14, 10)
+    swaps = [swapped(first)]
+    ahead = project_early([held[m] for m in first])
+    swaps[0], ahead = lax.optimization_barrier((swaps[0], ahead))
+    again = project_early(swaps)
+    held[14], held[10], ahead, again = lax.optimization_barrier(
+        (held[14], held[10], ahead, again)
     )
-    held[14] = exchange(held[12], 2, devices)
-    held[10] = exchange(held[8], 2, devices)
-    held[6] = exchange(held[2], 4, devices)
-    early = (0, 2, 4, 8, 12)
-    count = len(early)
-    ahead = pl.pallas_call(
-        functools.partial(early_kernel, (1,) * 5),
-        in_specs=[IN_VMEM] * 7,
-        out_shape=(
-            VMEM((count, tiles, hw, LANES), F32),
-            VMEM((count, tiles, hw, LANES), F32),
-            VMEM((count, tiles, channels, LANES), BF16),
-        ),
-        out_specs=(IN_VMEM,) * 3,
-        compiler_params=SMALL,
-        name="early",
-    )(*[held[m] for m in (0, 2, 4, 8, 12)], weights[0], weights[3])
-    held[14], held[10], held[6], ahead = lax.optimization_barrier(
-        (held[14], held[10], held[6], ahead)
-    )
-    group = (0, 12, 8, 4, 2, 14, 10, 6)
-    arrays = [held[m] for m in group] + [swapped(group)]
-    sources = [(m,) for m in group] + [tuple(m ^ 1 for m in group)]
+    swaps.append(swapped(last))
+    arrays = [held[m] for m in first + last] + swaps
+    sources = [(m,) for m in first + last]
+    sources += [tuple(m ^ 1 for m in group) for group in (first, last)]
+    early_groups = (first, sources[-2])
     result = pl.pallas_call(
-        functools.partial(both_kernel, rows, tokens, sources, early),
+        functools.partial(both_kernel, rows, tokens, sources, early_groups),
         out_shape=jax.ShapeDtypeStruct((size, channels), BF16),
-        in_specs=[IN_SMEM] + [IN_VMEM] * (len(arrays) + 10),
+        in_specs=[IN_SMEM] + [IN_VMEM] * (len(arrays) + len(weights) + len(ahead) + len(again)),
         scratch_shapes=[
             pltpu.VMEM((tiles, devices * hw, LANES), F32),
             pltpu.VMEM((tiles, devices * hw, LANES), F32),
-            pltpu.VMEM((devices - count, tiles, channels, LANES), BF16),
+            pltpu.VMEM((2 * len(last), tiles, channels, LANES), BF16),
             pltpu.VMEM((hw * devices * tiles, LANES), F32),
             pltpu.VMEM((2 * tiles, channels, LANES), BF16),
             pltpu.VMEM((devices * tiles * hw, LANES), BF16),
@@ -320,7 +339,7 @@
         ],
         compiler_params=pltpu.CompilerParams(vmem_limit_bytes=24 * 1024 * 1024),
         name="both",
-    )(me, *arrays, *weights, *ahead)
+    )(me, *arrays, *weights, *ahead, *again)
     return result.reshape(pair.shape)
 
 

time: 29.2 us -> 28.4 us (0.973)
  local copies, waits for them, and re-layouts: 3.91 us -> 0.08 us
  Pallas kernels: 8.45 us -> 9.96 us
  waiting for transfers between devices: 5.81 us -> 7.22 us
    unnamed x21 -> x5, local copies, waits for them, and re-layouts: 3.9 us -> 0.06 us
    ppermute x8 -> x9, waiting for transfers between devices: 5.81 us -> 7.22 us  [exchange(): return lax.ppermute(block, 'row', pairs)]
    pallas_call x1, Pallas kernels: 0.2 us -> 1.17 us  [small_plan(): pl.pallas_call(functools.partial(prepare_kernel, rows, tokens), in_specs=...]
    pallas_call x1, Pallas kernels: 0.31 us -> 1.15 us  [small_plan(): pl.pallas_call(functools.partial(pack_kernel, rows, tokens), out_shape=VM...]
    pallas_call x1, Pallas kernels: 7.48 us -> 6.66 us  [small_plan(): pl.pallas_call(functools.partial(both_kernel, rows, tokens, sources, earl...]
    pallas_call x1 -> x2, Pallas kernels: 0.45 us -> 0.99 us  [project_early(): pl.pallas_call(functools.partial(early_kernel, [block.shape[0] for block...]
    ppermute x8 -> x9, starting transfers between devices: 10.7 us -> 10.8 us  [exchange(): return lax.ppermute(block, 'row', pairs)]
  transfers between devices with their start and end apart: 8 -> 9, of which waited for: 5 -> 6; matrix products, arithmetic and copies ran while one was open for 0% -> 0% of each run, Pallas kernels for 2% -> 8%
where the time goes in v10:
time: 28.4 us; the launch traced here: 28.2 us
  starting transfers between devices  10.8 us (38%)
  Pallas kernels  9.96 us (35%)
  waiting for transfers between devices  7.22 us (25%)
    ppermute x9, starting transfers between devices, exchange(): return lax.ppermute(block, 'row', pairs)  10.8 us
    ppermute x9, waiting for transfers between devices, exchange(): return lax.ppermute(block, 'row', pairs)  7.22 us
    pallas_call x1, Pallas kernels, small_plan(): pl.pallas_call(functools.partial(both_kernel, rows, tokens, sources, earl...  6.66 us
    pallas_call x1, Pallas kernels, small_plan(): pl.pallas_call(functools.partial(prepare_kernel, rows, tokens), in_specs=...  1.17 us
    pallas_call x1, Pallas kernels, small_plan(): pl.pallas_call(functools.partial(pack_kernel, rows, tokens), out_shape=VM...  1.15 us
    pallas_call x2, Pallas kernels, project_early(): pl.pallas_call(functools.partial(early_kernel, [block.shape[0] for block...  0.99 us
  transfers between devices with their start and end apart: 9, of which 6 were waited for; matrix products, arithmetic and copies ran while one was open for 0% of the time, Pallas kernels for 8%

profile of v10, /device:TPU:0, one launch (start us, length us, event | category | flops | bytes accessed | tf_op | source)
XLA Modules:
  0.0 28.2 jit_solution(9632362733005446972)
XLA Ops:
  0.0 1.2 %pack.1.refs_0_ = bf16[1,272,128]{2,1,0:T(8,128)(2,1)S(1)} custom-call(bf16[4,64,128]{2,1,0:T(8,128)(2,1)} %pair_ref.1, s32[4,64]{1,0:T(4,128)} %mask_ref.1), custom_call_target="tpu_custom_call" | custom-call | tf_op jit(solution)/shard_map/pack/pallas_call | solution.py:264
  1.2 5.1 %collective-permute-start.4 = (bf16[1,272,128]{2,1,0:T(8,128)(2,1)S(1)}, bf16[1,272,128]{2,1,0:T(8,128)(2,1)S(1)}, u32[]{:S(2)}, u32[]{:S(2)}) collective-permute-start(bf16[1,272,128]{2,1,0:T(8,128)(2,1)S(1)} %pack.1.refs_0_), channel_id=1, source_target_pairs={{0,12},{1,13},{2,14},{3,15},{4,8},{5,9},{6,10},{7,11},{8,4},{9,5},... | collective-permute-start | bytes 208904 | tf_op jit(solution)/shard_map/ppermute | solution.py:257
  6.3 0.0 collective-permute-start.3
  6.3 1.7 %collective-permute-start.2 = (bf16[1,272,128]{2,1,0:T(8,128)(2,1)S(1)}, bf16[1,272,128]{2,1,0:T(8,128)(2,1)S(1)}, u32[]{:S(2)}, u32[]{:S(2)}) collective-permute-start(bf16[1,272,128]{2,1,0:T(8,128)(2,1)S(1)} %pack.1.refs_0_), channel_id=1, source_target_pairs={{0,6},{1,7},{2,4},{3,5},{4,2},{5,3},{6,0},{7,1},{8,14},{9,15},{10,... | collective-permute-start | bytes 208904 | tf_op jit(solution)/shard_map/ppermute | solution.py:257
  8.0 1.2 %collective-permute-start.1 = (bf16[1,272,128]{2,1,0:T(8,128)(2,1)S(1)}, bf16[1,272,128]{2,1,0:T(8,128)(2,1)S(1)}, u32[]{:S(2)}, u32[]{:S(2)}) collective-permute-start(bf16[1,272,128]{2,1,0:T(8,128)(2,1)S(1)} %pack.1.refs_0_), channel_id=1, source_target_pairs={{0,4},{1,5},{2,6},{3,7},{4,0},{5,1},{6,2},{7,3},{8,12},{9,13},{10,... | collective-permute-start | bytes 208904 | tf_op jit(solution)/shard_map/ppermute | solution.py:257
  9.3 0.5 %collective-permute-start = (bf16[1,272,128]{2,1,0:T(8,128)(2,1)S(1)}, bf16[1,272,128]{2,1,0:T(8,128)(2,1)S(1)}, u32[]{:S(2)}, u32[]{:S(2)}) collective-permute-start(bf16[1,272,128]{2,1,0:T(8,128)(2,1)S(1)} %pack.1.refs_0_), channel_id=1, source_target_pairs={{0,2},{1,3},{2,0},{3,1},{4,6},{5,7},{6,4},{7,5},{8,10},{9,11},{10,... | collective-permute-start | bytes 208904 | tf_op jit(solution)/shard_map/ppermute | solution.py:257
  9.8 1.2 %prepare.1 = (bf16[2,256,128]{2,1,0:T(8,128)(2,1)S(1)}, bf16[2,128,128]{2,1,0:T(8,128)(2,1)S(1)}, bf16[2,128,64]{2,1,0:T(8,128)(2,1)S(1)}, f32[2,128,128]{2,1,0:...) custom-call(s32[1]{0:T(128)} %bitcast.me_ref, ...), custom_call_target="tpu_custom_call" | custom-call | tf_op jit(solution)/shard_map/prepare/pallas_call | solution.py:271
  10.9 0.0 collective-permute-done.4.refs_1_
  11.0 1.3 %collective-permute-done.3.refs_2_ = bf16[1,272,128]{2,1,0:T(8,128)(2,1)S(1)} collective-permute-done((bf16[1,272,128]{2,1,0:T(8,128)(2,1)S(1)}, bf16[1,272,128]{2,1,0:T(8,128)(2,1)S(1)}, u32[]{:S(2)}, u32[]{:S(2)}) %collective-permute-start.3) | collective-permute-done | bytes 69664 | tf_op jit(solution)/shard_map/ppermute | solution.py:257
  12.3 1.3 %collective-permute-done.2.refs_5_ = bf16[1,272,128]{2,1,0:T(8,128)(2,1)S(1)} collective-permute-done((bf16[1,272,128]{2,1,0:T(8,128)(2,1)S(1)}, bf16[1,272,128]{2,1,0:T(8,128)(2,1)S(1)}, u32[]{:S(2)}, u32[]{:S(2)}) %collective-permute-start.2) | collective-permute-done | bytes 69664 | tf_op jit(solution)/shard_map/ppermute | solution.py:257
  13.6 0.2 collective-permute-done.1.refs_3_
  13.8 0.0 collective-permute-done.refs_4_
  13.9 0.1 collective-permute-start.7
  14.0 1.0 %collective-permute-start.5 = (bf16[1,272,128]{2,1,0:T(8,128)(2,1)S(1)}, bf16[1,272,128]{2,1,0:T(8,128)(2,1)S(1)}, u32[]{:S(2)}, u32[]{:S(2)}) collective-permute-start(bf16[1,272,128]{2,1,0:T(8,128)(2,1)S(1)} %collective-permute-done.4.refs_1_), channel_id=1, source_target_pairs={{0,2},{1,3},{2,0},{3,1},{4,6},{5,7},{6,4},{7,5},{8,10},{9,11},{10,... | collective-permute-start | bytes 208904 | tf_op jit(solution)/shard_map/ppermute | solution.py:257
  15.1 1.0 %collective-permute-start.6 = (bf16[1,272,128]{2,1,0:T(8,128)(2,1)S(1)}, bf16[1,272,128]{2,1,0:T(8,128)(2,1)S(1)}, u32[]{:S(2)}, u32[]{:S(2)}) collective-permute-start(bf16[1,272,128]{2,1,0:T(8,128)(2,1)S(1)} %collective-permute-done.3.refs_2_), channel_id=1, source_target_pairs={{0,2},{1,3},{2,0},{3,1},{4,6},{5,7},{6,4},{7,5},{8,10},{9,11},{10,... | collective-permute-start | bytes 208904 | tf_op jit(solution)/shard_map/ppermute | solution.py:257
  16.1 0.5 %early.2 = (f32[6,2,64,128]{3,2,1,0:T(8,128)S(1)}, f32[6,2,64,128]{3,2,1,0:T(8,128)S(1)}, bf16[6,2,128,128]{3,2,1,0:T(8,128)(2,1)S(1)}) custom-call(bf16[1,272,128]{2,1,0:T(8,128)(2,1)S(1)} %pack.1.refs_0_, bf16[1,272,128]{2,1,0:T(8,128)(2,1)S(1)} %collective-permute-done.4.refs_1_, bf16[1,272,128]{2,1,0:T(8,128)(2,1)S(1)} %collective-permute-done.3.refs_2_, ...), custom_call_target="tpu_custom_call" | custom-call | tf_op jit(solution)/shard_map/early/pallas_call | solution.py:292
  16.6 0.0 collective-permute-done.7.refs_0_.refs_8_
  16.6 0.5 %early.3 = (f32[6,2,64,128]{3,2,1,0:T(8,128)S(1)}, f32[6,2,64,128]{3,2,1,0:T(8,128)S(1)}, bf16[6,2,128,128]{3,2,1,0:T(8,128)(2,1)S(1)}) custom-call(bf16[6,272,128]{2,1,0:T(8,128)(2,1)S(1)} %collective-permute-done.7.refs_0_.refs_8_, bf16[2,256,128]{2,1,0:T(8,128)(2,1)S(1)} %get-tuple-element.54.refs_6_.refs_1_.refs_10_, ...), custom_call_target="tpu_custom_call" | custom-call | tf_op jit(solution)/shard_map/early/pallas_call | solution.py:292
  17.1 1.9 %collective-permute-done.5.refs_6_ = bf16[1,272,128]{2,1,0:T(8,128)(2,1)S(1)} collective-permute-done((bf16[1,272,128]{2,1,0:T(8,128)(2,1)S(1)}, bf16[1,272,128]{2,1,0:T(8,128)(2,1)S(1)}, u32[]{:S(2)}, u32[]{:S(2)}) %collective-permute-start.5) | collective-permute-done | bytes 69664 | tf_op jit(solution)/shard_map/ppermute | solution.py:257
  19.1 1.0 %collective-permute-done.6.refs_7_ = bf16[1,272,128]{2,1,0:T(8,128)(2,1)S(1)} collective-permute-done((bf16[1,272,128]{2,1,0:T(8,128)(2,1)S(1)}, bf16[1,272,128]{2,1,0:T(8,128)(2,1)S(1)}, u32[]{:S(2)}, u32[]{:S(2)}) %collective-permute-start.6) | collective-permute-done | bytes 69664 | tf_op jit(solution)/shard_map/ppermute | solution.py:257
  20.1 0.1 collective-permute-start.8
  20.2 1.3 %collective-permute-done.8.refs_9_ = bf16[2,272,128]{2,1,0:T(8,128)(2,1)S(1)} collective-permute-done((bf16[2,272,128]{2,1,0:T(8,128)(2,1)S(1)}, bf16[2,272,128]{2,1,0:T(8,128)(2,1)S(1)}, u32[]{:S(2)}, u32[]{:S(2)}) %collective-permute-start.8) | collective-permute-done | bytes 139296 | tf_op jit(solution)/shard_map/ppermute | solution.py:257
  21.6 6.7 %both.1 = bf16[256,128]{1,0:T(8,128)(2,1)} custom-call(s32[1]{0:T(128)} %bitcast.me_ref, bf16[1,272,128]{2,1,0:T(8,128)(2,1)S(1)} %pack.1.refs_0_, bf16[1,272,128]{2,1,0:T(8,128)(2,1)S(1)} %collective-permute-done.4.refs_1_, bf16[1,272,128]{2,1,0:T(8,128)(2,1)S(1)} %collective-permute-done.3.refs_2_, ...), custom_call_target="tpu_custom_call" | custom-call | tf_op jit(solution)/shard_map/both/pallas_call | solution.py:327
  (7 shorter events, 0.1 us)
Async XLA Ops:
  1.2 9.8 %collective-permute-start.4 = (bf16[1,272,128]{2,1,0:T(8,128)(2,1)S(1)}, bf16[1,272,128]{2,1,0:T(8,128)(2,1)S(1)}, u32[]{:S(2)}, u32[]{:S(2)}) collective-permute-start(bf16[1,272,128]{2,1,0:T(8,128)(2,1)S(1)} %pack.1.refs_0_), channel_id=1, source_target_pairs={{0,12},{1,13},{2,14},{3,15},{4,8},{5,9},{6,10},{7,11},{8,4},{9,5},... | collective-permute-start | bytes 208904 | tf_op jit(solution)/shard_map/ppermute | solution.py:257
  6.3 6.0 %collective-permute-start.3 = (bf16[1,272,128]{2,1,0:T(8,128)(2,1)S(1)}, bf16[1,272,128]{2,1,0:T(8,128)(2,1)S(1)}, u32[]{:S(2)}, u32[]{:S(2)}) collective-permute-start(bf16[1,272,128]{2,1,0:T(8,128)(2,1)S(1)} %pack.1.refs_0_), channel_id=1, source_target_pairs={{0,8},{1,9},{2,10},{3,11},{4,12},{5,13},{6,14},{7,15},{8,0},{9,1},... | collective-permute-start | bytes 208904 | tf_op jit(solution)/shard_map/ppermute | solution.py:257
  6.3 7.3 %collective-permute-start.2 = (bf16[1,272,128]{2,1,0:T(8,128)(2,1)S(1)}, bf16[1,272,128]{2,1,0:T(8,128)(2,1)S(1)}, u32[]{:S(2)}, u32[]{:S(2)}) collective-permute-start(bf16[1,272,128]{2,1,0:T(8,128)(2,1)S(1)} %pack.1.refs_0_), channel_id=1, source_target_pairs={{0,6},{1,7},{2,4},{3,5},{4,2},{5,3},{6,0},{7,1},{8,14},{9,15},{10,... | collective-permute-start | bytes 208904 | tf_op jit(solution)/shard_map/ppermute | solution.py:257
  8.0 5.8 %collective-permute-start.1 = (bf16[1,272,128]{2,1,0:T(8,128)(2,1)S(1)}, bf16[1,272,128]{2,1,0:T(8,128)(2,1)S(1)}, u32[]{:S(2)}, u32[]{:S(2)}) collective-permute-start(bf16[1,272,128]{2,1,0:T(8,128)(2,1)S(1)} %pack.1.refs_0_), channel_id=1, source_target_pairs={{0,4},{1,5},{2,6},{3,7},{4,0},{5,1},{6,2},{7,3},{8,12},{9,13},{10,... | collective-permute-start | bytes 208904 | tf_op jit(solution)/shard_map/ppermute | solution.py:257
  9.3 4.6 %collective-permute-start = (bf16[1,272,128]{2,1,0:T(8,128)(2,1)S(1)}, bf16[1,272,128]{2,1,0:T(8,128)(2,1)S(1)}, u32[]{:S(2)}, u32[]{:S(2)}) collective-permute-start(bf16[1,272,128]{2,1,0:T(8,128)(2,1)S(1)} %pack.1.refs_0_), channel_id=1, source_target_pairs={{0,2},{1,3},{2,0},{3,1},{4,6},{5,7},{6,4},{7,5},{8,10},{9,11},{10,... | collective-permute-start | bytes 208904 | tf_op jit(solution)/shard_map/ppermute | solution.py:257
  13.9 2.7 %collective-permute-start.7 = (bf16[6,272,128]{2,1,0:T(8,128)(2,1)S(1)}, bf16[6,272,128]{2,1,0:T(8,128)(2,1)S(1)}, u32[]{:S(2)}, u32[]{:S(2)}) collective-permute-start(bf16[6,272,128]{2,1,0:T(8,128)(2,1)S(1)} %constant_dynamic-update-slice_fusion), channel_id=1, source_target_pairs={{0,1},{1,0},{2,3},{3,2},{4,5},{5,4},{6,7},{7,6},{8,9},{9,8},{10,11... | collective-permute-start | bytes 1253384 | tf_op jit(solution)/shard_map/ppermute | solution.py:257
  14.0 5.0 %collective-permute-start.5 = (bf16[1,272,128]{2,1,0:T(8,128)(2,1)S(1)}, bf16[1,272,128]{2,1,0:T(8,128)(2,1)S(1)}, u32[]{:S(2)}, u32[]{:S(2)}) collective-permute-start(bf16[1,272,128]{2,1,0:T(8,128)(2,1)S(1)} %collective-permute-done.4.refs_1_), channel_id=1, source_target_pairs={{0,2},{1,3},{2,0},{3,1},{4,6},{5,7},{6,4},{7,5},{8,10},{9,11},{10,... | collective-permute-start | bytes 208904 | tf_op jit(solution)/shard_map/ppermute | solution.py:257
  15.1 5.0 %collective-permute-start.6 = (bf16[1,272,128]{2,1,0:T(8,128)(2,1)S(1)}, bf16[1,272,128]{2,1,0:T(8,128)(2,1)S(1)}, u32[]{:S(2)}, u32[]{:S(2)}) collective-permute-start(bf16[1,272,128]{2,1,0:T(8,128)(2,1)S(1)} %collective-permute-done.3.refs_2_), channel_id=1, source_target_pairs={{0,2},{1,3},{2,0},{3,1},{4,6},{5,7},{6,4},{7,5},{8,10},{9,11},{10,... | collective-permute-start | bytes 208904 | tf_op jit(solution)/shard_map/ppermute | solution.py:257
  20.1 1.4 %collective-permute-start.8 = (bf16[2,272,128]{2,1,0:T(8,128)(2,1)S(1)}, bf16[2,272,128]{2,1,0:T(8,128)(2,1)S(1)}, u32[]{:S(2)}, u32[]{:S(2)}) collective-permute-start(bf16[2,272,128]{2,1,0:T(8,128)(2,1)S(1)} %pad_maximum_fusion), channel_id=1, source_target_pairs={{0,1},{1,0},{2,3},{3,2},{4,5},{5,4},{6,7},{7,6},{8,9},{9,8},{10,11... | collective-permute-start | bytes 417800 | tf_op jit(solution)/shard_map/ppermute | solution.py:257

commit v11 on v10

--- a/solution.py
+++ b/solution.py
@@ -303,35 +303,28 @@
         )(*blocks, weights[0], weights[3])
 
     held = {0: packed}
-    for m in (12, 8, 6, 4, 2):
+    for m in (12, 8, 4, 2):
         held[m] = exchange(packed, m, devices)
-    near = (2, 4, 6, 8, 12)
-    *blocks, weights = lax.optimization_barrier([held[m] for m in near] + [weights])
-    held.update(zip(near, blocks))
-    for m in (12, 8):
-        held[m ^ 2] = exchange(held[m], 2, devices)
-    first = (0, 12, 8, 4, 2, 6)
-    last = (14, 10)
-    swaps = [swapped(first)]
-    ahead = project_early([held[m] for m in first])
-    swaps[0], ahead = lax.optimization_barrier((swaps[0], ahead))
-    again = project_early(swaps)
-    held[14], held[10], ahead, again = lax.optimization_barrier(
-        (held[14], held[10], ahead, again)
-    )
-    swaps.append(swapped(last))
+    held[12], weights = lax.optimization_barrier((held[12], weights))
+    held[14] = exchange(held[12], 2, devices)
+    held[6] = exchange(held[2], 4, devices)
+    held[10] = exchange(held[8], 2, devices)
+    first = (0, 4, 2, 8, 12)
+    last = (14, 6, 10)
+    swaps = [swapped(first), swapped(last)]
+    ahead = project_early([held[m] for m in first + last] + swaps[:1])
     arrays = [held[m] for m in first + last] + swaps
     sources = [(m,) for m in first + last]
     sources += [tuple(m ^ 1 for m in group) for group in (first, last)]
-    early_groups = (first, sources[-2])
+    early_groups = (first + last + sources[-2],)
     result = pl.pallas_call(
         functools.partial(both_kernel, rows, tokens, sources, early_groups),
         out_shape=jax.ShapeDtypeStruct((size, channels), BF16),
-        in_specs=[IN_SMEM] + [IN_VMEM] * (len(arrays) + len(weights) + len(ahead) + len(again)),
+        in_specs=[IN_SMEM] + [IN_VMEM] * (len(arrays) + len(weights) + len(ahead)),
         scratch_shapes=[
             pltpu.VMEM((tiles, devices * hw, LANES), F32),
             pltpu.VMEM((tiles, devices * hw, LANES), F32),
-            pltpu.VMEM((2 * len(last), tiles, channels, LANES), BF16),
+            pltpu.VMEM((len(last), tiles, channels, LANES), BF16),
             pltpu.VMEM((hw * devices * tiles, LANES), F32),
             pltpu.VMEM((2 * tiles, channels, LANES), BF16),
             pltpu.VMEM((devices * tiles * hw, LANES), BF16),
@@ -339,7 +332,7 @@
         ],
         compiler_params=pltpu.CompilerParams(vmem_limit_bytes=24 * 1024 * 1024),
         name="both",
-    )(me, *arrays, *weights, *ahead, *again)
+    )(me, *arrays, *weights, *ahead)
     return result.reshape(pair.shape)
 
 

time: 28.4 us -> 26.5 us (0.933)
  waiting for transfers between devices: 7.22 us -> 5.99 us
  starting transfers between devices: 10.8 us -> 10.2 us
    ppermute x9, waiting for transfers between devices: 7.22 us -> 5.99 us  [exchange(): return lax.ppermute(block, 'row', pairs)]
    ppermute x9, starting transfers between devices: 10.8 us -> 10.2 us  [exchange(): return lax.ppermute(block, 'row', pairs)]
    pallas_call x2 -> x1, Pallas kernels: 0.99 us -> 0.99 us  [project_early(): pl.pallas_call(functools.partial(early_kernel, [block.shape[0] for block...]
  transfers between devices with their start and end apart: 9 -> 9, of which waited for: 6 -> 4; matrix products, arithmetic and copies ran while one was open for 0% -> 0% of each run, Pallas kernels for 8% -> 8%
where the time goes in v11:
time: 26.5 us; the launch traced here: 26.3 us
  starting transfers between devices  10.2 us (38%)
  Pallas kernels  9.96 us (38%)
  waiting for transfers between devices  5.99 us (23%)
    ppermute x9, starting transfers between devices, exchange(): return lax.ppermute(block, 'row', pairs)  10.2 us
    pallas_call x1, Pallas kernels, small_plan(): pl.pallas_call(functools.partial(both_kernel, rows, tokens, sources, earl...  6.66 us
    ppermute x9, waiting for transfers between devices, exchange(): return lax.ppermute(block, 'row', pairs)  5.99 us
    pallas_call x1, Pallas kernels, small_plan(): pl.pallas_call(functools.partial(prepare_kernel, rows, tokens), in_specs=...  1.17 us
    pallas_call x1, Pallas kernels, small_plan(): pl.pallas_call(functools.partial(pack_kernel, rows, tokens), out_shape=VM...  1.15 us
    pallas_call x1, Pallas kernels, project_early(): pl.pallas_call(functools.partial(early_kernel, [block.shape[0] for block...  0.99 us
  transfers between devices with their start and end apart: 9, of which 4 were waited for; matrix products, arithmetic and copies ran while one was open for 0% of the time, Pallas kernels for 8%

profile of v11, /device:TPU:0, one launch (start us, length us, event | category | flops | bytes accessed | tf_op | source)
XLA Modules:
  0.0 26.3 jit_solution(598116723611004397)
XLA Ops:
  0.0 1.2 %pack.1.refs_0_ = bf16[1,272,128]{2,1,0:T(8,128)(2,1)S(1)} custom-call(bf16[4,64,128]{2,1,0:T(8,128)(2,1)} %pair_ref.1, s32[4,64]{1,0:T(4,128)} %mask_ref.1), custom_call_target="tpu_custom_call" | custom-call | tf_op jit(solution)/shard_map/pack/pallas_call | solution.py:264
  1.2 5.1 %collective-permute-start.3 = (bf16[1,272,128]{2,1,0:T(8,128)(2,1)S(1)}, bf16[1,272,128]{2,1,0:T(8,128)(2,1)S(1)}, u32[]{:S(2)}, u32[]{:S(2)}) collective-permute-start(bf16[1,272,128]{2,1,0:T(8,128)(2,1)S(1)} %pack.1.refs_0_), channel_id=1, source_target_pairs={{0,12},{1,13},{2,14},{3,15},{4,8},{5,9},{6,10},{7,11},{8,4},{9,5},... | collective-permute-start | bytes 208904 | tf_op jit(solution)/shard_map/ppermute | solution.py:257
  6.3 0.0 collective-permute-start.2
  6.3 1.5 %collective-permute-start.1 = (bf16[1,272,128]{2,1,0:T(8,128)(2,1)S(1)}, bf16[1,272,128]{2,1,0:T(8,128)(2,1)S(1)}, u32[]{:S(2)}, u32[]{:S(2)}) collective-permute-start(bf16[1,272,128]{2,1,0:T(8,128)(2,1)S(1)} %pack.1.refs_0_), channel_id=1, source_target_pairs={{0,2},{1,3},{2,0},{3,1},{4,6},{5,7},{6,4},{7,5},{8,10},{9,11},{10,... | collective-permute-start | bytes 208904 | tf_op jit(solution)/shard_map/ppermute | solution.py:257
  7.8 0.8 %collective-permute-start = (bf16[1,272,128]{2,1,0:T(8,128)(2,1)S(1)}, bf16[1,272,128]{2,1,0:T(8,128)(2,1)S(1)}, u32[]{:S(2)}, u32[]{:S(2)}) collective-permute-start(bf16[1,272,128]{2,1,0:T(8,128)(2,1)S(1)} %pack.1.refs_0_), channel_id=1, source_target_pairs={{0,4},{1,5},{2,6},{3,7},{4,0},{5,1},{6,2},{7,3},{8,12},{9,13},{10,... | collective-permute-start | bytes 208904 | tf_op jit(solution)/shard_map/ppermute | solution.py:257
  8.6 1.2 %prepare.1 = (bf16[2,256,128]{2,1,0:T(8,128)(2,1)S(1)}, bf16[2,128,128]{2,1,0:T(8,128)(2,1)S(1)}, bf16[2,128,64]{2,1,0:T(8,128)(2,1)S(1)}, f32[2,128,128]{2,1,0:...) custom-call(s32[1]{0:T(128)} %bitcast.me_ref, ...), custom_call_target="tpu_custom_call" | custom-call | tf_op jit(solution)/shard_map/prepare/pallas_call | solution.py:271
  9.8 0.0 collective-permute-done.3.refs_4_
  9.8 1.0 %collective-permute-start.4 = (bf16[1,272,128]{2,1,0:T(8,128)(2,1)S(1)}, bf16[1,272,128]{2,1,0:T(8,128)(2,1)S(1)}, u32[]{:S(2)}, u32[]{:S(2)}) collective-permute-start(bf16[1,272,128]{2,1,0:T(8,128)(2,1)S(1)} %collective-permute-done.3.refs_4_), channel_id=1, source_target_pairs={{0,2},{1,3},{2,0},{3,1},{4,6},{5,7},{6,4},{7,5},{8,10},{9,11},{10,... | collective-permute-start | bytes 208904 | tf_op jit(solution)/shard_map/ppermute | solution.py:257
  10.8 1.5 %collective-permute-done.2.refs_3_ = bf16[1,272,128]{2,1,0:T(8,128)(2,1)S(1)} collective-permute-done((bf16[1,272,128]{2,1,0:T(8,128)(2,1)S(1)}, bf16[1,272,128]{2,1,0:T(8,128)(2,1)S(1)}, u32[]{:S(2)}, u32[]{:S(2)}) %collective-permute-start.2) | collective-permute-done | bytes 69664 | tf_op jit(solution)/shard_map/ppermute | solution.py:257
  12.3 1.5 %collective-permute-start.6 = (bf16[1,272,128]{2,1,0:T(8,128)(2,1)S(1)}, bf16[1,272,128]{2,1,0:T(8,128)(2,1)S(1)}, u32[]{:S(2)}, u32[]{:S(2)}) collective-permute-start(bf16[1,272,128]{2,1,0:T(8,128)(2,1)S(1)} %collective-permute-done.2.refs_3_), channel_id=1, source_target_pairs={{0,2},{1,3},{2,0},{3,1},{4,6},{5,7},{6,4},{7,5},{8,10},{9,11},{10,... | collective-permute-start | bytes 208904 | tf_op jit(solution)/shard_map/ppermute | solution.py:257
  13.8 0.0 collective-permute-done.1.refs_2_
  13.8 0.1 collective-permute-start.5
  13.9 0.0 collective-permute-done.refs_1_
  14.0 0.1 collective-permute-start.7
  14.0 2.5 %collective-permute-done.6.refs_7_ = bf16[1,272,128]{2,1,0:T(8,128)(2,1)S(1)} collective-permute-done((bf16[1,272,128]{2,1,0:T(8,128)(2,1)S(1)}, bf16[1,272,128]{2,1,0:T(8,128)(2,1)S(1)}, u32[]{:S(2)}, u32[]{:S(2)}) %collective-permute-start.6) | collective-permute-done | bytes 69664 | tf_op jit(solution)/shard_map/ppermute | solution.py:257
  16.6 1.5 %collective-permute-done.5.refs_6_ = bf16[1,272,128]{2,1,0:T(8,128)(2,1)S(1)} collective-permute-done((bf16[1,272,128]{2,1,0:T(8,128)(2,1)S(1)}, bf16[1,272,128]{2,1,0:T(8,128)(2,1)S(1)}, u32[]{:S(2)}, u32[]{:S(2)}) %collective-permute-start.5) | collective-permute-done | bytes 69664 | tf_op jit(solution)/shard_map/ppermute | solution.py:257
  18.1 0.0 collective-permute-done.4.refs_5_
  18.2 0.1 collective-permute-start.8
  18.2 0.0 collective-permute-done.7.refs_8_
  18.2 1.0 %early.1 = (f32[13,2,64,128]{3,2,1,0:T(8,128)S(1)}, f32[13,2,64,128]{3,2,1,0:T(8,128)S(1)}, bf16[13,2,128,128]{3,2,1,0:T(8,128)(2,1)S(1)}) custom-call(bf16[1,272,128]{2,1,0:T(8,128)(2,1)S(1)} %pack.1.refs_0_, bf16[1,272,128]{2,1,0:T(8,128)(2,1)S(1)} %collective-permute-done.refs_1_, bf16[1,272,128]{2,1,0:T(8,128)(2,1)S(1)} %collective-permute-done.1.refs_2_, ...), custom_call_target="tpu_custom_call" | custom-call | tf_op jit(solution)/shard_map/early/pallas_call | solution.py:292
  19.2 0.4 %collective-permute-done.8.refs_9_ = bf16[3,272,128]{2,1,0:T(8,128)(2,1)S(1)} collective-permute-done((bf16[3,272,128]{2,1,0:T(8,128)(2,1)S(1)}, bf16[3,272,128]{2,1,0:T(8,128)(2,1)S(1)}, u32[]{:S(2)}, u32[]{:S(2)}) %collective-permute-start.8) | collective-permute-done | bytes 208928 | tf_op jit(solution)/shard_map/ppermute | solution.py:257
  19.7 6.7 %both.1 = bf16[256,128]{1,0:T(8,128)(2,1)} custom-call(s32[1]{0:T(128)} %bitcast.me_ref, bf16[1,272,128]{2,1,0:T(8,128)(2,1)S(1)} %pack.1.refs_0_, bf16[1,272,128]{2,1,0:T(8,128)(2,1)S(1)} %collective-permute-done.refs_1_, bf16[1,272,128]{2,1,0:T(8,128)(2,1)S(1)} %collective-permute-done.1.refs_2_, bf16[1,272,128]{2,1,0:T(8,128)(2,1)S(1)} %collective-permute-done.2.refs_3_, ...), custom_call_target="tpu_custom_call" | custom-call | tf_op jit(solution)/shard_map/both/pallas_call | solution.py:320
  (6 shorter events, 0.1 us)
Async XLA Ops:
  1.2 8.6 %collective-permute-start.3 = (bf16[1,272,128]{2,1,0:T(8,128)(2,1)S(1)}, bf16[1,272,128]{2,1,0:T(8,128)(2,1)S(1)}, u32[]{:S(2)}, u32[]{:S(2)}) collective-permute-start(bf16[1,272,128]{2,1,0:T(8,128)(2,1)S(1)} %pack.1.refs_0_), channel_id=1, source_target_pairs={{0,12},{1,13},{2,14},{3,15},{4,8},{5,9},{6,10},{7,11},{8,4},{9,5},... | collective-permute-start | bytes 208904 | tf_op jit(solution)/shard_map/ppermute | solution.py:257
  6.3 6.0 %collective-permute-start.2 = (bf16[1,272,128]{2,1,0:T(8,128)(2,1)S(1)}, bf16[1,272,128]{2,1,0:T(8,128)(2,1)S(1)}, u32[]{:S(2)}, u32[]{:S(2)}) collective-permute-start(bf16[1,272,128]{2,1,0:T(8,128)(2,1)S(1)} %pack.1.refs_0_), channel_id=1, source_target_pairs={{0,8},{1,9},{2,10},{3,11},{4,12},{5,13},{6,14},{7,15},{8,0},{9,1},... | collective-permute-start | bytes 208904 | tf_op jit(solution)/shard_map/ppermute | solution.py:257
  6.3 7.5 %collective-permute-start.1 = (bf16[1,272,128]{2,1,0:T(8,128)(2,1)S(1)}, bf16[1,272,128]{2,1,0:T(8,128)(2,1)S(1)}, u32[]{:S(2)}, u32[]{:S(2)}) collective-permute-start(bf16[1,272,128]{2,1,0:T(8,128)(2,1)S(1)} %pack.1.refs_0_), channel_id=1, source_target_pairs={{0,2},{1,3},{2,0},{3,1},{4,6},{5,7},{6,4},{7,5},{8,10},{9,11},{10,... | collective-permute-start | bytes 208904 | tf_op jit(solution)/shard_map/ppermute | solution.py:257
  7.8 6.1 %collective-permute-start = (bf16[1,272,128]{2,1,0:T(8,128)(2,1)S(1)}, bf16[1,272,128]{2,1,0:T(8,128)(2,1)S(1)}, u32[]{:S(2)}, u32[]{:S(2)}) collective-permute-start(bf16[1,272,128]{2,1,0:T(8,128)(2,1)S(1)} %pack.1.refs_0_), channel_id=1, source_target_pairs={{0,4},{1,5},{2,6},{3,7},{4,0},{5,1},{6,2},{7,3},{8,12},{9,13},{10,... | collective-permute-start | bytes 208904 | tf_op jit(solution)/shard_map/ppermute | solution.py:257
  9.8 8.4 %collective-permute-start.4 = (bf16[1,272,128]{2,1,0:T(8,128)(2,1)S(1)}, bf16[1,272,128]{2,1,0:T(8,128)(2,1)S(1)}, u32[]{:S(2)}, u32[]{:S(2)}) collective-permute-start(bf16[1,272,128]{2,1,0:T(8,128)(2,1)S(1)} %collective-permute-done.3.refs_4_), channel_id=1, source_target_pairs={{0,2},{1,3},{2,0},{3,1},{4,6},{5,7},{6,4},{7,5},{8,10},{9,11},{10,... | collective-permute-start | bytes 208904 | tf_op jit(solution)/shard_map/ppermute | solution.py:257
  12.3 4.3 %collective-permute-start.6 = (bf16[1,272,128]{2,1,0:T(8,128)(2,1)S(1)}, bf16[1,272,128]{2,1,0:T(8,128)(2,1)S(1)}, u32[]{:S(2)}, u32[]{:S(2)}) collective-permute-start(bf16[1,272,128]{2,1,0:T(8,128)(2,1)S(1)} %collective-permute-done.2.refs_3_), channel_id=1, source_target_pairs={{0,2},{1,3},{2,0},{3,1},{4,6},{5,7},{6,4},{7,5},{8,10},{9,11},{10,... | collective-permute-start | bytes 208904 | tf_op jit(solution)/shard_map/ppermute | solution.py:257
  13.8 4.3 %collective-permute-start.5 = (bf16[1,272,128]{2,1,0:T(8,128)(2,1)S(1)}, bf16[1,272,128]{2,1,0:T(8,128)(2,1)S(1)}, u32[]{:S(2)}, u32[]{:S(2)}) collective-permute-start(bf16[1,272,128]{2,1,0:T(8,128)(2,1)S(1)} %collective-permute-done.1.refs_2_), channel_id=1, source_target_pairs={{0,4},{1,5},{2,6},{3,7},{4,0},{5,1},{6,2},{7,3},{8,12},{9,13},{10,... | collective-permute-start | bytes 208904 | tf_op jit(solution)/shard_map/ppermute | solution.py:257
  14.0 4.3 %collective-permute-start.7 = (bf16[5,272,128]{2,1,0:T(8,128)(2,1)S(1)}, bf16[5,272,128]{2,1,0:T(8,128)(2,1)S(1)}, u32[]{:S(2)}, u32[]{:S(2)}) collective-permute-start(bf16[5,272,128]{2,1,0:T(8,128)(2,1)S(1)} %constant_dynamic-update-slice_fusion), channel_id=1, source_target_pairs={{0,1},{1,0},{2,3},{3,2},{4,5},{5,4},{6,7},{7,6},{8,9},{9,8},{10,11... | collective-permute-start | bytes 1044488 | tf_op jit(solution)/shard_map/ppermute | solution.py:257
  18.2 1.5 %collective-permute-start.8 = (bf16[3,272,128]{2,1,0:T(8,128)(2,1)S(1)}, bf16[3,272,128]{2,1,0:T(8,128)(2,1)S(1)}, u32[]{:S(2)}, u32[]{:S(2)}) collective-permute-start(bf16[3,272,128]{2,1,0:T(8,128)(2,1)S(1)} %pad_maximum_fusion), channel_id=1, source_target_pairs={{0,1},{1,0},{2,3},{3,2},{4,5},{5,4},{6,7},{7,6},{8,9},{9,8},{10,11... | collective-permute-start | bytes 626696 | tf_op jit(solution)/shard_map/ppermute | solution.py:257

commit v12 on v11

--- a/solution.py
+++ b/solution.py
@@ -11,6 +11,8 @@
 F32, BF16 = jnp.float32, jnp.bfloat16
 LANES = 128
 MASK_ROWS = 16
+BLOCKS_AT_ONCE = 4
+CHANNELS_AT_ONCE = 8
 NT = (((1,), (1,)), ((), ()))
 VMEM = pltpu.VMEM
 IN_VMEM = pl.BlockSpec(memory_space=pltpu.VMEM)
@@ -188,7 +190,7 @@
 
     low = iota((devices, LANES), 1) < tokens
 
-    def channel_sum(c):
+    def operands(c):
         here = pl.ds(c, devices, stride=hw)
         left = jnp.concatenate([left_s[h, here, :] for h in range(tiles)], axis=0)
         halves = [[], []]
@@ -199,36 +201,44 @@
                 straight, other = (right, turned) if q == 0 else (turned, right)
                 halves[0].append(jnp.where(low, straight, 0.0))
                 halves[1].append(jnp.where(low, 0.0, other))
-        against = jnp.concatenate(halves[0] + halves[1], axis=0).astype(BF16)
-        here = pl.ds(c * tiles * devices, tiles * devices)
-        sum_s[here, :] = dot_nt(left.astype(BF16), against)
-
-    for c in range(hw):
-        channel_sum(c)
-
-    for m in range(devices):
-        ref, k = where[m]
-        hidden, first = [], []
-        for h in range(tiles):
-            summed = sum_s[pl.ds(h * devices + (me ^ m), hw, stride=tiles * devices), :]
-            hidden.append(column_norm(summed, mid_ref[0]))
-            first.append(normed_of(m, h))
-        update = dot(out_ref[0], side_by_side(hidden))
-        logits = dot(gate_ref[0], side_by_side(first))
-        normed = []
-        for h in range(tiles):
-            gated = twice_sigmoid(tile(logits, h)) * tile(update, h)
-            now = (chunk_of(ref, channels, k, h) + gated).astype(BF16)
-            normed.append(column_norm(now.astype(F32), gain_ref[1]))
-            if m == 0:
-                now_s[h] = now
-                now_s[tiles + h] = normed[h]
-        projected = dot(proj_ref[1], side_by_side(normed))
-        for h in range(tiles):
-            left, right = factors(tile(projected, h), mask_of(ref, channels, k, h))
-            here = pl.ds((m * tiles + h) * hw, hw)
-            second_left_s[here, :] = left.astype(BF16)
-            second_right_s[here, :] = right.astype(BF16)
+        against = jnp.concatenate(halves[0] + halves[1], axis=0)
+        return left.astype(BF16), against.astype(BF16)
+
+    for c in range(0, hw, CHANNELS_AT_ONCE):
+        group = [operands(c + n) for n in range(CHANNELS_AT_ONCE)]
+        for n, (left, against) in enumerate(group):
+            here = pl.ds((c + n) * tiles * devices, tiles * devices)
+            sum_s[here, :] = dot_nt(left, against)
+
+    both_tiles = range(tiles)
+    for start in range(0, devices, BLOCKS_AT_ONCE):
+        group = range(start, start + BLOCKS_AT_ONCE)
+        hidden, updates, logits, normed, projected = {}, {}, {}, {}, {}
+        for m in group:
+            rows_of = [pl.ds(h * devices + (me ^ m), hw, stride=tiles * devices) for h in both_tiles]
+            hidden[m] = [column_norm(sum_s[here, :], mid_ref[0]) for here in rows_of]
+        for m in group:
+            updates[m] = dot(out_ref[0], side_by_side(hidden[m]))
+            logits[m] = dot(gate_ref[0], side_by_side([normed_of(m, h) for h in both_tiles]))
+        for m in group:
+            ref, k = where[m]
+            normed[m] = []
+            for h in both_tiles:
+                gated = twice_sigmoid(tile(logits[m], h)) * tile(updates[m], h)
+                now = (chunk_of(ref, channels, k, h) + gated).astype(BF16)
+                normed[m].append(column_norm(now.astype(F32), gain_ref[1]))
+                if m == 0:
+                    now_s[h] = now
+                    now_s[tiles + h] = normed[m][h]
+        for m in group:
+            projected[m] = dot(proj_ref[1], side_by_side(normed[m]))
+        for m in group:
+            ref, k = where[m]
+            for h in both_tiles:
+                left, right = factors(tile(projected[m], h), mask_of(ref, channels, k, h))
+                here = pl.ds((m * tiles + h) * hw, hw)
+                second_left_s[here, :] = left.astype(BF16)
+                second_right_s[here, :] = right.astype(BF16)
 
     depth = 2 * hw
     sums = []

time: 26.5 us -> 26.5 us (level)
  no operation moved by 1% of the time
where the time goes in v12:
time: 26.5 us; the launch traced here: 26.3 us
  starting transfers between devices  10.2 us (38%)
  Pallas kernels  9.95 us (38%)
  waiting for transfers between devices  5.99 us (23%)
    ppermute x9, starting transfers between devices, exchange(): return lax.ppermute(block, 'row', pairs)  10.2 us
    pallas_call x1, Pallas kernels, small_plan(): pl.pallas_call(functools.partial(both_kernel, rows, tokens, sources, earl...  6.64 us
    ppermute x9, waiting for transfers between devices, exchange(): return lax.ppermute(block, 'row', pairs)  5.99 us
    pallas_call x1, Pallas kernels, small_plan(): pl.pallas_call(functools.partial(prepare_kernel, rows, tokens), in_specs=...  1.17 us
    pallas_call x1, Pallas kernels, small_plan(): pl.pallas_call(functools.partial(pack_kernel, rows, tokens), out_shape=VM...  1.15 us
    pallas_call x1, Pallas kernels, project_early(): pl.pallas_call(functools.partial(early_kernel, [block.shape[0] for block...  0.99 us
  transfers between devices with their start and end apart: 9, of which 4 were waited for; matrix products, arithmetic and copies ran while one was open for 0% of the time, Pallas kernels for 8%

profile of v12, /device:TPU:0, one launch (start us, length us, event | category | flops | bytes accessed | tf_op | source)
XLA Modules:
  0.0 26.3 jit_solution(7448257285973370138)
XLA Ops:
  0.0 1.2 %pack.1.refs_0_ = bf16[1,272,128]{2,1,0:T(8,128)(2,1)S(1)} custom-call(bf16[4,64,128]{2,1,0:T(8,128)(2,1)} %pair_ref.1, s32[4,64]{1,0:T(4,128)} %mask_ref.1), custom_call_target="tpu_custom_call" | custom-call | tf_op jit(solution)/shard_map/pack/pallas_call | solution.py:274
  1.2 5.1 %collective-permute-start.3 = (bf16[1,272,128]{2,1,0:T(8,128)(2,1)S(1)}, bf16[1,272,128]{2,1,0:T(8,128)(2,1)S(1)}, u32[]{:S(2)}, u32[]{:S(2)}) collective-permute-start(bf16[1,272,128]{2,1,0:T(8,128)(2,1)S(1)} %pack.1.refs_0_), channel_id=1, source_target_pairs={{0,12},{1,13},{2,14},{3,15},{4,8},{5,9},{6,10},{7,11},{8,4},{9,5},... | collective-permute-start | bytes 208904 | tf_op jit(solution)/shard_map/ppermute | solution.py:267
  6.3 0.0 collective-permute-start.2
  6.3 1.5 %collective-permute-start.1 = (bf16[1,272,128]{2,1,0:T(8,128)(2,1)S(1)}, bf16[1,272,128]{2,1,0:T(8,128)(2,1)S(1)}, u32[]{:S(2)}, u32[]{:S(2)}) collective-permute-start(bf16[1,272,128]{2,1,0:T(8,128)(2,1)S(1)} %pack.1.refs_0_), channel_id=1, source_target_pairs={{0,2},{1,3},{2,0},{3,1},{4,6},{5,7},{6,4},{7,5},{8,10},{9,11},{10,... | collective-permute-start | bytes 208904 | tf_op jit(solution)/shard_map/ppermute | solution.py:267
  7.8 0.8 %collective-permute-start = (bf16[1,272,128]{2,1,0:T(8,128)(2,1)S(1)}, bf16[1,272,128]{2,1,0:T(8,128)(2,1)S(1)}, u32[]{:S(2)}, u32[]{:S(2)}) collective-permute-start(bf16[1,272,128]{2,1,0:T(8,128)(2,1)S(1)} %pack.1.refs_0_), channel_id=1, source_target_pairs={{0,4},{1,5},{2,6},{3,7},{4,0},{5,1},{6,2},{7,3},{8,12},{9,13},{10,... | collective-permute-start | bytes 208904 | tf_op jit(solution)/shard_map/ppermute | solution.py:267
  8.6 1.2 %prepare.1 = (bf16[2,256,128]{2,1,0:T(8,128)(2,1)S(1)}, bf16[2,128,128]{2,1,0:T(8,128)(2,1)S(1)}, bf16[2,128,64]{2,1,0:T(8,128)(2,1)S(1)}, f32[2,128,128]{2,1,0:...) custom-call(s32[1]{0:T(128)} %bitcast.me_ref, ...), custom_call_target="tpu_custom_call" | custom-call | tf_op jit(solution)/shard_map/prepare/pallas_call | solution.py:281
  9.8 0.0 collective-permute-done.3.refs_4_
  9.8 1.0 %collective-permute-start.4 = (bf16[1,272,128]{2,1,0:T(8,128)(2,1)S(1)}, bf16[1,272,128]{2,1,0:T(8,128)(2,1)S(1)}, u32[]{:S(2)}, u32[]{:S(2)}) collective-permute-start(bf16[1,272,128]{2,1,0:T(8,128)(2,1)S(1)} %collective-permute-done.3.refs_4_), channel_id=1, source_target_pairs={{0,2},{1,3},{2,0},{3,1},{4,6},{5,7},{6,4},{7,5},{8,10},{9,11},{10,... | collective-permute-start | bytes 208904 | tf_op jit(solution)/shard_map/ppermute | solution.py:267
  10.8 1.5 %collective-permute-done.2.refs_3_ = bf16[1,272,128]{2,1,0:T(8,128)(2,1)S(1)} collective-permute-done((bf16[1,272,128]{2,1,0:T(8,128)(2,1)S(1)}, bf16[1,272,128]{2,1,0:T(8,128)(2,1)S(1)}, u32[]{:S(2)}, u32[]{:S(2)}) %collective-permute-start.2) | collective-permute-done | bytes 69664 | tf_op jit(solution)/shard_map/ppermute | solution.py:267
  12.3 1.5 %collective-permute-start.6 = (bf16[1,272,128]{2,1,0:T(8,128)(2,1)S(1)}, bf16[1,272,128]{2,1,0:T(8,128)(2,1)S(1)}, u32[]{:S(2)}, u32[]{:S(2)}) collective-permute-start(bf16[1,272,128]{2,1,0:T(8,128)(2,1)S(1)} %collective-permute-done.2.refs_3_), channel_id=1, source_target_pairs={{0,2},{1,3},{2,0},{3,1},{4,6},{5,7},{6,4},{7,5},{8,10},{9,11},{10,... | collective-permute-start | bytes 208904 | tf_op jit(solution)/shard_map/ppermute | solution.py:267
  13.8 0.0 collective-permute-done.1.refs_2_
  13.8 0.1 collective-permute-start.5
  13.9 0.0 collective-permute-done.refs_1_
  14.0 0.1 collective-permute-start.7
  14.0 2.5 %collective-permute-done.6.refs_7_ = bf16[1,272,128]{2,1,0:T(8,128)(2,1)S(1)} collective-permute-done((bf16[1,272,128]{2,1,0:T(8,128)(2,1)S(1)}, bf16[1,272,128]{2,1,0:T(8,128)(2,1)S(1)}, u32[]{:S(2)}, u32[]{:S(2)}) %collective-permute-start.6) | collective-permute-done | bytes 69664 | tf_op jit(solution)/shard_map/ppermute | solution.py:267
  16.6 1.5 %collective-permute-done.5.refs_6_ = bf16[1,272,128]{2,1,0:T(8,128)(2,1)S(1)} collective-permute-done((bf16[1,272,128]{2,1,0:T(8,128)(2,1)S(1)}, bf16[1,272,128]{2,1,0:T(8,128)(2,1)S(1)}, u32[]{:S(2)}, u32[]{:S(2)}) %collective-permute-start.5) | collective-permute-done | bytes 69664 | tf_op jit(solution)/shard_map/ppermute | solution.py:267
  18.1 0.0 collective-permute-done.4.refs_5_
  18.2 0.1 collective-permute-start.8
  18.2 0.0 collective-permute-done.7.refs_8_
  18.2 1.0 %early.1 = (f32[13,2,64,128]{3,2,1,0:T(8,128)S(1)}, f32[13,2,64,128]{3,2,1,0:T(8,128)S(1)}, bf16[13,2,128,128]{3,2,1,0:T(8,128)(2,1)S(1)}) custom-call(bf16[1,272,128]{2,1,0:T(8,128)(2,1)S(1)} %pack.1.refs_0_, bf16[1,272,128]{2,1,0:T(8,128)(2,1)S(1)} %collective-permute-done.refs_1_, bf16[1,272,128]{2,1,0:T(8,128)(2,1)S(1)} %collective-permute-done.1.refs_2_, ...), custom_call_target="tpu_custom_call" | custom-call | tf_op jit(solution)/shard_map/early/pallas_call | solution.py:302
  19.2 0.4 %collective-permute-done.8.refs_9_ = bf16[3,272,128]{2,1,0:T(8,128)(2,1)S(1)} collective-permute-done((bf16[3,272,128]{2,1,0:T(8,128)(2,1)S(1)}, bf16[3,272,128]{2,1,0:T(8,128)(2,1)S(1)}, u32[]{:S(2)}, u32[]{:S(2)}) %collective-permute-start.8) | collective-permute-done | bytes 208928 | tf_op jit(solution)/shard_map/ppermute | solution.py:267
  19.7 6.6 %both.1 = bf16[256,128]{1,0:T(8,128)(2,1)} custom-call(s32[1]{0:T(128)} %bitcast.me_ref, bf16[1,272,128]{2,1,0:T(8,128)(2,1)S(1)} %pack.1.refs_0_, bf16[1,272,128]{2,1,0:T(8,128)(2,1)S(1)} %collective-permute-done.refs_1_, bf16[1,272,128]{2,1,0:T(8,128)(2,1)S(1)} %collective-permute-done.1.refs_2_, bf16[1,272,128]{2,1,0:T(8,128)(2,1)S(1)} %collective-permute-done.2.refs_3_, ...), custom_call_target="tpu_custom_call" | custom-call | tf_op jit(solution)/shard_map/both/pallas_call | solution.py:330
  (6 shorter events, 0.1 us)
Async XLA Ops:
  1.2 8.6 %collective-permute-start.3 = (bf16[1,272,128]{2,1,0:T(8,128)(2,1)S(1)}, bf16[1,272,128]{2,1,0:T(8,128)(2,1)S(1)}, u32[]{:S(2)}, u32[]{:S(2)}) collective-permute-start(bf16[1,272,128]{2,1,0:T(8,128)(2,1)S(1)} %pack.1.refs_0_), channel_id=1, source_target_pairs={{0,12},{1,13},{2,14},{3,15},{4,8},{5,9},{6,10},{7,11},{8,4},{9,5},... | collective-permute-start | bytes 208904 | tf_op jit(solution)/shard_map/ppermute | solution.py:267
  6.3 6.0 %collective-permute-start.2 = (bf16[1,272,128]{2,1,0:T(8,128)(2,1)S(1)}, bf16[1,272,128]{2,1,0:T(8,128)(2,1)S(1)}, u32[]{:S(2)}, u32[]{:S(2)}) collective-permute-start(bf16[1,272,128]{2,1,0:T(8,128)(2,1)S(1)} %pack.1.refs_0_), channel_id=1, source_target_pairs={{0,8},{1,9},{2,10},{3,11},{4,12},{5,13},{6,14},{7,15},{8,0},{9,1},... | collective-permute-start | bytes 208904 | tf_op jit(solution)/shard_map/ppermute | solution.py:267
  6.3 7.5 %collective-permute-start.1 = (bf16[1,272,128]{2,1,0:T(8,128)(2,1)S(1)}, bf16[1,272,128]{2,1,0:T(8,128)(2,1)S(1)}, u32[]{:S(2)}, u32[]{:S(2)}) collective-permute-start(bf16[1,272,128]{2,1,0:T(8,128)(2,1)S(1)} %pack.1.refs_0_), channel_id=1, source_target_pairs={{0,2},{1,3},{2,0},{3,1},{4,6},{5,7},{6,4},{7,5},{8,10},{9,11},{10,... | collective-permute-start | bytes 208904 | tf_op jit(solution)/shard_map/ppermute | solution.py:267
  7.8 6.1 %collective-permute-start = (bf16[1,272,128]{2,1,0:T(8,128)(2,1)S(1)}, bf16[1,272,128]{2,1,0:T(8,128)(2,1)S(1)}, u32[]{:S(2)}, u32[]{:S(2)}) collective-permute-start(bf16[1,272,128]{2,1,0:T(8,128)(2,1)S(1)} %pack.1.refs_0_), channel_id=1, source_target_pairs={{0,4},{1,5},{2,6},{3,7},{4,0},{5,1},{6,2},{7,3},{8,12},{9,13},{10,... | collective-permute-start | bytes 208904 | tf_op jit(solution)/shard_map/ppermute | solution.py:267
  9.8 8.4 %collective-permute-start.4 = (bf16[1,272,128]{2,1,0:T(8,128)(2,1)S(1)}, bf16[1,272,128]{2,1,0:T(8,128)(2,1)S(1)}, u32[]{:S(2)}, u32[]{:S(2)}) collective-permute-start(bf16[1,272,128]{2,1,0:T(8,128)(2,1)S(1)} %collective-permute-done.3.refs_4_), channel_id=1, source_target_pairs={{0,2},{1,3},{2,0},{3,1},{4,6},{5,7},{6,4},{7,5},{8,10},{9,11},{10,... | collective-permute-start | bytes 208904 | tf_op jit(solution)/shard_map/ppermute | solution.py:267
  12.3 4.3 %collective-permute-start.6 = (bf16[1,272,128]{2,1,0:T(8,128)(2,1)S(1)}, bf16[1,272,128]{2,1,0:T(8,128)(2,1)S(1)}, u32[]{:S(2)}, u32[]{:S(2)}) collective-permute-start(bf16[1,272,128]{2,1,0:T(8,128)(2,1)S(1)} %collective-permute-done.2.refs_3_), channel_id=1, source_target_pairs={{0,2},{1,3},{2,0},{3,1},{4,6},{5,7},{6,4},{7,5},{8,10},{9,11},{10,... | collective-permute-start | bytes 208904 | tf_op jit(solution)/shard_map/ppermute | solution.py:267
  13.8 4.3 %collective-permute-start.5 = (bf16[1,272,128]{2,1,0:T(8,128)(2,1)S(1)}, bf16[1,272,128]{2,1,0:T(8,128)(2,1)S(1)}, u32[]{:S(2)}, u32[]{:S(2)}) collective-permute-start(bf16[1,272,128]{2,1,0:T(8,128)(2,1)S(1)} %collective-permute-done.1.refs_2_), channel_id=1, source_target_pairs={{0,4},{1,5},{2,6},{3,7},{4,0},{5,1},{6,2},{7,3},{8,12},{9,13},{10,... | collective-permute-start | bytes 208904 | tf_op jit(solution)/shard_map/ppermute | solution.py:267
  14.0 4.3 %collective-permute-start.7 = (bf16[5,272,128]{2,1,0:T(8,128)(2,1)S(1)}, bf16[5,272,128]{2,1,0:T(8,128)(2,1)S(1)}, u32[]{:S(2)}, u32[]{:S(2)}) collective-permute-start(bf16[5,272,128]{2,1,0:T(8,128)(2,1)S(1)} %constant_dynamic-update-slice_fusion), channel_id=1, source_target_pairs={{0,1},{1,0},{2,3},{3,2},{4,5},{5,4},{6,7},{7,6},{8,9},{9,8},{10,11... | collective-permute-start | bytes 1044488 | tf_op jit(solution)/shard_map/ppermute | solution.py:267
  18.2 1.5 %collective-permute-start.8 = (bf16[3,272,128]{2,1,0:T(8,128)(2,1)S(1)}, bf16[3,272,128]{2,1,0:T(8,128)(2,1)S(1)}, u32[]{:S(2)}, u32[]{:S(2)}) collective-permute-start(bf16[3,272,128]{2,1,0:T(8,128)(2,1)S(1)} %pad_maximum_fusion), channel_id=1, source_target_pairs={{0,1},{1,0},{2,3},{3,2},{4,5},{5,4},{6,7},{7,6},{8,9},{9,8},{10,11... | collective-permute-start | bytes 626696 | tf_op jit(solution)/shard_map/ppermute | solution.py:267

commit v13 on v11

--- a/solution.py
+++ b/solution.py
@@ -166,7 +166,7 @@
     later = [m for m in range(devices) if m not in ahead]
 
     def place(m, h, left, right):
-        here = pl.ds(pl.multiple_of((me ^ m) * hw, hw), hw)
+        here = pl.ds((me ^ m) * (hw + 1), hw)
         left_s[h, here, :] = left
         right_s[h, here, :] = right
 
@@ -189,7 +189,7 @@
     low = iota((devices, LANES), 1) < tokens
 
     def channel_sum(c):
-        here = pl.ds(c, devices, stride=hw)
+        here = pl.ds(c, devices, stride=hw + 1)
         left = jnp.concatenate([left_s[h, here, :] for h in range(tiles)], axis=0)
         halves = [[], []]
         for h in range(tiles):
@@ -200,7 +200,7 @@
                 halves[0].append(jnp.where(low, straight, 0.0))
                 halves[1].append(jnp.where(low, 0.0, other))
         against = jnp.concatenate(halves[0] + halves[1], axis=0).astype(BF16)
-        here = pl.ds(c * tiles * devices, tiles * devices)
+        here = pl.ds(c * (tiles * devices + 1), tiles * devices)
         sum_s[here, :] = dot_nt(left.astype(BF16), against)
 
     for c in range(hw):
@@ -210,7 +210,7 @@
         ref, k = where[m]
         hidden, first = [], []
         for h in range(tiles):
-            summed = sum_s[pl.ds(h * devices + (me ^ m), hw, stride=tiles * devices), :]
+            summed = sum_s[pl.ds(h * devices + (me ^ m), hw, stride=tiles * devices + 1), :]
             hidden.append(column_norm(summed, mid_ref[0]))
             first.append(normed_of(m, h))
         update = dot(out_ref[0], side_by_side(hidden))
@@ -322,10 +322,10 @@
         out_shape=jax.ShapeDtypeStruct((size, channels), BF16),
         in_specs=[IN_SMEM] + [IN_VMEM] * (len(arrays) + len(weights) + len(ahead)),
         scratch_shapes=[
-            pltpu.VMEM((tiles, devices * hw, LANES), F32),
-            pltpu.VMEM((tiles, devices * hw, LANES), F32),
+            pltpu.VMEM((tiles, devices * (hw + 1), LANES), F32),
+            pltpu.VMEM((tiles, devices * (hw + 1), LANES), F32),
             pltpu.VMEM((len(last), tiles, channels, LANES), BF16),
-            pltpu.VMEM((hw * devices * tiles, LANES), F32),
+            pltpu.VMEM((hw * (devices * tiles + 1), LANES), F32),
             pltpu.VMEM((2 * tiles, channels, LANES), BF16),
             pltpu.VMEM((devices * tiles * hw, LANES), BF16),
             pltpu.VMEM((devices * tiles * hw, LANES), BF16),

time: 26.5 us -> 25.5 us (0.962)
  Pallas kernels: 9.96 us -> 8.94 us
    pallas_call x1, Pallas kernels: 6.66 us -> 5.63 us  [small_plan(): pl.pallas_call(functools.partial(both_kernel, rows, tokens, sources, earl...]
  transfers between devices with their start and end apart: 9 -> 9, of which waited for: 4 -> 4; matrix products, arithmetic and copies ran while one was open for 0% -> 0% of each run, Pallas kernels for 8% -> 9%
where the time goes in v13:
time: 25.5 us; the launch traced here: 25.3 us
  starting transfers between devices  10.2 us (40%)
  Pallas kernels  8.94 us (35%)
  waiting for transfers between devices  5.99 us (23%)
    ppermute x9, starting transfers between devices, exchange(): return lax.ppermute(block, 'row', pairs)  10.2 us
    ppermute x9, waiting for transfers between devices, exchange(): return lax.ppermute(block, 'row', pairs)  5.99 us
    pallas_call x1, Pallas kernels, small_plan(): pl.pallas_call(functools.partial(both_kernel, rows, tokens, sources, earl...  5.63 us
    pallas_call x1, Pallas kernels, small_plan(): pl.pallas_call(functools.partial(prepare_kernel, rows, tokens), in_specs=...  1.17 us
    pallas_call x1, Pallas kernels, small_plan(): pl.pallas_call(functools.partial(pack_kernel, rows, tokens), out_shape=VM...  1.15 us
    pallas_call x1, Pallas kernels, project_early(): pl.pallas_call(functools.partial(early_kernel, [block.shape[0] for block...  0.99 us
  transfers between devices with their start and end apart: 9, of which 4 were waited for; matrix products, arithmetic and copies ran while one was open for 0% of the time, Pallas kernels for 9%

profile of v13, /device:TPU:0, one launch (start us, length us, event | category | flops | bytes accessed | tf_op | source)
XLA Modules:
  0.0 25.3 jit_solution(8884066015324681963)
XLA Ops:
  0.0 1.2 %pack.1.refs_0_ = bf16[1,272,128]{2,1,0:T(8,128)(2,1)S(1)} custom-call(bf16[4,64,128]{2,1,0:T(8,128)(2,1)} %pair_ref.1, s32[4,64]{1,0:T(4,128)} %mask_ref.1), custom_call_target="tpu_custom_call" | custom-call | tf_op jit(solution)/shard_map/pack/pallas_call | solution.py:264
  1.2 5.1 %collective-permute-start.3 = (bf16[1,272,128]{2,1,0:T(8,128)(2,1)S(1)}, bf16[1,272,128]{2,1,0:T(8,128)(2,1)S(1)}, u32[]{:S(2)}, u32[]{:S(2)}) collective-permute-start(bf16[1,272,128]{2,1,0:T(8,128)(2,1)S(1)} %pack.1.refs_0_), channel_id=1, source_target_pairs={{0,12},{1,13},{2,14},{3,15},{4,8},{5,9},{6,10},{7,11},{8,4},{9,5},... | collective-permute-start | bytes 208904 | tf_op jit(solution)/shard_map/ppermute | solution.py:257
  6.3 0.0 collective-permute-start.2
  6.3 1.5 %collective-permute-start.1 = (bf16[1,272,128]{2,1,0:T(8,128)(2,1)S(1)}, bf16[1,272,128]{2,1,0:T(8,128)(2,1)S(1)}, u32[]{:S(2)}, u32[]{:S(2)}) collective-permute-start(bf16[1,272,128]{2,1,0:T(8,128)(2,1)S(1)} %pack.1.refs_0_), channel_id=1, source_target_pairs={{0,2},{1,3},{2,0},{3,1},{4,6},{5,7},{6,4},{7,5},{8,10},{9,11},{10,... | collective-permute-start | bytes 208904 | tf_op jit(solution)/shard_map/ppermute | solution.py:257
  7.8 0.8 %collective-permute-start = (bf16[1,272,128]{2,1,0:T(8,128)(2,1)S(1)}, bf16[1,272,128]{2,1,0:T(8,128)(2,1)S(1)}, u32[]{:S(2)}, u32[]{:S(2)}) collective-permute-start(bf16[1,272,128]{2,1,0:T(8,128)(2,1)S(1)} %pack.1.refs_0_), channel_id=1, source_target_pairs={{0,4},{1,5},{2,6},{3,7},{4,0},{5,1},{6,2},{7,3},{8,12},{9,13},{10,... | collective-permute-start | bytes 208904 | tf_op jit(solution)/shard_map/ppermute | solution.py:257
  8.6 1.2 %prepare.1 = (bf16[2,256,128]{2,1,0:T(8,128)(2,1)S(1)}, bf16[2,128,128]{2,1,0:T(8,128)(2,1)S(1)}, bf16[2,128,64]{2,1,0:T(8,128)(2,1)S(1)}, f32[2,128,128]{2,1,0:...) custom-call(s32[1]{0:T(128)} %bitcast.me_ref, ...), custom_call_target="tpu_custom_call" | custom-call | tf_op jit(solution)/shard_map/prepare/pallas_call | solution.py:271
  9.8 0.0 collective-permute-done.3.refs_4_
  9.8 1.0 %collective-permute-start.4 = (bf16[1,272,128]{2,1,0:T(8,128)(2,1)S(1)}, bf16[1,272,128]{2,1,0:T(8,128)(2,1)S(1)}, u32[]{:S(2)}, u32[]{:S(2)}) collective-permute-start(bf16[1,272,128]{2,1,0:T(8,128)(2,1)S(1)} %collective-permute-done.3.refs_4_), channel_id=1, source_target_pairs={{0,2},{1,3},{2,0},{3,1},{4,6},{5,7},{6,4},{7,5},{8,10},{9,11},{10,... | collective-permute-start | bytes 208904 | tf_op jit(solution)/shard_map/ppermute | solution.py:257
  10.8 1.5 %collective-permute-done.2.refs_3_ = bf16[1,272,128]{2,1,0:T(8,128)(2,1)S(1)} collective-permute-done((bf16[1,272,128]{2,1,0:T(8,128)(2,1)S(1)}, bf16[1,272,128]{2,1,0:T(8,128)(2,1)S(1)}, u32[]{:S(2)}, u32[]{:S(2)}) %collective-permute-start.2) | collective-permute-done | bytes 69664 | tf_op jit(solution)/shard_map/ppermute | solution.py:257
  12.3 1.5 %collective-permute-start.6 = (bf16[1,272,128]{2,1,0:T(8,128)(2,1)S(1)}, bf16[1,272,128]{2,1,0:T(8,128)(2,1)S(1)}, u32[]{:S(2)}, u32[]{:S(2)}) collective-permute-start(bf16[1,272,128]{2,1,0:T(8,128)(2,1)S(1)} %collective-permute-done.2.refs_3_), channel_id=1, source_target_pairs={{0,2},{1,3},{2,0},{3,1},{4,6},{5,7},{6,4},{7,5},{8,10},{9,11},{10,... | collective-permute-start | bytes 208904 | tf_op jit(solution)/shard_map/ppermute | solution.py:257
  13.8 0.0 collective-permute-done.1.refs_2_
  13.8 0.1 collective-permute-start.5
  13.9 0.0 collective-permute-done.refs_1_
  14.0 0.1 collective-permute-start.7
  14.0 2.5 %collective-permute-done.6.refs_7_ = bf16[1,272,128]{2,1,0:T(8,128)(2,1)S(1)} collective-permute-done((bf16[1,272,128]{2,1,0:T(8,128)(2,1)S(1)}, bf16[1,272,128]{2,1,0:T(8,128)(2,1)S(1)}, u32[]{:S(2)}, u32[]{:S(2)}) %collective-permute-start.6) | collective-permute-done | bytes 69664 | tf_op jit(solution)/shard_map/ppermute | solution.py:257
  16.6 1.5 %collective-permute-done.5.refs_6_ = bf16[1,272,128]{2,1,0:T(8,128)(2,1)S(1)} collective-permute-done((bf16[1,272,128]{2,1,0:T(8,128)(2,1)S(1)}, bf16[1,272,128]{2,1,0:T(8,128)(2,1)S(1)}, u32[]{:S(2)}, u32[]{:S(2)}) %collective-permute-start.5) | collective-permute-done | bytes 69664 | tf_op jit(solution)/shard_map/ppermute | solution.py:257
  18.1 0.0 collective-permute-done.4.refs_5_
  18.2 0.1 collective-permute-start.8
  18.2 0.0 collective-permute-done.7.refs_8_
  18.2 1.0 %early.1 = (f32[13,2,64,128]{3,2,1,0:T(8,128)S(1)}, f32[13,2,64,128]{3,2,1,0:T(8,128)S(1)}, bf16[13,2,128,128]{3,2,1,0:T(8,128)(2,1)S(1)}) custom-call(bf16[1,272,128]{2,1,0:T(8,128)(2,1)S(1)} %pack.1.refs_0_, bf16[1,272,128]{2,1,0:T(8,128)(2,1)S(1)} %collective-permute-done.refs_1_, bf16[1,272,128]{2,1,0:T(8,128)(2,1)S(1)} %collective-permute-done.1.refs_2_, ...), custom_call_target="tpu_custom_call" | custom-call | tf_op jit(solution)/shard_map/early/pallas_call | solution.py:292
  19.2 0.4 %collective-permute-done.8.refs_9_ = bf16[3,272,128]{2,1,0:T(8,128)(2,1)S(1)} collective-permute-done((bf16[3,272,128]{2,1,0:T(8,128)(2,1)S(1)}, bf16[3,272,128]{2,1,0:T(8,128)(2,1)S(1)}, u32[]{:S(2)}, u32[]{:S(2)}) %collective-permute-start.8) | collective-permute-done | bytes 208928 | tf_op jit(solution)/shard_map/ppermute | solution.py:257
  19.7 5.6 %both.1 = bf16[256,128]{1,0:T(8,128)(2,1)} custom-call(s32[1]{0:T(128)} %bitcast.me_ref, bf16[1,272,128]{2,1,0:T(8,128)(2,1)S(1)} %pack.1.refs_0_, bf16[1,272,128]{2,1,0:T(8,128)(2,1)S(1)} %collective-permute-done.refs_1_, bf16[1,272,128]{2,1,0:T(8,128)(2,1)S(1)} %collective-permute-done.1.refs_2_, bf16[1,272,128]{2,1,0:T(8,128)(2,1)S(1)} %collective-permute-done.2.refs_3_, ...), custom_call_target="tpu_custom_call" | custom-call | tf_op jit(solution)/shard_map/both/pallas_call | solution.py:320
  (6 shorter events, 0.1 us)
Async XLA Ops:
  1.2 8.6 %collective-permute-start.3 = (bf16[1,272,128]{2,1,0:T(8,128)(2,1)S(1)}, bf16[1,272,128]{2,1,0:T(8,128)(2,1)S(1)}, u32[]{:S(2)}, u32[]{:S(2)}) collective-permute-start(bf16[1,272,128]{2,1,0:T(8,128)(2,1)S(1)} %pack.1.refs_0_), channel_id=1, source_target_pairs={{0,12},{1,13},{2,14},{3,15},{4,8},{5,9},{6,10},{7,11},{8,4},{9,5},... | collective-permute-start | bytes 208904 | tf_op jit(solution)/shard_map/ppermute | solution.py:257
  6.3 6.0 %collective-permute-start.2 = (bf16[1,272,128]{2,1,0:T(8,128)(2,1)S(1)}, bf16[1,272,128]{2,1,0:T(8,128)(2,1)S(1)}, u32[]{:S(2)}, u32[]{:S(2)}) collective-permute-start(bf16[1,272,128]{2,1,0:T(8,128)(2,1)S(1)} %pack.1.refs_0_), channel_id=1, source_target_pairs={{0,8},{1,9},{2,10},{3,11},{4,12},{5,13},{6,14},{7,15},{8,0},{9,1},... | collective-permute-start | bytes 208904 | tf_op jit(solution)/shard_map/ppermute | solution.py:257
  6.3 7.5 %collective-permute-start.1 = (bf16[1,272,128]{2,1,0:T(8,128)(2,1)S(1)}, bf16[1,272,128]{2,1,0:T(8,128)(2,1)S(1)}, u32[]{:S(2)}, u32[]{:S(2)}) collective-permute-start(bf16[1,272,128]{2,1,0:T(8,128)(2,1)S(1)} %pack.1.refs_0_), channel_id=1, source_target_pairs={{0,2},{1,3},{2,0},{3,1},{4,6},{5,7},{6,4},{7,5},{8,10},{9,11},{10,... | collective-permute-start | bytes 208904 | tf_op jit(solution)/shard_map/ppermute | solution.py:257
  7.8 6.1 %collective-permute-start = (bf16[1,272,128]{2,1,0:T(8,128)(2,1)S(1)}, bf16[1,272,128]{2,1,0:T(8,128)(2,1)S(1)}, u32[]{:S(2)}, u32[]{:S(2)}) collective-permute-start(bf16[1,272,128]{2,1,0:T(8,128)(2,1)S(1)} %pack.1.refs_0_), channel_id=1, source_target_pairs={{0,4},{1,5},{2,6},{3,7},{4,0},{5,1},{6,2},{7,3},{8,12},{9,13},{10,... | collective-permute-start | bytes 208904 | tf_op jit(solution)/shard_map/ppermute | solution.py:257
  9.8 8.4 %collective-permute-start.4 = (bf16[1,272,128]{2,1,0:T(8,128)(2,1)S(1)}, bf16[1,272,128]{2,1,0:T(8,128)(2,1)S(1)}, u32[]{:S(2)}, u32[]{:S(2)}) collective-permute-start(bf16[1,272,128]{2,1,0:T(8,128)(2,1)S(1)} %collective-permute-done.3.refs_4_), channel_id=1, source_target_pairs={{0,2},{1,3},{2,0},{3,1},{4,6},{5,7},{6,4},{7,5},{8,10},{9,11},{10,... | collective-permute-start | bytes 208904 | tf_op jit(solution)/shard_map/ppermute | solution.py:257
  12.3 4.3 %collective-permute-start.6 = (bf16[1,272,128]{2,1,0:T(8,128)(2,1)S(1)}, bf16[1,272,128]{2,1,0:T(8,128)(2,1)S(1)}, u32[]{:S(2)}, u32[]{:S(2)}) collective-permute-start(bf16[1,272,128]{2,1,0:T(8,128)(2,1)S(1)} %collective-permute-done.2.refs_3_), channel_id=1, source_target_pairs={{0,2},{1,3},{2,0},{3,1},{4,6},{5,7},{6,4},{7,5},{8,10},{9,11},{10,... | collective-permute-start | bytes 208904 | tf_op jit(solution)/shard_map/ppermute | solution.py:257
  13.8 4.3 %collective-permute-start.5 = (bf16[1,272,128]{2,1,0:T(8,128)(2,1)S(1)}, bf16[1,272,128]{2,1,0:T(8,128)(2,1)S(1)}, u32[]{:S(2)}, u32[]{:S(2)}) collective-permute-start(bf16[1,272,128]{2,1,0:T(8,128)(2,1)S(1)} %collective-permute-done.1.refs_2_), channel_id=1, source_target_pairs={{0,4},{1,5},{2,6},{3,7},{4,0},{5,1},{6,2},{7,3},{8,12},{9,13},{10,... | collective-permute-start | bytes 208904 | tf_op jit(solution)/shard_map/ppermute | solution.py:257
  14.0 4.3 %collective-permute-start.7 = (bf16[5,272,128]{2,1,0:T(8,128)(2,1)S(1)}, bf16[5,272,128]{2,1,0:T(8,128)(2,1)S(1)}, u32[]{:S(2)}, u32[]{:S(2)}) collective-permute-start(bf16[5,272,128]{2,1,0:T(8,128)(2,1)S(1)} %constant_dynamic-update-slice_fusion), channel_id=1, source_target_pairs={{0,1},{1,0},{2,3},{3,2},{4,5},{5,4},{6,7},{7,6},{8,9},{9,8},{10,11... | collective-permute-start | bytes 1044488 | tf_op jit(solution)/shard_map/ppermute | solution.py:257
  18.2 1.5 %collective-permute-start.8 = (bf16[3,272,128]{2,1,0:T(8,128)(2,1)S(1)}, bf16[3,272,128]{2,1,0:T(8,128)(2,1)S(1)}, u32[]{:S(2)}, u32[]{:S(2)}) collective-permute-start(bf16[3,272,128]{2,1,0:T(8,128)(2,1)S(1)} %pad_maximum_fusion), channel_id=1, source_target_pairs={{0,1},{1,0},{2,3},{3,2},{4,5},{5,4},{6,7},{7,6},{8,9},{9,8},{10,11... | collective-permute-start | bytes 626696 | tf_op jit(solution)/shard_map/ppermute | solution.py:257

commit v14 on v13

--- a/solution.py
+++ b/solution.py
@@ -309,7 +309,7 @@
     held[14] = exchange(held[12], 2, devices)
     held[6] = exchange(held[2], 4, devices)
     held[10] = exchange(held[8], 2, devices)
-    first = (0, 4, 2, 8, 12)
+    first = (0, 4, 8, 2, 12)
     last = (14, 6, 10)
     swaps = [swapped(first), swapped(last)]
     ahead = project_early([held[m] for m in first + last] + swaps[:1])

time: 25.5 us -> 24.8 us (0.973)
  waiting for transfers between devices: 5.99 us -> 4.76 us
  starting transfers between devices: 10.2 us -> 10.8 us
    ppermute x9, waiting for transfers between devices: 5.99 us -> 4.76 us  [exchange(): return lax.ppermute(block, 'row', pairs)]
    ppermute x9, starting transfers between devices: 10.2 us -> 10.8 us  [exchange(): return lax.ppermute(block, 'row', pairs)]
where the time goes in v14:
time: 24.8 us; the launch traced here: 24.6 us
  starting transfers between devices  10.8 us (44%)
  Pallas kernels  8.94 us (36%)
  waiting for transfers between devices  4.76 us (19%)
    ppermute x9, starting transfers between devices, exchange(): return lax.ppermute(block, 'row', pairs)  10.8 us
    pallas_call x1, Pallas kernels, small_plan(): pl.pallas_call(functools.partial(both_kernel, rows, tokens, sources, earl...  5.64 us
    ppermute x9, waiting for transfers between devices, exchange(): return lax.ppermute(block, 'row', pairs)  4.76 us
    pallas_call x1, Pallas kernels, small_plan(): pl.pallas_call(functools.partial(prepare_kernel, rows, tokens), in_specs=...  1.17 us
    pallas_call x1, Pallas kernels, small_plan(): pl.pallas_call(functools.partial(pack_kernel, rows, tokens), out_shape=VM...  1.15 us
    pallas_call x1, Pallas kernels, project_early(): pl.pallas_call(functools.partial(early_kernel, [block.shape[0] for block...  0.99 us
  transfers between devices with their start and end apart: 9, of which 4 were waited for; matrix products, arithmetic and copies ran while one was open for 0% of the time, Pallas kernels for 9%

profile of v14, /device:TPU:0, one launch (start us, length us, event | category | flops | bytes accessed | tf_op | source)
XLA Modules:
  0.0 24.6 jit_solution(2110474618897763605)
XLA Ops:
  0.0 1.2 %pack.1.refs_0_ = bf16[1,272,128]{2,1,0:T(8,128)(2,1)S(1)} custom-call(bf16[4,64,128]{2,1,0:T(8,128)(2,1)} %pair_ref.1, s32[4,64]{1,0:T(4,128)} %mask_ref.1), custom_call_target="tpu_custom_call" | custom-call | tf_op jit(solution)/shard_map/pack/pallas_call | solution.py:264
  1.2 5.1 %collective-permute-start.3 = (bf16[1,272,128]{2,1,0:T(8,128)(2,1)S(1)}, bf16[1,272,128]{2,1,0:T(8,128)(2,1)S(1)}, u32[]{:S(2)}, u32[]{:S(2)}) collective-permute-start(bf16[1,272,128]{2,1,0:T(8,128)(2,1)S(1)} %pack.1.refs_0_), channel_id=1, source_target_pairs={{0,12},{1,13},{2,14},{3,15},{4,8},{5,9},{6,10},{7,11},{8,4},{9,5},... | collective-permute-start | bytes 208904 | tf_op jit(solution)/shard_map/ppermute | solution.py:257
  6.3 1.5 %collective-permute-start.2 = (bf16[1,272,128]{2,1,0:T(8,128)(2,1)S(1)}, bf16[1,272,128]{2,1,0:T(8,128)(2,1)S(1)}, u32[]{:S(2)}, u32[]{:S(2)}) collective-permute-start(bf16[1,272,128]{2,1,0:T(8,128)(2,1)S(1)} %pack.1.refs_0_), channel_id=1, source_target_pairs={{0,2},{1,3},{2,0},{3,1},{4,6},{5,7},{6,4},{7,5},{8,10},{9,11},{10,... | collective-permute-start | bytes 208904 | tf_op jit(solution)/shard_map/ppermute | solution.py:257
  7.8 0.0 collective-permute-start.1
  7.8 0.8 %collective-permute-start = (bf16[1,272,128]{2,1,0:T(8,128)(2,1)S(1)}, bf16[1,272,128]{2,1,0:T(8,128)(2,1)S(1)}, u32[]{:S(2)}, u32[]{:S(2)}) collective-permute-start(bf16[1,272,128]{2,1,0:T(8,128)(2,1)S(1)} %pack.1.refs_0_), channel_id=1, source_target_pairs={{0,4},{1,5},{2,6},{3,7},{4,0},{5,1},{6,2},{7,3},{8,12},{9,13},{10,... | collective-permute-start | bytes 208904 | tf_op jit(solution)/shard_map/ppermute | solution.py:257
  8.6 1.2 %prepare.1 = (bf16[2,256,128]{2,1,0:T(8,128)(2,1)S(1)}, bf16[2,128,128]{2,1,0:T(8,128)(2,1)S(1)}, bf16[2,128,64]{2,1,0:T(8,128)(2,1)S(1)}, f32[2,128,128]{2,1,0:...) custom-call(s32[1]{0:T(128)} %bitcast.me_ref, ...), custom_call_target="tpu_custom_call" | custom-call | tf_op jit(solution)/shard_map/prepare/pallas_call | solution.py:271
  9.8 0.0 collective-permute-done.3.refs_4_
  9.8 0.9 %collective-permute-start.4 = (bf16[1,272,128]{2,1,0:T(8,128)(2,1)S(1)}, bf16[1,272,128]{2,1,0:T(8,128)(2,1)S(1)}, u32[]{:S(2)}, u32[]{:S(2)}) collective-permute-start(bf16[1,272,128]{2,1,0:T(8,128)(2,1)S(1)} %collective-permute-done.3.refs_4_), channel_id=1, source_target_pairs={{0,2},{1,3},{2,0},{3,1},{4,6},{5,7},{6,4},{7,5},{8,10},{9,11},{10,... | collective-permute-start | bytes 208904 | tf_op jit(solution)/shard_map/ppermute | solution.py:257
  10.7 0.0 collective-permute-done.2.refs_3_
  10.7 1.7 %collective-permute-start.5 = (bf16[1,272,128]{2,1,0:T(8,128)(2,1)S(1)}, bf16[1,272,128]{2,1,0:T(8,128)(2,1)S(1)}, u32[]{:S(2)}, u32[]{:S(2)}) collective-permute-start(bf16[1,272,128]{2,1,0:T(8,128)(2,1)S(1)} %collective-permute-done.2.refs_3_), channel_id=1, source_target_pairs={{0,4},{1,5},{2,6},{3,7},{4,0},{5,1},{6,2},{7,3},{8,12},{9,13},{10,... | collective-permute-start | bytes 208904 | tf_op jit(solution)/shard_map/ppermute | solution.py:257
  12.3 0.8 %collective-permute-done.1.refs_2_ = bf16[1,272,128]{2,1,0:T(8,128)(2,1)S(1)} collective-permute-done((bf16[1,272,128]{2,1,0:T(8,128)(2,1)S(1)}, bf16[1,272,128]{2,1,0:T(8,128)(2,1)S(1)}, u32[]{:S(2)}, u32[]{:S(2)}) %collective-permute-start.1) | collective-permute-done | bytes 69664 | tf_op jit(solution)/shard_map/ppermute | solution.py:257
  13.1 0.6 %collective-permute-start.6 = (bf16[1,272,128]{2,1,0:T(8,128)(2,1)S(1)}, bf16[1,272,128]{2,1,0:T(8,128)(2,1)S(1)}, u32[]{:S(2)}, u32[]{:S(2)}) collective-permute-start(bf16[1,272,128]{2,1,0:T(8,128)(2,1)S(1)} %collective-permute-done.1.refs_2_), channel_id=1, source_target_pairs={{0,2},{1,3},{2,0},{3,1},{4,6},{5,7},{6,4},{7,5},{8,10},{9,11},{10,... | collective-permute-start | bytes 208904 | tf_op jit(solution)/shard_map/ppermute | solution.py:257
  13.8 0.0 collective-permute-done.refs_1_
  13.8 0.1 collective-permute-start.7
  13.9 1.1 %collective-permute-done.5.refs_6_ = bf16[1,272,128]{2,1,0:T(8,128)(2,1)S(1)} collective-permute-done((bf16[1,272,128]{2,1,0:T(8,128)(2,1)S(1)}, bf16[1,272,128]{2,1,0:T(8,128)(2,1)S(1)}, u32[]{:S(2)}, u32[]{:S(2)}) %collective-permute-start.5) | collective-permute-done | bytes 69664 | tf_op jit(solution)/shard_map/ppermute | solution.py:257
  15.0 2.5 %collective-permute-done.6.refs_7_ = bf16[1,272,128]{2,1,0:T(8,128)(2,1)S(1)} collective-permute-done((bf16[1,272,128]{2,1,0:T(8,128)(2,1)S(1)}, bf16[1,272,128]{2,1,0:T(8,128)(2,1)S(1)}, u32[]{:S(2)}, u32[]{:S(2)}) %collective-permute-start.6) | collective-permute-done | bytes 69664 | tf_op jit(solution)/shard_map/ppermute | solution.py:257
  17.4 0.0 collective-permute-done.4.refs_5_
  17.5 0.1 collective-permute-start.8
  17.6 0.0 collective-permute-done.7.refs_8_
  17.6 1.0 %early.1 = (f32[13,2,64,128]{3,2,1,0:T(8,128)S(1)}, f32[13,2,64,128]{3,2,1,0:T(8,128)S(1)}, bf16[13,2,128,128]{3,2,1,0:T(8,128)(2,1)S(1)}) custom-call(bf16[1,272,128]{2,1,0:T(8,128)(2,1)S(1)} %pack.1.refs_0_, bf16[1,272,128]{2,1,0:T(8,128)(2,1)S(1)} %collective-permute-done.refs_1_, bf16[1,272,128]{2,1,0:T(8,128)(2,1)S(1)} %collective-permute-done.1.refs_2_, ...), custom_call_target="tpu_custom_call" | custom-call | tf_op jit(solution)/shard_map/early/pallas_call | solution.py:292
  18.6 0.4 %collective-permute-done.8.refs_9_ = bf16[3,272,128]{2,1,0:T(8,128)(2,1)S(1)} collective-permute-done((bf16[3,272,128]{2,1,0:T(8,128)(2,1)S(1)}, bf16[3,272,128]{2,1,0:T(8,128)(2,1)S(1)}, u32[]{:S(2)}, u32[]{:S(2)}) %collective-permute-start.8) | collective-permute-done | bytes 208928 | tf_op jit(solution)/shard_map/ppermute | solution.py:257
  19.0 5.6 %both.1 = bf16[256,128]{1,0:T(8,128)(2,1)} custom-call(s32[1]{0:T(128)} %bitcast.me_ref, bf16[1,272,128]{2,1,0:T(8,128)(2,1)S(1)} %pack.1.refs_0_, bf16[1,272,128]{2,1,0:T(8,128)(2,1)S(1)} %collective-permute-done.refs_1_, bf16[1,272,128]{2,1,0:T(8,128)(2,1)S(1)} %collective-permute-done.1.refs_2_, bf16[1,272,128]{2,1,0:T(8,128)(2,1)S(1)} %collective-permute-done.2.refs_3_, ...), custom_call_target="tpu_custom_call" | custom-call | tf_op jit(solution)/shard_map/both/pallas_call | solution.py:320
  (6 shorter events, 0.1 us)
Async XLA Ops:
  1.2 8.6 %collective-permute-start.3 = (bf16[1,272,128]{2,1,0:T(8,128)(2,1)S(1)}, bf16[1,272,128]{2,1,0:T(8,128)(2,1)S(1)}, u32[]{:S(2)}, u32[]{:S(2)}) collective-permute-start(bf16[1,272,128]{2,1,0:T(8,128)(2,1)S(1)} %pack.1.refs_0_), channel_id=1, source_target_pairs={{0,12},{1,13},{2,14},{3,15},{4,8},{5,9},{6,10},{7,11},{8,4},{9,5},... | collective-permute-start | bytes 208904 | tf_op jit(solution)/shard_map/ppermute | solution.py:257
  6.3 4.4 %collective-permute-start.2 = (bf16[1,272,128]{2,1,0:T(8,128)(2,1)S(1)}, bf16[1,272,128]{2,1,0:T(8,128)(2,1)S(1)}, u32[]{:S(2)}, u32[]{:S(2)}) collective-permute-start(bf16[1,272,128]{2,1,0:T(8,128)(2,1)S(1)} %pack.1.refs_0_), channel_id=1, source_target_pairs={{0,2},{1,3},{2,0},{3,1},{4,6},{5,7},{6,4},{7,5},{8,10},{9,11},{10,... | collective-permute-start | bytes 208904 | tf_op jit(solution)/shard_map/ppermute | solution.py:257
  7.8 5.3 %collective-permute-start.1 = (bf16[1,272,128]{2,1,0:T(8,128)(2,1)S(1)}, bf16[1,272,128]{2,1,0:T(8,128)(2,1)S(1)}, u32[]{:S(2)}, u32[]{:S(2)}) collective-permute-start(bf16[1,272,128]{2,1,0:T(8,128)(2,1)S(1)} %pack.1.refs_0_), channel_id=1, source_target_pairs={{0,8},{1,9},{2,10},{3,11},{4,12},{5,13},{6,14},{7,15},{8,0},{9,1},... | collective-permute-start | bytes 208904 | tf_op jit(solution)/shard_map/ppermute | solution.py:257
  7.8 6.0 %collective-permute-start = (bf16[1,272,128]{2,1,0:T(8,128)(2,1)S(1)}, bf16[1,272,128]{2,1,0:T(8,128)(2,1)S(1)}, u32[]{:S(2)}, u32[]{:S(2)}) collective-permute-start(bf16[1,272,128]{2,1,0:T(8,128)(2,1)S(1)} %pack.1.refs_0_), channel_id=1, source_target_pairs={{0,4},{1,5},{2,6},{3,7},{4,0},{5,1},{6,2},{7,3},{8,12},{9,13},{10,... | collective-permute-start | bytes 208904 | tf_op jit(solution)/shard_map/ppermute | solution.py:257
  9.8 7.7 %collective-permute-start.4 = (bf16[1,272,128]{2,1,0:T(8,128)(2,1)S(1)}, bf16[1,272,128]{2,1,0:T(8,128)(2,1)S(1)}, u32[]{:S(2)}, u32[]{:S(2)}) collective-permute-start(bf16[1,272,128]{2,1,0:T(8,128)(2,1)S(1)} %collective-permute-done.3.refs_4_), channel_id=1, source_target_pairs={{0,2},{1,3},{2,0},{3,1},{4,6},{5,7},{6,4},{7,5},{8,10},{9,11},{10,... | collective-permute-start | bytes 208904 | tf_op jit(solution)/shard_map/ppermute | solution.py:257
  10.7 4.3 %collective-permute-start.5 = (bf16[1,272,128]{2,1,0:T(8,128)(2,1)S(1)}, bf16[1,272,128]{2,1,0:T(8,128)(2,1)S(1)}, u32[]{:S(2)}, u32[]{:S(2)}) collective-permute-start(bf16[1,272,128]{2,1,0:T(8,128)(2,1)S(1)} %collective-permute-done.2.refs_3_), channel_id=1, source_target_pairs={{0,4},{1,5},{2,6},{3,7},{4,0},{5,1},{6,2},{7,3},{8,12},{9,13},{10,... | collective-permute-start | bytes 208904 | tf_op jit(solution)/shard_map/ppermute | solution.py:257
  13.1 4.3 %collective-permute-start.6 = (bf16[1,272,128]{2,1,0:T(8,128)(2,1)S(1)}, bf16[1,272,128]{2,1,0:T(8,128)(2,1)S(1)}, u32[]{:S(2)}, u32[]{:S(2)}) collective-permute-start(bf16[1,272,128]{2,1,0:T(8,128)(2,1)S(1)} %collective-permute-done.1.refs_2_), channel_id=1, source_target_pairs={{0,2},{1,3},{2,0},{3,1},{4,6},{5,7},{6,4},{7,5},{8,10},{9,11},{10,... | collective-permute-start | bytes 208904 | tf_op jit(solution)/shard_map/ppermute | solution.py:257
  13.8 3.7 %collective-permute-start.7 = (bf16[5,272,128]{2,1,0:T(8,128)(2,1)S(1)}, bf16[5,272,128]{2,1,0:T(8,128)(2,1)S(1)}, u32[]{:S(2)}, u32[]{:S(2)}) collective-permute-start(bf16[5,272,128]{2,1,0:T(8,128)(2,1)S(1)} %constant_dynamic-update-slice_fusion), channel_id=1, source_target_pairs={{0,1},{1,0},{2,3},{3,2},{4,5},{5,4},{6,7},{7,6},{8,9},{9,8},{10,11... | collective-permute-start | bytes 1044488 | tf_op jit(solution)/shard_map/ppermute | solution.py:257
  17.5 1.5 %collective-permute-start.8 = (bf16[3,272,128]{2,1,0:T(8,128)(2,1)S(1)}, bf16[3,272,128]{2,1,0:T(8,128)(2,1)S(1)}, u32[]{:S(2)}, u32[]{:S(2)}) collective-permute-start(bf16[3,272,128]{2,1,0:T(8,128)(2,1)S(1)} %pad_maximum_fusion), channel_id=1, source_target_pairs={{0,1},{1,0},{2,3},{3,2},{4,5},{5,4},{6,7},{7,6},{8,9},{9,8},{10,11... | collective-permute-start | bytes 626696 | tf_op jit(solution)/shard_map/ppermute | solution.py:257

commit v15 on v14

--- a/solution.py
+++ b/solution.py
@@ -126,36 +126,38 @@
         spread_ref[i] = one_hot(same & (lane == i * devices + me_ref[0]))
 
 
-def early_kernel(counts, *refs):
+def place(me, m, h, left_ref, right_ref, left, right):
+    hw = left.shape[0]
+    here = pl.ds((me ^ m) * (hw + 1), hw)
+    left_ref[h, here, :] = left
+    right_ref[h, here, :] = right
+
+
+def early_kernel(held, me_ref, *refs):
     block_refs, (proj_ref, gain_ref, left_ref, right_ref, normed_ref) = refs[:-5], refs[-5:]
     channels, tiles = normed_ref.shape[2], normed_ref.shape[1]
-    place = 0
-    for block_ref, count in zip(block_refs, counts):
-        for k in range(count):
+    n = 0
+    for block_ref in block_refs:
+        for k in range(block_ref.shape[0]):
             normed = [
                 column_norm(chunk_of(block_ref, channels, k, h), gain_ref[0]) for h in range(tiles)
             ]
             projected = dot(proj_ref[0], side_by_side(normed))
             for h in range(tiles):
-                normed_ref[place, h] = normed[h]
-                left, right = factors(tile(projected, h), mask_of(block_ref, channels, k, h))
-                left_ref[place, h] = left
-                right_ref[place, h] = right
-            place += 1
-
-
-def both_kernel(rows, tokens, sources, early_groups, me_ref, *refs):
+                normed_ref[n, h] = normed[h]
+                both = factors(tile(projected, h), mask_of(block_ref, channels, k, h))
+                place(me_ref[0], held[n], h, left_ref, right_ref, *both)
+            n += 1
+
+
+def both_kernel(rows, tokens, sources, early, me_ref, *refs):
     devices = tokens // rows
     block_refs, refs = refs[: len(sources)], refs[len(sources) :]
     weight_refs, refs = refs[:7], refs[7:]
     proj_ref, gate_ref, out_ref, gain_ref, mid_ref, restore_ref, spread_ref = weight_refs
-    ahead = {}
-    for group in early_groups:
-        for n, m in enumerate(group):
-            ahead[m] = refs[:3] + (n,)
-        refs = refs[3:]
     (
-        result_ref, left_s, right_s, normed_s, sum_s, now_s, second_left_s, second_right_s,
+        _, _, early_normed_ref, result_ref, left_s, right_s,
+        normed_s, sum_s, now_s, second_left_s, second_right_s,
     ) = refs
     channels = gate_ref.shape[1]
     hw = mid_ref.shape[1]
@@ -163,30 +165,23 @@
     me = me_ref[0]
 
     where = {m: (ref, k) for ref, held in zip(block_refs, sources) for k, m in enumerate(held)}
-    later = [m for m in range(devices) if m not in ahead]
-
-    def place(m, h, left, right):
-        here = pl.ds((me ^ m) * (hw + 1), hw)
-        left_s[h, here, :] = left
-        right_s[h, here, :] = right
-
+    later = [m for m in range(devices) if m not in early]
     for m in later:
         ref, k = where[m]
         normed = [column_norm(chunk_of(ref, channels, k, h), gain_ref[0]) for h in range(tiles)]
         projected = dot(proj_ref[0], side_by_side(normed))
         for h in range(tiles):
             normed_s[later.index(m), h] = normed[h]
-            place(m, h, *factors(tile(projected, h), mask_of(ref, channels, k, h)))
-    for m, (left_ref, right_ref, _, n) in ahead.items():
-        for h in range(tiles):
-            place(m, h, left_ref[n, h], right_ref[n, h])
+            both = factors(tile(projected, h), mask_of(ref, channels, k, h))
+            place(me, m, h, left_s, right_s, *both)
 
     def normed_of(m, h):
-        if m in ahead:
-            return ahead[m][2][ahead[m][3], h]
+        if m in early:
+            return early_normed_ref[early.index(m), h]
         return normed_s[later.index(m), h]
 
-    low = iota((devices, LANES), 1) < tokens
+    in_low = one_hot(iota((devices, LANES), 1) < tokens)
+    in_high = one_hot(iota((devices, LANES), 1) >= tokens)
 
     def channel_sum(c):
         here = pl.ds(c, devices, stride=hw + 1)
@@ -194,12 +189,11 @@
         halves = [[], []]
         for h in range(tiles):
             right = right_s[h, here, :]
-            turned = pltpu.roll(right, tokens, 1)
-            for q in range(2):
-                straight, other = (right, turned) if q == 0 else (turned, right)
-                halves[0].append(jnp.where(low, straight, 0.0))
-                halves[1].append(jnp.where(low, 0.0, other))
-        against = jnp.concatenate(halves[0] + halves[1], axis=0).astype(BF16)
+            turned = pltpu.roll(right, tokens, 1).astype(BF16)
+            right = right.astype(BF16)
+            halves[0] += [right * in_low, turned * in_low]
+            halves[1] += [turned * in_high, right * in_high]
+        against = jnp.concatenate(halves[0] + halves[1], axis=0)
         here = pl.ds(c * (tiles * devices + 1), tiles * devices)
         sum_s[here, :] = dot_nt(left.astype(BF16), against)
 
@@ -287,20 +281,18 @@
     def swapped(group):
         return exchange(jnp.concatenate([held[m] for m in group]), 1, devices)
 
-    def project_early(blocks):
-        count = sum(block.shape[0] for block in blocks)
+    factor = VMEM((tiles, devices * (hw + 1), LANES), F32)
+
+    def project_early(blocks, held_there):
+        normed = VMEM((len(held_there), tiles, channels, LANES), BF16)
         return pl.pallas_call(
-            functools.partial(early_kernel, [block.shape[0] for block in blocks]),
-            in_specs=[IN_VMEM] * (len(blocks) + 2),
-            out_shape=(
-                VMEM((count, tiles, hw, LANES), F32),
-                VMEM((count, tiles, hw, LANES), F32),
-                VMEM((count, tiles, channels, LANES), BF16),
-            ),
+            functools.partial(early_kernel, held_there),
+            in_specs=[IN_SMEM] + [IN_VMEM] * (len(blocks) + 2),
+            out_shape=(factor, factor, normed),
             out_specs=(IN_VMEM,) * 3,
             compiler_params=SMALL,
             name="early",
-        )(*blocks, weights[0], weights[3])
+        )(me, *blocks, weights[0], weights[3])
 
     held = {0: packed}
     for m in (12, 8, 4, 2):
@@ -312,18 +304,18 @@
     first = (0, 4, 8, 2, 12)
     last = (14, 6, 10)
     swaps = [swapped(first), swapped(last)]
-    ahead = project_early([held[m] for m in first + last] + swaps[:1])
+    early = first + last + tuple(m ^ 1 for m in first)
+    ahead = project_early([held[m] for m in first + last] + swaps[:1], early)
     arrays = [held[m] for m in first + last] + swaps
     sources = [(m,) for m in first + last]
     sources += [tuple(m ^ 1 for m in group) for group in (first, last)]
-    early_groups = (first + last + sources[-2],)
-    result = pl.pallas_call(
-        functools.partial(both_kernel, rows, tokens, sources, early_groups),
-        out_shape=jax.ShapeDtypeStruct((size, channels), BF16),
+    result, _, _ = pl.pallas_call(
+        functools.partial(both_kernel, rows, tokens, sources, early),
+        out_shape=(jax.ShapeDtypeStruct((size, channels), BF16), factor, factor),
         in_specs=[IN_SMEM] + [IN_VMEM] * (len(arrays) + len(weights) + len(ahead)),
+        out_specs=(pl.BlockSpec(), IN_VMEM, IN_VMEM),
+        input_output_aliases={1 + len(arrays) + len(weights) + n: 1 + n for n in range(2)},
         scratch_shapes=[
-            pltpu.VMEM((tiles, devices * (hw + 1), LANES), F32),
-            pltpu.VMEM((tiles, devices * (hw + 1), LANES), F32),
             pltpu.VMEM((len(last), tiles, channels, LANES), BF16),
             pltpu.VMEM((hw * (devices * tiles + 1), LANES), F32),
             pltpu.VMEM((2 * tiles, channels, LANES), BF16),

time: 24.8 us -> 24.7 us (level)
  no operation moved by 1% of the time
where the time goes in v15:
time: 24.7 us; the launch traced here: 24.5 us
  starting transfers between devices  10.8 us (44%)
  Pallas kernels  8.8 us (36%)
  waiting for transfers between devices  4.77 us (19%)
    ppermute x9, starting transfers between devices, exchange(): return lax.ppermute(block, 'row', pairs)  10.8 us
    pallas_call x1, Pallas kernels, small_plan(): pl.pallas_call(functools.partial(both_kernel, rows, tokens, sources, earl...  5.5 us
    ppermute x9, waiting for transfers between devices, exchange(): return lax.ppermute(block, 'row', pairs)  4.77 us
    pallas_call x1, Pallas kernels, small_plan(): pl.pallas_call(functools.partial(prepare_kernel, rows, tokens), in_specs=...  1.17 us
    pallas_call x1, Pallas kernels, small_plan(): pl.pallas_call(functools.partial(pack_kernel, rows, tokens), out_shape=VM...  1.15 us
    pallas_call x1, Pallas kernels, project_early(): pl.pallas_call(functools.partial(early_kernel, held_there), in_specs=[IN_...  0.98 us
  transfers between devices with their start and end apart: 9, of which 4 were waited for; matrix products, arithmetic and copies ran while one was open for 0% of the time, Pallas kernels for 9%

profile of v15, /device:TPU:0, one launch (start us, length us, event | category | flops | bytes accessed | tf_op | source)
XLA Modules:
  0.0 24.5 jit_solution(8362436147191872195)
XLA Ops:
  0.0 1.2 %pack.1.refs_0_ = bf16[1,272,128]{2,1,0:T(8,128)(2,1)S(1)} custom-call(bf16[4,64,128]{2,1,0:T(8,128)(2,1)} %pair_ref.1, s32[4,64]{1,0:T(4,128)} %mask_ref.1), custom_call_target="tpu_custom_call" | custom-call | tf_op jit(solution)/shard_map/pack/pallas_call | solution.py:258
  1.2 5.1 %collective-permute-start.3 = (bf16[1,272,128]{2,1,0:T(8,128)(2,1)S(1)}, bf16[1,272,128]{2,1,0:T(8,128)(2,1)S(1)}, u32[]{:S(2)}, u32[]{:S(2)}) collective-permute-start(bf16[1,272,128]{2,1,0:T(8,128)(2,1)S(1)} %pack.1.refs_0_), channel_id=1, source_target_pairs={{0,12},{1,13},{2,14},{3,15},{4,8},{5,9},{6,10},{7,11},{8,4},{9,5},... | collective-permute-start | bytes 208904 | tf_op jit(solution)/shard_map/ppermute | solution.py:251
  6.3 1.5 %collective-permute-start.2 = (bf16[1,272,128]{2,1,0:T(8,128)(2,1)S(1)}, bf16[1,272,128]{2,1,0:T(8,128)(2,1)S(1)}, u32[]{:S(2)}, u32[]{:S(2)}) collective-permute-start(bf16[1,272,128]{2,1,0:T(8,128)(2,1)S(1)} %pack.1.refs_0_), channel_id=1, source_target_pairs={{0,2},{1,3},{2,0},{3,1},{4,6},{5,7},{6,4},{7,5},{8,10},{9,11},{10,... | collective-permute-start | bytes 208904 | tf_op jit(solution)/shard_map/ppermute | solution.py:251
  7.8 0.0 collective-permute-start.1
  7.8 0.8 %collective-permute-start = (bf16[1,272,128]{2,1,0:T(8,128)(2,1)S(1)}, bf16[1,272,128]{2,1,0:T(8,128)(2,1)S(1)}, u32[]{:S(2)}, u32[]{:S(2)}) collective-permute-start(bf16[1,272,128]{2,1,0:T(8,128)(2,1)S(1)} %pack.1.refs_0_), channel_id=1, source_target_pairs={{0,4},{1,5},{2,6},{3,7},{4,0},{5,1},{6,2},{7,3},{8,12},{9,13},{10,... | collective-permute-start | bytes 208904 | tf_op jit(solution)/shard_map/ppermute | solution.py:251
  8.6 1.2 %prepare.1 = (bf16[2,256,128]{2,1,0:T(8,128)(2,1)S(1)}, bf16[2,128,128]{2,1,0:T(8,128)(2,1)S(1)}, bf16[2,128,64]{2,1,0:T(8,128)(2,1)S(1)}, f32[2,128,128]{2,1,0:...) custom-call(s32[1]{0:T(128)} %bitcast.me_ref, ...), custom_call_target="tpu_custom_call" | custom-call | tf_op jit(solution)/shard_map/prepare/pallas_call | solution.py:265
  9.8 0.0 collective-permute-done.3.refs_4_
  9.8 0.9 %collective-permute-start.4 = (bf16[1,272,128]{2,1,0:T(8,128)(2,1)S(1)}, bf16[1,272,128]{2,1,0:T(8,128)(2,1)S(1)}, u32[]{:S(2)}, u32[]{:S(2)}) collective-permute-start(bf16[1,272,128]{2,1,0:T(8,128)(2,1)S(1)} %collective-permute-done.3.refs_4_), channel_id=1, source_target_pairs={{0,2},{1,3},{2,0},{3,1},{4,6},{5,7},{6,4},{7,5},{8,10},{9,11},{10,... | collective-permute-start | bytes 208904 | tf_op jit(solution)/shard_map/ppermute | solution.py:251
  10.7 0.0 collective-permute-done.2.refs_3_
  10.7 1.7 %collective-permute-start.5 = (bf16[1,272,128]{2,1,0:T(8,128)(2,1)S(1)}, bf16[1,272,128]{2,1,0:T(8,128)(2,1)S(1)}, u32[]{:S(2)}, u32[]{:S(2)}) collective-permute-start(bf16[1,272,128]{2,1,0:T(8,128)(2,1)S(1)} %collective-permute-done.2.refs_3_), channel_id=1, source_target_pairs={{0,4},{1,5},{2,6},{3,7},{4,0},{5,1},{6,2},{7,3},{8,12},{9,13},{10,... | collective-permute-start | bytes 208904 | tf_op jit(solution)/shard_map/ppermute | solution.py:251
  12.3 0.8 %collective-permute-done.1.refs_2_ = bf16[1,272,128]{2,1,0:T(8,128)(2,1)S(1)} collective-permute-done((bf16[1,272,128]{2,1,0:T(8,128)(2,1)S(1)}, bf16[1,272,128]{2,1,0:T(8,128)(2,1)S(1)}, u32[]{:S(2)}, u32[]{:S(2)}) %collective-permute-start.1) | collective-permute-done | bytes 69664 | tf_op jit(solution)/shard_map/ppermute | solution.py:251
  13.1 0.6 %collective-permute-start.6 = (bf16[1,272,128]{2,1,0:T(8,128)(2,1)S(1)}, bf16[1,272,128]{2,1,0:T(8,128)(2,1)S(1)}, u32[]{:S(2)}, u32[]{:S(2)}) collective-permute-start(bf16[1,272,128]{2,1,0:T(8,128)(2,1)S(1)} %collective-permute-done.1.refs_2_), channel_id=1, source_target_pairs={{0,2},{1,3},{2,0},{3,1},{4,6},{5,7},{6,4},{7,5},{8,10},{9,11},{10,... | collective-permute-start | bytes 208904 | tf_op jit(solution)/shard_map/ppermute | solution.py:251
  13.8 0.0 collective-permute-done.refs_1_
  13.8 0.1 collective-permute-start.7
  13.9 1.1 %collective-permute-done.5.refs_6_ = bf16[1,272,128]{2,1,0:T(8,128)(2,1)S(1)} collective-permute-done((bf16[1,272,128]{2,1,0:T(8,128)(2,1)S(1)}, bf16[1,272,128]{2,1,0:T(8,128)(2,1)S(1)}, u32[]{:S(2)}, u32[]{:S(2)}) %collective-permute-start.5) | collective-permute-done | bytes 69664 | tf_op jit(solution)/shard_map/ppermute | solution.py:251
  15.0 2.5 %collective-permute-done.6.refs_7_ = bf16[1,272,128]{2,1,0:T(8,128)(2,1)S(1)} collective-permute-done((bf16[1,272,128]{2,1,0:T(8,128)(2,1)S(1)}, bf16[1,272,128]{2,1,0:T(8,128)(2,1)S(1)}, u32[]{:S(2)}, u32[]{:S(2)}) %collective-permute-start.6) | collective-permute-done | bytes 69664 | tf_op jit(solution)/shard_map/ppermute | solution.py:251
  17.4 0.0 collective-permute-done.4.refs_5_
  17.5 0.1 collective-permute-start.8
  17.6 0.0 collective-permute-done.7.refs_8_
  17.6 1.0 %early.1 = (f32[2,1040,128]{2,1,0:T(8,128)S(1)}, f32[2,1040,128]{2,1,0:T(8,128)S(1)}, bf16[13,2,128,128]{3,2,1,0:T(8,128)(2,1)S(1)}) custom-call(s32[1]{0:T(128)} %bitcast.me_ref, bf16[1,272,128]{2,1,0:T(8,128)(2,1)S(1)} %pack.1.refs_0_, bf16[1,272,128]{2,1,0:T(8,128)(2,1)S(1)} %collective-permute-done.refs_1_, ...), custom_call_target="tpu_custom_call" | custom-call | tf_op jit(solution)/shard_map/early/pallas_call | solution.py:288
  18.6 0.4 %collective-permute-done.8.refs_9_ = bf16[3,272,128]{2,1,0:T(8,128)(2,1)S(1)} collective-permute-done((bf16[3,272,128]{2,1,0:T(8,128)(2,1)S(1)}, bf16[3,272,128]{2,1,0:T(8,128)(2,1)S(1)}, u32[]{:S(2)}, u32[]{:S(2)}) %collective-permute-start.8) | collective-permute-done | bytes 208928 | tf_op jit(solution)/shard_map/ppermute | solution.py:251
  19.0 5.5 %both.1 = (bf16[256,128]{1,0:T(8,128)(2,1)}, f32[2,1040,128]{2,1,0:T(8,128)S(1)}, f32[2,1040,128]{2,1,0:T(8,128)S(1)}) custom-call(s32[1]{0:T(128)} %bitcast.me_ref, bf16[1,272,128]{2,1,0:T(8,128)(2,1)S(1)} %pack.1.refs_0_, bf16[1,272,128]{2,1,0:T(8,128)(2,1)S(1)} %collective-permute-done.refs_1_, ...), custom_call_target="tpu_custom_call", output_to_operand_aliasing={{1}: (18, {}), {2}: (19, {})} | custom-call | tf_op jit(solution)/shard_map/both/pallas_call | solution.py:312
  (6 shorter events, 0.1 us)
Async XLA Ops:
  1.2 8.6 %collective-permute-start.3 = (bf16[1,272,128]{2,1,0:T(8,128)(2,1)S(1)}, bf16[1,272,128]{2,1,0:T(8,128)(2,1)S(1)}, u32[]{:S(2)}, u32[]{:S(2)}) collective-permute-start(bf16[1,272,128]{2,1,0:T(8,128)(2,1)S(1)} %pack.1.refs_0_), channel_id=1, source_target_pairs={{0,12},{1,13},{2,14},{3,15},{4,8},{5,9},{6,10},{7,11},{8,4},{9,5},... | collective-permute-start | bytes 208904 | tf_op jit(solution)/shard_map/ppermute | solution.py:251
  6.3 4.4 %collective-permute-start.2 = (bf16[1,272,128]{2,1,0:T(8,128)(2,1)S(1)}, bf16[1,272,128]{2,1,0:T(8,128)(2,1)S(1)}, u32[]{:S(2)}, u32[]{:S(2)}) collective-permute-start(bf16[1,272,128]{2,1,0:T(8,128)(2,1)S(1)} %pack.1.refs_0_), channel_id=1, source_target_pairs={{0,2},{1,3},{2,0},{3,1},{4,6},{5,7},{6,4},{7,5},{8,10},{9,11},{10,... | collective-permute-start | bytes 208904 | tf_op jit(solution)/shard_map/ppermute | solution.py:251
  7.8 5.3 %collective-permute-start.1 = (bf16[1,272,128]{2,1,0:T(8,128)(2,1)S(1)}, bf16[1,272,128]{2,1,0:T(8,128)(2,1)S(1)}, u32[]{:S(2)}, u32[]{:S(2)}) collective-permute-start(bf16[1,272,128]{2,1,0:T(8,128)(2,1)S(1)} %pack.1.refs_0_), channel_id=1, source_target_pairs={{0,8},{1,9},{2,10},{3,11},{4,12},{5,13},{6,14},{7,15},{8,0},{9,1},... | collective-permute-start | bytes 208904 | tf_op jit(solution)/shard_map/ppermute | solution.py:251
  7.8 6.0 %collective-permute-start = (bf16[1,272,128]{2,1,0:T(8,128)(2,1)S(1)}, bf16[1,272,128]{2,1,0:T(8,128)(2,1)S(1)}, u32[]{:S(2)}, u32[]{:S(2)}) collective-permute-start(bf16[1,272,128]{2,1,0:T(8,128)(2,1)S(1)} %pack.1.refs_0_), channel_id=1, source_target_pairs={{0,4},{1,5},{2,6},{3,7},{4,0},{5,1},{6,2},{7,3},{8,12},{9,13},{10,... | collective-permute-start | bytes 208904 | tf_op jit(solution)/shard_map/ppermute | solution.py:251
  9.8 7.7 %collective-permute-start.4 = (bf16[1,272,128]{2,1,0:T(8,128)(2,1)S(1)}, bf16[1,272,128]{2,1,0:T(8,128)(2,1)S(1)}, u32[]{:S(2)}, u32[]{:S(2)}) collective-permute-start(bf16[1,272,128]{2,1,0:T(8,128)(2,1)S(1)} %collective-permute-done.3.refs_4_), channel_id=1, source_target_pairs={{0,2},{1,3},{2,0},{3,1},{4,6},{5,7},{6,4},{7,5},{8,10},{9,11},{10,... | collective-permute-start | bytes 208904 | tf_op jit(solution)/shard_map/ppermute | solution.py:251
  10.7 4.3 %collective-permute-start.5 = (bf16[1,272,128]{2,1,0:T(8,128)(2,1)S(1)}, bf16[1,272,128]{2,1,0:T(8,128)(2,1)S(1)}, u32[]{:S(2)}, u32[]{:S(2)}) collective-permute-start(bf16[1,272,128]{2,1,0:T(8,128)(2,1)S(1)} %collective-permute-done.2.refs_3_), channel_id=1, source_target_pairs={{0,4},{1,5},{2,6},{3,7},{4,0},{5,1},{6,2},{7,3},{8,12},{9,13},{10,... | collective-permute-start | bytes 208904 | tf_op jit(solution)/shard_map/ppermute | solution.py:251
  13.1 4.3 %collective-permute-start.6 = (bf16[1,272,128]{2,1,0:T(8,128)(2,1)S(1)}, bf16[1,272,128]{2,1,0:T(8,128)(2,1)S(1)}, u32[]{:S(2)}, u32[]{:S(2)}) collective-permute-start(bf16[1,272,128]{2,1,0:T(8,128)(2,1)S(1)} %collective-permute-done.1.refs_2_), channel_id=1, source_target_pairs={{0,2},{1,3},{2,0},{3,1},{4,6},{5,7},{6,4},{7,5},{8,10},{9,11},{10,... | collective-permute-start | bytes 208904 | tf_op jit(solution)/shard_map/ppermute | solution.py:251
  13.8 3.7 %collective-permute-start.7 = (bf16[5,272,128]{2,1,0:T(8,128)(2,1)S(1)}, bf16[5,272,128]{2,1,0:T(8,128)(2,1)S(1)}, u32[]{:S(2)}, u32[]{:S(2)}) collective-permute-start(bf16[5,272,128]{2,1,0:T(8,128)(2,1)S(1)} %constant_dynamic-update-slice_fusion), channel_id=1, source_target_pairs={{0,1},{1,0},{2,3},{3,2},{4,5},{5,4},{6,7},{7,6},{8,9},{9,8},{10,11... | collective-permute-start | bytes 1044488 | tf_op jit(solution)/shard_map/ppermute | solution.py:251
  17.5 1.5 %collective-permute-start.8 = (bf16[3,272,128]{2,1,0:T(8,128)(2,1)S(1)}, bf16[3,272,128]{2,1,0:T(8,128)(2,1)S(1)}, u32[]{:S(2)}, u32[]{:S(2)}) collective-permute-start(bf16[3,272,128]{2,1,0:T(8,128)(2,1)S(1)} %pad_maximum_fusion), channel_id=1, source_target_pairs={{0,1},{1,0},{2,3},{3,2},{4,5},{5,4},{6,7},{7,6},{8,9},{9,8},{10,11... | collective-permute-start | bytes 626696 | tf_op jit(solution)/shard_map/ppermute | solution.py:251

commit v16 on v14

--- a/solution.py
+++ b/solution.py
@@ -186,7 +186,8 @@
             return ahead[m][2][ahead[m][3], h]
         return normed_s[later.index(m), h]
 
-    low = iota((devices, LANES), 1) < tokens
+    in_low = one_hot(iota((devices, LANES), 1) < tokens)
+    in_high = one_hot(iota((devices, LANES), 1) >= tokens)
 
     def channel_sum(c):
         here = pl.ds(c, devices, stride=hw + 1)
@@ -194,12 +195,11 @@
         halves = [[], []]
         for h in range(tiles):
             right = right_s[h, here, :]
-            turned = pltpu.roll(right, tokens, 1)
-            for q in range(2):
-                straight, other = (right, turned) if q == 0 else (turned, right)
-                halves[0].append(jnp.where(low, straight, 0.0))
-                halves[1].append(jnp.where(low, 0.0, other))
-        against = jnp.concatenate(halves[0] + halves[1], axis=0).astype(BF16)
+            turned = pltpu.roll(right, tokens, 1).astype(BF16)
+            right = right.astype(BF16)
+            halves[0] += [right * in_low, turned * in_low]
+            halves[1] += [turned * in_high, right * in_high]
+        against = jnp.concatenate(halves[0] + halves[1], axis=0)
         here = pl.ds(c * (tiles * devices + 1), tiles * devices)
         sum_s[here, :] = dot_nt(left.astype(BF16), against)
 

time: 24.8 us -> 24.8 us (level)
  no operation moved by 1% of the time
where the time goes in v16:
time: 24.8 us; the launch traced here: 24.6 us
  starting transfers between devices  10.8 us (44%)
  Pallas kernels  8.9 us (36%)
  waiting for transfers between devices  4.76 us (19%)
    ppermute x9, starting transfers between devices, exchange(): return lax.ppermute(block, 'row', pairs)  10.8 us
    pallas_call x1, Pallas kernels, small_plan(): pl.pallas_call(functools.partial(both_kernel, rows, tokens, sources, earl...  5.6 us
    ppermute x9, waiting for transfers between devices, exchange(): return lax.ppermute(block, 'row', pairs)  4.76 us
    pallas_call x1, Pallas kernels, small_plan(): pl.pallas_call(functools.partial(prepare_kernel, rows, tokens), in_specs=...  1.17 us
    pallas_call x1, Pallas kernels, small_plan(): pl.pallas_call(functools.partial(pack_kernel, rows, tokens), out_shape=VM...  1.15 us
    pallas_call x1, Pallas kernels, project_early(): pl.pallas_call(functools.partial(early_kernel, [block.shape[0] for block...  0.99 us
  transfers between devices with their start and end apart: 9, of which 4 were waited for; matrix products, arithmetic and copies ran while one was open for 0% of the time, Pallas kernels for 9%

profile of v16, /device:TPU:0, one launch (start us, length us, event | category | flops | bytes accessed | tf_op | source)
XLA Modules:
  0.0 24.6 jit_solution(10193562644182727160)
XLA Ops:
  0.0 1.2 %pack.1.refs_0_ = bf16[1,272,128]{2,1,0:T(8,128)(2,1)S(1)} custom-call(bf16[4,64,128]{2,1,0:T(8,128)(2,1)} %pair_ref.1, s32[4,64]{1,0:T(4,128)} %mask_ref.1), custom_call_target="tpu_custom_call" | custom-call | tf_op jit(solution)/shard_map/pack/pallas_call | solution.py:264
  1.2 5.1 %collective-permute-start.3 = (bf16[1,272,128]{2,1,0:T(8,128)(2,1)S(1)}, bf16[1,272,128]{2,1,0:T(8,128)(2,1)S(1)}, u32[]{:S(2)}, u32[]{:S(2)}) collective-permute-start(bf16[1,272,128]{2,1,0:T(8,128)(2,1)S(1)} %pack.1.refs_0_), channel_id=1, source_target_pairs={{0,12},{1,13},{2,14},{3,15},{4,8},{5,9},{6,10},{7,11},{8,4},{9,5},... | collective-permute-start | bytes 208904 | tf_op jit(solution)/shard_map/ppermute | solution.py:257
  6.3 1.5 %collective-permute-start.2 = (bf16[1,272,128]{2,1,0:T(8,128)(2,1)S(1)}, bf16[1,272,128]{2,1,0:T(8,128)(2,1)S(1)}, u32[]{:S(2)}, u32[]{:S(2)}) collective-permute-start(bf16[1,272,128]{2,1,0:T(8,128)(2,1)S(1)} %pack.1.refs_0_), channel_id=1, source_target_pairs={{0,2},{1,3},{2,0},{3,1},{4,6},{5,7},{6,4},{7,5},{8,10},{9,11},{10,... | collective-permute-start | bytes 208904 | tf_op jit(solution)/shard_map/ppermute | solution.py:257
  7.8 0.0 collective-permute-start.1
  7.8 0.8 %collective-permute-start = (bf16[1,272,128]{2,1,0:T(8,128)(2,1)S(1)}, bf16[1,272,128]{2,1,0:T(8,128)(2,1)S(1)}, u32[]{:S(2)}, u32[]{:S(2)}) collective-permute-start(bf16[1,272,128]{2,1,0:T(8,128)(2,1)S(1)} %pack.1.refs_0_), channel_id=1, source_target_pairs={{0,4},{1,5},{2,6},{3,7},{4,0},{5,1},{6,2},{7,3},{8,12},{9,13},{10,... | collective-permute-start | bytes 208904 | tf_op jit(solution)/shard_map/ppermute | solution.py:257
  8.6 1.2 %prepare.1 = (bf16[2,256,128]{2,1,0:T(8,128)(2,1)S(1)}, bf16[2,128,128]{2,1,0:T(8,128)(2,1)S(1)}, bf16[2,128,64]{2,1,0:T(8,128)(2,1)S(1)}, f32[2,128,128]{2,1,0:...) custom-call(s32[1]{0:T(128)} %bitcast.me_ref, ...), custom_call_target="tpu_custom_call" | custom-call | tf_op jit(solution)/shard_map/prepare/pallas_call | solution.py:271
  9.8 0.0 collective-permute-done.3.refs_4_
  9.8 0.9 %collective-permute-start.4 = (bf16[1,272,128]{2,1,0:T(8,128)(2,1)S(1)}, bf16[1,272,128]{2,1,0:T(8,128)(2,1)S(1)}, u32[]{:S(2)}, u32[]{:S(2)}) collective-permute-start(bf16[1,272,128]{2,1,0:T(8,128)(2,1)S(1)} %collective-permute-done.3.refs_4_), channel_id=1, source_target_pairs={{0,2},{1,3},{2,0},{3,1},{4,6},{5,7},{6,4},{7,5},{8,10},{9,11},{10,... | collective-permute-start | bytes 208904 | tf_op jit(solution)/shard_map/ppermute | solution.py:257
  10.7 0.0 collective-permute-done.2.refs_3_
  10.7 1.7 %collective-permute-start.5 = (bf16[1,272,128]{2,1,0:T(8,128)(2,1)S(1)}, bf16[1,272,128]{2,1,0:T(8,128)(2,1)S(1)}, u32[]{:S(2)}, u32[]{:S(2)}) collective-permute-start(bf16[1,272,128]{2,1,0:T(8,128)(2,1)S(1)} %collective-permute-done.2.refs_3_), channel_id=1, source_target_pairs={{0,4},{1,5},{2,6},{3,7},{4,0},{5,1},{6,2},{7,3},{8,12},{9,13},{10,... | collective-permute-start | bytes 208904 | tf_op jit(solution)/shard_map/ppermute | solution.py:257
  12.3 0.8 %collective-permute-done.1.refs_2_ = bf16[1,272,128]{2,1,0:T(8,128)(2,1)S(1)} collective-permute-done((bf16[1,272,128]{2,1,0:T(8,128)(2,1)S(1)}, bf16[1,272,128]{2,1,0:T(8,128)(2,1)S(1)}, u32[]{:S(2)}, u32[]{:S(2)}) %collective-permute-start.1) | collective-permute-done | bytes 69664 | tf_op jit(solution)/shard_map/ppermute | solution.py:257
  13.1 0.6 %collective-permute-start.6 = (bf16[1,272,128]{2,1,0:T(8,128)(2,1)S(1)}, bf16[1,272,128]{2,1,0:T(8,128)(2,1)S(1)}, u32[]{:S(2)}, u32[]{:S(2)}) collective-permute-start(bf16[1,272,128]{2,1,0:T(8,128)(2,1)S(1)} %collective-permute-done.1.refs_2_), channel_id=1, source_target_pairs={{0,2},{1,3},{2,0},{3,1},{4,6},{5,7},{6,4},{7,5},{8,10},{9,11},{10,... | collective-permute-start | bytes 208904 | tf_op jit(solution)/shard_map/ppermute | solution.py:257
  13.8 0.0 collective-permute-done.refs_1_
  13.8 0.1 collective-permute-start.7
  13.9 1.1 %collective-permute-done.5.refs_6_ = bf16[1,272,128]{2,1,0:T(8,128)(2,1)S(1)} collective-permute-done((bf16[1,272,128]{2,1,0:T(8,128)(2,1)S(1)}, bf16[1,272,128]{2,1,0:T(8,128)(2,1)S(1)}, u32[]{:S(2)}, u32[]{:S(2)}) %collective-permute-start.5) | collective-permute-done | bytes 69664 | tf_op jit(solution)/shard_map/ppermute | solution.py:257
  15.0 2.5 %collective-permute-done.6.refs_7_ = bf16[1,272,128]{2,1,0:T(8,128)(2,1)S(1)} collective-permute-done((bf16[1,272,128]{2,1,0:T(8,128)(2,1)S(1)}, bf16[1,272,128]{2,1,0:T(8,128)(2,1)S(1)}, u32[]{:S(2)}, u32[]{:S(2)}) %collective-permute-start.6) | collective-permute-done | bytes 69664 | tf_op jit(solution)/shard_map/ppermute | solution.py:257
  17.4 0.0 collective-permute-done.4.refs_5_
  17.5 0.1 collective-permute-start.8
  17.6 0.0 collective-permute-done.7.refs_8_
  17.6 1.0 %early.1 = (f32[13,2,64,128]{3,2,1,0:T(8,128)S(1)}, f32[13,2,64,128]{3,2,1,0:T(8,128)S(1)}, bf16[13,2,128,128]{3,2,1,0:T(8,128)(2,1)S(1)}) custom-call(bf16[1,272,128]{2,1,0:T(8,128)(2,1)S(1)} %pack.1.refs_0_, bf16[1,272,128]{2,1,0:T(8,128)(2,1)S(1)} %collective-permute-done.refs_1_, bf16[1,272,128]{2,1,0:T(8,128)(2,1)S(1)} %collective-permute-done.1.refs_2_, ...), custom_call_target="tpu_custom_call" | custom-call | tf_op jit(solution)/shard_map/early/pallas_call | solution.py:292
  18.6 0.4 %collective-permute-done.8.refs_9_ = bf16[3,272,128]{2,1,0:T(8,128)(2,1)S(1)} collective-permute-done((bf16[3,272,128]{2,1,0:T(8,128)(2,1)S(1)}, bf16[3,272,128]{2,1,0:T(8,128)(2,1)S(1)}, u32[]{:S(2)}, u32[]{:S(2)}) %collective-permute-start.8) | collective-permute-done | bytes 208928 | tf_op jit(solution)/shard_map/ppermute | solution.py:257
  19.0 5.6 %both.1 = bf16[256,128]{1,0:T(8,128)(2,1)} custom-call(s32[1]{0:T(128)} %bitcast.me_ref, bf16[1,272,128]{2,1,0:T(8,128)(2,1)S(1)} %pack.1.refs_0_, bf16[1,272,128]{2,1,0:T(8,128)(2,1)S(1)} %collective-permute-done.refs_1_, bf16[1,272,128]{2,1,0:T(8,128)(2,1)S(1)} %collective-permute-done.1.refs_2_, bf16[1,272,128]{2,1,0:T(8,128)(2,1)S(1)} %collective-permute-done.2.refs_3_, ...), custom_call_target="tpu_custom_call" | custom-call | tf_op jit(solution)/shard_map/both/pallas_call | solution.py:320
  (6 shorter events, 0.1 us)
Async XLA Ops:
  1.2 8.6 %collective-permute-start.3 = (bf16[1,272,128]{2,1,0:T(8,128)(2,1)S(1)}, bf16[1,272,128]{2,1,0:T(8,128)(2,1)S(1)}, u32[]{:S(2)}, u32[]{:S(2)}) collective-permute-start(bf16[1,272,128]{2,1,0:T(8,128)(2,1)S(1)} %pack.1.refs_0_), channel_id=1, source_target_pairs={{0,12},{1,13},{2,14},{3,15},{4,8},{5,9},{6,10},{7,11},{8,4},{9,5},... | collective-permute-start | bytes 208904 | tf_op jit(solution)/shard_map/ppermute | solution.py:257
  6.3 4.4 %collective-permute-start.2 = (bf16[1,272,128]{2,1,0:T(8,128)(2,1)S(1)}, bf16[1,272,128]{2,1,0:T(8,128)(2,1)S(1)}, u32[]{:S(2)}, u32[]{:S(2)}) collective-permute-start(bf16[1,272,128]{2,1,0:T(8,128)(2,1)S(1)} %pack.1.refs_0_), channel_id=1, source_target_pairs={{0,2},{1,3},{2,0},{3,1},{4,6},{5,7},{6,4},{7,5},{8,10},{9,11},{10,... | collective-permute-start | bytes 208904 | tf_op jit(solution)/shard_map/ppermute | solution.py:257
  7.8 5.3 %collective-permute-start.1 = (bf16[1,272,128]{2,1,0:T(8,128)(2,1)S(1)}, bf16[1,272,128]{2,1,0:T(8,128)(2,1)S(1)}, u32[]{:S(2)}, u32[]{:S(2)}) collective-permute-start(bf16[1,272,128]{2,1,0:T(8,128)(2,1)S(1)} %pack.1.refs_0_), channel_id=1, source_target_pairs={{0,8},{1,9},{2,10},{3,11},{4,12},{5,13},{6,14},{7,15},{8,0},{9,1},... | collective-permute-start | bytes 208904 | tf_op jit(solution)/shard_map/ppermute | solution.py:257
  7.8 6.0 %collective-permute-start = (bf16[1,272,128]{2,1,0:T(8,128)(2,1)S(1)}, bf16[1,272,128]{2,1,0:T(8,128)(2,1)S(1)}, u32[]{:S(2)}, u32[]{:S(2)}) collective-permute-start(bf16[1,272,128]{2,1,0:T(8,128)(2,1)S(1)} %pack.1.refs_0_), channel_id=1, source_target_pairs={{0,4},{1,5},{2,6},{3,7},{4,0},{5,1},{6,2},{7,3},{8,12},{9,13},{10,... | collective-permute-start | bytes 208904 | tf_op jit(solution)/shard_map/ppermute | solution.py:257
  9.8 7.7 %collective-permute-start.4 = (bf16[1,272,128]{2,1,0:T(8,128)(2,1)S(1)}, bf16[1,272,128]{2,1,0:T(8,128)(2,1)S(1)}, u32[]{:S(2)}, u32[]{:S(2)}) collective-permute-start(bf16[1,272,128]{2,1,0:T(8,128)(2,1)S(1)} %collective-permute-done.3.refs_4_), channel_id=1, source_target_pairs={{0,2},{1,3},{2,0},{3,1},{4,6},{5,7},{6,4},{7,5},{8,10},{9,11},{10,... | collective-permute-start | bytes 208904 | tf_op jit(solution)/shard_map/ppermute | solution.py:257
  10.7 4.3 %collective-permute-start.5 = (bf16[1,272,128]{2,1,0:T(8,128)(2,1)S(1)}, bf16[1,272,128]{2,1,0:T(8,128)(2,1)S(1)}, u32[]{:S(2)}, u32[]{:S(2)}) collective-permute-start(bf16[1,272,128]{2,1,0:T(8,128)(2,1)S(1)} %collective-permute-done.2.refs_3_), channel_id=1, source_target_pairs={{0,4},{1,5},{2,6},{3,7},{4,0},{5,1},{6,2},{7,3},{8,12},{9,13},{10,... | collective-permute-start | bytes 208904 | tf_op jit(solution)/shard_map/ppermute | solution.py:257
  13.1 4.3 %collective-permute-start.6 = (bf16[1,272,128]{2,1,0:T(8,128)(2,1)S(1)}, bf16[1,272,128]{2,1,0:T(8,128)(2,1)S(1)}, u32[]{:S(2)}, u32[]{:S(2)}) collective-permute-start(bf16[1,272,128]{2,1,0:T(8,128)(2,1)S(1)} %collective-permute-done.1.refs_2_), channel_id=1, source_target_pairs={{0,2},{1,3},{2,0},{3,1},{4,6},{5,7},{6,4},{7,5},{8,10},{9,11},{10,... | collective-permute-start | bytes 208904 | tf_op jit(solution)/shard_map/ppermute | solution.py:257
  13.8 3.7 %collective-permute-start.7 = (bf16[5,272,128]{2,1,0:T(8,128)(2,1)S(1)}, bf16[5,272,128]{2,1,0:T(8,128)(2,1)S(1)}, u32[]{:S(2)}, u32[]{:S(2)}) collective-permute-start(bf16[5,272,128]{2,1,0:T(8,128)(2,1)S(1)} %constant_dynamic-update-slice_fusion), channel_id=1, source_target_pairs={{0,1},{1,0},{2,3},{3,2},{4,5},{5,4},{6,7},{7,6},{8,9},{9,8},{10,11... | collective-permute-start | bytes 1044488 | tf_op jit(solution)/shard_map/ppermute | solution.py:257
  17.5 1.5 %collective-permute-start.8 = (bf16[3,272,128]{2,1,0:T(8,128)(2,1)S(1)}, bf16[3,272,128]{2,1,0:T(8,128)(2,1)S(1)}, u32[]{:S(2)}, u32[]{:S(2)}) collective-permute-start(bf16[3,272,128]{2,1,0:T(8,128)(2,1)S(1)} %pad_maximum_fusion), channel_id=1, source_target_pairs={{0,1},{1,0},{2,3},{3,2},{4,5},{5,4},{6,7},{7,6},{8,9},{9,8},{10,11... | collective-permute-start | bytes 626696 | tf_op jit(solution)/shard_map/ppermute | solution.py:257

commit v17 on v15

--- a/solution.py
+++ b/solution.py
@@ -224,18 +224,18 @@
             second_left_s[here, :] = left.astype(BF16)
             second_right_s[here, :] = right.astype(BF16)
 
-    depth = 2 * hw
+    depth = 4 * hw
     sums = []
     for i in range(0, rows, 2):
         pair = side_by_side([spread_ref[i], spread_ref[i + 1]])
         totals = [jnp.zeros((hw, LANES), F32)] * 2
-        for n in range(devices * tiles // 2):
+        for n in range(devices * tiles // 4):
             here = pl.ds(n * depth, depth)
             spread = dot(second_left_s[here, :], pair)
             right = second_right_s[here, :].astype(F32)
             for o in range(2):
                 terms = tile(spread, o) * right
-                totals[o] = totals[o] + (terms[:hw] + terms[hw:])
+                totals[o] = totals[o] + sum(terms[k * hw : (k + 1) * hw] for k in range(4))
         sums += [total + pltpu.roll(total, tokens, 1) for total in totals]
     low = iota((hw, LANES), 1) < tokens
     for h in range(tiles):

time: 24.7 us -> 24.7 us (level)
  no operation moved by 1% of the time
where the time goes in v17:
time: 24.7 us; the launch traced here: 24.5 us
  starting transfers between devices  10.8 us (44%)
  Pallas kernels  8.82 us (36%)
  waiting for transfers between devices  4.77 us (19%)
    ppermute x9, starting transfers between devices, exchange(): return lax.ppermute(block, 'row', pairs)  10.8 us
    pallas_call x1, Pallas kernels, small_plan(): pl.pallas_call(functools.partial(both_kernel, rows, tokens, sources, earl...  5.52 us
    ppermute x9, waiting for transfers between devices, exchange(): return lax.ppermute(block, 'row', pairs)  4.77 us
    pallas_call x1, Pallas kernels, small_plan(): pl.pallas_call(functools.partial(prepare_kernel, rows, tokens), in_specs=...  1.17 us
    pallas_call x1, Pallas kernels, small_plan(): pl.pallas_call(functools.partial(pack_kernel, rows, tokens), out_shape=VM...  1.15 us
    pallas_call x1, Pallas kernels, project_early(): pl.pallas_call(functools.partial(early_kernel, held_there), in_specs=[IN_...  0.98 us
  transfers between devices with their start and end apart: 9, of which 4 were waited for; matrix products, arithmetic and copies ran while one was open for 0% of the time, Pallas kernels for 9%

profile of v17, /device:TPU:0, one launch (start us, length us, event | category | flops | bytes accessed | tf_op | source)
XLA Modules:
  0.0 24.5 jit_solution(14188614975701464247)
XLA Ops:
  0.0 1.2 %pack.1.refs_0_ = bf16[1,272,128]{2,1,0:T(8,128)(2,1)S(1)} custom-call(bf16[4,64,128]{2,1,0:T(8,128)(2,1)} %pair_ref.1, s32[4,64]{1,0:T(4,128)} %mask_ref.1), custom_call_target="tpu_custom_call" | custom-call | tf_op jit(solution)/shard_map/pack/pallas_call | solution.py:258
  1.2 5.1 %collective-permute-start.3 = (bf16[1,272,128]{2,1,0:T(8,128)(2,1)S(1)}, bf16[1,272,128]{2,1,0:T(8,128)(2,1)S(1)}, u32[]{:S(2)}, u32[]{:S(2)}) collective-permute-start(bf16[1,272,128]{2,1,0:T(8,128)(2,1)S(1)} %pack.1.refs_0_), channel_id=1, source_target_pairs={{0,12},{1,13},{2,14},{3,15},{4,8},{5,9},{6,10},{7,11},{8,4},{9,5},... | collective-permute-start | bytes 208904 | tf_op jit(solution)/shard_map/ppermute | solution.py:251
  6.3 1.5 %collective-permute-start.2 = (bf16[1,272,128]{2,1,0:T(8,128)(2,1)S(1)}, bf16[1,272,128]{2,1,0:T(8,128)(2,1)S(1)}, u32[]{:S(2)}, u32[]{:S(2)}) collective-permute-start(bf16[1,272,128]{2,1,0:T(8,128)(2,1)S(1)} %pack.1.refs_0_), channel_id=1, source_target_pairs={{0,2},{1,3},{2,0},{3,1},{4,6},{5,7},{6,4},{7,5},{8,10},{9,11},{10,... | collective-permute-start | bytes 208904 | tf_op jit(solution)/shard_map/ppermute | solution.py:251
  7.8 0.0 collective-permute-start.1
  7.8 0.8 %collective-permute-start = (bf16[1,272,128]{2,1,0:T(8,128)(2,1)S(1)}, bf16[1,272,128]{2,1,0:T(8,128)(2,1)S(1)}, u32[]{:S(2)}, u32[]{:S(2)}) collective-permute-start(bf16[1,272,128]{2,1,0:T(8,128)(2,1)S(1)} %pack.1.refs_0_), channel_id=1, source_target_pairs={{0,4},{1,5},{2,6},{3,7},{4,0},{5,1},{6,2},{7,3},{8,12},{9,13},{10,... | collective-permute-start | bytes 208904 | tf_op jit(solution)/shard_map/ppermute | solution.py:251
  8.6 1.2 %prepare.1 = (bf16[2,256,128]{2,1,0:T(8,128)(2,1)S(1)}, bf16[2,128,128]{2,1,0:T(8,128)(2,1)S(1)}, bf16[2,128,64]{2,1,0:T(8,128)(2,1)S(1)}, f32[2,128,128]{2,1,0:...) custom-call(s32[1]{0:T(128)} %bitcast.me_ref, ...), custom_call_target="tpu_custom_call" | custom-call | tf_op jit(solution)/shard_map/prepare/pallas_call | solution.py:265
  9.8 0.0 collective-permute-done.3.refs_4_
  9.8 0.9 %collective-permute-start.4 = (bf16[1,272,128]{2,1,0:T(8,128)(2,1)S(1)}, bf16[1,272,128]{2,1,0:T(8,128)(2,1)S(1)}, u32[]{:S(2)}, u32[]{:S(2)}) collective-permute-start(bf16[1,272,128]{2,1,0:T(8,128)(2,1)S(1)} %collective-permute-done.3.refs_4_), channel_id=1, source_target_pairs={{0,2},{1,3},{2,0},{3,1},{4,6},{5,7},{6,4},{7,5},{8,10},{9,11},{10,... | collective-permute-start | bytes 208904 | tf_op jit(solution)/shard_map/ppermute | solution.py:251
  10.7 0.0 collective-permute-done.2.refs_3_
  10.7 1.7 %collective-permute-start.5 = (bf16[1,272,128]{2,1,0:T(8,128)(2,1)S(1)}, bf16[1,272,128]{2,1,0:T(8,128)(2,1)S(1)}, u32[]{:S(2)}, u32[]{:S(2)}) collective-permute-start(bf16[1,272,128]{2,1,0:T(8,128)(2,1)S(1)} %collective-permute-done.2.refs_3_), channel_id=1, source_target_pairs={{0,4},{1,5},{2,6},{3,7},{4,0},{5,1},{6,2},{7,3},{8,12},{9,13},{10,... | collective-permute-start | bytes 208904 | tf_op jit(solution)/shard_map/ppermute | solution.py:251
  12.3 0.8 %collective-permute-done.1.refs_2_ = bf16[1,272,128]{2,1,0:T(8,128)(2,1)S(1)} collective-permute-done((bf16[1,272,128]{2,1,0:T(8,128)(2,1)S(1)}, bf16[1,272,128]{2,1,0:T(8,128)(2,1)S(1)}, u32[]{:S(2)}, u32[]{:S(2)}) %collective-permute-start.1) | collective-permute-done | bytes 69664 | tf_op jit(solution)/shard_map/ppermute | solution.py:251
  13.1 0.6 %collective-permute-start.6 = (bf16[1,272,128]{2,1,0:T(8,128)(2,1)S(1)}, bf16[1,272,128]{2,1,0:T(8,128)(2,1)S(1)}, u32[]{:S(2)}, u32[]{:S(2)}) collective-permute-start(bf16[1,272,128]{2,1,0:T(8,128)(2,1)S(1)} %collective-permute-done.1.refs_2_), channel_id=1, source_target_pairs={{0,2},{1,3},{2,0},{3,1},{4,6},{5,7},{6,4},{7,5},{8,10},{9,11},{10,... | collective-permute-start | bytes 208904 | tf_op jit(solution)/shard_map/ppermute | solution.py:251
  13.8 0.0 collective-permute-done.refs_1_
  13.8 0.1 collective-permute-start.7
  13.9 1.1 %collective-permute-done.5.refs_6_ = bf16[1,272,128]{2,1,0:T(8,128)(2,1)S(1)} collective-permute-done((bf16[1,272,128]{2,1,0:T(8,128)(2,1)S(1)}, bf16[1,272,128]{2,1,0:T(8,128)(2,1)S(1)}, u32[]{:S(2)}, u32[]{:S(2)}) %collective-permute-start.5) | collective-permute-done | bytes 69664 | tf_op jit(solution)/shard_map/ppermute | solution.py:251
  15.0 2.5 %collective-permute-done.6.refs_7_ = bf16[1,272,128]{2,1,0:T(8,128)(2,1)S(1)} collective-permute-done((bf16[1,272,128]{2,1,0:T(8,128)(2,1)S(1)}, bf16[1,272,128]{2,1,0:T(8,128)(2,1)S(1)}, u32[]{:S(2)}, u32[]{:S(2)}) %collective-permute-start.6) | collective-permute-done | bytes 69664 | tf_op jit(solution)/shard_map/ppermute | solution.py:251
  17.4 0.0 collective-permute-done.4.refs_5_
  17.5 0.1 collective-permute-start.8
  17.6 0.0 collective-permute-done.7.refs_8_
  17.6 1.0 %early.1 = (f32[2,1040,128]{2,1,0:T(8,128)S(1)}, f32[2,1040,128]{2,1,0:T(8,128)S(1)}, bf16[13,2,128,128]{3,2,1,0:T(8,128)(2,1)S(1)}) custom-call(s32[1]{0:T(128)} %bitcast.me_ref, bf16[1,272,128]{2,1,0:T(8,128)(2,1)S(1)} %pack.1.refs_0_, bf16[1,272,128]{2,1,0:T(8,128)(2,1)S(1)} %collective-permute-done.refs_1_, ...), custom_call_target="tpu_custom_call" | custom-call | tf_op jit(solution)/shard_map/early/pallas_call | solution.py:288
  18.6 0.4 %collective-permute-done.8.refs_9_ = bf16[3,272,128]{2,1,0:T(8,128)(2,1)S(1)} collective-permute-done((bf16[3,272,128]{2,1,0:T(8,128)(2,1)S(1)}, bf16[3,272,128]{2,1,0:T(8,128)(2,1)S(1)}, u32[]{:S(2)}, u32[]{:S(2)}) %collective-permute-start.8) | collective-permute-done | bytes 208928 | tf_op jit(solution)/shard_map/ppermute | solution.py:251
  19.0 5.5 %both.1 = (bf16[256,128]{1,0:T(8,128)(2,1)}, f32[2,1040,128]{2,1,0:T(8,128)S(1)}, f32[2,1040,128]{2,1,0:T(8,128)S(1)}) custom-call(s32[1]{0:T(128)} %bitcast.me_ref, bf16[1,272,128]{2,1,0:T(8,128)(2,1)S(1)} %pack.1.refs_0_, bf16[1,272,128]{2,1,0:T(8,128)(2,1)S(1)} %collective-permute-done.refs_1_, ...), custom_call_target="tpu_custom_call", output_to_operand_aliasing={{1}: (18, {}), {2}: (19, {})} | custom-call | tf_op jit(solution)/shard_map/both/pallas_call | solution.py:312
  (6 shorter events, 0.1 us)
Async XLA Ops:
  1.2 8.6 %collective-permute-start.3 = (bf16[1,272,128]{2,1,0:T(8,128)(2,1)S(1)}, bf16[1,272,128]{2,1,0:T(8,128)(2,1)S(1)}, u32[]{:S(2)}, u32[]{:S(2)}) collective-permute-start(bf16[1,272,128]{2,1,0:T(8,128)(2,1)S(1)} %pack.1.refs_0_), channel_id=1, source_target_pairs={{0,12},{1,13},{2,14},{3,15},{4,8},{5,9},{6,10},{7,11},{8,4},{9,5},... | collective-permute-start | bytes 208904 | tf_op jit(solution)/shard_map/ppermute | solution.py:251
  6.3 4.4 %collective-permute-start.2 = (bf16[1,272,128]{2,1,0:T(8,128)(2,1)S(1)}, bf16[1,272,128]{2,1,0:T(8,128)(2,1)S(1)}, u32[]{:S(2)}, u32[]{:S(2)}) collective-permute-start(bf16[1,272,128]{2,1,0:T(8,128)(2,1)S(1)} %pack.1.refs_0_), channel_id=1, source_target_pairs={{0,2},{1,3},{2,0},{3,1},{4,6},{5,7},{6,4},{7,5},{8,10},{9,11},{10,... | collective-permute-start | bytes 208904 | tf_op jit(solution)/shard_map/ppermute | solution.py:251
  7.8 5.3 %collective-permute-start.1 = (bf16[1,272,128]{2,1,0:T(8,128)(2,1)S(1)}, bf16[1,272,128]{2,1,0:T(8,128)(2,1)S(1)}, u32[]{:S(2)}, u32[]{:S(2)}) collective-permute-start(bf16[1,272,128]{2,1,0:T(8,128)(2,1)S(1)} %pack.1.refs_0_), channel_id=1, source_target_pairs={{0,8},{1,9},{2,10},{3,11},{4,12},{5,13},{6,14},{7,15},{8,0},{9,1},... | collective-permute-start | bytes 208904 | tf_op jit(solution)/shard_map/ppermute | solution.py:251
  7.8 6.0 %collective-permute-start = (bf16[1,272,128]{2,1,0:T(8,128)(2,1)S(1)}, bf16[1,272,128]{2,1,0:T(8,128)(2,1)S(1)}, u32[]{:S(2)}, u32[]{:S(2)}) collective-permute-start(bf16[1,272,128]{2,1,0:T(8,128)(2,1)S(1)} %pack.1.refs_0_), channel_id=1, source_target_pairs={{0,4},{1,5},{2,6},{3,7},{4,0},{5,1},{6,2},{7,3},{8,12},{9,13},{10,... | collective-permute-start | bytes 208904 | tf_op jit(solution)/shard_map/ppermute | solution.py:251
  9.8 7.7 %collective-permute-start.4 = (bf16[1,272,128]{2,1,0:T(8,128)(2,1)S(1)}, bf16[1,272,128]{2,1,0:T(8,128)(2,1)S(1)}, u32[]{:S(2)}, u32[]{:S(2)}) collective-permute-start(bf16[1,272,128]{2,1,0:T(8,128)(2,1)S(1)} %collective-permute-done.3.refs_4_), channel_id=1, source_target_pairs={{0,2},{1,3},{2,0},{3,1},{4,6},{5,7},{6,4},{7,5},{8,10},{9,11},{10,... | collective-permute-start | bytes 208904 | tf_op jit(solution)/shard_map/ppermute | solution.py:251
  10.7 4.3 %collective-permute-start.5 = (bf16[1,272,128]{2,1,0:T(8,128)(2,1)S(1)}, bf16[1,272,128]{2,1,0:T(8,128)(2,1)S(1)}, u32[]{:S(2)}, u32[]{:S(2)}) collective-permute-start(bf16[1,272,128]{2,1,0:T(8,128)(2,1)S(1)} %collective-permute-done.2.refs_3_), channel_id=1, source_target_pairs={{0,4},{1,5},{2,6},{3,7},{4,0},{5,1},{6,2},{7,3},{8,12},{9,13},{10,... | collective-permute-start | bytes 208904 | tf_op jit(solution)/shard_map/ppermute | solution.py:251
  13.1 4.3 %collective-permute-start.6 = (bf16[1,272,128]{2,1,0:T(8,128)(2,1)S(1)}, bf16[1,272,128]{2,1,0:T(8,128)(2,1)S(1)}, u32[]{:S(2)}, u32[]{:S(2)}) collective-permute-start(bf16[1,272,128]{2,1,0:T(8,128)(2,1)S(1)} %collective-permute-done.1.refs_2_), channel_id=1, source_target_pairs={{0,2},{1,3},{2,0},{3,1},{4,6},{5,7},{6,4},{7,5},{8,10},{9,11},{10,... | collective-permute-start | bytes 208904 | tf_op jit(solution)/shard_map/ppermute | solution.py:251
  13.8 3.7 %collective-permute-start.7 = (bf16[5,272,128]{2,1,0:T(8,128)(2,1)S(1)}, bf16[5,272,128]{2,1,0:T(8,128)(2,1)S(1)}, u32[]{:S(2)}, u32[]{:S(2)}) collective-permute-start(bf16[5,272,128]{2,1,0:T(8,128)(2,1)S(1)} %constant_dynamic-update-slice_fusion), channel_id=1, source_target_pairs={{0,1},{1,0},{2,3},{3,2},{4,5},{5,4},{6,7},{7,6},{8,9},{9,8},{10,11... | collective-permute-start | bytes 1044488 | tf_op jit(solution)/shard_map/ppermute | solution.py:251
  17.5 1.5 %collective-permute-start.8 = (bf16[3,272,128]{2,1,0:T(8,128)(2,1)S(1)}, bf16[3,272,128]{2,1,0:T(8,128)(2,1)S(1)}, u32[]{:S(2)}, u32[]{:S(2)}) collective-permute-start(bf16[3,272,128]{2,1,0:T(8,128)(2,1)S(1)} %pad_maximum_fusion), channel_id=1, source_target_pairs={{0,1},{1,0},{2,3},{3,2},{4,5},{5,4},{6,7},{7,6},{8,9},{9,8},{10,11... | collective-permute-start | bytes 626696 | tf_op jit(solution)/shard_map/ppermute | solution.py:251
